TPU v7x, 512 devices: a whole 4x8x8 slice. The times are simulated.
512 devices in a mesh: blk: 32 (over x, z_lo, core), dp: 16 (over y, z_hi).
Axes of the slice: x: 4, y: 8, z: 8 (z_hi: 2, z_lo: 4; z = z_hi * 4 + z_lo), core: 2. Of those that a mesh axis runs over, the one named last changes fastest.
Arguments:
- inputs: bfloat16 [4096, 2560], P('blk'), may hold values from -400 to 400
- gain: float32 [2560], replicated, may hold values from 0.1 to 1.9
- w_gate: bfloat16 [2560, 6912], P('blk', 'dp'), may hold values from -0.125 to 0.125
- w_up: bfloat16 [2560, 6912], P('blk', 'dp'), may hold values from -0.125 to 0.125
- upstream: bfloat16 [4096, 6912], P('blk', 'dp'), may hold values from -6 to 6
Outputs:
- hidden: bfloat16 [4096, 6912], P('blk', 'dp')
- grad_gate: float32 [2560, 6912], P('blk', 'dp')
- grad_up: float32 [2560, 6912], P('blk', 'dp')
- grad_input: bfloat16 [4096, 2560], P('blk', 'dp')
- grad_gain: float32 [2560], P('dp')
All inputs are finite; a program needn't handle non-finite values.
Results may differ from a plain program's by a relative error of at most 0.028.
Values may be sent and summed in bfloat16 or wider, within the bound.
No kernel may reach another device: no remote copies, remote signals or barrier semaphores. Data moves between devices by JAX's collectives and lax.ppermute only.
A program may use at most 64 MiB of HBM per device.

v0:
```python
import jax
import jax.numpy as jnp
from jax import lax
from jax.sharding import PartitionSpec as P


def passed_along(value, axis, steps):
    count = lax.axis_size(axis)
    pairs = [(source, (source + steps) % count) for source in range(count)]
    return lax.ppermute(value, axis, pairs)


def column_terms(normed, block, block_rows, grad_gating, grad_upper):
    columns = lax.dynamic_slice_in_dim(normed, block * block_rows, block_rows, 1)
    dims = (((0,), (0,)), ((), ()))
    first = lax.dot_general(columns, grad_gating, dims, preferred_element_type=jnp.float32)
    second = lax.dot_general(columns, grad_upper, dims, preferred_element_type=jnp.float32)
    return (first, second)


def per_device(inputs, gain, w_gate, w_up, upstream):
    wide_input = inputs.astype(jnp.float32)
    root_mean = jnp.sqrt(jnp.mean(wide_input * wide_input, axis=1, keepdims=True) + 1e-05)
    unit_input = wide_input / root_mean
    normed = (unit_input * gain).astype(jnp.bfloat16)
    gate_whole, up_whole = (
        lax.all_gather(w_gate, "blk", axis=0, tiled=True),
        lax.all_gather(w_up, "blk", axis=0, tiled=True),
    )
    gate_pre = jnp.dot(normed, gate_whole, preferred_element_type=jnp.float32)
    up_pre = jnp.dot(normed, up_whole, preferred_element_type=jnp.float32)
    sigmoid_gate = jax.nn.sigmoid(gate_pre)
    activated = gate_pre * sigmoid_gate
    hidden = (activated * up_pre).astype(jnp.bfloat16)
    upstream_wide = upstream.astype(jnp.float32)
    grad_upper = (upstream_wide * activated).astype(jnp.bfloat16)
    grad_gating = (
        upstream_wide * up_pre * sigmoid_gate * (1.0 + gate_pre * (1.0 - sigmoid_gate))
    ).astype(jnp.bfloat16)
    local_part = jnp.dot(grad_gating, gate_whole.T, preferred_element_type=jnp.float32) + jnp.dot(
        grad_upper, up_whole.T, preferred_element_type=jnp.float32
    )
    back_normed = lax.optimization_barrier(local_part.astype(jnp.bfloat16)).astype(jnp.float32)
    cycle_size = lax.axis_size("blk")
    block_rows = w_gate.shape[0]
    position = lax.axis_index("blk")

    def advance(index, totals):
        totals = (
            passed_along(totals[0].astype(jnp.bfloat16), "blk", 1).astype(jnp.float32),
            passed_along(totals[1].astype(jnp.bfloat16), "blk", 1).astype(jnp.float32),
        )
        fresh = column_terms(
            normed, (position - index - 1) % cycle_size, block_rows, grad_gating, grad_upper
        )
        return (totals[0] + fresh[0], totals[1] + fresh[1])

    start = column_terms(normed, (position - 1) % cycle_size, block_rows, grad_gating, grad_upper)
    grad_gate, grad_up = lax.fori_loop(1, cycle_size, advance, start)
    feature_count = back_normed.shape[1] // lax.axis_size("dp")
    feature_start = lax.axis_index("dp") * feature_count
    gain_slice = lax.dynamic_slice_in_dim(gain, feature_start, feature_count, 0)
    unit_slice = lax.dynamic_slice_in_dim(unit_input, feature_start, feature_count, 1)
    own_sums = lax.psum_scatter(
        back_normed.astype(jnp.bfloat16), "dp", scatter_dimension=1, tiled=True
    ).astype(jnp.float32)
    token_totals = lax.psum(jnp.sum(own_sums * gain_slice * unit_slice, axis=1), "dp")
    token_means = token_totals[:, None] / back_normed.shape[1]
    grad_input = ((own_sums * gain_slice - unit_slice * token_means) / root_mean).astype(
        jnp.bfloat16
    )
    grad_gain = lax.psum(jnp.sum(own_sums * unit_slice, axis=0), "blk")
    return (hidden, grad_gate, grad_up, grad_input, grad_gain)


def solution(mesh):
    return jax.shard_map(
        per_device,
        mesh=mesh,
        in_specs=(P("blk", None), P(), P("blk", "dp"), P("blk", "dp"), P("blk", "dp")),
        out_specs=(P("blk", "dp"), P("blk", "dp"), P("blk", "dp"), P("blk", "dp"), P("dp")),
        check_vma=False,
    )
```

profile of v0, /device:TPU:1, one launch (start us, length us, event | category | flops | bytes accessed | tf_op | source)
XLA Modules:
  0.0 866.0 jit_solution(12111471976404032301)
XLA Ops:
  10.0 2.5 convert_divide_fusion
  12.5 67.6 %all-gather.3.cloned.1.call-done = bf16[2560,432]{1,0:T(8,128)(2,1)} async-done(((bf16[80,432]{1,0:T(8,128)(2,1)}), bf16[2560,432]{1,0:T(8,128)(2,1)}) %all-gather.3.cloned.1.call-update) | async-done | bytes 2211856 | tf_op jit(solution)/shard_map/all_gather | solution.py:27
  80.1 3.5 fusion.29
  83.6 61.4 %all-gather.5.cloned.1.call-done = bf16[2560,432]{1,0:T(8,128)(2,1)} async-done(((bf16[80,432]{1,0:T(8,128)(2,1)}), bf16[2560,432]{1,0:T(8,128)(2,1)}) %all-gather.5.cloned.1.call-update) | async-done | bytes 2211856 | tf_op jit(solution)/shard_map/all_gather | solution.py:28
  144.9 3.5 fusion.14
  154.0 215.8 %reduce-scatter.4.cloned.1.call-done = bf16[160,128]{1,0:T(8,128)(2,1)} async-done(((bf16[2560,128]{1,0:T(8,128)(2,1)}), bf16[160,128]{1,0:T(8,128)(2,1)}) %reduce-scatter.4.cloned.1.call-update) | async-done | bytes 40976
  371.7 41.7 %psum.14 = f32[128]{0:T(128)S(1)} all-reduce(f32[128]{0:T(128)S(1)} %get-tuple-element.211), channel_id=1, replica_groups=mesh['blk'=32,'dp'=16] {'dp'}, use_global_device_ids=true, to_apply=%region_5.6 | all-reduce | flops 128 | bytes 1024 | tf_op jit(solution)/shard_map/psum | solution.py:67
  415.2 80.2 %psum.15 = f32[160]{0:T(256)} all-reduce(f32[160]{0:T(256)S(1)} %get-tuple-element.210), channel_id=1, replica_groups=mesh['blk'=32,'dp'=16] {'blk'}, use_global_device_ids=true, to_apply=%region_7.8 | all-reduce | flops 160 | bytes 1280 | tf_op jit(solution)/shard_map/psum | solution.py:72
  495.5 363.2 %while.17 = (s32[]{:T(128)}, f32[80,432]{1,0:T(8,128)S(1)}, f32[80,432]{1,0:T(8,128)S(1)}, s32[]{:T(128)}, bf16[128,2560]{1,0:T(8,128)(2,1)S(1)}, /*index=5*/bf1...) while((s32[]{:T(128)}, f32[80,432]{1,0:T(8,128)S(1)}, ...), condition=%wide.region_2.3_spmd, body=%wide.region_1.2_spmd.sunk | while | flops 17902100 | bytes 1736080 | solution.py:59
  495.5 1.9 collective-permute-start
  497.4 1.9 collective-permute-start.1
  501.1 4.3 collective-permute-start
  505.5 1.9 collective-permute-start.1
  507.4 3.3 collective-permute-done
  513.0 1.9 collective-permute-start
  514.9 1.9 collective-permute-start.1
  516.9 5.8 collective-permute-done
  528.8 5.8 collective-permute-done
  536.8 1.9 collective-permute-start
  538.8 1.9 collective-permute-start.1
  540.8 5.8 collective-permute-done
  552.7 5.8 collective-permute-done
  564.6 5.8 collective-permute-done
  576.5 5.8 collective-permute-done
  588.4 5.8 collective-permute-done
  600.4 5.8 collective-permute-done
  612.3 5.8 collective-permute-done
  620.3 1.9 collective-permute-start
  624.2 5.8 collective-permute-done
  636.1 5.8 collective-permute-done
  648.1 5.8 collective-permute-done
  660.0 5.8 collective-permute-done
  671.9 5.8 collective-permute-done
  683.8 5.8 collective-permute-done
  695.7 5.8 collective-permute-done
  707.7 5.8 collective-permute-done
  719.6 5.8 collective-permute-done
  731.5 5.8 collective-permute-done
  743.4 5.8 collective-permute-done
  755.4 5.8 collective-permute-done
  767.3 5.8 collective-permute-done
  779.2 5.8 collective-permute-done
  791.1 5.8 collective-permute-done
  803.1 5.8 collective-permute-done
  815.0 5.8 collective-permute-done
  826.9 5.8 collective-permute-done
  838.8 5.8 collective-permute-done
  850.7 5.8 collective-permute-done
  (238 shorter events, 183.6 us)
Async XLA Ops:
  7.2 72.9 %all-gather.3.cloned.1.call-start = ((), (), s32[]{:S(2)}) async-start(), calls=%async_computation.1 | async-start | bytes 2703360 | tf_op jit(solution)/shard_map/all_gather | solution.py:27
  7.9 137.0 %all-gather.5.cloned.1.call-start = ((), (), s32[]{:S(2)}) async-start(), calls=%async_computation.2 | async-start | bytes 2703360 | tf_op jit(solution)/shard_map/all_gather | solution.py:28
  8.6 361.1 %reduce-scatter.4.cloned.1.call-start = ((), (), s32[]{:S(2)}) async-start(), calls=%async_computation.3 | async-start | bytes 696320
  513.0 9.7 %collective-permute-start = (bf16[80,432]{1,0:T(8,128)(2,1)S(1)}, bf16[80,432]{1,0:T(8,128)(2,1)S(1)}, u32[]{:S(2)}, u32[]{:S(2)}) collective-permute-start(bf16[80,432]{1,0:T(8,128)(2,1)S(1)} %convert_element_type.122), channel_id=1, source_target_pairs={{0,16},{16,32},{32,48},{48,64},{64,80},{80,96},{96,112},{112,128},... | collective-permute-start | bytes 207368 | tf_op jit(solution)/shard_map/while/body/eval_jaxpr/ppermute | solution.py:10
  514.9 9.7 %collective-permute-start.1 = (bf16[80,432]{1,0:T(8,128)(2,1)S(1)}, bf16[80,432]{1,0:T(8,128)(2,1)S(1)}, u32[]{:S(2)}, u32[]{:S(2)}) collective-permute-start(bf16[80,432]{1,0:T(8,128)(2,1)S(1)} %convert_element_type.123), channel_id=1, source_target_pairs={{0,16},{16,32},{32,48},{48,64},{64,80},{80,96},{96,112},{112,128},... | collective-permute-start | bytes 207368 | tf_op jit(solution)/shard_map/while/body/eval_jaxpr/ppermute | solution.py:10
  536.8 9.7 %collective-permute-start = (bf16[80,432]{1,0:T(8,128)(2,1)S(1)}, bf16[80,432]{1,0:T(8,128)(2,1)S(1)}, u32[]{:S(2)}, u32[]{:S(2)}) collective-permute-start(bf16[80,432]{1,0:T(8,128)(2,1)S(1)} %convert_element_type.122), channel_id=1, source_target_pairs={{0,16},{16,32},{32,48},{48,64},{64,80},{80,96},{96,112},{112,128},... | collective-permute-start | bytes 207368 | tf_op jit(solution)/shard_map/while/body/eval_jaxpr/ppermute | solution.py:10
  538.8 9.7 %collective-permute-start.1 = (bf16[80,432]{1,0:T(8,128)(2,1)S(1)}, bf16[80,432]{1,0:T(8,128)(2,1)S(1)}, u32[]{:S(2)}, u32[]{:S(2)}) collective-permute-start(bf16[80,432]{1,0:T(8,128)(2,1)S(1)} %convert_element_type.123), channel_id=1, source_target_pairs={{0,16},{16,32},{32,48},{48,64},{64,80},{80,96},{96,112},{112,128},... | collective-permute-start | bytes 207368 | tf_op jit(solution)/shard_map/while/body/eval_jaxpr/ppermute | solution.py:10
  548.8 9.7 %collective-permute-start = (bf16[80,432]{1,0:T(8,128)(2,1)S(1)}, bf16[80,432]{1,0:T(8,128)(2,1)S(1)}, u32[]{:S(2)}, u32[]{:S(2)}) collective-permute-start(bf16[80,432]{1,0:T(8,128)(2,1)S(1)} %convert_element_type.122), channel_id=1, source_target_pairs={{0,16},{16,32},{32,48},{48,64},{64,80},{80,96},{96,112},{112,128},... | collective-permute-start | bytes 207368 | tf_op jit(solution)/shard_map/while/body/eval_jaxpr/ppermute | solution.py:10
  550.7 9.7 %collective-permute-start.1 = (bf16[80,432]{1,0:T(8,128)(2,1)S(1)}, bf16[80,432]{1,0:T(8,128)(2,1)S(1)}, u32[]{:S(2)}, u32[]{:S(2)}) collective-permute-start(bf16[80,432]{1,0:T(8,128)(2,1)S(1)} %convert_element_type.123), channel_id=1, source_target_pairs={{0,16},{16,32},{32,48},{48,64},{64,80},{80,96},{96,112},{112,128},... | collective-permute-start | bytes 207368 | tf_op jit(solution)/shard_map/while/body/eval_jaxpr/ppermute | solution.py:10
  560.7 9.7 %collective-permute-start = (bf16[80,432]{1,0:T(8,128)(2,1)S(1)}, bf16[80,432]{1,0:T(8,128)(2,1)S(1)}, u32[]{:S(2)}, u32[]{:S(2)}) collective-permute-start(bf16[80,432]{1,0:T(8,128)(2,1)S(1)} %convert_element_type.122), channel_id=1, source_target_pairs={{0,16},{16,32},{32,48},{48,64},{64,80},{80,96},{96,112},{112,128},... | collective-permute-start | bytes 207368 | tf_op jit(solution)/shard_map/while/body/eval_jaxpr/ppermute | solution.py:10
  562.6 9.7 %collective-permute-start.1 = (bf16[80,432]{1,0:T(8,128)(2,1)S(1)}, bf16[80,432]{1,0:T(8,128)(2,1)S(1)}, u32[]{:S(2)}, u32[]{:S(2)}) collective-permute-start(bf16[80,432]{1,0:T(8,128)(2,1)S(1)} %convert_element_type.123), channel_id=1, source_target_pairs={{0,16},{16,32},{32,48},{48,64},{64,80},{80,96},{96,112},{112,128},... | collective-permute-start | bytes 207368 | tf_op jit(solution)/shard_map/while/body/eval_jaxpr/ppermute | solution.py:10
  572.6 9.7 %collective-permute-start = (bf16[80,432]{1,0:T(8,128)(2,1)S(1)}, bf16[80,432]{1,0:T(8,128)(2,1)S(1)}, u32[]{:S(2)}, u32[]{:S(2)}) collective-permute-start(bf16[80,432]{1,0:T(8,128)(2,1)S(1)} %convert_element_type.122), channel_id=1, source_target_pairs={{0,16},{16,32},{32,48},{48,64},{64,80},{80,96},{96,112},{112,128},... | collective-permute-start | bytes 207368 | tf_op jit(solution)/shard_map/while/body/eval_jaxpr/ppermute | solution.py:10
  574.6 9.7 %collective-permute-start.1 = (bf16[80,432]{1,0:T(8,128)(2,1)S(1)}, bf16[80,432]{1,0:T(8,128)(2,1)S(1)}, u32[]{:S(2)}, u32[]{:S(2)}) collective-permute-start(bf16[80,432]{1,0:T(8,128)(2,1)S(1)} %convert_element_type.123), channel_id=1, source_target_pairs={{0,16},{16,32},{32,48},{48,64},{64,80},{80,96},{96,112},{112,128},... | collective-permute-start | bytes 207368 | tf_op jit(solution)/shard_map/while/body/eval_jaxpr/ppermute | solution.py:10
  584.5 9.7 %collective-permute-start = (bf16[80,432]{1,0:T(8,128)(2,1)S(1)}, bf16[80,432]{1,0:T(8,128)(2,1)S(1)}, u32[]{:S(2)}, u32[]{:S(2)}) collective-permute-start(bf16[80,432]{1,0:T(8,128)(2,1)S(1)} %convert_element_type.122), channel_id=1, source_target_pairs={{0,16},{16,32},{32,48},{48,64},{64,80},{80,96},{96,112},{112,128},... | collective-permute-start | bytes 207368 | tf_op jit(solution)/shard_map/while/body/eval_jaxpr/ppermute | solution.py:10
  586.5 9.7 %collective-permute-start.1 = (bf16[80,432]{1,0:T(8,128)(2,1)S(1)}, bf16[80,432]{1,0:T(8,128)(2,1)S(1)}, u32[]{:S(2)}, u32[]{:S(2)}) collective-permute-start(bf16[80,432]{1,0:T(8,128)(2,1)S(1)} %convert_element_type.123), channel_id=1, source_target_pairs={{0,16},{16,32},{32,48},{48,64},{64,80},{80,96},{96,112},{112,128},... | collective-permute-start | bytes 207368 | tf_op jit(solution)/shard_map/while/body/eval_jaxpr/ppermute | solution.py:10
  608.4 9.7 %collective-permute-start = (bf16[80,432]{1,0:T(8,128)(2,1)S(1)}, bf16[80,432]{1,0:T(8,128)(2,1)S(1)}, u32[]{:S(2)}, u32[]{:S(2)}) collective-permute-start(bf16[80,432]{1,0:T(8,128)(2,1)S(1)} %convert_element_type.122), channel_id=1, source_target_pairs={{0,16},{16,32},{32,48},{48,64},{64,80},{80,96},{96,112},{112,128},... | collective-permute-start | bytes 207368 | tf_op jit(solution)/shard_map/while/body/eval_jaxpr/ppermute | solution.py:10
  610.3 9.7 %collective-permute-start.1 = (bf16[80,432]{1,0:T(8,128)(2,1)S(1)}, bf16[80,432]{1,0:T(8,128)(2,1)S(1)}, u32[]{:S(2)}, u32[]{:S(2)}) collective-permute-start(bf16[80,432]{1,0:T(8,128)(2,1)S(1)} %convert_element_type.123), channel_id=1, source_target_pairs={{0,16},{16,32},{32,48},{48,64},{64,80},{80,96},{96,112},{112,128},... | collective-permute-start | bytes 207368 | tf_op jit(solution)/shard_map/while/body/eval_jaxpr/ppermute | solution.py:10
  620.3 9.7 %collective-permute-start = (bf16[80,432]{1,0:T(8,128)(2,1)S(1)}, bf16[80,432]{1,0:T(8,128)(2,1)S(1)}, u32[]{:S(2)}, u32[]{:S(2)}) collective-permute-start(bf16[80,432]{1,0:T(8,128)(2,1)S(1)} %convert_element_type.122), channel_id=1, source_target_pairs={{0,16},{16,32},{32,48},{48,64},{64,80},{80,96},{96,112},{112,128},... | collective-permute-start | bytes 207368 | tf_op jit(solution)/shard_map/while/body/eval_jaxpr/ppermute | solution.py:10
  622.3 9.7 %collective-permute-start.1 = (bf16[80,432]{1,0:T(8,128)(2,1)S(1)}, bf16[80,432]{1,0:T(8,128)(2,1)S(1)}, u32[]{:S(2)}, u32[]{:S(2)}) collective-permute-start(bf16[80,432]{1,0:T(8,128)(2,1)S(1)} %convert_element_type.123), channel_id=1, source_target_pairs={{0,16},{16,32},{32,48},{48,64},{64,80},{80,96},{96,112},{112,128},... | collective-permute-start | bytes 207368 | tf_op jit(solution)/shard_map/while/body/eval_jaxpr/ppermute | solution.py:10
  632.2 9.7 %collective-permute-start = (bf16[80,432]{1,0:T(8,128)(2,1)S(1)}, bf16[80,432]{1,0:T(8,128)(2,1)S(1)}, u32[]{:S(2)}, u32[]{:S(2)}) collective-permute-start(bf16[80,432]{1,0:T(8,128)(2,1)S(1)} %convert_element_type.122), channel_id=1, source_target_pairs={{0,16},{16,32},{32,48},{48,64},{64,80},{80,96},{96,112},{112,128},... | collective-permute-start | bytes 207368 | tf_op jit(solution)/shard_map/while/body/eval_jaxpr/ppermute | solution.py:10
  634.2 9.7 %collective-permute-start.1 = (bf16[80,432]{1,0:T(8,128)(2,1)S(1)}, bf16[80,432]{1,0:T(8,128)(2,1)S(1)}, u32[]{:S(2)}, u32[]{:S(2)}) collective-permute-start(bf16[80,432]{1,0:T(8,128)(2,1)S(1)} %convert_element_type.123), channel_id=1, source_target_pairs={{0,16},{16,32},{32,48},{48,64},{64,80},{80,96},{96,112},{112,128},... | collective-permute-start | bytes 207368 | tf_op jit(solution)/shard_map/while/body/eval_jaxpr/ppermute | solution.py:10
  644.1 9.7 %collective-permute-start = (bf16[80,432]{1,0:T(8,128)(2,1)S(1)}, bf16[80,432]{1,0:T(8,128)(2,1)S(1)}, u32[]{:S(2)}, u32[]{:S(2)}) collective-permute-start(bf16[80,432]{1,0:T(8,128)(2,1)S(1)} %convert_element_type.122), channel_id=1, source_target_pairs={{0,16},{16,32},{32,48},{48,64},{64,80},{80,96},{96,112},{112,128},... | collective-permute-start | bytes 207368 | tf_op jit(solution)/shard_map/while/body/eval_jaxpr/ppermute | solution.py:10
  646.1 9.7 %collective-permute-start.1 = (bf16[80,432]{1,0:T(8,128)(2,1)S(1)}, bf16[80,432]{1,0:T(8,128)(2,1)S(1)}, u32[]{:S(2)}, u32[]{:S(2)}) collective-permute-start(bf16[80,432]{1,0:T(8,128)(2,1)S(1)} %convert_element_type.123), channel_id=1, source_target_pairs={{0,16},{16,32},{32,48},{48,64},{64,80},{80,96},{96,112},{112,128},... | collective-permute-start | bytes 207368 | tf_op jit(solution)/shard_map/while/body/eval_jaxpr/ppermute | solution.py:10
  656.1 9.7 %collective-permute-start = (bf16[80,432]{1,0:T(8,128)(2,1)S(1)}, bf16[80,432]{1,0:T(8,128)(2,1)S(1)}, u32[]{:S(2)}, u32[]{:S(2)}) collective-permute-start(bf16[80,432]{1,0:T(8,128)(2,1)S(1)} %convert_element_type.122), channel_id=1, source_target_pairs={{0,16},{16,32},{32,48},{48,64},{64,80},{80,96},{96,112},{112,128},... | collective-permute-start | bytes 207368 | tf_op jit(solution)/shard_map/while/body/eval_jaxpr/ppermute | solution.py:10
  658.0 9.7 %collective-permute-start.1 = (bf16[80,432]{1,0:T(8,128)(2,1)S(1)}, bf16[80,432]{1,0:T(8,128)(2,1)S(1)}, u32[]{:S(2)}, u32[]{:S(2)}) collective-permute-start(bf16[80,432]{1,0:T(8,128)(2,1)S(1)} %convert_element_type.123), channel_id=1, source_target_pairs={{0,16},{16,32},{32,48},{48,64},{64,80},{80,96},{96,112},{112,128},... | collective-permute-start | bytes 207368 | tf_op jit(solution)/shard_map/while/body/eval_jaxpr/ppermute | solution.py:10
  668.0 9.7 %collective-permute-start = (bf16[80,432]{1,0:T(8,128)(2,1)S(1)}, bf16[80,432]{1,0:T(8,128)(2,1)S(1)}, u32[]{:S(2)}, u32[]{:S(2)}) collective-permute-start(bf16[80,432]{1,0:T(8,128)(2,1)S(1)} %convert_element_type.122), channel_id=1, source_target_pairs={{0,16},{16,32},{32,48},{48,64},{64,80},{80,96},{96,112},{112,128},... | collective-permute-start | bytes 207368 | tf_op jit(solution)/shard_map/while/body/eval_jaxpr/ppermute | solution.py:10
  669.9 9.7 %collective-permute-start.1 = (bf16[80,432]{1,0:T(8,128)(2,1)S(1)}, bf16[80,432]{1,0:T(8,128)(2,1)S(1)}, u32[]{:S(2)}, u32[]{:S(2)}) collective-permute-start(bf16[80,432]{1,0:T(8,128)(2,1)S(1)} %convert_element_type.123), channel_id=1, source_target_pairs={{0,16},{16,32},{32,48},{48,64},{64,80},{80,96},{96,112},{112,128},... | collective-permute-start | bytes 207368 | tf_op jit(solution)/shard_map/while/body/eval_jaxpr/ppermute | solution.py:10
  691.8 9.7 %collective-permute-start = (bf16[80,432]{1,0:T(8,128)(2,1)S(1)}, bf16[80,432]{1,0:T(8,128)(2,1)S(1)}, u32[]{:S(2)}, u32[]{:S(2)}) collective-permute-start(bf16[80,432]{1,0:T(8,128)(2,1)S(1)} %convert_element_type.122), channel_id=1, source_target_pairs={{0,16},{16,32},{32,48},{48,64},{64,80},{80,96},{96,112},{112,128},... | collective-permute-start | bytes 207368 | tf_op jit(solution)/shard_map/while/body/eval_jaxpr/ppermute | solution.py:10
  693.8 9.7 %collective-permute-start.1 = (bf16[80,432]{1,0:T(8,128)(2,1)S(1)}, bf16[80,432]{1,0:T(8,128)(2,1)S(1)}, u32[]{:S(2)}, u32[]{:S(2)}) collective-permute-start(bf16[80,432]{1,0:T(8,128)(2,1)S(1)} %convert_element_type.123), channel_id=1, source_target_pairs={{0,16},{16,32},{32,48},{48,64},{64,80},{80,96},{96,112},{112,128},... | collective-permute-start | bytes 207368 | tf_op jit(solution)/shard_map/while/body/eval_jaxpr/ppermute | solution.py:10
  703.8 9.7 %collective-permute-start = (bf16[80,432]{1,0:T(8,128)(2,1)S(1)}, bf16[80,432]{1,0:T(8,128)(2,1)S(1)}, u32[]{:S(2)}, u32[]{:S(2)}) collective-permute-start(bf16[80,432]{1,0:T(8,128)(2,1)S(1)} %convert_element_type.122), channel_id=1, source_target_pairs={{0,16},{16,32},{32,48},{48,64},{64,80},{80,96},{96,112},{112,128},... | collective-permute-start | bytes 207368 | tf_op jit(solution)/shard_map/while/body/eval_jaxpr/ppermute | solution.py:10
  705.7 9.7 %collective-permute-start.1 = (bf16[80,432]{1,0:T(8,128)(2,1)S(1)}, bf16[80,432]{1,0:T(8,128)(2,1)S(1)}, u32[]{:S(2)}, u32[]{:S(2)}) collective-permute-start(bf16[80,432]{1,0:T(8,128)(2,1)S(1)} %convert_element_type.123), channel_id=1, source_target_pairs={{0,16},{16,32},{32,48},{48,64},{64,80},{80,96},{96,112},{112,128},... | collective-permute-start | bytes 207368 | tf_op jit(solution)/shard_map/while/body/eval_jaxpr/ppermute | solution.py:10
  715.7 9.7 %collective-permute-start = (bf16[80,432]{1,0:T(8,128)(2,1)S(1)}, bf16[80,432]{1,0:T(8,128)(2,1)S(1)}, u32[]{:S(2)}, u32[]{:S(2)}) collective-permute-start(bf16[80,432]{1,0:T(8,128)(2,1)S(1)} %convert_element_type.122), channel_id=1, source_target_pairs={{0,16},{16,32},{32,48},{48,64},{64,80},{80,96},{96,112},{112,128},... | collective-permute-start | bytes 207368 | tf_op jit(solution)/shard_map/while/body/eval_jaxpr/ppermute | solution.py:10
  717.6 9.7 %collective-permute-start.1 = (bf16[80,432]{1,0:T(8,128)(2,1)S(1)}, bf16[80,432]{1,0:T(8,128)(2,1)S(1)}, u32[]{:S(2)}, u32[]{:S(2)}) collective-permute-start(bf16[80,432]{1,0:T(8,128)(2,1)S(1)} %convert_element_type.123), channel_id=1, source_target_pairs={{0,16},{16,32},{32,48},{48,64},{64,80},{80,96},{96,112},{112,128},... | collective-permute-start | bytes 207368 | tf_op jit(solution)/shard_map/while/body/eval_jaxpr/ppermute | solution.py:10
  727.6 9.7 %collective-permute-start = (bf16[80,432]{1,0:T(8,128)(2,1)S(1)}, bf16[80,432]{1,0:T(8,128)(2,1)S(1)}, u32[]{:S(2)}, u32[]{:S(2)}) collective-permute-start(bf16[80,432]{1,0:T(8,128)(2,1)S(1)} %convert_element_type.122), channel_id=1, source_target_pairs={{0,16},{16,32},{32,48},{48,64},{64,80},{80,96},{96,112},{112,128},... | collective-permute-start | bytes 207368 | tf_op jit(solution)/shard_map/while/body/eval_jaxpr/ppermute | solution.py:10
  729.6 9.7 %collective-permute-start.1 = (bf16[80,432]{1,0:T(8,128)(2,1)S(1)}, bf16[80,432]{1,0:T(8,128)(2,1)S(1)}, u32[]{:S(2)}, u32[]{:S(2)}) collective-permute-start(bf16[80,432]{1,0:T(8,128)(2,1)S(1)} %convert_element_type.123), channel_id=1, source_target_pairs={{0,16},{16,32},{32,48},{48,64},{64,80},{80,96},{96,112},{112,128},... | collective-permute-start | bytes 207368 | tf_op jit(solution)/shard_map/while/body/eval_jaxpr/ppermute | solution.py:10
  739.5 9.7 %collective-permute-start = (bf16[80,432]{1,0:T(8,128)(2,1)S(1)}, bf16[80,432]{1,0:T(8,128)(2,1)S(1)}, u32[]{:S(2)}, u32[]{:S(2)}) collective-permute-start(bf16[80,432]{1,0:T(8,128)(2,1)S(1)} %convert_element_type.122), channel_id=1, source_target_pairs={{0,16},{16,32},{32,48},{48,64},{64,80},{80,96},{96,112},{112,128},... | collective-permute-start | bytes 207368 | tf_op jit(solution)/shard_map/while/body/eval_jaxpr/ppermute | solution.py:10
  741.5 9.7 %collective-permute-start.1 = (bf16[80,432]{1,0:T(8,128)(2,1)S(1)}, bf16[80,432]{1,0:T(8,128)(2,1)S(1)}, u32[]{:S(2)}, u32[]{:S(2)}) collective-permute-start(bf16[80,432]{1,0:T(8,128)(2,1)S(1)} %convert_element_type.123), channel_id=1, source_target_pairs={{0,16},{16,32},{32,48},{48,64},{64,80},{80,96},{96,112},{112,128},... | collective-permute-start | bytes 207368 | tf_op jit(solution)/shard_map/while/body/eval_jaxpr/ppermute | solution.py:10
  763.4 9.7 %collective-permute-start = (bf16[80,432]{1,0:T(8,128)(2,1)S(1)}, bf16[80,432]{1,0:T(8,128)(2,1)S(1)}, u32[]{:S(2)}, u32[]{:S(2)}) collective-permute-start(bf16[80,432]{1,0:T(8,128)(2,1)S(1)} %convert_element_type.122), channel_id=1, source_target_pairs={{0,16},{16,32},{32,48},{48,64},{64,80},{80,96},{96,112},{112,128},... | collective-permute-start | bytes 207368 | tf_op jit(solution)/shard_map/while/body/eval_jaxpr/ppermute | solution.py:10
  765.3 9.7 %collective-permute-start.1 = (bf16[80,432]{1,0:T(8,128)(2,1)S(1)}, bf16[80,432]{1,0:T(8,128)(2,1)S(1)}, u32[]{:S(2)}, u32[]{:S(2)}) collective-permute-start(bf16[80,432]{1,0:T(8,128)(2,1)S(1)} %convert_element_type.123), channel_id=1, source_target_pairs={{0,16},{16,32},{32,48},{48,64},{64,80},{80,96},{96,112},{112,128},... | collective-permute-start | bytes 207368 | tf_op jit(solution)/shard_map/while/body/eval_jaxpr/ppermute | solution.py:10
  775.3 9.7 %collective-permute-start = (bf16[80,432]{1,0:T(8,128)(2,1)S(1)}, bf16[80,432]{1,0:T(8,128)(2,1)S(1)}, u32[]{:S(2)}, u32[]{:S(2)}) collective-permute-start(bf16[80,432]{1,0:T(8,128)(2,1)S(1)} %convert_element_type.122), channel_id=1, source_target_pairs={{0,16},{16,32},{32,48},{48,64},{64,80},{80,96},{96,112},{112,128},... | collective-permute-start | bytes 207368 | tf_op jit(solution)/shard_map/while/body/eval_jaxpr/ppermute | solution.py:10
  777.2 9.7 %collective-permute-start.1 = (bf16[80,432]{1,0:T(8,128)(2,1)S(1)}, bf16[80,432]{1,0:T(8,128)(2,1)S(1)}, u32[]{:S(2)}, u32[]{:S(2)}) collective-permute-start(bf16[80,432]{1,0:T(8,128)(2,1)S(1)} %convert_element_type.123), channel_id=1, source_target_pairs={{0,16},{16,32},{32,48},{48,64},{64,80},{80,96},{96,112},{112,128},... | collective-permute-start | bytes 207368 | tf_op jit(solution)/shard_map/while/body/eval_jaxpr/ppermute | solution.py:10
  787.2 9.7 %collective-permute-start = (bf16[80,432]{1,0:T(8,128)(2,1)S(1)}, bf16[80,432]{1,0:T(8,128)(2,1)S(1)}, u32[]{:S(2)}, u32[]{:S(2)}) collective-permute-start(bf16[80,432]{1,0:T(8,128)(2,1)S(1)} %convert_element_type.122), channel_id=1, source_target_pairs={{0,16},{16,32},{32,48},{48,64},{64,80},{80,96},{96,112},{112,128},... | collective-permute-start | bytes 207368 | tf_op jit(solution)/shard_map/while/body/eval_jaxpr/ppermute | solution.py:10
  789.2 9.7 %collective-permute-start.1 = (bf16[80,432]{1,0:T(8,128)(2,1)S(1)}, bf16[80,432]{1,0:T(8,128)(2,1)S(1)}, u32[]{:S(2)}, u32[]{:S(2)}) collective-permute-start(bf16[80,432]{1,0:T(8,128)(2,1)S(1)} %convert_element_type.123), channel_id=1, source_target_pairs={{0,16},{16,32},{32,48},{48,64},{64,80},{80,96},{96,112},{112,128},... | collective-permute-start | bytes 207368 | tf_op jit(solution)/shard_map/while/body/eval_jaxpr/ppermute | solution.py:10
  799.1 9.7 %collective-permute-start = (bf16[80,432]{1,0:T(8,128)(2,1)S(1)}, bf16[80,432]{1,0:T(8,128)(2,1)S(1)}, u32[]{:S(2)}, u32[]{:S(2)}) collective-permute-start(bf16[80,432]{1,0:T(8,128)(2,1)S(1)} %convert_element_type.122), channel_id=1, source_target_pairs={{0,16},{16,32},{32,48},{48,64},{64,80},{80,96},{96,112},{112,128},... | collective-permute-start | bytes 207368 | tf_op jit(solution)/shard_map/while/body/eval_jaxpr/ppermute | solution.py:10
  801.1 9.7 %collective-permute-start.1 = (bf16[80,432]{1,0:T(8,128)(2,1)S(1)}, bf16[80,432]{1,0:T(8,128)(2,1)S(1)}, u32[]{:S(2)}, u32[]{:S(2)}) collective-permute-start(bf16[80,432]{1,0:T(8,128)(2,1)S(1)} %convert_element_type.123), channel_id=1, source_target_pairs={{0,16},{16,32},{32,48},{48,64},{64,80},{80,96},{96,112},{112,128},... | collective-permute-start | bytes 207368 | tf_op jit(solution)/shard_map/while/body/eval_jaxpr/ppermute | solution.py:10
  811.1 9.7 %collective-permute-start = (bf16[80,432]{1,0:T(8,128)(2,1)S(1)}, bf16[80,432]{1,0:T(8,128)(2,1)S(1)}, u32[]{:S(2)}, u32[]{:S(2)}) collective-permute-start(bf16[80,432]{1,0:T(8,128)(2,1)S(1)} %convert_element_type.122), channel_id=1, source_target_pairs={{0,16},{16,32},{32,48},{48,64},{64,80},{80,96},{96,112},{112,128},... | collective-permute-start | bytes 207368 | tf_op jit(solution)/shard_map/while/body/eval_jaxpr/ppermute | solution.py:10
  813.0 9.7 %collective-permute-start.1 = (bf16[80,432]{1,0:T(8,128)(2,1)S(1)}, bf16[80,432]{1,0:T(8,128)(2,1)S(1)}, u32[]{:S(2)}, u32[]{:S(2)}) collective-permute-start(bf16[80,432]{1,0:T(8,128)(2,1)S(1)} %convert_element_type.123), channel_id=1, source_target_pairs={{0,16},{16,32},{32,48},{48,64},{64,80},{80,96},{96,112},{112,128},... | collective-permute-start | bytes 207368 | tf_op jit(solution)/shard_map/while/body/eval_jaxpr/ppermute | solution.py:10
  834.9 9.7 %collective-permute-start = (bf16[80,432]{1,0:T(8,128)(2,1)S(1)}, bf16[80,432]{1,0:T(8,128)(2,1)S(1)}, u32[]{:S(2)}, u32[]{:S(2)}) collective-permute-start(bf16[80,432]{1,0:T(8,128)(2,1)S(1)} %convert_element_type.122), channel_id=1, source_target_pairs={{0,16},{16,32},{32,48},{48,64},{64,80},{80,96},{96,112},{112,128},... | collective-permute-start | bytes 207368 | tf_op jit(solution)/shard_map/while/body/eval_jaxpr/ppermute | solution.py:10
  (21 other events, 217.8 us)
Sparse Core Ops, SparseCore 0:
  10.1 69.8 all-gather.2
  82.2 62.6 all-gather.4
  152.5 217.2 reduce-scatter.3
where the time goes:
time: 872 us; the launch traced here: 866 us
  waiting for transfers between devices  568 us (65%)
  starting transfers between devices  122 us (14%)
  blocking collectives  122 us (14%)
  matrix products  26.4 us (3%)
  between operations  13.9 us (2%)
    ppermute x62, waiting for transfers between devices, passed_along(): return lax.ppermute(value, axis, pairs)  222 us
    unnamed x4, waiting for transfers between devices  217 us
    ppermute x62, starting transfers between devices, passed_along(): return lax.ppermute(value, axis, pairs)  121 us
    psum x1, blocking collectives, per_device(): grad_gain = lax.psum(jnp.sum(own_sums * unit_slice, axis=0), 'blk')  80.2 us
    all_gather x1, waiting for transfers between devices, per_device(): lax.all_gather(w_gate, 'blk', axis=0, tiled=True)  67.6 us
    all_gather x1, waiting for transfers between devices, per_device(): lax.all_gather(w_up, 'blk', axis=0, tiled=True)  61.4 us
    psum x1, blocking collectives, per_device(): lax.psum(jnp.sum(own_sums * gain_slice * unit_slice, axis=1), 'dp')  41.7 us
  transfers between devices with their start and end apart: 65, of which 64 were waited for; matrix products, arithmetic and copies ran while one was open for 2% of the time, Pallas kernels for 0%

commit v1 on v0

v1 whole, which is shorter than its diff:
```python
import jax
import jax.numpy as jnp
from jax import lax
from jax.sharding import PartitionSpec as P

BF = jnp.bfloat16
F32 = jnp.float32
NX, NZ, NC = 4, 4, 2


def place(x, z, c):
    return (x * NZ + z) * NC + c


def pairs(move):
    return [
        (place(x, z, c), place(*move(x, z, c)))
        for x in range(NX)
        for z in range(NZ)
        for c in range(NC)
    ]


def swap_core(value):
    return lax.ppermute(value, "blk", pairs(lambda x, z, c: (x, z, 1 - c)))


def shift_x(value, steps):
    return lax.ppermute(value, "blk", pairs(lambda x, z, c: ((x + steps) % NX, z, c)))


X_GROUPS = [[place(x, z, c) for x in range(NX)] for z in range(NZ) for c in range(NC)]
Z_GROUPS = [[place(x, z, c) for z in range(NZ)] for x in range(NX) for c in range(NC)]


def per_device(inputs, gain, w_gate, w_up, upstream):
    position = lax.axis_index("blk")
    core = position % NC
    x_place = position // (NZ * NC)
    first = core == 0
    tokens, width = inputs.shape
    rows, columns = w_gate.shape
    half = columns // 2
    n_dp = lax.axis_size("dp")
    features = width // n_dp

    def ordered(own, other, axis):
        return jnp.where(
            first, jnp.concatenate([own, other], axis), jnp.concatenate([other, own], axis)
        )

    def halves(value):
        low, high = value[:, :half], value[:, half:]
        return jnp.where(first, low, high), jnp.where(first, high, low)

    gate_mine, gate_other = halves(w_gate)
    up_mine, up_other = halves(w_up)
    weight_other = swap_core(jnp.concatenate([gate_other, up_other], 1))
    weight_mine = jnp.concatenate([gate_mine, up_mine], 1)
    weight_chip = ordered(weight_mine, weight_other, 0)
    upstream_mine, upstream_other = halves(upstream)
    upstream_pair = jnp.concatenate([upstream_mine, swap_core(upstream_other)], 0)
    inputs_pair = jnp.concatenate([inputs, swap_core(inputs)], 0)

    wide_input = inputs_pair.astype(F32)
    root_mean = jnp.sqrt(jnp.mean(wide_input * wide_input, axis=1, keepdims=True) + 1e-05)
    normed = (wide_input / root_mean * gain).astype(BF)

    column = lax.all_gather(weight_chip, "blk", axis=0, tiled=True, axis_index_groups=Z_GROUPS)
    weight = lax.all_gather(column, "blk", axis=0, tiled=True, axis_index_groups=X_GROUPS)

    pre = jnp.dot(normed, weight, preferred_element_type=F32)
    gate_pre, up_pre = pre[:, :half], pre[:, half:]
    sigmoid_gate = jax.nn.sigmoid(gate_pre)
    activated = gate_pre * sigmoid_gate
    hidden_pair = (activated * up_pre).astype(BF)
    upstream_wide = upstream_pair.astype(F32)
    back_up = (upstream_wide * activated).astype(BF)
    back_gate = (
        upstream_wide * up_pre * sigmoid_gate * (1.0 + gate_pre * (1.0 - sigmoid_gate))
    ).astype(BF)
    back = jnp.concatenate([back_gate, back_up], 1)

    part = lax.dot_general(
        weight, back, (((1,), (1,)), ((), ())), preferred_element_type=F32
    )
    part_other = swap_core(part[:, tokens:].astype(BF))
    hidden_other = swap_core(hidden_pair[tokens:])
    hidden = ordered(hidden_pair[:tokens], hidden_other, 1)

    def term(steps):
        size = rows * NZ * NC
        block = lax.dynamic_slice_in_dim(normed, ((x_place + steps) % NX) * size, size, 1)
        return lax.dot_general(block, back, (((0,), (0,)), ((), ())), preferred_element_type=F32)

    travelling = [shift_x(term(steps).astype(BF), steps) for steps in (2, 1, 3)]

    unit_t = (wide_input[:tokens] / root_mean[:tokens]).T
    group_part = (part[:, :tokens] + part_other.astype(F32)).astype(BF)
    dots = jnp.sum(group_part.astype(F32) * gain[:, None] * unit_t, axis=0)
    dots_high = dots.astype(BF)
    rest = dots - dots_high.astype(F32)
    dots_mid = rest.astype(BF)
    dots_low = (rest - dots_mid.astype(F32)).astype(BF)
    dots_rows = jnp.stack([dots_high, dots_mid, dots_low], 0)
    dots_rows = jnp.pad(dots_rows, ((0, 13), (0, 0)))
    sending = jnp.concatenate(
        [
            group_part.reshape(n_dp, features, tokens),
            jnp.broadcast_to(dots_rows, (n_dp,) + dots_rows.shape),
        ],
        1,
    )
    got = lax.all_to_all(sending, "dp", 0, 0, tiled=True)
    totals = jnp.sum(got.astype(F32), axis=0)
    own_sums = totals[:features]
    token_totals = totals[features] + totals[features + 1] + totals[features + 2]

    start = lax.axis_index("dp") * features
    gain_slice = lax.dynamic_slice_in_dim(gain, start, features, 0)[:, None]
    unit_slice = lax.dynamic_slice_in_dim(unit_t, start, features, 0)
    grad_input = (
        (own_sums * gain_slice - unit_slice * (token_totals / width)[None, :])
        / root_mean[:tokens, 0][None, :]
    ).astype(BF).T
    gain_part = jnp.sum(own_sums * unit_slice, axis=1)
    gain_part = lax.psum(gain_part, "blk", axis_index_groups=X_GROUPS)
    gain_part = lax.psum(gain_part, "blk", axis_index_groups=Z_GROUPS)
    grad_gain = gain_part + swap_core(gain_part)

    column_sum = term(0)
    for value in travelling:
        column_sum = column_sum + value.astype(F32)
    blocks = column_sum.astype(BF).reshape(NZ, rows * NC, 2 * half)
    blocks = lax.all_to_all(blocks, "blk", 0, 0, tiled=True, axis_index_groups=Z_GROUPS)
    chip_sum = jnp.sum(blocks.astype(F32), axis=0)
    sum_mine = jnp.where(first, chip_sum[:rows], chip_sum[rows:])
    sum_other = swap_core(jnp.where(first, chip_sum[rows:], chip_sum[:rows]))
    grad_gate = ordered(sum_mine[:, :half], sum_other[:, :half], 1)
    grad_up = ordered(sum_mine[:, half:], sum_other[:, half:], 1)
    return (hidden, grad_gate, grad_up, grad_input, grad_gain)


def solution(mesh):
    return jax.shard_map(
        per_device,
        mesh=mesh,
        in_specs=(P("blk", None), P(), P("blk", "dp"), P("blk", "dp"), P("blk", "dp")),
        out_specs=(P("blk", "dp"), P("blk", "dp"), P("blk", "dp"), P("blk", "dp"), P("dp")),
        check_vma=False,
    )
```

time: 872 us -> 202 us (0.23)
  waiting for transfers between devices: 568 us -> 78.2 us
  blocking collectives: 122 us -> 26.8 us
  starting transfers between devices: 122 us -> 57.7 us
  matrix products: 26.4 us -> 6.14 us
    unnamed x4 -> x1, waiting for transfers between devices: 217 us -> 0.02 us
    ppermute x62 -> x10, waiting for transfers between devices: 222 us -> 15.5 us  [the longest x3 12.9 us: shift_x(): lax.ppermute(value, 'blk', pairs(lambda x, z, c: ((x + steps) % NX, z, c)))]
    psum x2, blocking collectives: 122 us -> 12.6 us  [the longest x1 6.61 us: per_device(): gain_part = lax.psum(gain_part, 'blk', axis_index_groups=Z_GROUPS)]
    all_gather x2 -> x1, waiting for transfers between devices: 129 us -> 34.6 us  [per_device(): lax.all_gather(column, 'blk', axis=0, tiled=True, axis_index_groups=X_GRO...]
    ppermute x62 -> x10, starting transfers between devices: 121 us -> 42 us  [the longest x7 33.1 us: swap_core(): return lax.ppermute(value, 'blk', pairs(lambda x, z, c: (x, z, 1 - c)))]
    all_to_all x0 -> x2, waiting for transfers between devices: none -> 28 us  [the longest x1 15.2 us: per_device(): got = lax.all_to_all(sending, 'dp', 0, 0, tiled=True)]
    dot_general x68 -> x6, matrix products: 26.4 us -> 6.14 us  [the longest x1 2.83 us: per_device(): pre = jnp.dot(normed, weight, preferred_element_type=F32)]
    all_to_all x0 -> x2, starting transfers between devices: none -> 15.7 us  [the longest x1 10.9 us: per_device(): got = lax.all_to_all(sending, 'dp', 0, 0, tiled=True)]
  transfers between devices with their start and end apart: 65 -> 13, of which waited for: 64 -> 8; matrix products, arithmetic and copies ran while one was open for 2% -> 9% of each run, Pallas kernels for 0% -> 0%
where the time goes in v1:
time: 202 us; the launch traced here: 201 us
  waiting for transfers between devices  78.2 us (39%)
  starting transfers between devices  57.7 us (29%)
  blocking collectives  26.8 us (13%)
  between operations  14.5 us (7%)
  other arithmetic  14.2 us (7%)
  matrix products  6.14 us (3%)
  local copies, waits for them, and re-layouts  3.56 us (2%)
    all_gather x1, waiting for transfers between devices, per_device(): lax.all_gather(column, 'blk', axis=0, tiled=True, axis_index_groups=X_GRO...  34.6 us
    ppermute x7, starting transfers between devices, swap_core(): return lax.ppermute(value, 'blk', pairs(lambda x, z, c: (x, z, 1 - c)))  33.1 us
    all_to_all x1, waiting for transfers between devices, per_device(): got = lax.all_to_all(sending, 'dp', 0, 0, tiled=True)  15.2 us
    all_gather x1, blocking collectives, per_device(): lax.all_gather(weight_chip, 'blk', axis=0, tiled=True, axis_index_groups=...  14.2 us
    ppermute x3, waiting for transfers between devices, shift_x(): lax.ppermute(value, 'blk', pairs(lambda x, z, c: ((x + steps) % NX, z, c)))  12.9 us
    all_to_all x1, waiting for transfers between devices, per_device(): lax.all_to_all(blocks, 'blk', 0, 0, tiled=True, axis_index_groups=Z_GROUPS)  12.8 us
    all_to_all x1, starting transfers between devices, per_device(): got = lax.all_to_all(sending, 'dp', 0, 0, tiled=True)  10.9 us
    ppermute x3, starting transfers between devices, shift_x(): lax.ppermute(value, 'blk', pairs(lambda x, z, c: ((x + steps) % NX, z, c)))  8.87 us
  transfers between devices with their start and end apart: 13, of which 8 were waited for; matrix products, arithmetic and copies ran while one was open for 9% of the time, Pallas kernels for 0%

profile of v1, /device:TPU:1, one launch (start us, length us, event | category | flops | bytes accessed | tf_op | source)
XLA Modules:
  0.0 201.0 jit_solution(11134223855764845385)
XLA Ops:
  7.2 1.0 broadcast_select_fusion.4
  8.2 1.0 broadcast_select_fusion.5
  9.3 8.8 %collective-permute-start.1 = (bf16[80,432]{1,0:T(8,128)(2,1)S(1)}, bf16[80,432]{1,0:T(8,128)(2,1)S(1)}, u32[]{:S(2)}, u32[]{:S(2)}) collective-permute-start(bf16[80,432]{1,0:T(8,128)(2,1)S(1)} %pad_maximum_fusion.3), channel_id=1, source_target_pairs={{0,16},{16,0},{32,48},{48,32},{64,80},{80,64},{96,112},{112,96},{1... | collective-permute-start | bytes 207368 | tf_op jit(solution)/shard_map/ppermute | solution.py:25
  18.1 0.9 collective-permute-done.1
  19.0 0.1 maximum_select_fusion
  19.1 14.2 %all_gather.6 = bf16[640,432]{1,0:T(8,128)(2,1)} all-gather(bf16[160,432]{1,0:T(8,128)(2,1)S(1)} %maximum_select_fusion), channel_id=1, replica_groups={{0,32,64,96},{16,48,80,112},{128,160,192,224},{144,176,208,240},{256,28..., dimensions={0}, use_global_device_ids=true | all-gather | bytes 691200 | tf_op jit(solution)/shard_map/all_gather | solution.py:69
  33.4 0.3 copy.13
  33.7 5.7 %collective-permute-start = (bf16[128,2560]{0,1:T(8,128)(2,1)S(1)}, bf16[128,2560]{0,1:T(8,128)(2,1)S(1)}, u32[]{:S(2)}, u32[]{:S(2)}) collective-permute-start(bf16[128,2560]{0,1:T(8,128)(2,1)S(1)} %copy.13), channel_id=1, source_target_pairs={{0,16},{16,0},{32,48},{48,32},{64,80},{80,64},{96,112},{112,96},{1... | collective-permute-start | bytes 1966088 | tf_op jit(solution)/shard_map/ppermute | solution.py:25
  39.5 1.9 collective-permute-start.3
  41.5 0.4 multiply_reduce_fusion
  42.0 0.4 multiply_convert_fusion
  42.4 34.6 %all-gather.2.cloned.1.call-done = bf16[2560,432]{1,0:T(8,128)(2,1)} async-done(((bf16[640,432]{1,0:T(8,128)(2,1)}), bf16[2560,432]{1,0:T(8,128)(2,1)}) %all-gather.2.cloned.1.call-update) | async-done | bytes 2211856 | tf_op jit(solution)/shard_map/all_gather | solution.py:70
  77.0 2.8 %fusion.34 = f32[256,432]{0,1:T(8,128)S(1)} fusion(bf16[256,2560]{0,1:T(8,128)(2,1)S(1)} %multiply_convert_fusion, bf16[2560,432]{1,0:T(8,128)(2,1)} %all-gather.2.cloned.1.call-done), kind=kOutput, calls=%fused_computation.75 | convolution fusion | flops 566231040 | bytes 3964928 | tf_op jit(solution)/shard_map/dot_general | solution.py:72
  79.9 0.1 fusion.9
  80.0 0.4 convolution_convert_fusion
  80.4 2.6 %collective-permute-start.6 = (bf16[640,432]{0,1:T(8,128)(2,1)S(1)}, bf16[640,432]{0,1:T(8,128)(2,1)S(1)}, u32[]{:S(2)}, u32[]{:S(2)}) collective-permute-start(bf16[640,432]{0,1:T(8,128)(2,1)S(1)} %convolution_convert_fusion), channel_id=1, source_target_pairs={{0,384},{16,400},{32,416},{48,432},{64,448},{80,464},{96,480},{112... | collective-permute-start | bytes 1658888 | tf_op jit(solution)/shard_map/ppermute | solution.py:29
  83.0 0.4 convolution_convert_fusion.1
  83.4 2.8 %collective-permute-start.5 = (bf16[640,432]{0,1:T(8,128)(2,1)S(1)}, bf16[640,432]{0,1:T(8,128)(2,1)S(1)}, u32[]{:S(2)}, u32[]{:S(2)}) collective-permute-start(bf16[640,432]{0,1:T(8,128)(2,1)S(1)} %convolution_convert_fusion.1), channel_id=1, source_target_pairs={{0,128},{16,144},{32,160},{48,176},{64,192},{80,208},{96,224},{112... | collective-permute-start | bytes 1658888 | tf_op jit(solution)/shard_map/ppermute | solution.py:29
  86.2 0.4 convolution_convert_fusion.2
  86.6 3.5 %collective-permute-start.4 = (bf16[640,432]{0,1:T(8,128)(2,1)S(1)}, bf16[640,432]{0,1:T(8,128)(2,1)S(1)}, u32[]{:S(2)}, u32[]{:S(2)}) collective-permute-start(bf16[640,432]{0,1:T(8,128)(2,1)S(1)} %convolution_convert_fusion.2), channel_id=1, source_target_pairs={{0,256},{16,272},{32,288},{48,304},{64,320},{80,336},{96,352},{112... | collective-permute-start | bytes 1658888 | tf_op jit(solution)/shard_map/ppermute | solution.py:29
  90.1 0.8 fusion.29
  91.0 1.0 slice.164
  91.9 3.4 %collective-permute-start.8 = (bf16[2560,128]{1,0:T(8,128)(2,1)}, bf16[2560,128]{1,0:T(8,128)(2,1)}, u32[]{:S(2)}, u32[]{:S(2)}) collective-permute-start(bf16[2560,128]{1,0:T(8,128)(2,1)} %slice.164), channel_id=1, source_target_pairs={{0,16},{16,0},{32,48},{48,32},{64,80},{80,64},{96,112},{112,96},{1... | collective-permute-start | bytes 1966088 | tf_op jit(solution)/shard_map/ppermute | solution.py:25
  95.4 1.7 maximum_convert_fusion
  97.0 1.3 fusion.5
  98.4 1.4 collective-permute-done.5
  99.8 11.4 %collective-permute-done.4 = bf16[640,432]{0,1:T(8,128)(2,1)S(1)} collective-permute-done((bf16[640,432]{0,1:T(8,128)(2,1)S(1)}, bf16[640,432]{0,1:T(8,128)(2,1)S(1)}, u32[]{:S(2)}, u32[]{:S(2)}) %collective-permute-start.4) | collective-permute-done | bytes 552992 | tf_op jit(solution)/shard_map/ppermute | solution.py:29
  111.3 0.3 add_convert_fusion
  111.6 1.1 copy.14
  112.7 4.8 %all-to-all-start = ((bf16[4,160,432]{2,1,0:T(8,128)(2,1)}), bf16[4,160,432]{2,1,0:T(8,128)(2,1)S(1)}, u32[]{:S(2)}, u32[]{:S(2)}) async-start(bf16[4,160,432]{2,1,0:T(8,128)(2,1)} %bitcast.40), calls=%async_computation | async-start | bytes 1310720 | tf_op jit(solution)/shard_map/all_to_all | solution.py:135
  117.5 2.9 %fusion.1 = (f32[128]{0:T(128)S(1)}, bf16[2560,128]{1,0:T(8,128)(2,1)S(1)}, f32[128,2560]{0,1:T(8,128)}) fusion(f32[2560]{0:T(1024)S(1)} %copy-done.7, bf16[2560,128]{1,0:T(8,128)(2,1)} %collective-permute-done.8, f32[2560,256]{1,0:T(8,128)S(1)} %fusion.29, f32[128]{0:T(128)S(1)} %slice.96, f32[256,2560]{0,1:T(8,128)} %maximum_convert_fusion), kind=kLoop, calls=%fused_computation.12 | loop fusion | flops 2621312 | bytes 5254144 | tf_op jit(solution)/shard_map/reduce_sum | solution.py:100
  120.5 0.9 pad_maximum_fusion
  121.4 12.8 %all-to-all-done = bf16[4,160,432]{2,1,0:T(8,128)(2,1)S(1)} async-done(((bf16[4,160,432]{2,1,0:T(8,128)(2,1)}), bf16[4,160,432]{2,1,0:T(8,128)(2,1)S(1)}, u32[]{:S(2)}, u32[]{:S(2)}) %all-to-all-start) | async-done | bytes 552992 | tf_op jit(solution)/shard_map/all_to_all | solution.py:135
  134.1 0.9 copy-done.4
  135.0 10.9 %all-to-all-start.1 = ((bf16[16,176,128]{2,1,0:T(8,128)(2,1)}), bf16[16,176,128]{2,1,0:T(8,128)(2,1)S(1)}, u32[]{:S(2)}, u32[]{:S(2)}) async-start(bf16[16,176,128]{2,1,0:T(8,128)(2,1)} %pad_maximum_fusion), calls=%async_computation.1 | async-start | bytes 1441792 | tf_op jit(solution)/shard_map/all_to_all | solution.py:114
  145.9 3.7 %collective-permute-start.2 = (bf16[128,216]{0,1:T(8,128)(2,1)S(1)}, bf16[128,216]{0,1:T(8,128)(2,1)S(1)}, u32[]{:S(2)}, u32[]{:S(2)}) collective-permute-start(bf16[128,216]{0,1:T(8,128)(2,1)S(1)} %get-tuple-element.22), channel_id=1, source_target_pairs={{0,16},{16,0},{32,48},{48,32},{64,80},{80,64},{96,112},{112,96},{1... | collective-permute-start | bytes 165896 | tf_op jit(solution)/shard_map/ppermute | solution.py:25
  149.6 0.8 collective-permute-done.2
  150.4 0.7 maximum_select_fusion.3
  151.1 1.2 convert_reduce_fusion.1
  152.4 2.3 %collective-permute-start.7 = (f32[80,432]{1,0:T(8,128)S(1)}, f32[80,432]{1,0:T(8,128)S(1)}, u32[]{:S(2)}, u32[]{:S(2)}) collective-permute-start(f32[80,432]{1,0:T(8,128)S(1)} %get-tuple-element.14), channel_id=1, source_target_pairs={{0,16},{16,0},{32,48},{48,32},{64,80},{80,64},{96,112},{112,96},{1... | collective-permute-start | bytes 414728 | tf_op jit(solution)/shard_map/ppermute | solution.py:25
  154.7 0.9 collective-permute-done.7
  155.7 15.2 %all-to-all-done.1 = bf16[16,176,128]{2,1,0:T(8,128)(2,1)S(1)} async-done(((bf16[16,176,128]{2,1,0:T(8,128)(2,1)}), bf16[16,176,128]{2,1,0:T(8,128)(2,1)S(1)}, u32[]{:S(2)}, u32[]{:S(2)}) %all-to-all-start.1) | async-done | bytes 720928 | tf_op jit(solution)/shard_map/all_to_all | solution.py:114
  171.1 1.7 fusion.15
  172.8 6.0 %psum.14 = f32[160]{0:T(256)S(1)} all-reduce(f32[160]{0:T(256)S(1)} %get-tuple-element.8), channel_id=1, replica_groups={{0,128,256,384},{16,144,272,400},{32,160,288,416},{48,176,304,432},{64,..., use_global_device_ids=true, to_apply=%region_5.6 | all-reduce | flops 160 | bytes 1280 | tf_op jit(solution)/shard_map/psum | solution.py:127
  178.7 6.6 %psum.15 = f32[160]{0:T(256)S(1)} all-reduce(f32[160]{0:T(256)S(1)} %psum.14), channel_id=1, replica_groups={{0,32,64,96},{16,48,80,112},{128,160,192,224},{144,176,208,240},{256,28..., use_global_device_ids=true, to_apply=%region_6.7 | all-reduce | flops 160 | bytes 1280 | tf_op jit(solution)/shard_map/psum | solution.py:128
  185.3 7.3 %collective-permute-start.9 = (f32[160]{0:T(256)S(1)}, f32[160]{0:T(256)S(1)}, u32[]{:S(2)}, u32[]{:S(2)}) collective-permute-start(f32[160]{0:T(256)S(1)} %psum.15), channel_id=1, source_target_pairs={{0,16},{16,0},{32,48},{48,32},{64,80},{80,64},{96,112},{112,96},{1... | collective-permute-start | bytes 1928 | tf_op jit(solution)/shard_map/ppermute | solution.py:25
  192.6 0.9 maximum_select_fusion.1
  193.6 0.6 add.116
  (37 shorter events, 0.7 us)
Async XLA Ops:
  7.2 26.2 %copy-start.5 = (bf16[128,2560]{1,0:T(8,128)(2,1)S(1)}, bf16[128,2560]{1,0:T(8,128)(2,1)}, u32[]{:S(2)}) copy-start(bf16[128,2560]{1,0:T(8,128)(2,1)} %param.5) | copy-start | bytes 1966084
  7.2 69.8 %all-gather.2.cloned.1.call-start = ((), (), s32[]{:S(2)}) async-start(), calls=%async_computation.2 | async-start | bytes 3276800 | tf_op jit(solution)/shard_map/all_gather | solution.py:70
  9.3 9.7 %collective-permute-start.1 = (bf16[80,432]{1,0:T(8,128)(2,1)S(1)}, bf16[80,432]{1,0:T(8,128)(2,1)S(1)}, u32[]{:S(2)}, u32[]{:S(2)}) collective-permute-start(bf16[80,432]{1,0:T(8,128)(2,1)S(1)} %pad_maximum_fusion.3), channel_id=1, source_target_pairs={{0,16},{16,0},{32,48},{48,32},{64,80},{80,64},{96,112},{112,96},{1... | collective-permute-start | bytes 207368 | tf_op jit(solution)/shard_map/ppermute | solution.py:25
  19.1 20.3 %copy-start.6 = (bf16[128,432]{0,1:T(8,128)(2,1)S(1)}, bf16[128,432]{0,1:T(8,128)(2,1)}, u32[]{:S(2)}) copy-start(bf16[128,432]{0,1:T(8,128)(2,1)} %param.9) | copy-start | bytes 331780
  33.4 8.6 %copy-start.7 = (f32[2560]{0:T(1024)S(1)}, f32[2560]{0:T(1024)}, u32[]{:S(2)}) copy-start(f32[2560]{0:T(1024)} %param.6) | copy-start | bytes 30724
  33.7 7.8 %collective-permute-start = (bf16[128,2560]{0,1:T(8,128)(2,1)S(1)}, bf16[128,2560]{0,1:T(8,128)(2,1)S(1)}, u32[]{:S(2)}, u32[]{:S(2)}) collective-permute-start(bf16[128,2560]{0,1:T(8,128)(2,1)S(1)} %copy.13), channel_id=1, source_target_pairs={{0,16},{16,0},{32,48},{48,32},{64,80},{80,64},{96,112},{112,96},{1... | collective-permute-start | bytes 1966088 | tf_op jit(solution)/shard_map/ppermute | solution.py:25
  39.5 40.4 %collective-permute-start.3 = (bf16[128,216]{0,1:T(8,128)(2,1)S(1)}, bf16[128,216]{0,1:T(8,128)(2,1)S(1)}, u32[]{:S(2)}, u32[]{:S(2)}) collective-permute-start(bf16[128,216]{0,1:T(8,128)(2,1)S(1)} %get-tuple-element.20), channel_id=1, source_target_pairs={{0,16},{16,0},{32,48},{48,32},{64,80},{80,64},{96,112},{112,96},{1... | collective-permute-start | bytes 165896 | tf_op jit(solution)/shard_map/ppermute | solution.py:25
  41.5 0.8 copy-start.2
  42.4 43.9 %copy-start.1 = (bf16[256,2560]{0,1:T(8,128)(2,1)}, bf16[256,2560]{0,1:T(8,128)(2,1)S(1)}, u32[]{:S(2)}) copy-start(bf16[256,2560]{0,1:T(8,128)(2,1)S(1)} %multiply_convert_fusion) | copy-start | bytes 3932164
  80.0 10.1 %copy-start = (bf16[2560,432]{1,0:T(8,128)(2,1)S(1)}, bf16[2560,432]{1,0:T(8,128)(2,1)}, u32[]{:S(2)}) copy-start(bf16[2560,432]{1,0:T(8,128)(2,1)} %all-gather.2.cloned.1.call-done) | copy-start | bytes 6635524
  80.4 18.0 %collective-permute-start.6 = (bf16[640,432]{0,1:T(8,128)(2,1)S(1)}, bf16[640,432]{0,1:T(8,128)(2,1)S(1)}, u32[]{:S(2)}, u32[]{:S(2)}) collective-permute-start(bf16[640,432]{0,1:T(8,128)(2,1)S(1)} %convolution_convert_fusion), channel_id=1, source_target_pairs={{0,384},{16,400},{32,416},{48,432},{64,448},{80,464},{96,480},{112... | collective-permute-start | bytes 1658888 | tf_op jit(solution)/shard_map/ppermute | solution.py:29
  83.4 16.4 %collective-permute-start.5 = (bf16[640,432]{0,1:T(8,128)(2,1)S(1)}, bf16[640,432]{0,1:T(8,128)(2,1)S(1)}, u32[]{:S(2)}, u32[]{:S(2)}) collective-permute-start(bf16[640,432]{0,1:T(8,128)(2,1)S(1)} %convolution_convert_fusion.1), channel_id=1, source_target_pairs={{0,128},{16,144},{32,160},{48,176},{64,192},{80,208},{96,224},{112... | collective-permute-start | bytes 1658888 | tf_op jit(solution)/shard_map/ppermute | solution.py:29
  86.6 24.6 %collective-permute-start.4 = (bf16[640,432]{0,1:T(8,128)(2,1)S(1)}, bf16[640,432]{0,1:T(8,128)(2,1)S(1)}, u32[]{:S(2)}, u32[]{:S(2)}) collective-permute-start(bf16[640,432]{0,1:T(8,128)(2,1)S(1)} %convolution_convert_fusion.2), channel_id=1, source_target_pairs={{0,256},{16,272},{32,288},{48,304},{64,320},{80,336},{96,352},{112... | collective-permute-start | bytes 1658888 | tf_op jit(solution)/shard_map/ppermute | solution.py:29
  91.0 4.4 %copy-start.3 = (bf16[128,2560]{0,1:T(8,128)(2,1)S(1)}, bf16[128,2560]{0,1:T(8,128)(2,1)}, u32[]{:S(2)}) copy-start(bf16[128,2560]{0,1:T(8,128)(2,1)} %copy-done.2) | copy-start | bytes 1966084
  91.9 25.5 %collective-permute-start.8 = (bf16[2560,128]{1,0:T(8,128)(2,1)}, bf16[2560,128]{1,0:T(8,128)(2,1)}, u32[]{:S(2)}, u32[]{:S(2)}) collective-permute-start(bf16[2560,128]{1,0:T(8,128)(2,1)} %slice.164), channel_id=1, source_target_pairs={{0,16},{16,0},{32,48},{48,32},{64,80},{80,64},{96,112},{112,96},{1... | collective-permute-start | bytes 1966088 | tf_op jit(solution)/shard_map/ppermute | solution.py:25
  112.7 21.5 %all-to-all-start = ((bf16[4,160,432]{2,1,0:T(8,128)(2,1)}), bf16[4,160,432]{2,1,0:T(8,128)(2,1)S(1)}, u32[]{:S(2)}, u32[]{:S(2)}) async-start(bf16[4,160,432]{2,1,0:T(8,128)(2,1)} %bitcast.40), calls=%async_computation | async-start | bytes 1310720 | tf_op jit(solution)/shard_map/all_to_all | solution.py:135
  134.1 0.9 copy-start.4
  135.0 36.0 %all-to-all-start.1 = ((bf16[16,176,128]{2,1,0:T(8,128)(2,1)}), bf16[16,176,128]{2,1,0:T(8,128)(2,1)S(1)}, u32[]{:S(2)}, u32[]{:S(2)}) async-start(bf16[16,176,128]{2,1,0:T(8,128)(2,1)} %pad_maximum_fusion), calls=%async_computation.1 | async-start | bytes 1441792 | tf_op jit(solution)/shard_map/all_to_all | solution.py:114
  145.9 4.5 %collective-permute-start.2 = (bf16[128,216]{0,1:T(8,128)(2,1)S(1)}, bf16[128,216]{0,1:T(8,128)(2,1)S(1)}, u32[]{:S(2)}, u32[]{:S(2)}) collective-permute-start(bf16[128,216]{0,1:T(8,128)(2,1)S(1)} %get-tuple-element.22), channel_id=1, source_target_pairs={{0,16},{16,0},{32,48},{48,32},{64,80},{80,64},{96,112},{112,96},{1... | collective-permute-start | bytes 165896 | tf_op jit(solution)/shard_map/ppermute | solution.py:25
  152.4 3.3 %collective-permute-start.7 = (f32[80,432]{1,0:T(8,128)S(1)}, f32[80,432]{1,0:T(8,128)S(1)}, u32[]{:S(2)}, u32[]{:S(2)}) collective-permute-start(f32[80,432]{1,0:T(8,128)S(1)} %get-tuple-element.14), channel_id=1, source_target_pairs={{0,16},{16,0},{32,48},{48,32},{64,80},{80,64},{96,112},{112,96},{1... | collective-permute-start | bytes 414728 | tf_op jit(solution)/shard_map/ppermute | solution.py:25
  185.3 8.2 %collective-permute-start.9 = (f32[160]{0:T(256)S(1)}, f32[160]{0:T(256)S(1)}, u32[]{:S(2)}, u32[]{:S(2)}) collective-permute-start(f32[160]{0:T(256)S(1)} %psum.15), channel_id=1, source_target_pairs={{0,16},{16,0},{32,48},{48,32},{64,80},{80,64},{96,112},{112,96},{1... | collective-permute-start | bytes 1928 | tf_op jit(solution)/shard_map/ppermute | solution.py:25
Sparse Core Ops, SparseCore 0:
  33.5 43.5 all-gather.1

commit v2 on v1

v2 whole, which is shorter than its diff:
```python
import jax
import jax.numpy as jnp
from jax import lax
from jax.experimental import pallas as pl
from jax.experimental.pallas import tpu as pltpu
from jax.sharding import PartitionSpec as P

BF = jnp.bfloat16
F32 = jnp.float32
NX, NZ, NC = 4, 4, 2
VMEM = pl.BlockSpec(memory_space=pltpu.VMEM)
SMEM = pl.BlockSpec(memory_space=pltpu.SMEM)
PARAMS = pltpu.CompilerParams(vmem_limit_bytes=48 * 1024 * 1024)
NT = (((1,), (1,)), ((), ()))
TN = (((0,), (0,)), ((), ()))


def place(x, z, c):
    return (x * NZ + z) * NC + c


def pairs(move):
    return [
        (place(x, z, c), place(*move(x, z, c)))
        for x in range(NX)
        for z in range(NZ)
        for c in range(NC)
    ]


def swap_core(value):
    return lax.ppermute(value, "blk", pairs(lambda x, z, c: (x, z, 1 - c)))


def shift_x(value, steps):
    return lax.ppermute(value, "blk", pairs(lambda x, z, c: ((x + steps) % NX, z, c)))


def shift_z(value, steps):
    return lax.ppermute(value, "blk", pairs(lambda x, z, c: (x, (z + steps) % NZ, c)))


X_GROUPS = [[place(x, z, c) for x in range(NX)] for z in range(NZ) for c in range(NC)]
Z_GROUPS = [[place(x, z, c) for z in range(NZ)] for x in range(NX) for c in range(NC)]


def block_order(spot_ref, index):
    return ((spot_ref[0] + index // NZ) % NX) * NZ + (spot_ref[1] + index % NZ) % NZ


def norm_kernel(spot_ref, x_ref, gain_ref, normed_ref, root_ref):
    width, tokens = x_ref.shape
    size = width // (NX * NZ)
    total = jnp.zeros((size, tokens), F32)
    for index in range(NX * NZ):
        value = x_ref[pl.ds(index * size, size), :].astype(F32)
        total += value * value
    root = jnp.sqrt(jnp.sum(total, axis=0, keepdims=True) / width + 1e-05)
    root_ref[...] = root
    for index in range(NX * NZ):
        rows = pl.ds(pl.multiple_of(block_order(spot_ref, index) * size, size), size)
        unit = x_ref[rows, :].astype(F32) / root
        gain = gain_ref[rows, :]
        gain = jnp.concatenate([gain, gain], axis=1)
        normed_ref[pl.ds(index * size, size), :] = (unit * gain).astype(BF)


def forward_kernel(normed_ref, upstream_ref, *refs):
    gates, ups = refs[:NX], refs[NX : 2 * NX]
    hidden_ref, back_ref, own_ref, other_ref = refs[2 * NX :]
    size = gates[0].shape[1]
    tokens = own_ref.shape[1]

    def product(pieces):
        total = None
        for index in range(NX):
            term = jnp.dot(
                pieces[index][...],
                normed_ref[pl.ds(index * size, size), :],
                preferred_element_type=F32,
            )
            total = term if total is None else total + term
        return total

    gate_pre = product(gates)
    up_pre = product(ups)
    sigmoid = 1.0 / (1.0 + jnp.exp(-gate_pre))
    activated = gate_pre * sigmoid
    hidden_ref[...] = (activated * up_pre).astype(BF)
    upstream = upstream_ref[...].astype(F32)
    back_up = (upstream * activated).astype(BF)
    back_gate = (upstream * up_pre * sigmoid * (1.0 + gate_pre * (1.0 - sigmoid))).astype(BF)
    back_ref[0] = back_gate
    back_ref[1] = back_up
    for index in range(NX):
        part = lax.dot_general(gates[index][...], back_gate, TN, preferred_element_type=F32)
        part += lax.dot_general(ups[index][...], back_up, TN, preferred_element_type=F32)
        rows = pl.ds(index * size, size)
        own_ref[rows, :] = part[:, :tokens]
        other_ref[rows, :] = part[:, tokens:].astype(BF)


def gradient_kernel(normed_ref, back_ref, *outs):
    size = outs[0].shape[2]
    for index in range(NX):
        rows = normed_ref[pl.ds(index * size, size), :]
        for which in range(2):
            term = lax.dot_general(back_ref[which], rows, NT, preferred_element_type=F32)
            outs[index][which] = term.astype(outs[index].dtype)


def blocks_kernel(spot_ref, own_ref, other_ref, x_ref, root_ref, gain_ref, out_ref):
    width, tokens = own_ref.shape
    size = width // (NX * NZ)
    root = root_ref[...]
    total = jnp.zeros((size, tokens), F32)
    for index in range(NX * NZ):
        here = pl.ds(index * size, size)
        block = block_order(spot_ref, index)
        rows = pl.ds(pl.multiple_of(block * size, size), size)
        part = (own_ref[here, :] + other_ref[here, :].astype(F32)).astype(BF)
        out_ref[block, 0:size, :] = part
        unit = x_ref[rows, :].astype(F32) / root
        total += part.astype(F32) * gain_ref[rows, :] * unit
    dots = jnp.sum(total, axis=0, keepdims=True)
    high = dots.astype(BF).astype(F32)
    mid = (dots - high).astype(BF).astype(F32)
    low = dots - high - mid
    spare = out_ref.shape[1] - size
    line = lax.broadcasted_iota(jnp.int32, (spare, tokens), 0)
    rows = jnp.where(line == 0, high, jnp.where(line == 1, mid, jnp.where(line == 2, low, 0.0)))
    for index in range(NX * NZ):
        out_ref[index, size : size + spare, :] = rows.astype(BF)


def call(kernel, outs, specs):
    return pl.pallas_call(
        kernel,
        out_shape=outs,
        in_specs=specs,
        out_specs=jax.tree.map(lambda _: VMEM, outs),
        compiler_params=PARAMS,
    )


def shape(dims, dtype):
    return jax.ShapeDtypeStruct(dims, dtype)


def per_device(inputs, gain, w_gate, w_up, upstream):
    position = lax.axis_index("blk")
    core = position % NC
    spot = jnp.stack([position // (NZ * NC), (position // NC) % NZ]).astype(jnp.int32)
    first = core == 0
    tokens, width = inputs.shape
    rows, columns = w_gate.shape
    half = columns // 2
    n_dp = lax.axis_size("dp")
    features = width // n_dp
    column_rows = rows * NZ * NC

    def ordered(own, other, axis):
        return jnp.where(
            first, jnp.concatenate([own, other], axis), jnp.concatenate([other, own], axis)
        )

    def halves(value, axis):
        low, high = jnp.split(value, 2, axis)
        return jnp.where(first, low, high), jnp.where(first, high, low)

    gate_mine, gate_other = halves(w_gate, 1)
    up_mine, up_other = halves(w_up, 1)
    got = swap_core(jnp.stack([gate_other, up_other]))
    chip = [ordered(gate_mine, got[0], 0), ordered(up_mine, got[1], 0)]
    pieces = []
    for chunk in chip:
        column = jnp.concatenate([chunk] + [shift_z(chunk, -step) for step in (1, 2, 3)], 0).T
        pieces.append([column] + [shift_x(column, -step) for step in (1, 2, 3)])

    inputs_t = jnp.concatenate([inputs, swap_core(inputs)], 0).T
    upstream_mine, upstream_other = halves(upstream.T, 0)
    upstream_pair = jnp.concatenate([upstream_mine, swap_core(upstream_other)], 1)
    gain_wide = jnp.broadcast_to(gain[:, None], (width, tokens))
    normed, root_mean = call(
        norm_kernel,
        (shape((width, 2 * tokens), BF), shape((1, 2 * tokens), F32)),
        [SMEM, VMEM, VMEM],
    )(spot, inputs_t, gain_wide)

    hidden_pair, back, part_own, part_other = call(
        forward_kernel,
        (
            shape((half, 2 * tokens), BF),
            shape((2, half, 2 * tokens), BF),
            shape((width, tokens), F32),
            shape((width, tokens), BF),
        ),
        [VMEM] * (2 + 2 * NX),
    )(normed, upstream_pair, *pieces[0], *pieces[1])
    part_other = swap_core(part_other)
    terms = call(
        gradient_kernel,
        tuple(shape((2, half, column_rows), F32 if index == 0 else BF) for index in range(NX)),
        [VMEM] * 2,
    )(normed, back)
    travelling = [shift_x(terms[steps], steps) for steps in (2, 1, 3)]
    hidden_other = swap_core(hidden_pair[:, tokens:])
    hidden = ordered(hidden_pair[:, :tokens], hidden_other, 0).T

    spare = 16
    sending = call(
        blocks_kernel, shape((n_dp, features + spare, tokens), BF), [SMEM] + [VMEM] * 5
    )(spot, part_own, part_other, inputs_t[:, :tokens], root_mean[:, :tokens], gain_wide)
    got = lax.all_to_all(sending, "dp", 0, 0, tiled=True)
    totals = jnp.sum(got.astype(F32), axis=0)
    own_sums = totals[:features]
    token_totals = totals[features] + totals[features + 1] + totals[features + 2]
    start = lax.axis_index("dp") * features
    gain_slice = lax.dynamic_slice_in_dim(gain, start, features, 0)[:, None]
    root_own = root_mean[:, :tokens]
    unit_slice = (
        lax.dynamic_slice_in_dim(inputs_t[:, :tokens], start, features, 0).astype(F32) / root_own
    )
    grad_input = (
        ((own_sums * gain_slice - unit_slice * (token_totals / width)[None, :]) / root_own)
        .astype(BF)
        .T
    )
    gain_part = jnp.sum(own_sums * unit_slice, axis=1)
    gain_part = lax.psum(gain_part, "blk", axis_index_groups=X_GROUPS)
    gain_part = lax.psum(gain_part, "blk", axis_index_groups=Z_GROUPS)
    grad_gain = gain_part + swap_core(gain_part)

    column_sum = terms[0]
    for value in travelling:
        column_sum = column_sum + value.astype(F32)
    column_sum = column_sum.reshape(columns, column_rows).T.reshape(NZ, rows * NC, columns)
    chip_sum = column_sum[0]
    for step in (2, 1, 3):
        chip_sum = chip_sum + shift_z(column_sum[step].astype(BF), step).astype(F32)
    sum_mine, sum_other = chip_sum[:rows], chip_sum[rows:]
    sum_mine, sum_other = (
        jnp.where(first, sum_mine, sum_other),
        jnp.where(first, sum_other, sum_mine),
    )
    sum_other = swap_core(sum_other)
    grad_gate = ordered(sum_mine[:, :half], sum_other[:, :half], 1)
    grad_up = ordered(sum_mine[:, half:], sum_other[:, half:], 1)
    return (hidden, grad_gate, grad_up, grad_input, grad_gain)


def solution(mesh):
    return jax.shard_map(
        per_device,
        mesh=mesh,
        in_specs=(P("blk", None), P(), P("blk", "dp"), P("blk", "dp"), P("blk", "dp")),
        out_specs=(P("blk", "dp"), P("blk", "dp"), P("blk", "dp"), P("blk", "dp"), P("dp")),
        check_vma=False,
    )
```

time: 202 us -> 187 us (0.926)
  starting transfers between devices: 57.7 us -> 92.5 us
  waiting for transfers between devices: 78.2 us -> 51.6 us
  between operations: 14.5 us -> 1.2 us
  other arithmetic: 14.2 us -> 6.38 us
  blocking collectives: 26.8 us -> 19.3 us
  Pallas kernels: 0 us -> 7.16 us
  matrix products: 6.14 us -> 0 us
  local copies, waits for them, and re-layouts: 3.56 us -> 7.62 us
    all_gather x1 -> x0, waiting for transfers between devices: 34.6 us -> none  [per_device(): lax.all_gather(column, 'blk', axis=0, tiled=True, axis_index_groups=X_GRO...]
    ppermute x0 -> x9, waiting for transfers between devices: none -> 26.7 us  [shift_z(): lax.ppermute(value, 'blk', pairs(lambda x, z, c: (x, (z + steps) % NZ, c)))]
    ppermute x0 -> x9, starting transfers between devices: none -> 26.7 us  [shift_z(): lax.ppermute(value, 'blk', pairs(lambda x, z, c: (x, (z + steps) % NZ, c)))]
    ppermute x3 -> x9, starting transfers between devices: 8.87 us -> 28.3 us  [shift_x(): lax.ppermute(value, 'blk', pairs(lambda x, z, c: ((x + steps) % NX, z, c)))]
    all_to_all x1, waiting for transfers between devices: 15.2 us -> 0.01 us  [per_device(): got = lax.all_to_all(sending, 'dp', 0, 0, tiled=True)]
    all_gather x1 -> x0, blocking collectives: 14.2 us -> none  [per_device(): lax.all_gather(weight_chip, 'blk', axis=0, tiled=True, axis_index_groups=...]
    all_to_all x1 -> x0, waiting for transfers between devices: 12.8 us -> none  [per_device(): lax.all_to_all(blocks, 'blk', 0, 0, tiled=True, axis_index_groups=Z_GROUPS)]
    ppermute x3 -> x9, waiting for transfers between devices: 12.9 us -> 24 us  [shift_x(): lax.ppermute(value, 'blk', pairs(lambda x, z, c: ((x + steps) % NX, z, c)))]
  transfers between devices with their start and end apart: 13 -> 26, of which waited for: 8 -> 12; matrix products, arithmetic and copies ran while one was open for 9% -> 5% of each run, Pallas kernels for 0% -> 2%
where the time goes in v2:
time: 187 us; the launch traced here: 186 us
  starting transfers between devices  92.5 us (49%)
  waiting for transfers between devices  51.6 us (28%)
  blocking collectives  19.3 us (10%)
  local copies, waits for them, and re-layouts  7.62 us (4%)
  Pallas kernels  7.16 us (4%)
  other arithmetic  6.38 us (3%)
    ppermute x9, starting transfers between devices, shift_x(): lax.ppermute(value, 'blk', pairs(lambda x, z, c: ((x + steps) % NX, z, c)))  28.3 us
    ppermute x7, starting transfers between devices, swap_core(): return lax.ppermute(value, 'blk', pairs(lambda x, z, c: (x, z, 1 - c)))  27.2 us
    ppermute x9, waiting for transfers between devices, shift_z(): lax.ppermute(value, 'blk', pairs(lambda x, z, c: (x, (z + steps) % NZ, c)))  26.7 us
    ppermute x9, starting transfers between devices, shift_z(): lax.ppermute(value, 'blk', pairs(lambda x, z, c: (x, (z + steps) % NZ, c)))  26.7 us
    ppermute x9, waiting for transfers between devices, shift_x(): lax.ppermute(value, 'blk', pairs(lambda x, z, c: ((x + steps) % NX, z, c)))  24 us
    all_to_all x1, starting transfers between devices, per_device(): got = lax.all_to_all(sending, 'dp', 0, 0, tiled=True)  10.4 us
    psum x1, blocking collectives, per_device(): gain_part = lax.psum(gain_part, 'blk', axis_index_groups=X_GROUPS)  9.9 us
    psum x1, blocking collectives, per_device(): gain_part = lax.psum(gain_part, 'blk', axis_index_groups=Z_GROUPS)  9.44 us
  transfers between devices with their start and end apart: 26, of which 12 were waited for; matrix products, arithmetic and copies ran while one was open for 5% of the time, Pallas kernels for 2%

profile of v2, /device:TPU:1, one launch (start us, length us, event | category | flops | bytes accessed | tf_op | source)
XLA Modules:
  0.0 185.8 jit_solution(9859986225186644048)
XLA Ops:
  0.7 1.0 fusion.10
  1.9 1.0 fusion.11
  3.2 8.8 %collective-permute-start.2 = (bf16[2,80,216]{1,2,0:T(8,128)(2,1)S(1)}, bf16[2,80,216]{1,2,0:T(8,128)(2,1)S(1)}, u32[]{:S(2)}, u32[]{:S(2)}) collective-permute-start(bf16[2,80,216]{1,2,0:T(8,128)(2,1)S(1)} %pad_maximum_fusion.1), channel_id=1, source_target_pairs={{0,16},{16,0},{32,48},{48,32},{64,80},{80,64},{96,112},{112,96},{1... | collective-permute-start | bytes 207368 | tf_op jit(solution)/shard_map/ppermute | solution.py:32
  12.1 1.9 %collective-permute-start.1 = (bf16[216,128]{1,0:T(8,128)(2,1)S(1)}, bf16[216,128]{1,0:T(8,128)(2,1)S(1)}, u32[]{:S(2)}, u32[]{:S(2)}) collective-permute-start(bf16[216,128]{1,0:T(8,128)(2,1)S(1)} %get-tuple-element.45), channel_id=1, source_target_pairs={{0,16},{16,0},{32,48},{48,32},{64,80},{80,64},{96,112},{112,96},{1... | collective-permute-start | bytes 165896 | tf_op jit(solution)/shard_map/ppermute | solution.py:32
  14.4 2.4 %collective-permute-start = (bf16[128,2560]{0,1:T(8,128)(2,1)S(1)}, bf16[128,2560]{0,1:T(8,128)(2,1)S(1)}, u32[]{:S(2)}, u32[]{:S(2)}) collective-permute-start(bf16[128,2560]{0,1:T(8,128)(2,1)S(1)} %copy.11), channel_id=1, source_target_pairs={{0,16},{16,0},{32,48},{48,32},{64,80},{80,64},{96,112},{112,96},{1... | collective-permute-start | bytes 1966088 | tf_op jit(solution)/shard_map/ppermute | solution.py:32
  17.0 1.9 %collective-permute-start.11 = (bf16[160,216]{0,1:T(8,128)(2,1)S(1)}, bf16[160,216]{0,1:T(8,128)(2,1)S(1)}, u32[]{:S(2)}, u32[]{:S(2)}) collective-permute-start(bf16[160,216]{0,1:T(8,128)(2,1)S(1)} %maximum_select_fusion.3), channel_id=1, source_target_pairs={{0,32},{16,48},{32,64},{48,80},{64,96},{80,112},{96,0},{112,16},{1... | collective-permute-start | bytes 207368 | tf_op jit(solution)/shard_map/ppermute | solution.py:40
  18.9 2.5 %collective-permute-start.10 = (bf16[160,216]{0,1:T(8,128)(2,1)S(1)}, bf16[160,216]{0,1:T(8,128)(2,1)S(1)}, u32[]{:S(2)}, u32[]{:S(2)}) collective-permute-start(bf16[160,216]{0,1:T(8,128)(2,1)S(1)} %maximum_select_fusion.3), channel_id=1, source_target_pairs={{0,64},{16,80},{32,96},{48,112},{64,0},{80,16},{96,32},{112,48},{1... | collective-permute-start | bytes 207368 | tf_op jit(solution)/shard_map/ppermute | solution.py:40
  21.4 4.6 %collective-permute-start.9 = (bf16[160,216]{0,1:T(8,128)(2,1)S(1)}, bf16[160,216]{0,1:T(8,128)(2,1)S(1)}, u32[]{:S(2)}, u32[]{:S(2)}) collective-permute-start(bf16[160,216]{0,1:T(8,128)(2,1)S(1)} %maximum_select_fusion.3), channel_id=1, source_target_pairs={{0,96},{16,112},{32,0},{48,16},{64,32},{80,48},{96,64},{112,80},{1... | collective-permute-start | bytes 207368 | tf_op jit(solution)/shard_map/ppermute | solution.py:40
  26.1 4.4 %collective-permute-done.10 = bf16[160,216]{0,1:T(8,128)(2,1)S(1)} collective-permute-done((bf16[160,216]{0,1:T(8,128)(2,1)S(1)}, bf16[160,216]{0,1:T(8,128)(2,1)S(1)}, u32[]{:S(2)}, u32[]{:S(2)}) %collective-permute-start.10) | collective-permute-done | bytes 69152 | tf_op jit(solution)/shard_map/ppermute | solution.py:40
  30.5 1.1 collective-permute-done.9
  31.8 1.9 %collective-permute-start.14 = (bf16[216,640]{1,0:T(8,128)(2,1)S(1)}, bf16[216,640]{1,0:T(8,128)(2,1)S(1)}, u32[]{:S(2)}, u32[]{:S(2)}) collective-permute-start(bf16[216,640]{1,0:T(8,128)(2,1)S(1)} %maximum_bitcast_fusion.2.refs_4_), channel_id=1, source_target_pairs={{0,128},{16,144},{32,160},{48,176},{64,192},{80,208},{96,224},{112... | collective-permute-start | bytes 829448 | tf_op jit(solution)/shard_map/ppermute | solution.py:36
  33.9 3.4 %collective-permute-start.5 = (bf16[160,216]{0,1:T(8,128)(2,1)S(1)}, bf16[160,216]{0,1:T(8,128)(2,1)S(1)}, u32[]{:S(2)}, u32[]{:S(2)}) collective-permute-start(bf16[160,216]{0,1:T(8,128)(2,1)S(1)} %maximum_select_fusion.2), channel_id=1, source_target_pairs={{0,32},{16,48},{32,64},{48,80},{64,96},{80,112},{96,0},{112,16},{1... | collective-permute-start | bytes 207368 | tf_op jit(solution)/shard_map/ppermute | solution.py:40
  37.3 1.9 %collective-permute-start.4 = (bf16[160,216]{0,1:T(8,128)(2,1)S(1)}, bf16[160,216]{0,1:T(8,128)(2,1)S(1)}, u32[]{:S(2)}, u32[]{:S(2)}) collective-permute-start(bf16[160,216]{0,1:T(8,128)(2,1)S(1)} %maximum_select_fusion.2), channel_id=1, source_target_pairs={{0,64},{16,80},{32,96},{48,112},{64,0},{80,16},{96,32},{112,48},{1... | collective-permute-start | bytes 207368 | tf_op jit(solution)/shard_map/ppermute | solution.py:40
  39.3 4.0 %collective-permute-start.3 = (bf16[160,216]{0,1:T(8,128)(2,1)S(1)}, bf16[160,216]{0,1:T(8,128)(2,1)S(1)}, u32[]{:S(2)}, u32[]{:S(2)}) collective-permute-start(bf16[160,216]{0,1:T(8,128)(2,1)S(1)} %maximum_select_fusion.2), channel_id=1, source_target_pairs={{0,96},{16,112},{32,0},{48,16},{64,32},{80,48},{96,64},{112,80},{1... | collective-permute-start | bytes 207368 | tf_op jit(solution)/shard_map/ppermute | solution.py:40
  43.3 3.4 %collective-permute-start.13 = (bf16[216,640]{1,0:T(8,128)(2,1)S(1)}, bf16[216,640]{1,0:T(8,128)(2,1)S(1)}, u32[]{:S(2)}, u32[]{:S(2)}) collective-permute-start(bf16[216,640]{1,0:T(8,128)(2,1)S(1)} %maximum_bitcast_fusion.2.refs_4_), channel_id=1, source_target_pairs={{0,256},{16,272},{32,288},{48,304},{64,320},{80,336},{96,352},{112... | collective-permute-start | bytes 829448 | tf_op jit(solution)/shard_map/ppermute | solution.py:36
  46.7 0.8 collective-permute-done.4
  47.5 4.8 %collective-permute-start.12 = (bf16[216,640]{1,0:T(8,128)(2,1)S(1)}, bf16[216,640]{1,0:T(8,128)(2,1)S(1)}, u32[]{:S(2)}, u32[]{:S(2)}) collective-permute-start(bf16[216,640]{1,0:T(8,128)(2,1)S(1)} %maximum_bitcast_fusion.2.refs_4_), channel_id=1, source_target_pairs={{0,384},{16,400},{32,416},{48,432},{64,448},{80,464},{96,480},{112... | collective-permute-start | bytes 829448 | tf_op jit(solution)/shard_map/ppermute | solution.py:36
  52.6 1.9 %collective-permute-start.8 = (bf16[216,640]{1,0:T(8,128)(2,1)S(1)}, bf16[216,640]{1,0:T(8,128)(2,1)S(1)}, u32[]{:S(2)}, u32[]{:S(2)}) collective-permute-start(bf16[216,640]{1,0:T(8,128)(2,1)S(1)} %maximum_bitcast_fusion.1.refs_0_), channel_id=1, source_target_pairs={{0,128},{16,144},{32,160},{48,176},{64,192},{80,208},{96,224},{112... | collective-permute-start | bytes 829448 | tf_op jit(solution)/shard_map/ppermute | solution.py:36
  54.5 3.1 %collective-permute-start.7 = (bf16[216,640]{1,0:T(8,128)(2,1)S(1)}, bf16[216,640]{1,0:T(8,128)(2,1)S(1)}, u32[]{:S(2)}, u32[]{:S(2)}) collective-permute-start(bf16[216,640]{1,0:T(8,128)(2,1)S(1)} %maximum_bitcast_fusion.1.refs_0_), channel_id=1, source_target_pairs={{0,256},{16,272},{32,288},{48,304},{64,320},{80,336},{96,352},{112... | collective-permute-start | bytes 829448 | tf_op jit(solution)/shard_map/ppermute | solution.py:36
  57.6 3.4 %collective-permute-start.6 = (bf16[216,640]{1,0:T(8,128)(2,1)S(1)}, bf16[216,640]{1,0:T(8,128)(2,1)S(1)}, u32[]{:S(2)}, u32[]{:S(2)}) collective-permute-start(bf16[216,640]{1,0:T(8,128)(2,1)S(1)} %maximum_bitcast_fusion.1.refs_0_), channel_id=1, source_target_pairs={{0,384},{16,400},{32,416},{48,432},{64,448},{80,464},{96,480},{112... | collective-permute-start | bytes 829448 | tf_op jit(solution)/shard_map/ppermute | solution.py:36
  61.6 1.1 shard_map.92
  62.7 1.3 collective-permute-done.8.refs_3_
  64.0 3.7 %collective-permute-done.7.refs_2_ = bf16[216,640]{1,0:T(8,128)(2,1)S(1)} collective-permute-done((bf16[216,640]{1,0:T(8,128)(2,1)S(1)}, bf16[216,640]{1,0:T(8,128)(2,1)S(1)}, u32[]{:S(2)}, u32[]{:S(2)}) %collective-permute-start.7) | collective-permute-done | bytes 276512 | tf_op jit(solution)/shard_map/ppermute | solution.py:36
  67.7 4.7 %collective-permute-done.6.refs_1_ = bf16[216,640]{1,0:T(8,128)(2,1)S(1)} collective-permute-done((bf16[216,640]{1,0:T(8,128)(2,1)S(1)}, bf16[216,640]{1,0:T(8,128)(2,1)S(1)}, u32[]{:S(2)}, u32[]{:S(2)}) %collective-permute-start.6) | collective-permute-done | bytes 276512 | tf_op jit(solution)/shard_map/ppermute | solution.py:36
  72.5 2.6 %shard_map.93 = (bf16[216,256]{1,0:T(8,128)(2,1)S(1)}, bf16[2,216,256]{2,1,0:T(8,128)(2,1)S(1)}, f32[2560,128]{1,0:T(8,128)S(1)}, bf16[2560,128]{1,0:T(8,128)(2,1)}) custom-call(bf16[2560,256]{1,0:T(8,128)(2,1)S(1)} %get-tuple-element.15.normed_ref, bf16[216,256]{1,0:T(8,128)(2,1)S(1)} %pad_maximum_fusion.upstream_ref, ...), custom_call_target="tpu_custom_call" | custom-call | tf_op jit(solution)/shard_map/pallas_call | solution.py:190
  75.1 1.0 shard_map.94
  76.1 2.3 %collective-permute-start.16 = (bf16[2,216,640]{2,1,0:T(8,128)(2,1)S(1)}, bf16[2,216,640]{2,1,0:T(8,128)(2,1)S(1)}, u32[]{:S(2)}, u32[]{:S(2)}) collective-permute-start(bf16[2,216,640]{2,1,0:T(8,128)(2,1)S(1)} %get-tuple-element.19), channel_id=1, source_target_pairs={{0,256},{16,272},{32,288},{48,304},{64,320},{80,336},{96,352},{112... | collective-permute-start | bytes 1658888 | tf_op jit(solution)/shard_map/ppermute | solution.py:36
  78.5 5.5 %collective-permute-start.17 = (bf16[2,216,640]{2,1,0:T(8,128)(2,1)S(1)}, bf16[2,216,640]{2,1,0:T(8,128)(2,1)S(1)}, u32[]{:S(2)}, u32[]{:S(2)}) collective-permute-start(bf16[2,216,640]{2,1,0:T(8,128)(2,1)S(1)} %get-tuple-element.20), channel_id=1, source_target_pairs={{0,128},{16,144},{32,160},{48,176},{64,192},{80,208},{96,224},{112... | collective-permute-start | bytes 1658888 | tf_op jit(solution)/shard_map/ppermute | solution.py:36
  83.9 1.9 %collective-permute-start.18 = (bf16[2,216,640]{2,1,0:T(8,128)(2,1)S(1)}, bf16[2,216,640]{2,1,0:T(8,128)(2,1)S(1)}, u32[]{:S(2)}, u32[]{:S(2)}) collective-permute-start(bf16[2,216,640]{2,1,0:T(8,128)(2,1)S(1)} %get-tuple-element.21), channel_id=1, source_target_pairs={{0,384},{16,400},{32,416},{48,432},{64,448},{80,464},{96,480},{112... | collective-permute-start | bytes 1658888 | tf_op jit(solution)/shard_map/ppermute | solution.py:36
  85.9 3.4 %collective-permute-start.23 = (bf16[2560,128]{1,0:T(8,128)(2,1)}, bf16[2560,128]{1,0:T(8,128)(2,1)}, u32[]{:S(2)}, u32[]{:S(2)}) collective-permute-start(bf16[2560,128]{1,0:T(8,128)(2,1)} %get-tuple-element.23), channel_id=1, source_target_pairs={{0,16},{16,0},{32,48},{48,32},{64,80},{80,64},{96,112},{112,96},{1... | collective-permute-start | bytes 1966088 | tf_op jit(solution)/shard_map/ppermute | solution.py:32
  90.0 1.9 %collective-permute-start.15 = (bf16[216,128]{1,0:T(8,128)(2,1)}, bf16[216,128]{1,0:T(8,128)(2,1)}, u32[]{:S(2)}, u32[]{:S(2)}) collective-permute-start(bf16[216,128]{1,0:T(8,128)(2,1)} %get-tuple-element.37), channel_id=1, source_target_pairs={{0,16},{16,0},{32,48},{48,32},{64,80},{80,64},{96,112},{112,96},{1... | collective-permute-start | bytes 165896 | tf_op jit(solution)/shard_map/ppermute | solution.py:32
  92.2 13.6 %collective-permute-done.17 = bf16[2,216,640]{2,1,0:T(8,128)(2,1)S(1)} collective-permute-done((bf16[2,216,640]{2,1,0:T(8,128)(2,1)S(1)}, bf16[2,216,640]{2,1,0:T(8,128)(2,1)S(1)}, u32[]{:S(2)}, u32[]{:S(2)}) %collective-permute-start.17) | collective-permute-done | bytes 552992 | tf_op jit(solution)/shard_map/ppermute | solution.py:36
  106.1 1.3 convert_add_fusion
  107.4 2.7 %copy.16 = f32[432,640]{0,1:T(8,128)} copy(f32[432,640]{1,0:T(8,128)} %bitcast.29) | data formatting | bytes 2211840 | tf_op jit(solution)/shard_map/reshape | solution.py:237
  110.1 2.4 %shard_map.95 = bf16[16,176,128]{2,1,0:T(8,128)(2,1)} custom-call(s32[2]{0:T(128)S(1)} %pad_add_fusion.spot_ref, f32[2560,128]{1,0:T(8,128)S(1)} %get-tuple-element.22.own_ref, bf16[2560,128]{1,0:T(8,128)(2,1)} %collective-permute-done.23.other_ref, bf16[2560,128]{1,0:T(8,128)(2,1)S(1)} %slice.101.x_ref, f32[1,128]{1,0:T(1,128)S(1)} %get-tuple-element.51.root_ref, ...), custom_call_target="tpu_custom_call" | custom-call | tf_op jit(solution)/shard_map/pallas_call | solution.py:211
  112.5 10.4 %all-to-all-start = ((bf16[16,176,128]{2,1,0:T(8,128)(2,1)}), bf16[16,176,128]{2,1,0:T(8,128)(2,1)S(1)}, u32[]{:S(2)}, u32[]{:S(2)}) async-start(bf16[16,176,128]{2,1,0:T(8,128)(2,1)} %shard_map.95), calls=%async_computation | async-start | bytes 1441792 | tf_op jit(solution)/shard_map/all_to_all | solution.py:214
  123.8 3.1 %collective-permute-start.19 = (bf16[160,432]{1,0:T(8,128)(2,1)}, bf16[160,432]{1,0:T(8,128)(2,1)S(1)}, u32[]{:S(2)}, u32[]{:S(2)}) collective-permute-start(bf16[160,432]{1,0:T(8,128)(2,1)} %get-tuple-element.27), channel_id=1, source_target_pairs={{0,64},{16,80},{32,96},{48,112},{64,0},{80,16},{96,32},{112,48},{1... | collective-permute-start | bytes 414728 | tf_op jit(solution)/shard_map/ppermute | solution.py:40
  126.8 2.2 %collective-permute-start.21 = (bf16[160,432]{1,0:T(8,128)(2,1)}, bf16[160,432]{1,0:T(8,128)(2,1)S(1)}, u32[]{:S(2)}, u32[]{:S(2)}) collective-permute-start(bf16[160,432]{1,0:T(8,128)(2,1)} %get-tuple-element.28), channel_id=1, source_target_pairs={{0,96},{16,112},{32,0},{48,16},{64,32},{80,48},{96,64},{112,80},{1... | collective-permute-start | bytes 414728 | tf_op jit(solution)/shard_map/ppermute | solution.py:40
  129.1 3.0 %collective-permute-start.20 = (bf16[160,432]{1,0:T(8,128)(2,1)S(1)}, bf16[160,432]{1,0:T(8,128)(2,1)S(1)}, u32[]{:S(2)}, u32[]{:S(2)}) collective-permute-start(bf16[160,432]{1,0:T(8,128)(2,1)S(1)} %get-tuple-element.29), channel_id=1, source_target_pairs={{0,32},{16,48},{32,64},{48,80},{64,96},{80,112},{96,0},{112,16},{1... | collective-permute-start | bytes 414728 | tf_op jit(solution)/shard_map/ppermute | solution.py:40
  132.2 1.6 fusion.2
  133.8 20.1 %collective-permute-done.19 = bf16[160,432]{1,0:T(8,128)(2,1)S(1)} collective-permute-done((bf16[160,432]{1,0:T(8,128)(2,1)}, bf16[160,432]{1,0:T(8,128)(2,1)S(1)}, u32[]{:S(2)}, u32[]{:S(2)}) %collective-permute-start.19) | collective-permute-done | bytes 138272 | tf_op jit(solution)/shard_map/ppermute | solution.py:40
  154.2 2.4 %collective-permute-start.22 = (f32[80,432]{1,0:T(8,128)S(1)}, f32[80,432]{1,0:T(8,128)S(1)}, u32[]{:S(2)}, u32[]{:S(2)}) collective-permute-start(f32[80,432]{1,0:T(8,128)S(1)} %get-tuple-element.31), channel_id=1, source_target_pairs={{0,16},{16,0},{32,48},{48,32},{64,80},{80,64},{96,112},{112,96},{1... | collective-permute-start | bytes 414728 | tf_op jit(solution)/shard_map/ppermute | solution.py:32
  156.8 0.9 collective-permute-done.22
  157.9 0.8 multiply_reduce_fusion
  158.7 9.9 %psum.14 = f32[160]{0:T(256)S(1)} all-reduce(f32[160]{0:T(256)S(1)} %get-tuple-element.25), channel_id=1, replica_groups={{0,128,256,384},{16,144,272,400},{32,160,288,416},{48,176,304,432},{64,..., use_global_device_ids=true, to_apply=%region_2.3 | all-reduce | flops 160 | bytes 1280 | tf_op jit(solution)/shard_map/psum | solution.py:230
  168.6 9.4 %psum.15 = f32[160]{0:T(256)S(1)} all-reduce(f32[160]{0:T(256)S(1)} %psum.14), channel_id=1, replica_groups={{0,32,64,96},{16,48,80,112},{128,160,192,224},{144,176,208,240},{256,28..., use_global_device_ids=true, to_apply=%region_3.4 | all-reduce | flops 160 | bytes 1280 | tf_op jit(solution)/shard_map/psum | solution.py:231
  178.0 6.3 %collective-permute-start.24 = (f32[160]{0:T(256)S(1)}, f32[160]{0:T(256)S(1)}, u32[]{:S(2)}, u32[]{:S(2)}) collective-permute-start(f32[160]{0:T(256)S(1)} %psum.15), channel_id=1, source_target_pairs={{0,16},{16,0},{32,48},{48,32},{64,80},{80,64},{96,112},{112,96},{1... | collective-permute-start | bytes 1928 | tf_op jit(solution)/shard_map/ppermute | solution.py:32
  184.3 0.9 maximum_select_fusion
  (56 shorter events, 5.7 us)
Async XLA Ops:
  0.6 11.4 %copy-start.2 = (bf16[128,432]{0,1:T(8,128)(2,1)S(1)}, bf16[128,432]{0,1:T(8,128)(2,1)}, u32[]{:S(2)}) copy-start(bf16[128,432]{0,1:T(8,128)(2,1)} %param.9) | copy-start | bytes 331780
  0.6 13.4 %copy-start.1 = (bf16[128,2560]{1,0:T(8,128)(2,1)S(1)}, bf16[128,2560]{1,0:T(8,128)(2,1)}, u32[]{:S(2)}) copy-start(bf16[128,2560]{1,0:T(8,128)(2,1)} %param.5) | copy-start | bytes 1966084
  3.2 13.6 %collective-permute-start.2 = (bf16[2,80,216]{1,2,0:T(8,128)(2,1)S(1)}, bf16[2,80,216]{1,2,0:T(8,128)(2,1)S(1)}, u32[]{:S(2)}, u32[]{:S(2)}) collective-permute-start(bf16[2,80,216]{1,2,0:T(8,128)(2,1)S(1)} %pad_maximum_fusion.1), channel_id=1, source_target_pairs={{0,16},{16,0},{32,48},{48,32},{64,80},{80,64},{96,112},{112,96},{1... | collective-permute-start | bytes 207368 | tf_op jit(solution)/shard_map/ppermute | solution.py:32
  12.1 27.2 %collective-permute-start.1 = (bf16[216,128]{1,0:T(8,128)(2,1)S(1)}, bf16[216,128]{1,0:T(8,128)(2,1)S(1)}, u32[]{:S(2)}, u32[]{:S(2)}) collective-permute-start(bf16[216,128]{1,0:T(8,128)(2,1)S(1)} %get-tuple-element.45), channel_id=1, source_target_pairs={{0,16},{16,0},{32,48},{48,32},{64,80},{80,64},{96,112},{112,96},{1... | collective-permute-start | bytes 165896 | tf_op jit(solution)/shard_map/ppermute | solution.py:32
  14.4 43.3 %collective-permute-start = (bf16[128,2560]{0,1:T(8,128)(2,1)S(1)}, bf16[128,2560]{0,1:T(8,128)(2,1)S(1)}, u32[]{:S(2)}, u32[]{:S(2)}) collective-permute-start(bf16[128,2560]{0,1:T(8,128)(2,1)S(1)} %copy.11), channel_id=1, source_target_pairs={{0,16},{16,0},{32,48},{48,32},{64,80},{80,64},{96,112},{112,96},{1... | collective-permute-start | bytes 1966088 | tf_op jit(solution)/shard_map/ppermute | solution.py:32
  17.0 9.1 %collective-permute-start.11 = (bf16[160,216]{0,1:T(8,128)(2,1)S(1)}, bf16[160,216]{0,1:T(8,128)(2,1)S(1)}, u32[]{:S(2)}, u32[]{:S(2)}) collective-permute-start(bf16[160,216]{0,1:T(8,128)(2,1)S(1)} %maximum_select_fusion.3), channel_id=1, source_target_pairs={{0,32},{16,48},{32,64},{48,80},{64,96},{80,112},{96,0},{112,16},{1... | collective-permute-start | bytes 207368 | tf_op jit(solution)/shard_map/ppermute | solution.py:40
  18.9 11.6 %collective-permute-start.10 = (bf16[160,216]{0,1:T(8,128)(2,1)S(1)}, bf16[160,216]{0,1:T(8,128)(2,1)S(1)}, u32[]{:S(2)}, u32[]{:S(2)}) collective-permute-start(bf16[160,216]{0,1:T(8,128)(2,1)S(1)} %maximum_select_fusion.3), channel_id=1, source_target_pairs={{0,64},{16,80},{32,96},{48,112},{64,0},{80,16},{96,32},{112,48},{1... | collective-permute-start | bytes 207368 | tf_op jit(solution)/shard_map/ppermute | solution.py:40
  21.4 10.2 %collective-permute-start.9 = (bf16[160,216]{0,1:T(8,128)(2,1)S(1)}, bf16[160,216]{0,1:T(8,128)(2,1)S(1)}, u32[]{:S(2)}, u32[]{:S(2)}) collective-permute-start(bf16[160,216]{0,1:T(8,128)(2,1)S(1)} %maximum_select_fusion.3), channel_id=1, source_target_pairs={{0,96},{16,112},{32,0},{48,16},{64,32},{80,48},{96,64},{112,80},{1... | collective-permute-start | bytes 207368 | tf_op jit(solution)/shard_map/ppermute | solution.py:40
  31.8 22.7 %collective-permute-start.14 = (bf16[216,640]{1,0:T(8,128)(2,1)S(1)}, bf16[216,640]{1,0:T(8,128)(2,1)S(1)}, u32[]{:S(2)}, u32[]{:S(2)}) collective-permute-start(bf16[216,640]{1,0:T(8,128)(2,1)S(1)} %maximum_bitcast_fusion.2.refs_4_), channel_id=1, source_target_pairs={{0,128},{16,144},{32,160},{48,176},{64,192},{80,208},{96,224},{112... | collective-permute-start | bytes 829448 | tf_op jit(solution)/shard_map/ppermute | solution.py:36
  33.9 9.4 %collective-permute-start.5 = (bf16[160,216]{0,1:T(8,128)(2,1)S(1)}, bf16[160,216]{0,1:T(8,128)(2,1)S(1)}, u32[]{:S(2)}, u32[]{:S(2)}) collective-permute-start(bf16[160,216]{0,1:T(8,128)(2,1)S(1)} %maximum_select_fusion.2), channel_id=1, source_target_pairs={{0,32},{16,48},{32,64},{48,80},{64,96},{80,112},{96,0},{112,16},{1... | collective-permute-start | bytes 207368 | tf_op jit(solution)/shard_map/ppermute | solution.py:40
  37.3 10.2 %collective-permute-start.4 = (bf16[160,216]{0,1:T(8,128)(2,1)S(1)}, bf16[160,216]{0,1:T(8,128)(2,1)S(1)}, u32[]{:S(2)}, u32[]{:S(2)}) collective-permute-start(bf16[160,216]{0,1:T(8,128)(2,1)S(1)} %maximum_select_fusion.2), channel_id=1, source_target_pairs={{0,64},{16,80},{32,96},{48,112},{64,0},{80,16},{96,32},{112,48},{1... | collective-permute-start | bytes 207368 | tf_op jit(solution)/shard_map/ppermute | solution.py:40
  39.3 13.1 %collective-permute-start.3 = (bf16[160,216]{0,1:T(8,128)(2,1)S(1)}, bf16[160,216]{0,1:T(8,128)(2,1)S(1)}, u32[]{:S(2)}, u32[]{:S(2)}) collective-permute-start(bf16[160,216]{0,1:T(8,128)(2,1)S(1)} %maximum_select_fusion.2), channel_id=1, source_target_pairs={{0,96},{16,112},{32,0},{48,16},{64,32},{80,48},{96,64},{112,80},{1... | collective-permute-start | bytes 207368 | tf_op jit(solution)/shard_map/ppermute | solution.py:40
  43.3 19.4 %collective-permute-start.13 = (bf16[216,640]{1,0:T(8,128)(2,1)S(1)}, bf16[216,640]{1,0:T(8,128)(2,1)S(1)}, u32[]{:S(2)}, u32[]{:S(2)}) collective-permute-start(bf16[216,640]{1,0:T(8,128)(2,1)S(1)} %maximum_bitcast_fusion.2.refs_4_), channel_id=1, source_target_pairs={{0,256},{16,272},{32,288},{48,304},{64,320},{80,336},{96,352},{112... | collective-permute-start | bytes 829448 | tf_op jit(solution)/shard_map/ppermute | solution.py:36
  47.5 15.2 %collective-permute-start.12 = (bf16[216,640]{1,0:T(8,128)(2,1)S(1)}, bf16[216,640]{1,0:T(8,128)(2,1)S(1)}, u32[]{:S(2)}, u32[]{:S(2)}) collective-permute-start(bf16[216,640]{1,0:T(8,128)(2,1)S(1)} %maximum_bitcast_fusion.2.refs_4_), channel_id=1, source_target_pairs={{0,384},{16,400},{32,416},{48,432},{64,448},{80,464},{96,480},{112... | collective-permute-start | bytes 829448 | tf_op jit(solution)/shard_map/ppermute | solution.py:36
  52.6 8.6 %copy-start.3 = (f32[2560]{0:T(1024)S(1)}, f32[2560]{0:T(1024)}, u32[]{:S(2)}) copy-start(f32[2560]{0:T(1024)} %param.6) | copy-start | bytes 30724
  52.6 11.4 %collective-permute-start.8 = (bf16[216,640]{1,0:T(8,128)(2,1)S(1)}, bf16[216,640]{1,0:T(8,128)(2,1)S(1)}, u32[]{:S(2)}, u32[]{:S(2)}) collective-permute-start(bf16[216,640]{1,0:T(8,128)(2,1)S(1)} %maximum_bitcast_fusion.1.refs_0_), channel_id=1, source_target_pairs={{0,128},{16,144},{32,160},{48,176},{64,192},{80,208},{96,224},{112... | collective-permute-start | bytes 829448 | tf_op jit(solution)/shard_map/ppermute | solution.py:36
  54.5 13.2 %collective-permute-start.7 = (bf16[216,640]{1,0:T(8,128)(2,1)S(1)}, bf16[216,640]{1,0:T(8,128)(2,1)S(1)}, u32[]{:S(2)}, u32[]{:S(2)}) collective-permute-start(bf16[216,640]{1,0:T(8,128)(2,1)S(1)} %maximum_bitcast_fusion.1.refs_0_), channel_id=1, source_target_pairs={{0,256},{16,272},{32,288},{48,304},{64,320},{80,336},{96,352},{112... | collective-permute-start | bytes 829448 | tf_op jit(solution)/shard_map/ppermute | solution.py:36
  57.6 14.8 %collective-permute-start.6 = (bf16[216,640]{1,0:T(8,128)(2,1)S(1)}, bf16[216,640]{1,0:T(8,128)(2,1)S(1)}, u32[]{:S(2)}, u32[]{:S(2)}) collective-permute-start(bf16[216,640]{1,0:T(8,128)(2,1)S(1)} %maximum_bitcast_fusion.1.refs_0_), channel_id=1, source_target_pairs={{0,384},{16,400},{32,416},{48,432},{64,448},{80,464},{96,480},{112... | collective-permute-start | bytes 829448 | tf_op jit(solution)/shard_map/ppermute | solution.py:36
  76.1 16.1 %collective-permute-start.16 = (bf16[2,216,640]{2,1,0:T(8,128)(2,1)S(1)}, bf16[2,216,640]{2,1,0:T(8,128)(2,1)S(1)}, u32[]{:S(2)}, u32[]{:S(2)}) collective-permute-start(bf16[2,216,640]{2,1,0:T(8,128)(2,1)S(1)} %get-tuple-element.19), channel_id=1, source_target_pairs={{0,256},{16,272},{32,288},{48,304},{64,320},{80,336},{96,352},{112... | collective-permute-start | bytes 1658888 | tf_op jit(solution)/shard_map/ppermute | solution.py:36
  78.5 27.4 %collective-permute-start.17 = (bf16[2,216,640]{2,1,0:T(8,128)(2,1)S(1)}, bf16[2,216,640]{2,1,0:T(8,128)(2,1)S(1)}, u32[]{:S(2)}, u32[]{:S(2)}) collective-permute-start(bf16[2,216,640]{2,1,0:T(8,128)(2,1)S(1)} %get-tuple-element.20), channel_id=1, source_target_pairs={{0,128},{16,144},{32,160},{48,176},{64,192},{80,208},{96,224},{112... | collective-permute-start | bytes 1658888 | tf_op jit(solution)/shard_map/ppermute | solution.py:36
  83.9 22.2 %collective-permute-start.18 = (bf16[2,216,640]{2,1,0:T(8,128)(2,1)S(1)}, bf16[2,216,640]{2,1,0:T(8,128)(2,1)S(1)}, u32[]{:S(2)}, u32[]{:S(2)}) collective-permute-start(bf16[2,216,640]{2,1,0:T(8,128)(2,1)S(1)} %get-tuple-element.21), channel_id=1, source_target_pairs={{0,384},{16,400},{32,416},{48,432},{64,448},{80,464},{96,480},{112... | collective-permute-start | bytes 1658888 | tf_op jit(solution)/shard_map/ppermute | solution.py:36
  85.9 24.3 %collective-permute-start.23 = (bf16[2560,128]{1,0:T(8,128)(2,1)}, bf16[2560,128]{1,0:T(8,128)(2,1)}, u32[]{:S(2)}, u32[]{:S(2)}) collective-permute-start(bf16[2560,128]{1,0:T(8,128)(2,1)} %get-tuple-element.23), channel_id=1, source_target_pairs={{0,16},{16,0},{32,48},{48,32},{64,80},{80,64},{96,112},{112,96},{1... | collective-permute-start | bytes 1966088 | tf_op jit(solution)/shard_map/ppermute | solution.py:32
  90.0 42.3 %collective-permute-start.15 = (bf16[216,128]{1,0:T(8,128)(2,1)}, bf16[216,128]{1,0:T(8,128)(2,1)}, u32[]{:S(2)}, u32[]{:S(2)}) collective-permute-start(bf16[216,128]{1,0:T(8,128)(2,1)} %get-tuple-element.37), channel_id=1, source_target_pairs={{0,16},{16,0},{32,48},{48,32},{64,80},{80,64},{96,112},{112,96},{1... | collective-permute-start | bytes 165896 | tf_op jit(solution)/shard_map/ppermute | solution.py:32
  112.5 10.4 %copy-start = (f32[432,640]{0,1:T(8,128)S(1)}, f32[432,640]{0,1:T(8,128)}, u32[]{:S(2)}) copy-start(f32[432,640]{0,1:T(8,128)} %copy.16) | copy-start | bytes 3317764
  112.5 45.3 %all-to-all-start = ((bf16[16,176,128]{2,1,0:T(8,128)(2,1)}), bf16[16,176,128]{2,1,0:T(8,128)(2,1)S(1)}, u32[]{:S(2)}, u32[]{:S(2)}) async-start(bf16[16,176,128]{2,1,0:T(8,128)(2,1)} %shard_map.95), calls=%async_computation | async-start | bytes 1441792 | tf_op jit(solution)/shard_map/all_to_all | solution.py:214
  123.8 30.1 %collective-permute-start.19 = (bf16[160,432]{1,0:T(8,128)(2,1)}, bf16[160,432]{1,0:T(8,128)(2,1)S(1)}, u32[]{:S(2)}, u32[]{:S(2)}) collective-permute-start(bf16[160,432]{1,0:T(8,128)(2,1)} %get-tuple-element.27), channel_id=1, source_target_pairs={{0,64},{16,80},{32,96},{48,112},{64,0},{80,16},{96,32},{112,48},{1... | collective-permute-start | bytes 414728 | tf_op jit(solution)/shard_map/ppermute | solution.py:40
  126.8 27.3 %collective-permute-start.21 = (bf16[160,432]{1,0:T(8,128)(2,1)}, bf16[160,432]{1,0:T(8,128)(2,1)S(1)}, u32[]{:S(2)}, u32[]{:S(2)}) collective-permute-start(bf16[160,432]{1,0:T(8,128)(2,1)} %get-tuple-element.28), channel_id=1, source_target_pairs={{0,96},{16,112},{32,0},{48,16},{64,32},{80,48},{96,64},{112,80},{1... | collective-permute-start | bytes 414728 | tf_op jit(solution)/shard_map/ppermute | solution.py:40
  129.1 25.0 %collective-permute-start.20 = (bf16[160,432]{1,0:T(8,128)(2,1)S(1)}, bf16[160,432]{1,0:T(8,128)(2,1)S(1)}, u32[]{:S(2)}, u32[]{:S(2)}) collective-permute-start(bf16[160,432]{1,0:T(8,128)(2,1)S(1)} %get-tuple-element.29), channel_id=1, source_target_pairs={{0,32},{16,48},{32,64},{48,80},{64,96},{80,112},{96,0},{112,16},{1... | collective-permute-start | bytes 414728 | tf_op jit(solution)/shard_map/ppermute | solution.py:40
  154.2 3.4 %collective-permute-start.22 = (f32[80,432]{1,0:T(8,128)S(1)}, f32[80,432]{1,0:T(8,128)S(1)}, u32[]{:S(2)}, u32[]{:S(2)}) collective-permute-start(f32[80,432]{1,0:T(8,128)S(1)} %get-tuple-element.31), channel_id=1, source_target_pairs={{0,16},{16,0},{32,48},{48,32},{64,80},{80,64},{96,112},{112,96},{1... | collective-permute-start | bytes 414728 | tf_op jit(solution)/shard_map/ppermute | solution.py:32
  178.0 7.2 %collective-permute-start.24 = (f32[160]{0:T(256)S(1)}, f32[160]{0:T(256)S(1)}, u32[]{:S(2)}, u32[]{:S(2)}) collective-permute-start(f32[160]{0:T(256)S(1)} %psum.15), channel_id=1, source_target_pairs={{0,16},{16,0},{32,48},{48,32},{64,80},{80,64},{96,112},{112,96},{1... | collective-permute-start | bytes 1928 | tf_op jit(solution)/shard_map/ppermute | solution.py:32

commit v3 on v2

--- a/solution.py
+++ b/solution.py
@@ -36,19 +36,18 @@
     return lax.ppermute(value, "blk", pairs(lambda x, z, c: ((x + steps) % NX, z, c)))
 
 
-def shift_z(value, steps):
-    return lax.ppermute(value, "blk", pairs(lambda x, z, c: (x, (z + steps) % NZ, c)))
+NH = 2
+
+
+def y_groups(count):
+    return [[index * NH + high for index in range(count // NH)] for high in range(NH)]
 
 
 X_GROUPS = [[place(x, z, c) for x in range(NX)] for z in range(NZ) for c in range(NC)]
 Z_GROUPS = [[place(x, z, c) for z in range(NZ)] for x in range(NX) for c in range(NC)]
 
 
-def block_order(spot_ref, index):
-    return ((spot_ref[0] + index // NZ) % NX) * NZ + (spot_ref[1] + index % NZ) % NZ
-
-
-def norm_kernel(spot_ref, x_ref, gain_ref, normed_ref, root_ref):
+def norm_kernel(x_ref, gain_ref, normed_ref, root_ref):
     width, tokens = x_ref.shape
     size = width // (NX * NZ)
     total = jnp.zeros((size, tokens), F32)
@@ -58,32 +57,32 @@
     root = jnp.sqrt(jnp.sum(total, axis=0, keepdims=True) / width + 1e-05)
     root_ref[...] = root
     for index in range(NX * NZ):
-        rows = pl.ds(pl.multiple_of(block_order(spot_ref, index) * size, size), size)
+        rows = pl.ds(index * size, size)
         unit = x_ref[rows, :].astype(F32) / root
         gain = gain_ref[rows, :]
         gain = jnp.concatenate([gain, gain], axis=1)
-        normed_ref[pl.ds(index * size, size), :] = (unit * gain).astype(BF)
-
-
-def forward_kernel(normed_ref, upstream_ref, *refs):
-    gates, ups = refs[:NX], refs[NX : 2 * NX]
-    hidden_ref, back_ref, own_ref, other_ref = refs[2 * NX :]
-    size = gates[0].shape[1]
+        normed_ref[rows, :] = (unit * gain).astype(BF)
+
+
+def forward_kernel(
+    normed_ref, upstream_ref, weight_ref, hidden_ref, back_ref, own_ref, other_ref
+):
+    size = weight_ref.shape[3]
     tokens = own_ref.shape[1]
 
-    def product(pieces):
+    def product(which):
         total = None
         for index in range(NX):
             term = jnp.dot(
-                pieces[index][...],
+                weight_ref[index, which],
                 normed_ref[pl.ds(index * size, size), :],
                 preferred_element_type=F32,
             )
             total = term if total is None else total + term
         return total
 
-    gate_pre = product(gates)
-    up_pre = product(ups)
+    gate_pre = product(0)
+    up_pre = product(1)
     sigmoid = 1.0 / (1.0 + jnp.exp(-gate_pre))
     activated = gate_pre * sigmoid
     hidden_ref[...] = (activated * up_pre).astype(BF)
@@ -93,33 +92,32 @@
     back_ref[0] = back_gate
     back_ref[1] = back_up
     for index in range(NX):
-        part = lax.dot_general(gates[index][...], back_gate, TN, preferred_element_type=F32)
-        part += lax.dot_general(ups[index][...], back_up, TN, preferred_element_type=F32)
+        part = lax.dot_general(weight_ref[index, 0], back_gate, TN, preferred_element_type=F32)
+        part += lax.dot_general(weight_ref[index, 1], back_up, TN, preferred_element_type=F32)
         rows = pl.ds(index * size, size)
         own_ref[rows, :] = part[:, :tokens]
         other_ref[rows, :] = part[:, tokens:].astype(BF)
 
 
-def gradient_kernel(normed_ref, back_ref, *outs):
+def gradient_kernel(spot_ref, normed_ref, back_ref, *outs):
     size = outs[0].shape[2]
     for index in range(NX):
-        rows = normed_ref[pl.ds(index * size, size), :]
+        block = (spot_ref[0] + index) % NX
+        rows = normed_ref[pl.ds(pl.multiple_of(block * size, size), size), :]
         for which in range(2):
             term = lax.dot_general(back_ref[which], rows, NT, preferred_element_type=F32)
             outs[index][which] = term.astype(outs[index].dtype)
 
 
-def blocks_kernel(spot_ref, own_ref, other_ref, x_ref, root_ref, gain_ref, out_ref):
+def blocks_kernel(own_ref, other_ref, x_ref, root_ref, gain_ref, out_ref):
     width, tokens = own_ref.shape
     size = width // (NX * NZ)
     root = root_ref[...]
     total = jnp.zeros((size, tokens), F32)
     for index in range(NX * NZ):
-        here = pl.ds(index * size, size)
-        block = block_order(spot_ref, index)
-        rows = pl.ds(pl.multiple_of(block * size, size), size)
-        part = (own_ref[here, :] + other_ref[here, :].astype(F32)).astype(BF)
-        out_ref[block, 0:size, :] = part
+        rows = pl.ds(index * size, size)
+        part = (own_ref[rows, :] + other_ref[rows, :].astype(F32)).astype(BF)
+        out_ref[index, 0:size, :] = part
         unit = x_ref[rows, :].astype(F32) / root
         total += part.astype(F32) * gain_ref[rows, :] * unit
     dots = jnp.sum(total, axis=0, keepdims=True)
@@ -150,7 +148,7 @@
 def per_device(inputs, gain, w_gate, w_up, upstream):
     position = lax.axis_index("blk")
     core = position % NC
-    spot = jnp.stack([position // (NZ * NC), (position // NC) % NZ]).astype(jnp.int32)
+    spot = (position // (NZ * NC)).astype(jnp.int32).reshape(1)
     first = core == 0
     tokens, width = inputs.shape
     rows, columns = w_gate.shape
@@ -170,12 +168,11 @@
 
     gate_mine, gate_other = halves(w_gate, 1)
     up_mine, up_other = halves(w_up, 1)
-    got = swap_core(jnp.stack([gate_other, up_other]))
-    chip = [ordered(gate_mine, got[0], 0), ordered(up_mine, got[1], 0)]
-    pieces = []
-    for chunk in chip:
-        column = jnp.concatenate([chunk] + [shift_z(chunk, -step) for step in (1, 2, 3)], 0).T
-        pieces.append([column] + [shift_x(column, -step) for step in (1, 2, 3)])
+    weight_other = swap_core(jnp.concatenate([gate_other, up_other], 1))
+    chip = ordered(jnp.concatenate([gate_mine, up_mine], 1), weight_other, 0)
+    column = lax.all_gather(chip, "blk", axis=0, tiled=True, axis_index_groups=Z_GROUPS).T
+    copies = jnp.broadcast_to(column.reshape(2, half, column_rows), (NX, 2, half, column_rows))
+    weight = lax.all_to_all(copies, "blk", 0, 0, tiled=True, axis_index_groups=X_GROUPS)
 
     inputs_t = jnp.concatenate([inputs, swap_core(inputs)], 0).T
     upstream_mine, upstream_other = halves(upstream.T, 0)
@@ -184,8 +181,8 @@
     normed, root_mean = call(
         norm_kernel,
         (shape((width, 2 * tokens), BF), shape((1, 2 * tokens), F32)),
-        [SMEM, VMEM, VMEM],
-    )(spot, inputs_t, gain_wide)
+        [VMEM] * 2,
+    )(inputs_t, gain_wide)
 
     hidden_pair, back, part_own, part_other = call(
         forward_kernel,
@@ -195,24 +192,32 @@
             shape((width, tokens), F32),
             shape((width, tokens), BF),
         ),
-        [VMEM] * (2 + 2 * NX),
-    )(normed, upstream_pair, *pieces[0], *pieces[1])
+        [VMEM] * 3,
+    )(normed, upstream_pair, weight)
     part_other = swap_core(part_other)
     terms = call(
         gradient_kernel,
         tuple(shape((2, half, column_rows), F32 if index == 0 else BF) for index in range(NX)),
-        [VMEM] * 2,
-    )(normed, back)
+        [SMEM] + [VMEM] * 2,
+    )(spot, normed, back)
     travelling = [shift_x(terms[steps], steps) for steps in (2, 1, 3)]
     hidden_other = swap_core(hidden_pair[:, tokens:])
     hidden = ordered(hidden_pair[:, :tokens], hidden_other, 0).T
 
     spare = 16
-    sending = call(
-        blocks_kernel, shape((n_dp, features + spare, tokens), BF), [SMEM] + [VMEM] * 5
-    )(spot, part_own, part_other, inputs_t[:, :tokens], root_mean[:, :tokens], gain_wide)
-    got = lax.all_to_all(sending, "dp", 0, 0, tiled=True)
-    totals = jnp.sum(got.astype(F32), axis=0)
+    sending = call(blocks_kernel, shape((n_dp, features + spare, tokens), BF), [VMEM] * 5)(
+        part_own, part_other, inputs_t[:, :tokens], root_mean[:, :tokens], gain_wide
+    )
+    sending = sending.reshape(n_dp // NH, NH * (features + spare), tokens)
+    got = lax.all_to_all(sending, "dp", 0, 0, tiled=True, axis_index_groups=y_groups(n_dp))
+    got, travelling = lax.optimization_barrier((got, travelling))
+    y_sums = jnp.sum(got.astype(F32), axis=0).reshape(NH, features + spare, tokens)
+    low_half = lax.axis_index("dp") % NH == 0
+    totals = jnp.where(low_half, y_sums[0], y_sums[1]) + lax.ppermute(
+        jnp.where(low_half, y_sums[1], y_sums[0]),
+        "dp",
+        [(index, index ^ 1) for index in range(n_dp)],
+    )
     own_sums = totals[:features]
     token_totals = totals[features] + totals[features + 1] + totals[features + 2]
     start = lax.axis_index("dp") * features
@@ -229,21 +234,29 @@
     gain_part = jnp.sum(own_sums * unit_slice, axis=1)
     gain_part = lax.psum(gain_part, "blk", axis_index_groups=X_GROUPS)
     gain_part = lax.psum(gain_part, "blk", axis_index_groups=Z_GROUPS)
-    grad_gain = gain_part + swap_core(gain_part)
 
     column_sum = terms[0]
     for value in travelling:
         column_sum = column_sum + value.astype(F32)
-    column_sum = column_sum.reshape(columns, column_rows).T.reshape(NZ, rows * NC, columns)
-    chip_sum = column_sum[0]
-    for step in (2, 1, 3):
-        chip_sum = chip_sum + shift_z(column_sum[step].astype(BF), step).astype(F32)
+    column_sum = column_sum.reshape(columns, column_rows).T.astype(BF)
+    blocks = lax.all_to_all(
+        column_sum.reshape(NZ, rows * NC, columns),
+        "blk",
+        0,
+        0,
+        tiled=True,
+        axis_index_groups=Z_GROUPS,
+    )
+    chip_sum = jnp.sum(blocks.astype(F32), axis=0)
     sum_mine, sum_other = chip_sum[:rows], chip_sum[rows:]
     sum_mine, sum_other = (
         jnp.where(first, sum_mine, sum_other),
         jnp.where(first, sum_other, sum_mine),
     )
-    sum_other = swap_core(sum_other)
+    gain_row = jnp.pad(gain_part, (0, columns - features))[None, :]
+    other = swap_core(jnp.concatenate([sum_other, gain_row], 0))
+    sum_other = other[:rows]
+    grad_gain = gain_part + other[rows, :features]
     grad_gate = ordered(sum_mine[:, :half], sum_other[:, :half], 1)
     grad_up = ordered(sum_mine[:, half:], sum_other[:, half:], 1)
     return (hidden, grad_gate, grad_up, grad_input, grad_gain)

time: 187 us -> 165 us (0.88)
  starting transfers between devices: 92.5 us -> 64.2 us
  blocking collectives: 19.3 us -> 30 us
  waiting for transfers between devices: 51.6 us -> 42 us
  other arithmetic: 6.38 us -> 10.4 us
  local copies, waits for them, and re-layouts: 7.62 us -> 10.9 us
    ppermute x9 -> x3, starting transfers between devices: 28.3 us -> 8.67 us  [shift_x(): lax.ppermute(value, 'blk', pairs(lambda x, z, c: ((x + steps) % NX, z, c)))]
    ppermute x9 -> x1, starting transfers between devices: 26.7 us -> 7.94 us  [per_device(): lax.ppermute(jnp.where(low_half, y_sums[1], y_sums[0]), 'dp', [(index, in...]
    ppermute x9 -> x1, waiting for transfers between devices: 26.7 us -> 10.5 us  [per_device(): lax.ppermute(jnp.where(low_half, y_sums[1], y_sums[0]), 'dp', [(index, in...]
    all_gather x0 -> x1, blocking collectives: none -> 13.4 us  [per_device(): lax.all_gather(chip, 'blk', axis=0, tiled=True, axis_index_groups=Z_GROUPS)]
    all_to_all x1 -> x3, waiting for transfers between devices: 0.01 us -> 9.78 us  [the longest x1 9.78 us: per_device(): lax.all_to_all(copies, 'blk', 0, 0, tiled=True, axis_index_groups=X_GROUPS)]
    ppermute x9 -> x3, waiting for transfers between devices: 24 us -> 17.1 us  [shift_x(): lax.ppermute(value, 'blk', pairs(lambda x, z, c: ((x + steps) % NX, z, c)))]
    ppermute x7 -> x6, starting transfers between devices: 27.2 us -> 33.4 us  [swap_core(): return lax.ppermute(value, 'blk', pairs(lambda x, z, c: (x, z, 1 - c)))]
    unnamed x13 -> x29, local copies, waits for them, and re-layouts: 0.81 us -> 6.59 us
  transfers between devices with their start and end apart: 26 -> 13, of which waited for: 12 -> 8; matrix products, arithmetic and copies ran while one was open for 5% -> 6% of each run, Pallas kernels for 2% -> 1%
where the time goes in v3:
time: 165 us; the launch traced here: 164 us
  starting transfers between devices  64.2 us (39%)
  waiting for transfers between devices  42 us (25%)
  blocking collectives  30 us (18%)
  local copies, waits for them, and re-layouts  10.9 us (7%)
  other arithmetic  10.4 us (6%)
  Pallas kernels  5.5 us (3%)
    ppermute x6, starting transfers between devices, swap_core(): return lax.ppermute(value, 'blk', pairs(lambda x, z, c: (x, z, 1 - c)))  33.4 us
    ppermute x3, waiting for transfers between devices, shift_x(): lax.ppermute(value, 'blk', pairs(lambda x, z, c: ((x + steps) % NX, z, c)))  17.1 us
    all_gather x1, blocking collectives, per_device(): lax.all_gather(chip, 'blk', axis=0, tiled=True, axis_index_groups=Z_GROUPS)  13.4 us
    ppermute x1, waiting for transfers between devices, per_device(): lax.ppermute(jnp.where(low_half, y_sums[1], y_sums[0]), 'dp', [(index, in...  10.5 us
    all_to_all x1, waiting for transfers between devices, per_device(): lax.all_to_all(copies, 'blk', 0, 0, tiled=True, axis_index_groups=X_GROUPS)  9.78 us
    psum x1, blocking collectives, per_device(): gain_part = lax.psum(gain_part, 'blk', axis_index_groups=Z_GROUPS)  9.75 us
    ppermute x3, starting transfers between devices, shift_x(): lax.ppermute(value, 'blk', pairs(lambda x, z, c: ((x + steps) % NX, z, c)))  8.67 us
    ppermute x1, starting transfers between devices, per_device(): lax.ppermute(jnp.where(low_half, y_sums[1], y_sums[0]), 'dp', [(index, in...  7.94 us
  transfers between devices with their start and end apart: 13, of which 8 were waited for; matrix products, arithmetic and copies ran while one was open for 6% of the time, Pallas kernels for 1%

profile of v3, /device:TPU:1, one launch (start us, length us, event | category | flops | bytes accessed | tf_op | source)
XLA Modules:
  0.0 164.1 jit_solution(13498401152737854053)
XLA Ops:
  0.6 1.0 broadcast_select_fusion.5
  1.6 1.0 broadcast_select_fusion.4
  2.7 8.8 %collective-permute-start.2 = (bf16[80,432]{1,0:T(8,128)(2,1)S(1)}, bf16[80,432]{1,0:T(8,128)(2,1)S(1)}, u32[]{:S(2)}, u32[]{:S(2)}) collective-permute-start(bf16[80,432]{1,0:T(8,128)(2,1)S(1)} %pad_maximum_fusion.2), channel_id=1, source_target_pairs={{0,16},{16,0},{32,48},{48,32},{64,80},{80,64},{96,112},{112,96},{1... | collective-permute-start | bytes 207368 | tf_op jit(solution)/shard_map/ppermute | solution.py:32
  11.5 0.9 collective-permute-done.2
  12.5 13.4 %all_gather.3 = bf16[640,432]{1,0:T(8,128)(2,1)S(1)} all-gather(bf16[160,432]{1,0:T(8,128)(2,1)S(1)} %maximum_select_fusion), channel_id=1, replica_groups={{0,32,64,96},{16,48,80,112},{128,160,192,224},{144,176,208,240},{256,28..., dimensions={0}, use_global_device_ids=true | all-gather | bytes 691200 | tf_op jit(solution)/shard_map/all_gather | solution.py:173
  26.3 1.6 broadcast_in_dim.7
  27.8 3.7 %all-to-all-start = ((bf16[4,2,216,640]{3,2,1,0:T(8,128)(2,1)}), bf16[4,2,216,640]{3,2,1,0:T(8,128)(2,1)S(1)}, u32[]{:S(2)}, u32[]{:S(2)}) async-start(bf16[4,2,216,640]{3,2,1,0:T(8,128)(2,1)} %broadcast_in_dim.7), calls=%async_computation | async-start | bytes 4423680 | tf_op jit(solution)/shard_map/all_to_all | solution.py:175
  31.9 5.6 %collective-permute-start = (bf16[128,2560]{0,1:T(8,128)(2,1)S(1)}, bf16[128,2560]{0,1:T(8,128)(2,1)S(1)}, u32[]{:S(2)}, u32[]{:S(2)}) collective-permute-start(bf16[128,2560]{0,1:T(8,128)(2,1)S(1)} %copy.21), channel_id=1, source_target_pairs={{0,16},{16,0},{32,48},{48,32},{64,80},{80,64},{96,112},{112,96},{1... | collective-permute-start | bytes 1966088 | tf_op jit(solution)/shard_map/ppermute | solution.py:32
  37.6 0.9 broadcast_select_fusion.1
  38.4 1.9 %collective-permute-start.1 = (bf16[216,128]{1,0:T(8,128)(2,1)S(1)}, bf16[216,128]{1,0:T(8,128)(2,1)S(1)}, u32[]{:S(2)}, u32[]{:S(2)}) collective-permute-start(bf16[216,128]{1,0:T(8,128)(2,1)S(1)} %get-tuple-element.44), channel_id=1, source_target_pairs={{0,16},{16,0},{32,48},{48,32},{64,80},{80,64},{96,112},{112,96},{1... | collective-permute-start | bytes 165896 | tf_op jit(solution)/shard_map/ppermute | solution.py:32
  40.4 1.2 collective-permute-done.1
  41.6 0.7 pad_maximum_fusion.1.upstream_ref
  42.4 0.6 copy-done.13
  43.3 0.7 copy-done
  44.0 0.6 shard_map.92
  44.6 1.1 copy-done.2
  45.7 9.8 %all-to-all-done.weight_ref = bf16[4,2,216,640]{3,2,1,0:T(8,128)(2,1)S(1)} async-done(((bf16[4,2,216,640]{3,2,1,0:T(8,128)(2,1)}), bf16[4,2,216,640]{3,2,1,0:T(8,128)(2,1)S(1)}, u32[]{:S(2)}, u32[]{:S(2)}) %all-to-all-start) | async-done | bytes 2211872 | tf_op jit(solution)/shard_map/all_to_all | solution.py:175
  55.4 1.3 copy-done.3
  56.7 0.9 copy-done.5
  57.6 1.8 %shard_map.93 = (bf16[216,256]{1,0:T(8,128)(2,1)S(1)}, bf16[2,216,256]{2,1,0:T(8,128)(2,1)S(1)}, f32[2560,128]{1,0:T(8,128)S(1)}, bf16[2560,128]{1,0:T(8,128)(2,1)S(1)}) custom-call(bf16[2560,256]{1,0:T(8,128)(2,1)S(1)} %copy-done.3, bf16[216,256]{1,0:T(8,128)(2,1)S(1)} %copy-done.5, bf16[4,2,216,640]{3,2,1,0:T(8,128)(2,1)S(1)} %all-to-all-done.weight_ref), custom_call_target="tpu_custom_call" | custom-call | tf_op jit(solution)/shard_map/pallas_call | solution.py:187
  59.5 6.6 %collective-permute-start.4 = (bf16[2560,128]{1,0:T(8,128)(2,1)S(1)}, bf16[2560,128]{1,0:T(8,128)(2,1)S(1)}, u32[]{:S(2)}, u32[]{:S(2)}) collective-permute-start(bf16[2560,128]{1,0:T(8,128)(2,1)S(1)} %get-tuple-element.24), channel_id=1, source_target_pairs={{0,16},{16,0},{32,48},{48,32},{64,80},{80,64},{96,112},{112,96},{1... | collective-permute-start | bytes 1966088 | tf_op jit(solution)/shard_map/ppermute | solution.py:32
  66.1 1.6 collective-permute-done.4.other_ref
  67.7 1.3 shard_map.95
  69.1 6.9 %all-to-all-start.1 = ((bf16[8,352,128]{2,1,0:T(8,128)(2,1)}), bf16[8,352,128]{2,1,0:T(8,128)(2,1)}, u32[]{:S(2)}, u32[]{:S(2)}) async-start(bf16[8,352,128]{2,1,0:T(8,128)(2,1)} %bitcast.6), calls=%async_computation.1 | async-start | bytes 1441792 | tf_op jit(solution)/shard_map/all_to_all | solution.py:212
  75.9 0.9 copy-done.7
  76.9 1.8 %shard_map.94 = (f32[2,216,640]{2,1,0:T(8,128)S(1)}, bf16[2,216,640]{2,1,0:T(8,128)(2,1)}, bf16[2,216,640]{2,1,0:T(8,128)(2,1)}, bf16[2,216,640]{2,1,0:T(8,128)(2,1)}) custom-call(s32[1]{0:T(128)} %bitcast.5.spot_ref, bf16[2560,256]{1,0:T(8,128)(2,1)S(1)} %copy-done.4, bf16[2,216,256]{2,1,0:T(8,128)(2,1)S(1)} %copy-done.7), custom_call_target="tpu_custom_call" | custom-call | tf_op jit(solution)/shard_map/pallas_call | solution.py:198
  78.7 2.2 %collective-permute-start.5 = (bf16[2,216,640]{2,1,0:T(8,128)(2,1)}, bf16[2,216,640]{2,1,0:T(8,128)(2,1)S(1)}, u32[]{:S(2)}, u32[]{:S(2)}) collective-permute-start(bf16[2,216,640]{2,1,0:T(8,128)(2,1)} %get-tuple-element.26), channel_id=1, source_target_pairs={{0,256},{16,272},{32,288},{48,304},{64,320},{80,336},{96,352},{112... | collective-permute-start | bytes 1658888 | tf_op jit(solution)/shard_map/ppermute | solution.py:36
  80.9 3.1 %collective-permute-start.6 = (bf16[2,216,640]{2,1,0:T(8,128)(2,1)}, bf16[2,216,640]{2,1,0:T(8,128)(2,1)S(1)}, u32[]{:S(2)}, u32[]{:S(2)}) collective-permute-start(bf16[2,216,640]{2,1,0:T(8,128)(2,1)} %get-tuple-element.27), channel_id=1, source_target_pairs={{0,128},{16,144},{32,160},{48,176},{64,192},{80,208},{96,224},{112... | collective-permute-start | bytes 1658888 | tf_op jit(solution)/shard_map/ppermute | solution.py:36
  84.0 3.4 %collective-permute-start.7 = (bf16[2,216,640]{2,1,0:T(8,128)(2,1)}, bf16[2,216,640]{2,1,0:T(8,128)(2,1)S(1)}, u32[]{:S(2)}, u32[]{:S(2)}) collective-permute-start(bf16[2,216,640]{2,1,0:T(8,128)(2,1)} %get-tuple-element.28), channel_id=1, source_target_pairs={{0,384},{16,400},{32,416},{48,432},{64,448},{80,464},{96,480},{112... | collective-permute-start | bytes 1658888 | tf_op jit(solution)/shard_map/ppermute | solution.py:36
  87.5 0.6 fusion.6
  88.1 3.4 %collective-permute-start.3 = (bf16[216,128]{1,0:T(8,128)(2,1)}, bf16[216,128]{1,0:T(8,128)(2,1)}, u32[]{:S(2)}, u32[]{:S(2)}) collective-permute-start(bf16[216,128]{1,0:T(8,128)(2,1)} %get-tuple-element.42), channel_id=1, source_target_pairs={{0,16},{16,0},{32,48},{48,32},{64,80},{80,64},{96,112},{112,96},{1... | collective-permute-start | bytes 165896 | tf_op jit(solution)/shard_map/ppermute | solution.py:32
  91.5 4.3 %collective-permute-done.5 = bf16[2,216,640]{2,1,0:T(8,128)(2,1)S(1)} collective-permute-done((bf16[2,216,640]{2,1,0:T(8,128)(2,1)}, bf16[2,216,640]{2,1,0:T(8,128)(2,1)S(1)}, u32[]{:S(2)}, u32[]{:S(2)}) %collective-permute-start.5) | collective-permute-done | bytes 552992 | tf_op jit(solution)/shard_map/ppermute | solution.py:36
  95.9 12.7 %collective-permute-done.6 = bf16[2,216,640]{2,1,0:T(8,128)(2,1)S(1)} collective-permute-done((bf16[2,216,640]{2,1,0:T(8,128)(2,1)}, bf16[2,216,640]{2,1,0:T(8,128)(2,1)S(1)}, u32[]{:S(2)}, u32[]{:S(2)}) %collective-permute-start.6) | collective-permute-done | bytes 552992 | tf_op jit(solution)/shard_map/ppermute | solution.py:36
  108.6 0.8 copy-done.11
  109.4 1.4 add_convert_fusion
  110.8 1.1 copy.23
  111.9 3.6 %all-to-all-start.2 = ((bf16[4,160,432]{2,1,0:T(8,128)(2,1)}), bf16[4,160,432]{2,1,0:T(8,128)(2,1)S(1)}, u32[]{:S(2)}, u32[]{:S(2)}) async-start(bf16[4,160,432]{2,1,0:T(8,128)(2,1)} %bitcast.9), calls=%async_computation.2 | async-start | bytes 1310720 | tf_op jit(solution)/shard_map/all_to_all | solution.py:242
  115.5 1.2 convert_reduce_fusion
  116.8 7.9 %collective-permute-start.8 = (f32[176,128]{1,0:T(8,128)S(1)}, f32[176,128]{1,0:T(8,128)S(1)}, u32[]{:S(2)}, u32[]{:S(2)}) collective-permute-start(f32[176,128]{1,0:T(8,128)S(1)} %slice_select_fusion.2), channel_id=1, source_target_pairs={{0,1},{1,0},{2,3},{3,2},{4,5},{5,4},{6,7},{7,6},{8,9},{9,8},{10,11... | collective-permute-start | bytes 270344 | tf_op jit(solution)/shard_map/ppermute | solution.py:216
  124.8 1.6 fusion
  126.3 10.5 %collective-permute-done.8 = f32[176,128]{1,0:T(8,128)S(1)} collective-permute-done((f32[176,128]{1,0:T(8,128)S(1)}, f32[176,128]{1,0:T(8,128)S(1)}, u32[]{:S(2)}, u32[]{:S(2)}) %collective-permute-start.8) | collective-permute-done | bytes 90144 | tf_op jit(solution)/shard_map/ppermute | solution.py:216
  136.9 0.8 fusion.1
  137.6 6.8 %psum.14 = f32[160]{0:T(256)S(1)} all-reduce(f32[160]{0:T(256)S(1)} %get-tuple-element.34), channel_id=1, replica_groups={{0,128,256,384},{16,144,272,400},{32,160,288,416},{48,176,304,432},{64,..., use_global_device_ids=true, to_apply=%region_3.4 | all-reduce | flops 160 | bytes 1280 | tf_op jit(solution)/shard_map/psum | solution.py:235
  144.5 9.8 %psum.15 = f32[160]{0:T(256)S(1)} all-reduce(f32[160]{0:T(256)S(1)} %psum.14), channel_id=1, replica_groups={{0,32,64,96},{16,48,80,112},{128,160,192,224},{144,176,208,240},{256,28..., use_global_device_ids=true, to_apply=%region_4.5 | all-reduce | flops 160 | bytes 1280 | tf_op jit(solution)/shard_map/psum | solution.py:236
  154.4 7.1 %collective-permute-start.9 = (f32[81,432]{1,0:T(8,128)S(1)}, f32[81,432]{1,0:T(8,128)S(1)}, u32[]{:S(2)}, u32[]{:S(2)}) collective-permute-start(f32[81,432]{1,0:T(8,128)S(1)} %pad_maximum_fusion), channel_id=1, source_target_pairs={{0,16},{16,0},{32,48},{48,32},{64,80},{80,64},{96,112},{112,96},{1... | collective-permute-start | bytes 419912 | tf_op jit(solution)/shard_map/ppermute | solution.py:32
  161.6 0.9 collective-permute-done.9
  162.5 0.6 add.50
  163.2 0.9 maximum_select_fusion.1
  (45 shorter events, 1.9 us)
Async XLA Ops:
  2.7 9.7 %collective-permute-start.2 = (bf16[80,432]{1,0:T(8,128)(2,1)S(1)}, bf16[80,432]{1,0:T(8,128)(2,1)S(1)}, u32[]{:S(2)}, u32[]{:S(2)}) collective-permute-start(bf16[80,432]{1,0:T(8,128)(2,1)S(1)} %pad_maximum_fusion.2), channel_id=1, source_target_pairs={{0,16},{16,0},{32,48},{48,32},{64,80},{80,64},{96,112},{112,96},{1... | collective-permute-start | bytes 207368 | tf_op jit(solution)/shard_map/ppermute | solution.py:32
  27.8 3.8 %copy-start.10 = (bf16[128,2560]{1,0:T(8,128)(2,1)S(1)}, bf16[128,2560]{1,0:T(8,128)(2,1)}, u32[]{:S(2)}) copy-start(bf16[128,2560]{1,0:T(8,128)(2,1)} %param.5) | copy-start | bytes 1966084
  27.8 27.6 %all-to-all-start = ((bf16[4,2,216,640]{3,2,1,0:T(8,128)(2,1)}), bf16[4,2,216,640]{3,2,1,0:T(8,128)(2,1)S(1)}, u32[]{:S(2)}, u32[]{:S(2)}) async-start(bf16[4,2,216,640]{3,2,1,0:T(8,128)(2,1)} %broadcast_in_dim.7), calls=%async_computation | async-start | bytes 4423680 | tf_op jit(solution)/shard_map/all_to_all | solution.py:175
  31.9 10.3 %collective-permute-start = (bf16[128,2560]{0,1:T(8,128)(2,1)S(1)}, bf16[128,2560]{0,1:T(8,128)(2,1)S(1)}, u32[]{:S(2)}, u32[]{:S(2)}) collective-permute-start(bf16[128,2560]{0,1:T(8,128)(2,1)S(1)} %copy.21), channel_id=1, source_target_pairs={{0,16},{16,0},{32,48},{48,32},{64,80},{80,64},{96,112},{112,96},{1... | collective-permute-start | bytes 1966088 | tf_op jit(solution)/shard_map/ppermute | solution.py:32
  38.4 3.1 %collective-permute-start.1 = (bf16[216,128]{1,0:T(8,128)(2,1)S(1)}, bf16[216,128]{1,0:T(8,128)(2,1)S(1)}, u32[]{:S(2)}, u32[]{:S(2)}) collective-permute-start(bf16[216,128]{1,0:T(8,128)(2,1)S(1)} %get-tuple-element.44), channel_id=1, source_target_pairs={{0,16},{16,0},{32,48},{48,32},{64,80},{80,64},{96,112},{112,96},{1... | collective-permute-start | bytes 165896 | tf_op jit(solution)/shard_map/ppermute | solution.py:32
  42.2 0.7 copy-start.13
  42.9 1.1 copy-start
  44.6 1.1 copy-start.2
  55.4 1.3 copy-start.3
  56.7 0.9 copy-start.5
  57.6 8.4 %copy-start.1 = (bf16[2560,256]{1,0:T(8,128)(2,1)S(1)}, bf16[2560,256]{1,0:T(8,128)(2,1)}, u32[]{:S(2)}) copy-start(bf16[2560,256]{1,0:T(8,128)(2,1)} %copy-done) | copy-start | bytes 3932164
  59.4 9.6 %copy-start.6 = (bf16[2,216,256]{2,1,0:T(8,128)(2,1)}, bf16[2,216,256]{2,1,0:T(8,128)(2,1)S(1)}, u32[]{:S(2)}) copy-start(bf16[2,216,256]{2,1,0:T(8,128)(2,1)S(1)} %get-tuple-element.21.back_ref) | copy-start | bytes 663556
  59.4 9.6 %copy-start.8 = (bf16[216,256]{1,0:T(8,128)(2,1)}, bf16[216,256]{1,0:T(8,128)(2,1)S(1)}, u32[]{:S(2)}) copy-start(bf16[216,256]{1,0:T(8,128)(2,1)S(1)} %get-tuple-element.20) | copy-start | bytes 331780
  59.5 8.3 %collective-permute-start.4 = (bf16[2560,128]{1,0:T(8,128)(2,1)S(1)}, bf16[2560,128]{1,0:T(8,128)(2,1)S(1)}, u32[]{:S(2)}, u32[]{:S(2)}) collective-permute-start(bf16[2560,128]{1,0:T(8,128)(2,1)S(1)} %get-tuple-element.24), channel_id=1, source_target_pairs={{0,16},{16,0},{32,48},{48,32},{64,80},{80,64},{96,112},{112,96},{1... | collective-permute-start | bytes 1966088 | tf_op jit(solution)/shard_map/ppermute | solution.py:32
  69.0 6.9 %copy-start.4 = (bf16[2560,256]{1,0:T(8,128)(2,1)S(1)}, bf16[2560,256]{1,0:T(8,128)(2,1)}, u32[]{:S(2)}) copy-start(bf16[2560,256]{1,0:T(8,128)(2,1)} %copy-done.2) | copy-start | bytes 3932164
  69.0 18.4 %copy-start.9 = (bf16[216,256]{1,0:T(8,128)(2,1)S(1)}, bf16[216,256]{1,0:T(8,128)(2,1)}, u32[]{:S(2)}) copy-start(bf16[216,256]{1,0:T(8,128)(2,1)} %copy-done.8) | copy-start | bytes 331780
  69.1 39.6 %all-to-all-start.1 = ((bf16[8,352,128]{2,1,0:T(8,128)(2,1)}), bf16[8,352,128]{2,1,0:T(8,128)(2,1)}, u32[]{:S(2)}, u32[]{:S(2)}) async-start(bf16[8,352,128]{2,1,0:T(8,128)(2,1)} %bitcast.6), calls=%async_computation.1 | async-start | bytes 1441792 | tf_op jit(solution)/shard_map/all_to_all | solution.py:212
  75.9 0.9 copy-start.7
  78.7 17.2 %collective-permute-start.5 = (bf16[2,216,640]{2,1,0:T(8,128)(2,1)}, bf16[2,216,640]{2,1,0:T(8,128)(2,1)S(1)}, u32[]{:S(2)}, u32[]{:S(2)}) collective-permute-start(bf16[2,216,640]{2,1,0:T(8,128)(2,1)} %get-tuple-element.26), channel_id=1, source_target_pairs={{0,256},{16,272},{32,288},{48,304},{64,320},{80,336},{96,352},{112... | collective-permute-start | bytes 1658888 | tf_op jit(solution)/shard_map/ppermute | solution.py:36
  80.9 27.7 %collective-permute-start.6 = (bf16[2,216,640]{2,1,0:T(8,128)(2,1)}, bf16[2,216,640]{2,1,0:T(8,128)(2,1)S(1)}, u32[]{:S(2)}, u32[]{:S(2)}) collective-permute-start(bf16[2,216,640]{2,1,0:T(8,128)(2,1)} %get-tuple-element.27), channel_id=1, source_target_pairs={{0,128},{16,144},{32,160},{48,176},{64,192},{80,208},{96,224},{112... | collective-permute-start | bytes 1658888 | tf_op jit(solution)/shard_map/ppermute | solution.py:36
  84.0 24.6 %collective-permute-start.7 = (bf16[2,216,640]{2,1,0:T(8,128)(2,1)}, bf16[2,216,640]{2,1,0:T(8,128)(2,1)S(1)}, u32[]{:S(2)}, u32[]{:S(2)}) collective-permute-start(bf16[2,216,640]{2,1,0:T(8,128)(2,1)} %get-tuple-element.28), channel_id=1, source_target_pairs={{0,384},{16,400},{32,416},{48,432},{64,448},{80,464},{96,480},{112... | collective-permute-start | bytes 1658888 | tf_op jit(solution)/shard_map/ppermute | solution.py:36
  88.1 36.6 %collective-permute-start.3 = (bf16[216,128]{1,0:T(8,128)(2,1)}, bf16[216,128]{1,0:T(8,128)(2,1)}, u32[]{:S(2)}, u32[]{:S(2)}) collective-permute-start(bf16[216,128]{1,0:T(8,128)(2,1)} %get-tuple-element.42), channel_id=1, source_target_pairs={{0,16},{16,0},{32,48},{48,32},{64,80},{80,64},{96,112},{112,96},{1... | collective-permute-start | bytes 165896 | tf_op jit(solution)/shard_map/ppermute | solution.py:32
  108.6 0.8 copy-start.11
  111.9 12.8 %copy-start.12 = (bf16[216,128]{1,0:T(8,128)(2,1)S(1)}, bf16[216,128]{1,0:T(8,128)(2,1)}, u32[]{:S(2)}) copy-start(bf16[216,128]{1,0:T(8,128)(2,1)} %get-tuple-element.41) | copy-start | bytes 165892
  111.9 42.3 %all-to-all-start.2 = ((bf16[4,160,432]{2,1,0:T(8,128)(2,1)}), bf16[4,160,432]{2,1,0:T(8,128)(2,1)S(1)}, u32[]{:S(2)}, u32[]{:S(2)}) async-start(bf16[4,160,432]{2,1,0:T(8,128)(2,1)} %bitcast.9), calls=%async_computation.2 | async-start | bytes 1310720 | tf_op jit(solution)/shard_map/all_to_all | solution.py:242
  116.8 20.0 %collective-permute-start.8 = (f32[176,128]{1,0:T(8,128)S(1)}, f32[176,128]{1,0:T(8,128)S(1)}, u32[]{:S(2)}, u32[]{:S(2)}) collective-permute-start(f32[176,128]{1,0:T(8,128)S(1)} %slice_select_fusion.2), channel_id=1, source_target_pairs={{0,1},{1,0},{2,3},{3,2},{4,5},{5,4},{6,7},{7,6},{8,9},{9,8},{10,11... | collective-permute-start | bytes 270344 | tf_op jit(solution)/shard_map/ppermute | solution.py:216
  154.4 8.1 %collective-permute-start.9 = (f32[81,432]{1,0:T(8,128)S(1)}, f32[81,432]{1,0:T(8,128)S(1)}, u32[]{:S(2)}, u32[]{:S(2)}) collective-permute-start(f32[81,432]{1,0:T(8,128)S(1)} %pad_maximum_fusion), channel_id=1, source_target_pairs={{0,16},{16,0},{32,48},{48,32},{64,80},{80,64},{96,112},{112,96},{1... | collective-permute-start | bytes 419912 | tf_op jit(solution)/shard_map/ppermute | solution.py:32

commit v4 on v3

--- a/solution.py
+++ b/solution.py
@@ -7,7 +7,7 @@
 
 BF = jnp.bfloat16
 F32 = jnp.float32
-NX, NZ, NC = 4, 4, 2
+NX, NZ, NC, NH = 4, 4, 2, 2
 VMEM = pl.BlockSpec(memory_space=pltpu.VMEM)
 SMEM = pl.BlockSpec(memory_space=pltpu.SMEM)
 PARAMS = pltpu.CompilerParams(vmem_limit_bytes=48 * 1024 * 1024)
@@ -15,36 +15,16 @@
 TN = (((0,), (0,)), ((), ()))
 
 
-def place(x, z, c):
-    return (x * NZ + z) * NC + c
-
-
-def pairs(move):
-    return [
-        (place(x, z, c), place(*move(x, z, c)))
-        for x in range(NX)
-        for z in range(NZ)
-        for c in range(NC)
-    ]
+def swap(value, axis):
+    return lax.ppermute(value, axis, [(0, 1), (1, 0)])
 
 
 def swap_core(value):
-    return lax.ppermute(value, "blk", pairs(lambda x, z, c: (x, z, 1 - c)))
+    return swap(value, "c")
 
 
 def shift_x(value, steps):
-    return lax.ppermute(value, "blk", pairs(lambda x, z, c: ((x + steps) % NX, z, c)))
-
-
-NH = 2
-
-
-def y_groups(count):
-    return [[index * NH + high for index in range(count // NH)] for high in range(NH)]
-
-
-X_GROUPS = [[place(x, z, c) for x in range(NX)] for z in range(NZ) for c in range(NC)]
-Z_GROUPS = [[place(x, z, c) for z in range(NZ)] for x in range(NX) for c in range(NC)]
+    return lax.ppermute(value, "x", [(x, (x + steps) % NX) for x in range(NX)])
 
 
 def norm_kernel(x_ref, gain_ref, normed_ref, root_ref):
@@ -146,14 +126,12 @@
 
 
 def per_device(inputs, gain, w_gate, w_up, upstream):
-    position = lax.axis_index("blk")
-    core = position % NC
-    spot = (position // (NZ * NC)).astype(jnp.int32).reshape(1)
-    first = core == 0
+    spot = lax.axis_index("x").astype(jnp.int32).reshape(1)
+    first = lax.axis_index("c") == 0
     tokens, width = inputs.shape
     rows, columns = w_gate.shape
     half = columns // 2
-    n_dp = lax.axis_size("dp")
+    n_dp = lax.axis_size(("y", "h"))
     features = width // n_dp
     column_rows = rows * NZ * NC
 
@@ -170,9 +148,9 @@
     up_mine, up_other = halves(w_up, 1)
     weight_other = swap_core(jnp.concatenate([gate_other, up_other], 1))
     chip = ordered(jnp.concatenate([gate_mine, up_mine], 1), weight_other, 0)
-    column = lax.all_gather(chip, "blk", axis=0, tiled=True, axis_index_groups=Z_GROUPS).T
+    column = lax.all_gather(chip, "z", axis=0, tiled=True).T
     copies = jnp.broadcast_to(column.reshape(2, half, column_rows), (NX, 2, half, column_rows))
-    weight = lax.all_to_all(copies, "blk", 0, 0, tiled=True, axis_index_groups=X_GROUPS)
+    weight = lax.all_to_all(copies, "x", 0, 0, tiled=True)
 
     inputs_t = jnp.concatenate([inputs, swap_core(inputs)], 0).T
     upstream_mine, upstream_other = halves(upstream.T, 0)
@@ -209,18 +187,15 @@
         part_own, part_other, inputs_t[:, :tokens], root_mean[:, :tokens], gain_wide
     )
     sending = sending.reshape(n_dp // NH, NH * (features + spare), tokens)
-    got = lax.all_to_all(sending, "dp", 0, 0, tiled=True, axis_index_groups=y_groups(n_dp))
-    got, travelling = lax.optimization_barrier((got, travelling))
+    got = lax.all_to_all(sending, "y", 0, 0, tiled=True)
     y_sums = jnp.sum(got.astype(F32), axis=0).reshape(NH, features + spare, tokens)
-    low_half = lax.axis_index("dp") % NH == 0
-    totals = jnp.where(low_half, y_sums[0], y_sums[1]) + lax.ppermute(
-        jnp.where(low_half, y_sums[1], y_sums[0]),
-        "dp",
-        [(index, index ^ 1) for index in range(n_dp)],
+    low_half = lax.axis_index("h") == 0
+    totals = jnp.where(low_half, y_sums[0], y_sums[1]) + swap(
+        jnp.where(low_half, y_sums[1], y_sums[0]), "h"
     )
     own_sums = totals[:features]
     token_totals = totals[features] + totals[features + 1] + totals[features + 2]
-    start = lax.axis_index("dp") * features
+    start = lax.axis_index(("y", "h")) * features
     gain_slice = lax.dynamic_slice_in_dim(gain, start, features, 0)[:, None]
     root_own = root_mean[:, :tokens]
     unit_slice = (
@@ -232,41 +207,32 @@
         .T
     )
     gain_part = jnp.sum(own_sums * unit_slice, axis=1)
-    gain_part = lax.psum(gain_part, "blk", axis_index_groups=X_GROUPS)
-    gain_part = lax.psum(gain_part, "blk", axis_index_groups=Z_GROUPS)
+    grad_input, gain_part, travelling = lax.optimization_barrier(
+        (grad_input, gain_part, travelling)
+    )
+    grad_gain = lax.psum(lax.psum(gain_part, "x"), "z")
+    grad_gain = grad_gain + swap_core(grad_gain)
 
     column_sum = terms[0]
     for value in travelling:
         column_sum = column_sum + value.astype(F32)
     column_sum = column_sum.reshape(columns, column_rows).T.astype(BF)
     blocks = lax.all_to_all(
-        column_sum.reshape(NZ, rows * NC, columns),
-        "blk",
-        0,
-        0,
-        tiled=True,
-        axis_index_groups=Z_GROUPS,
-    )
-    chip_sum = jnp.sum(blocks.astype(F32), axis=0)
-    sum_mine, sum_other = chip_sum[:rows], chip_sum[rows:]
-    sum_mine, sum_other = (
-        jnp.where(first, sum_mine, sum_other),
-        jnp.where(first, sum_other, sum_mine),
-    )
-    gain_row = jnp.pad(gain_part, (0, columns - features))[None, :]
-    other = swap_core(jnp.concatenate([sum_other, gain_row], 0))
-    sum_other = other[:rows]
-    grad_gain = gain_part + other[rows, :features]
-    grad_gate = ordered(sum_mine[:, :half], sum_other[:, :half], 1)
-    grad_up = ordered(sum_mine[:, half:], sum_other[:, half:], 1)
+        column_sum.reshape(NZ * NC, rows, columns), ("z", "c"), 0, 0, tiled=True
+    )
+    sums = jnp.sum(blocks.reshape(NZ, NC, rows, columns).astype(F32), axis=0)
+    grad_gate = jnp.concatenate([sums[0, :, :half], sums[1, :, :half]], 1)
+    grad_up = jnp.concatenate([sums[0, :, half:], sums[1, :, half:]], 1)
     return (hidden, grad_gate, grad_up, grad_input, grad_gain)
 
 
 def solution(mesh):
+    fine = jax.sharding.Mesh(mesh.devices.reshape(NX, NZ, NC, -1, NH), ("x", "z", "c", "y", "h"))
+    blk, dp = ("x", "z", "c"), ("y", "h")
     return jax.shard_map(
         per_device,
-        mesh=mesh,
-        in_specs=(P("blk", None), P(), P("blk", "dp"), P("blk", "dp"), P("blk", "dp")),
-        out_specs=(P("blk", "dp"), P("blk", "dp"), P("blk", "dp"), P("blk", "dp"), P("dp")),
+        mesh=fine,
+        in_specs=(P(blk, None), P(), P(blk, dp), P(blk, dp), P(blk, dp)),
+        out_specs=(P(blk, dp), P(blk, dp), P(blk, dp), P(blk, dp), P(dp)),
         check_vma=False,
     )

time: 165 us -> 170 us (1.030)
  waiting for transfers between devices: 42 us -> 55.9 us
  other arithmetic: 10.4 us -> 6.91 us
  local copies, waits for them, and re-layouts: 10.9 us -> 8.48 us
  starting transfers between devices: 64.2 us -> 61.8 us
    all_to_all x3, waiting for transfers between devices: 9.78 us -> 31.9 us  [the longest x1 22.2 us: per_device(): got = lax.all_to_all(sending, 'y', 0, 0, tiled=True)]
    ppermute x10, waiting for transfers between devices: 32.2 us -> 24 us  [the longest x3 20.2 us: shift_x(): return lax.ppermute(value, 'x', [(x, (x + steps) % NX) for x in range(NX)])]
    ppermute x10, starting transfers between devices: 50 us -> 47.2 us  [the longest x7 38.6 us: swap(): return lax.ppermute(value, axis, [(0, 1), (1, 0)])]
    unnamed x29 -> x25, local copies, waits for them, and re-layouts: 6.59 us -> 4.89 us
  transfers between devices with their start and end apart: 13 -> 13, of which waited for: 8 -> 8; matrix products, arithmetic and copies ran while one was open for 6% -> 3% of each run, Pallas kernels for 1% -> 1%
where the time goes in v4:
time: 170 us; the launch traced here: 169 us
  starting transfers between devices  61.8 us (36%)
  waiting for transfers between devices  55.9 us (33%)
  blocking collectives  30.8 us (18%)
  local copies, waits for them, and re-layouts  8.48 us (5%)
  other arithmetic  6.91 us (4%)
  Pallas kernels  4.65 us (3%)
    ppermute x7, starting transfers between devices, swap(): return lax.ppermute(value, axis, [(0, 1), (1, 0)])  38.6 us
    all_to_all x1, waiting for transfers between devices, per_device(): got = lax.all_to_all(sending, 'y', 0, 0, tiled=True)  22.2 us
    ppermute x3, waiting for transfers between devices, shift_x(): return lax.ppermute(value, 'x', [(x, (x + steps) % NX) for x in range(NX)])  20.2 us
    psum x2, blocking collectives, per_device(): grad_gain = lax.psum(lax.psum(gain_part, 'x'), 'z')  17.3 us
    all_gather x1, blocking collectives, per_device(): column = lax.all_gather(chip, 'z', axis=0, tiled=True).T  13.4 us
    all_to_all x1, waiting for transfers between devices, per_device(): weight = lax.all_to_all(copies, 'x', 0, 0, tiled=True)  9.74 us
    ppermute x3, starting transfers between devices, shift_x(): return lax.ppermute(value, 'x', [(x, (x + steps) % NX) for x in range(NX)])  8.68 us
    all_to_all x1, starting transfers between devices, per_device(): got = lax.all_to_all(sending, 'y', 0, 0, tiled=True)  6.87 us
  transfers between devices with their start and end apart: 13, of which 8 were waited for; matrix products, arithmetic and copies ran while one was open for 3% of the time, Pallas kernels for 1%

profile of v4, /device:TPU:1, one launch (start us, length us, event | category | flops | bytes accessed | tf_op | source)
XLA Modules:
  0.0 169.5 jit_solution(4287309922778965299)
XLA Ops:
  0.6 1.0 broadcast_select_fusion.4
  1.7 8.8 %collective-permute-start.2 = (bf16[80,432]{1,0:T(8,128)(2,1)S(1)}, bf16[80,432]{1,0:T(8,128)(2,1)S(1)}, u32[]{:S(2)}, u32[]{:S(2)}) collective-permute-start(bf16[80,432]{1,0:T(8,128)(2,1)S(1)} %pad_maximum_fusion.3), channel_id=1, source_target_pairs={{0,16},{16,0},{1,17},{17,1},{2,18},{18,2},{3,19},{19,3},{4,20},{20... | collective-permute-start | bytes 207368 | tf_op jit(solution)/shard_map/ppermute | solution.py:19
  10.5 0.9 collective-permute-done.2
  11.5 13.4 %all_gather.3 = bf16[640,432]{1,0:T(8,128)(2,1)S(1)} all-gather(bf16[160,432]{1,0:T(8,128)(2,1)S(1)} %maximum_select_fusion), channel_id=1, replica_groups=mesh['x'=4,'z'=4,'c'=2,'y'=8,'h'=2] {'z'}, dimensions={0}, use_global_device_ids=true | all-gather | bytes 691200 | tf_op jit(solution)/shard_map/all_gather | solution.py:151
  25.0 0.3 copy.22
  25.3 1.5 broadcast_in_dim.5
  26.8 3.7 %all-to-all-start = ((bf16[4,2,216,640]{3,2,1,0:T(8,128)(2,1)}), bf16[4,2,216,640]{3,2,1,0:T(8,128)(2,1)S(1)}, u32[]{:S(2)}, u32[]{:S(2)}) async-start(bf16[4,2,216,640]{3,2,1,0:T(8,128)(2,1)} %broadcast_in_dim.5), calls=%async_computation | async-start | bytes 4423680 | tf_op jit(solution)/shard_map/all_to_all | solution.py:153
  30.6 0.3 copy.21
  30.9 5.6 %collective-permute-start = (bf16[128,2560]{0,1:T(8,128)(2,1)S(1)}, bf16[128,2560]{0,1:T(8,128)(2,1)S(1)}, u32[]{:S(2)}, u32[]{:S(2)}) collective-permute-start(bf16[128,2560]{0,1:T(8,128)(2,1)S(1)} %copy.21), channel_id=1, source_target_pairs={{0,16},{16,0},{1,17},{17,1},{2,18},{18,2},{3,19},{19,3},{4,20},{20... | collective-permute-start | bytes 1966088 | tf_op jit(solution)/shard_map/ppermute | solution.py:19
  36.5 0.9 broadcast_select_fusion.1
  37.4 1.9 %collective-permute-start.1 = (bf16[216,128]{1,0:T(8,128)(2,1)S(1)}, bf16[216,128]{1,0:T(8,128)(2,1)S(1)}, u32[]{:S(2)}, u32[]{:S(2)}) collective-permute-start(bf16[216,128]{1,0:T(8,128)(2,1)S(1)} %get-tuple-element.44), channel_id=1, source_target_pairs={{0,16},{16,0},{1,17},{17,1},{2,18},{18,2},{3,19},{19,3},{4,20},{20... | collective-permute-start | bytes 165896 | tf_op jit(solution)/shard_map/ppermute | solution.py:19
  39.3 1.2 collective-permute-done.1
  40.5 0.7 pad_maximum_fusion.2.upstream_ref
  41.2 0.1 maximum_bitcast_fusion.x_ref
  41.4 0.6 copy-done.11
  41.9 0.4 broadcast_in_dim.4.gain_ref
  42.3 0.7 copy-done
  43.0 0.6 shard_map.92
  43.6 1.1 copy-done.2
  44.7 9.7 %all-to-all-done.weight_ref = bf16[4,2,216,640]{3,2,1,0:T(8,128)(2,1)S(1)} async-done(((bf16[4,2,216,640]{3,2,1,0:T(8,128)(2,1)}), bf16[4,2,216,640]{3,2,1,0:T(8,128)(2,1)S(1)}, u32[]{:S(2)}, u32[]{:S(2)}) %all-to-all-start) | async-done | bytes 2211872 | tf_op jit(solution)/shard_map/all_to_all | solution.py:153
  54.4 1.3 copy-done.3
  55.7 0.9 copy-done.5
  56.6 1.8 %shard_map.93 = (bf16[216,256]{1,0:T(8,128)(2,1)S(1)}, bf16[2,216,256]{2,1,0:T(8,128)(2,1)S(1)}, f32[2560,128]{1,0:T(8,128)S(1)}, bf16[2560,128]{1,0:T(8,128)(2,1)S(1)}) custom-call(bf16[2560,256]{1,0:T(8,128)(2,1)S(1)} %copy-done.3, bf16[216,256]{1,0:T(8,128)(2,1)S(1)} %copy-done.5, bf16[4,2,216,640]{3,2,1,0:T(8,128)(2,1)S(1)} %all-to-all-done.weight_ref), custom_call_target="tpu_custom_call" | custom-call | tf_op jit(solution)/shard_map/pallas_call | solution.py:165
  58.4 6.6 %collective-permute-start.4 = (bf16[2560,128]{1,0:T(8,128)(2,1)S(1)}, bf16[2560,128]{1,0:T(8,128)(2,1)S(1)}, u32[]{:S(2)}, u32[]{:S(2)}) collective-permute-start(bf16[2560,128]{1,0:T(8,128)(2,1)S(1)} %get-tuple-element.25), channel_id=1, source_target_pairs={{0,16},{16,0},{1,17},{17,1},{2,18},{18,2},{3,19},{19,3},{4,20},{20... | collective-permute-start | bytes 1966088 | tf_op jit(solution)/shard_map/ppermute | solution.py:19
  65.1 1.6 collective-permute-done.4.other_ref
  66.7 1.3 shard_map.95
  68.0 6.9 %all-to-all-start.1 = ((bf16[8,352,128]{2,1,0:T(8,128)(2,1)}), bf16[8,352,128]{2,1,0:T(8,128)(2,1)S(1)}, u32[]{:S(2)}, u32[]{:S(2)}) async-start(bf16[8,352,128]{2,1,0:T(8,128)(2,1)} %bitcast.6), calls=%async_computation.1 | async-start | bytes 1441792 | tf_op jit(solution)/shard_map/all_to_all | solution.py:190
  74.9 22.2 %all-to-all-done.1 = bf16[8,352,128]{2,1,0:T(8,128)(2,1)S(1)} async-done(((bf16[8,352,128]{2,1,0:T(8,128)(2,1)}), bf16[8,352,128]{2,1,0:T(8,128)(2,1)S(1)}, u32[]{:S(2)}, u32[]{:S(2)}) %all-to-all-start.1) | async-done | bytes 720928 | tf_op jit(solution)/shard_map/all_to_all | solution.py:190
  97.1 7.9 %collective-permute-start.5 = (f32[176,128]{1,0:T(8,128)S(1)}, f32[176,128]{1,0:T(8,128)S(1)}, u32[]{:S(2)}, u32[]{:S(2)}) collective-permute-start(f32[176,128]{1,0:T(8,128)S(1)} %slice_select_fusion), channel_id=1, source_target_pairs={{0,1},{1,0},{2,3},{3,2},{4,5},{5,4},{6,7},{7,6},{8,9},{9,8},{10,11... | collective-permute-start | bytes 270344 | tf_op jit(solution)/shard_map/ppermute | solution.py:19
  105.2 1.0 shard_map.94
  106.2 2.2 %collective-permute-start.6 = (bf16[2,216,640]{2,1,0:T(8,128)(2,1)S(1)}, bf16[2,216,640]{2,1,0:T(8,128)(2,1)S(1)}, u32[]{:S(2)}, u32[]{:S(2)}) collective-permute-start(bf16[2,216,640]{2,1,0:T(8,128)(2,1)S(1)} %get-tuple-element.27), channel_id=1, source_target_pairs={{0,256},{128,384},{256,0},{384,128},{1,257},{129,385},{257,1},{385... | collective-permute-start | bytes 1658888 | tf_op jit(solution)/shard_map/ppermute | solution.py:27
  108.4 3.1 %collective-permute-start.7 = (bf16[2,216,640]{2,1,0:T(8,128)(2,1)S(1)}, bf16[2,216,640]{2,1,0:T(8,128)(2,1)S(1)}, u32[]{:S(2)}, u32[]{:S(2)}) collective-permute-start(bf16[2,216,640]{2,1,0:T(8,128)(2,1)S(1)} %get-tuple-element.28), channel_id=1, source_target_pairs={{0,128},{128,256},{256,384},{384,0},{1,129},{129,257},{257,385},{3... | collective-permute-start | bytes 1658888 | tf_op jit(solution)/shard_map/ppermute | solution.py:27
  111.5 3.4 %collective-permute-start.8 = (bf16[2,216,640]{2,1,0:T(8,128)(2,1)S(1)}, bf16[2,216,640]{2,1,0:T(8,128)(2,1)S(1)}, u32[]{:S(2)}, u32[]{:S(2)}) collective-permute-start(bf16[2,216,640]{2,1,0:T(8,128)(2,1)S(1)} %get-tuple-element.29), channel_id=1, source_target_pairs={{0,384},{128,0},{256,128},{384,256},{1,385},{129,1},{257,129},{385... | collective-permute-start | bytes 1658888 | tf_op jit(solution)/shard_map/ppermute | solution.py:27
  115.0 0.8 multiply_reduce_fusion
  115.7 7.2 %collective-permute-done.6 = bf16[2,216,640]{2,1,0:T(8,128)(2,1)S(1)} collective-permute-done((bf16[2,216,640]{2,1,0:T(8,128)(2,1)S(1)}, bf16[2,216,640]{2,1,0:T(8,128)(2,1)S(1)}, u32[]{:S(2)}, u32[]{:S(2)}) %collective-permute-start.6) | collective-permute-done | bytes 552992 | tf_op jit(solution)/shard_map/ppermute | solution.py:27
  122.9 13.0 %collective-permute-done.7 = bf16[2,216,640]{2,1,0:T(8,128)(2,1)S(1)} collective-permute-done((bf16[2,216,640]{2,1,0:T(8,128)(2,1)S(1)}, bf16[2,216,640]{2,1,0:T(8,128)(2,1)S(1)}, u32[]{:S(2)}, u32[]{:S(2)}) %collective-permute-start.7) | collective-permute-done | bytes 552992 | tf_op jit(solution)/shard_map/ppermute | solution.py:27
  135.9 0.3 add_convert_fusion
  136.2 1.1 copy.23
  137.3 3.9 %all-to-all-start.2 = ((bf16[8,80,432]{2,1,0:T(8,128)(2,1)}), bf16[8,80,432]{2,1,0:T(8,128)(2,1)S(1)}, u32[]{:S(2)}, u32[]{:S(2)}) async-start(bf16[8,80,432]{2,1,0:T(8,128)(2,1)} %bitcast.12), calls=%async_computation.2 | async-start | bytes 1310720 | tf_op jit(solution)/shard_map/all_to_all | solution.py:220
  141.3 2.0 %collective-permute-start.3 = (bf16[216,128]{1,0:T(8,128)(2,1)S(1)}, bf16[216,128]{1,0:T(8,128)(2,1)S(1)}, u32[]{:S(2)}, u32[]{:S(2)}) collective-permute-start(bf16[216,128]{1,0:T(8,128)(2,1)S(1)} %get-tuple-element.42), channel_id=1, source_target_pairs={{0,16},{16,0},{1,17},{17,1},{2,18},{18,2},{3,19},{19,3},{4,20},{20... | collective-permute-start | bytes 165896 | tf_op jit(solution)/shard_map/ppermute | solution.py:19
  143.3 6.9 %psum.14 = f32[160]{0:T(256)S(1)} all-reduce(f32[160]{0:T(256)S(1)} %get-tuple-element.34), channel_id=1, replica_groups=mesh['x'=4,'z'=4,'c'=2,'y'=8,'h'=2] {'x'}, use_global_device_ids=true, to_apply=%region_3.4 | all-reduce | flops 160 | bytes 1280 | tf_op jit(solution)/shard_map/psum | solution.py:213
  150.2 10.5 %psum.15 = f32[160]{0:T(256)S(1)} all-reduce(f32[160]{0:T(256)S(1)} %psum.14), channel_id=1, replica_groups=mesh['x'=4,'z'=4,'c'=2,'y'=8,'h'=2] {'z'}, use_global_device_ids=true, to_apply=%region_4.5 | all-reduce | flops 160 | bytes 1280 | tf_op jit(solution)/shard_map/psum | solution.py:213
  160.7 5.7 %collective-permute-start.9 = (f32[160]{0:T(256)S(1)}, f32[160]{0:T(256)S(1)}, u32[]{:S(2)}, u32[]{:S(2)}) collective-permute-start(f32[160]{0:T(256)S(1)} %psum.15), channel_id=1, source_target_pairs={{0,16},{16,0},{1,17},{17,1},{2,18},{18,2},{3,19},{19,3},{4,20},{20... | collective-permute-start | bytes 1928 | tf_op jit(solution)/shard_map/ppermute | solution.py:19
  166.4 0.7 fusion
  167.1 0.1 collective-permute-done.9
  167.2 0.6 add.42
  167.9 0.8 pad_maximum_fusion.1
  168.7 0.8 pad_maximum_fusion
  (36 shorter events, 0.7 us)
Async XLA Ops:
  1.7 9.7 %collective-permute-start.2 = (bf16[80,432]{1,0:T(8,128)(2,1)S(1)}, bf16[80,432]{1,0:T(8,128)(2,1)S(1)}, u32[]{:S(2)}, u32[]{:S(2)}) collective-permute-start(bf16[80,432]{1,0:T(8,128)(2,1)S(1)} %pad_maximum_fusion.3), channel_id=1, source_target_pairs={{0,16},{16,0},{1,17},{17,1},{2,18},{18,2},{3,19},{19,3},{4,20},{20... | collective-permute-start | bytes 207368 | tf_op jit(solution)/shard_map/ppermute | solution.py:19
  26.8 3.8 %copy-start.10 = (bf16[128,2560]{1,0:T(8,128)(2,1)S(1)}, bf16[128,2560]{1,0:T(8,128)(2,1)}, u32[]{:S(2)}) copy-start(bf16[128,2560]{1,0:T(8,128)(2,1)} %param.5) | copy-start | bytes 1966084
  26.8 27.6 %all-to-all-start = ((bf16[4,2,216,640]{3,2,1,0:T(8,128)(2,1)}), bf16[4,2,216,640]{3,2,1,0:T(8,128)(2,1)S(1)}, u32[]{:S(2)}, u32[]{:S(2)}) async-start(bf16[4,2,216,640]{3,2,1,0:T(8,128)(2,1)} %broadcast_in_dim.5), calls=%async_computation | async-start | bytes 4423680 | tf_op jit(solution)/shard_map/all_to_all | solution.py:153
  30.9 10.3 %collective-permute-start = (bf16[128,2560]{0,1:T(8,128)(2,1)S(1)}, bf16[128,2560]{0,1:T(8,128)(2,1)S(1)}, u32[]{:S(2)}, u32[]{:S(2)}) collective-permute-start(bf16[128,2560]{0,1:T(8,128)(2,1)S(1)} %copy.21), channel_id=1, source_target_pairs={{0,16},{16,0},{1,17},{17,1},{2,18},{18,2},{3,19},{19,3},{4,20},{20... | collective-permute-start | bytes 1966088 | tf_op jit(solution)/shard_map/ppermute | solution.py:19
  37.4 3.1 %collective-permute-start.1 = (bf16[216,128]{1,0:T(8,128)(2,1)S(1)}, bf16[216,128]{1,0:T(8,128)(2,1)S(1)}, u32[]{:S(2)}, u32[]{:S(2)}) collective-permute-start(bf16[216,128]{1,0:T(8,128)(2,1)S(1)} %get-tuple-element.44), channel_id=1, source_target_pairs={{0,16},{16,0},{1,17},{17,1},{2,18},{18,2},{3,19},{19,3},{4,20},{20... | collective-permute-start | bytes 165896 | tf_op jit(solution)/shard_map/ppermute | solution.py:19
  41.2 0.7 copy-start.11
  41.9 1.1 copy-start
  43.6 1.1 copy-start.2
  54.4 1.3 copy-start.3
  55.7 0.9 copy-start.5
  56.6 8.4 %copy-start.1 = (bf16[2560,256]{1,0:T(8,128)(2,1)S(1)}, bf16[2560,256]{1,0:T(8,128)(2,1)}, u32[]{:S(2)}) copy-start(bf16[2560,256]{1,0:T(8,128)(2,1)} %copy-done) | copy-start | bytes 3932164
  58.4 9.6 %copy-start.6 = (bf16[2,216,256]{2,1,0:T(8,128)(2,1)}, bf16[2,216,256]{2,1,0:T(8,128)(2,1)S(1)}, u32[]{:S(2)}) copy-start(bf16[2,216,256]{2,1,0:T(8,128)(2,1)S(1)} %get-tuple-element.22.back_ref) | copy-start | bytes 663556
  58.4 9.6 %copy-start.8 = (bf16[216,256]{1,0:T(8,128)(2,1)}, bf16[216,256]{1,0:T(8,128)(2,1)S(1)}, u32[]{:S(2)}) copy-start(bf16[216,256]{1,0:T(8,128)(2,1)S(1)} %get-tuple-element.21) | copy-start | bytes 331780
  58.4 8.3 %collective-permute-start.4 = (bf16[2560,128]{1,0:T(8,128)(2,1)S(1)}, bf16[2560,128]{1,0:T(8,128)(2,1)S(1)}, u32[]{:S(2)}, u32[]{:S(2)}) collective-permute-start(bf16[2560,128]{1,0:T(8,128)(2,1)S(1)} %get-tuple-element.25), channel_id=1, source_target_pairs={{0,16},{16,0},{1,17},{17,1},{2,18},{18,2},{3,19},{19,3},{4,20},{20... | collective-permute-start | bytes 1966088 | tf_op jit(solution)/shard_map/ppermute | solution.py:19
  68.0 37.2 %copy-start.4 = (bf16[2560,256]{1,0:T(8,128)(2,1)S(1)}, bf16[2560,256]{1,0:T(8,128)(2,1)}, u32[]{:S(2)}) copy-start(bf16[2560,256]{1,0:T(8,128)(2,1)} %copy-done.2) | copy-start | bytes 3932164
  68.0 37.2 %copy-start.7 = (bf16[2,216,256]{2,1,0:T(8,128)(2,1)S(1)}, bf16[2,216,256]{2,1,0:T(8,128)(2,1)}, u32[]{:S(2)}) copy-start(bf16[2,216,256]{2,1,0:T(8,128)(2,1)} %copy-done.6) | copy-start | bytes 663556
  68.0 29.0 %all-to-all-start.1 = ((bf16[8,352,128]{2,1,0:T(8,128)(2,1)}), bf16[8,352,128]{2,1,0:T(8,128)(2,1)S(1)}, u32[]{:S(2)}, u32[]{:S(2)}) async-start(bf16[8,352,128]{2,1,0:T(8,128)(2,1)} %bitcast.6), calls=%async_computation.1 | async-start | bytes 1441792 | tf_op jit(solution)/shard_map/all_to_all | solution.py:190
  97.1 17.8 %collective-permute-start.5 = (f32[176,128]{1,0:T(8,128)S(1)}, f32[176,128]{1,0:T(8,128)S(1)}, u32[]{:S(2)}, u32[]{:S(2)}) collective-permute-start(f32[176,128]{1,0:T(8,128)S(1)} %slice_select_fusion), channel_id=1, source_target_pairs={{0,1},{1,0},{2,3},{3,2},{4,5},{5,4},{6,7},{7,6},{8,9},{9,8},{10,11... | collective-permute-start | bytes 270344 | tf_op jit(solution)/shard_map/ppermute | solution.py:19
  106.2 16.7 %collective-permute-start.6 = (bf16[2,216,640]{2,1,0:T(8,128)(2,1)S(1)}, bf16[2,216,640]{2,1,0:T(8,128)(2,1)S(1)}, u32[]{:S(2)}, u32[]{:S(2)}) collective-permute-start(bf16[2,216,640]{2,1,0:T(8,128)(2,1)S(1)} %get-tuple-element.27), channel_id=1, source_target_pairs={{0,256},{128,384},{256,0},{384,128},{1,257},{129,385},{257,1},{385... | collective-permute-start | bytes 1658888 | tf_op jit(solution)/shard_map/ppermute | solution.py:27
  108.4 27.5 %collective-permute-start.7 = (bf16[2,216,640]{2,1,0:T(8,128)(2,1)S(1)}, bf16[2,216,640]{2,1,0:T(8,128)(2,1)S(1)}, u32[]{:S(2)}, u32[]{:S(2)}) collective-permute-start(bf16[2,216,640]{2,1,0:T(8,128)(2,1)S(1)} %get-tuple-element.28), channel_id=1, source_target_pairs={{0,128},{128,256},{256,384},{384,0},{1,129},{129,257},{257,385},{3... | collective-permute-start | bytes 1658888 | tf_op jit(solution)/shard_map/ppermute | solution.py:27
  111.5 24.4 %collective-permute-start.8 = (bf16[2,216,640]{2,1,0:T(8,128)(2,1)S(1)}, bf16[2,216,640]{2,1,0:T(8,128)(2,1)S(1)}, u32[]{:S(2)}, u32[]{:S(2)}) collective-permute-start(bf16[2,216,640]{2,1,0:T(8,128)(2,1)S(1)} %get-tuple-element.29), channel_id=1, source_target_pairs={{0,384},{128,0},{256,128},{384,256},{1,385},{129,1},{257,129},{385... | collective-permute-start | bytes 1658888 | tf_op jit(solution)/shard_map/ppermute | solution.py:27
  136.2 5.1 %copy-start.9 = (bf16[216,256]{1,0:T(8,128)(2,1)S(1)}, bf16[216,256]{1,0:T(8,128)(2,1)}, u32[]{:S(2)}) copy-start(bf16[216,256]{1,0:T(8,128)(2,1)} %copy-done.8) | copy-start | bytes 331780
  137.3 30.4 %all-to-all-start.2 = ((bf16[8,80,432]{2,1,0:T(8,128)(2,1)}), bf16[8,80,432]{2,1,0:T(8,128)(2,1)S(1)}, u32[]{:S(2)}, u32[]{:S(2)}) async-start(bf16[8,80,432]{2,1,0:T(8,128)(2,1)} %bitcast.12), calls=%async_computation.2 | async-start | bytes 1310720 | tf_op jit(solution)/shard_map/all_to_all | solution.py:220
  141.3 25.1 %collective-permute-start.3 = (bf16[216,128]{1,0:T(8,128)(2,1)S(1)}, bf16[216,128]{1,0:T(8,128)(2,1)S(1)}, u32[]{:S(2)}, u32[]{:S(2)}) collective-permute-start(bf16[216,128]{1,0:T(8,128)(2,1)S(1)} %get-tuple-element.42), channel_id=1, source_target_pairs={{0,16},{16,0},{1,17},{17,1},{2,18},{18,2},{3,19},{19,3},{4,20},{20... | collective-permute-start | bytes 165896 | tf_op jit(solution)/shard_map/ppermute | solution.py:19
  160.7 6.5 %collective-permute-start.9 = (f32[160]{0:T(256)S(1)}, f32[160]{0:T(256)S(1)}, u32[]{:S(2)}, u32[]{:S(2)}) collective-permute-start(f32[160]{0:T(256)S(1)} %psum.15), channel_id=1, source_target_pairs={{0,16},{16,0},{1,17},{17,1},{2,18},{18,2},{3,19},{19,3},{4,20},{20... | collective-permute-start | bytes 1928 | tf_op jit(solution)/shard_map/ppermute | solution.py:19

commit v5 on v4

--- a/solution.py
+++ b/solution.py
@@ -27,6 +27,10 @@
     return lax.ppermute(value, "x", [(x, (x + steps) % NX) for x in range(NX)])
 
 
+def moved(block, core):
+    return (block // NZ * NC + core) * NZ + block % NZ
+
+
 def norm_kernel(x_ref, gain_ref, normed_ref, root_ref):
     width, tokens = x_ref.shape
     size = width // (NX * NZ)
@@ -40,21 +44,28 @@
         rows = pl.ds(index * size, size)
         unit = x_ref[rows, :].astype(F32) / root
         gain = gain_ref[rows, :]
-        gain = jnp.concatenate([gain, gain], axis=1)
-        normed_ref[rows, :] = (unit * gain).astype(BF)
+        value = (unit * jnp.concatenate([gain, gain], axis=1)).astype(BF)
+        for core in range(NC):
+            chunk = size // NC
+            normed_ref[pl.ds(moved(index, core) * chunk, chunk), :] = value[
+                core * chunk : (core + 1) * chunk
+            ]
 
 
 def forward_kernel(
     normed_ref, upstream_ref, weight_ref, hidden_ref, back_ref, own_ref, other_ref
 ):
-    size = weight_ref.shape[3]
+    size = weight_ref.shape[2] // 2
     tokens = own_ref.shape[1]
+
+    def piece(index, which):
+        return weight_ref[index, :, which * size : (which + 1) * size]
 
     def product(which):
         total = None
-        for index in range(NX):
+        for index in range(NX * NC):
             term = jnp.dot(
-                weight_ref[index, which],
+                piece(index, which),
                 normed_ref[pl.ds(index * size, size), :],
                 preferred_element_type=F32,
             )
@@ -71,9 +82,9 @@
     back_gate = (upstream * up_pre * sigmoid * (1.0 + gate_pre * (1.0 - sigmoid))).astype(BF)
     back_ref[0] = back_gate
     back_ref[1] = back_up
-    for index in range(NX):
-        part = lax.dot_general(weight_ref[index, 0], back_gate, TN, preferred_element_type=F32)
-        part += lax.dot_general(weight_ref[index, 1], back_up, TN, preferred_element_type=F32)
+    for index in range(NX * NC):
+        part = lax.dot_general(piece(index, 0), back_gate, TN, preferred_element_type=F32)
+        part += lax.dot_general(piece(index, 1), back_up, TN, preferred_element_type=F32)
         rows = pl.ds(index * size, size)
         own_ref[rows, :] = part[:, :tokens]
         other_ref[rows, :] = part[:, tokens:].astype(BF)
@@ -96,7 +107,11 @@
     total = jnp.zeros((size, tokens), F32)
     for index in range(NX * NZ):
         rows = pl.ds(index * size, size)
-        part = (own_ref[rows, :] + other_ref[rows, :].astype(F32)).astype(BF)
+        chunk = size // NC
+        places = [pl.ds(moved(index, core) * chunk, chunk) for core in range(NC)]
+        own = jnp.concatenate([own_ref[here, :] for here in places], axis=0)
+        other = jnp.concatenate([other_ref[here, :] for here in places], axis=0)
+        part = (own + other.astype(F32)).astype(BF)
         out_ref[index, 0:size, :] = part
         unit = x_ref[rows, :].astype(F32) / root
         total += part.astype(F32) * gain_ref[rows, :] * unit
@@ -144,13 +159,12 @@
         low, high = jnp.split(value, 2, axis)
         return jnp.where(first, low, high), jnp.where(first, high, low)
 
-    gate_mine, gate_other = halves(w_gate, 1)
-    up_mine, up_other = halves(w_up, 1)
-    weight_other = swap_core(jnp.concatenate([gate_other, up_other], 1))
-    chip = ordered(jnp.concatenate([gate_mine, up_mine], 1), weight_other, 0)
-    column = lax.all_gather(chip, "z", axis=0, tiled=True).T
-    copies = jnp.broadcast_to(column.reshape(2, half, column_rows), (NX, 2, half, column_rows))
-    weight = lax.all_to_all(copies, "x", 0, 0, tiled=True)
+    column = lax.all_gather(jnp.concatenate([w_gate, w_up], 1), "z", axis=0, tiled=True).T
+    column = jnp.concatenate([column[:columns], column[columns:]], 1)
+    copies = jnp.broadcast_to(
+        column.reshape(NC, half, column_rows), (NX, NC, half, column_rows)
+    ).reshape(NX * NC, half, column_rows)
+    weight = lax.all_to_all(copies, ("x", "c"), 0, 0, tiled=True)
 
     inputs_t = jnp.concatenate([inputs, swap_core(inputs)], 0).T
     upstream_mine, upstream_other = halves(upstream.T, 0)
@@ -186,13 +200,9 @@
     sending = call(blocks_kernel, shape((n_dp, features + spare, tokens), BF), [VMEM] * 5)(
         part_own, part_other, inputs_t[:, :tokens], root_mean[:, :tokens], gain_wide
     )
-    sending = sending.reshape(n_dp // NH, NH * (features + spare), tokens)
-    got = lax.all_to_all(sending, "y", 0, 0, tiled=True)
-    y_sums = jnp.sum(got.astype(F32), axis=0).reshape(NH, features + spare, tokens)
-    low_half = lax.axis_index("h") == 0
-    totals = jnp.where(low_half, y_sums[0], y_sums[1]) + swap(
-        jnp.where(low_half, y_sums[1], y_sums[0]), "h"
-    )
+    got = lax.all_to_all(sending, ("y", "h"), 0, 0, tiled=True)
+    got, travelling = lax.optimization_barrier((got, travelling))
+    totals = jnp.sum(got.astype(F32), axis=0)
     own_sums = totals[:features]
     token_totals = totals[features] + totals[features + 1] + totals[features + 2]
     start = lax.axis_index(("y", "h")) * features
@@ -207,9 +217,6 @@
         .T
     )
     gain_part = jnp.sum(own_sums * unit_slice, axis=1)
-    grad_input, gain_part, travelling = lax.optimization_barrier(
-        (grad_input, gain_part, travelling)
-    )
     grad_gain = lax.psum(lax.psum(gain_part, "x"), "z")
     grad_gain = grad_gain + swap_core(grad_gain)
 
@@ -218,9 +225,9 @@
         column_sum = column_sum + value.astype(F32)
     column_sum = column_sum.reshape(columns, column_rows).T.astype(BF)
     blocks = lax.all_to_all(
-        column_sum.reshape(NZ * NC, rows, columns), ("z", "c"), 0, 0, tiled=True
-    )
-    sums = jnp.sum(blocks.reshape(NZ, NC, rows, columns).astype(F32), axis=0)
+        column_sum.reshape(NC * NZ, rows, columns), ("c", "z"), 0, 0, tiled=True
+    )
+    sums = jnp.sum(blocks.reshape(NC, NZ, rows, columns).astype(F32), axis=1)
     grad_gate = jnp.concatenate([sums[0, :, :half], sums[1, :, :half]], 1)
     grad_up = jnp.concatenate([sums[0, :, half:], sums[1, :, half:]], 1)
     return (hidden, grad_gate, grad_up, grad_input, grad_gain)

time: 170 us -> 150 us (0.88)
  waiting for transfers between devices: 55.9 us -> 40.9 us
  starting transfers between devices: 61.8 us -> 48.5 us
  blocking collectives: 30.8 us -> 35.5 us
    ppermute x7 -> x5, starting transfers between devices: 38.6 us -> 14.8 us  [swap(): return lax.ppermute(value, axis, [(0, 1), (1, 0)])]
    all_to_all x3, waiting for transfers between devices: 31.9 us -> 17.1 us  [the longest x1 17.1 us: per_device(): weight = lax.all_to_all(copies, ('x', 'c'), 0, 0, tiled=True)]
    all_to_all x3, starting transfers between devices: 14.6 us -> 25.2 us  [the longest x1 10.9 us: per_device(): got = lax.all_to_all(sending, ('y', 'h'), 0, 0, tiled=True)]
    all_gather x1, blocking collectives: 13.4 us -> 18.1 us  [per_device(): lax.all_gather(jnp.concatenate([w_gate, w_up], 1), 'z', axis=0, tiled=True)]
    ppermute x7 -> x5, waiting for transfers between devices: 3.85 us -> 2.61 us  [swap(): return lax.ppermute(value, axis, [(0, 1), (1, 0)])]
  transfers between devices with their start and end apart: 13 -> 11, of which waited for: 8 -> 6; matrix products, arithmetic and copies ran while one was open for 3% -> 4% of each run, Pallas kernels for 1% -> 1%
where the time goes in v5:
time: 150 us; the launch traced here: 149 us
  starting transfers between devices  48.5 us (32%)
  waiting for transfers between devices  40.9 us (27%)
  blocking collectives  35.5 us (24%)
  local copies, waits for them, and re-layouts  9.52 us (6%)
  other arithmetic  8.41 us (6%)
  Pallas kernels  4.89 us (3%)
    ppermute x3, waiting for transfers between devices, shift_x(): return lax.ppermute(value, 'x', [(x, (x + steps) % NX) for x in range(NX)])  21.2 us
    all_gather x1, blocking collectives, per_device(): lax.all_gather(jnp.concatenate([w_gate, w_up], 1), 'z', axis=0, tiled=True)  18.1 us
    psum x2, blocking collectives, per_device(): grad_gain = lax.psum(lax.psum(gain_part, 'x'), 'z')  17.4 us
    all_to_all x1, waiting for transfers between devices, per_device(): weight = lax.all_to_all(copies, ('x', 'c'), 0, 0, tiled=True)  17.1 us
    ppermute x5, starting transfers between devices, swap(): return lax.ppermute(value, axis, [(0, 1), (1, 0)])  14.8 us
    all_to_all x1, starting transfers between devices, per_device(): got = lax.all_to_all(sending, ('y', 'h'), 0, 0, tiled=True)  10.9 us
    all_to_all x1, starting transfers between devices, per_device(): weight = lax.all_to_all(copies, ('x', 'c'), 0, 0, tiled=True)  8.54 us
    ppermute x3, starting transfers between devices, shift_x(): return lax.ppermute(value, 'x', [(x, (x + steps) % NX) for x in range(NX)])  8.5 us
  transfers between devices with their start and end apart: 11, of which 6 were waited for; matrix products, arithmetic and copies ran while one was open for 4% of the time, Pallas kernels for 1%

profile of v5, /device:TPU:1, one launch (start us, length us, event | category | flops | bytes accessed | tf_op | source)
XLA Modules:
  0.0 148.6 jit_solution(15183077972786817482)
XLA Ops:
  0.6 1.0 pad_maximum_fusion.3
  1.7 18.1 %all_gather.3 = bf16[320,864]{1,0:T(8,128)(2,1)S(1)} all-gather(bf16[80,864]{1,0:T(8,128)(2,1)S(1)} %pad_maximum_fusion.3), channel_id=1, replica_groups=mesh['x'=4,'z'=4,'c'=2,'y'=8,'h'=2] {'z'}, dimensions={0}, use_global_device_ids=true | all-gather | bytes 691200 | tf_op jit(solution)/shard_map/all_gather | solution.py:162
  19.8 0.4 copy.20
  20.2 0.2 pad_maximum_fusion
  20.4 1.6 %broadcast_in_dim.5 = bf16[4,2,216,640]{3,2,1,0:T(8,128)(2,1)} broadcast(bf16[2,216,640]{2,1,0:T(8,128)(2,1)S(1)} %bitcast.33), dimensions={1,2,3} | broadcast | bytes 2764800 | tf_op jit(solution)/shard_map/broadcast_in_dim | solution.py:164
  22.0 8.5 %all-to-all-start = ((bf16[8,216,640]{2,1,0:T(8,128)(2,1)}), bf16[8,216,640]{2,1,0:T(8,128)(2,1)S(1)}, u32[]{:S(2)}, u32[]{:S(2)}) async-start(bf16[8,216,640]{2,1,0:T(8,128)(2,1)} %bitcast.30), calls=%async_computation | async-start | bytes 4423680 | tf_op jit(solution)/shard_map/all_to_all | solution.py:167
  30.5 0.3 copy.19
  30.8 2.0 %collective-permute-start = (bf16[128,2560]{0,1:T(8,128)(2,1)S(1)}, bf16[128,2560]{0,1:T(8,128)(2,1)S(1)}, u32[]{:S(2)}, u32[]{:S(2)}) collective-permute-start(bf16[128,2560]{0,1:T(8,128)(2,1)S(1)} %copy.19), channel_id=1, source_target_pairs={{0,16},{16,0},{1,17},{17,1},{2,18},{18,2},{3,19},{19,3},{4,20},{20... | collective-permute-start | bytes 1966088 | tf_op jit(solution)/shard_map/ppermute | solution.py:19
  32.9 0.9 broadcast_select_fusion.1
  33.8 2.3 %collective-permute-start.1 = (bf16[216,128]{1,0:T(8,128)(2,1)S(1)}, bf16[216,128]{1,0:T(8,128)(2,1)S(1)}, u32[]{:S(2)}, u32[]{:S(2)}) collective-permute-start(bf16[216,128]{1,0:T(8,128)(2,1)S(1)} %get-tuple-element.44), channel_id=1, source_target_pairs={{0,16},{16,0},{1,17},{17,1},{2,18},{18,2},{3,19},{19,3},{4,20},{20... | collective-permute-start | bytes 165896 | tf_op jit(solution)/shard_map/ppermute | solution.py:19
  36.1 0.9 collective-permute-done.1
  36.9 0.7 pad_maximum_fusion.4.upstream_ref
  37.6 0.1 maximum_bitcast_fusion.x_ref
  37.7 0.6 copy-done.11
  38.3 0.4 broadcast_in_dim.4.gain_ref
  38.7 0.7 copy-done
  39.4 0.5 shard_map.92
  39.9 1.1 copy-done.2
  41.0 17.1 %all-to-all-done.weight_ref = bf16[8,216,640]{2,1,0:T(8,128)(2,1)S(1)} async-done(((bf16[8,216,640]{2,1,0:T(8,128)(2,1)}), bf16[8,216,640]{2,1,0:T(8,128)(2,1)S(1)}, u32[]{:S(2)}, u32[]{:S(2)}) %all-to-all-start) | async-done | bytes 2211872 | tf_op jit(solution)/shard_map/all_to_all | solution.py:167
  58.1 1.3 copy-done.3
  59.4 0.9 copy-done.5
  60.3 2.1 %shard_map.93 = (bf16[216,256]{1,0:T(8,128)(2,1)S(1)}, bf16[2,216,256]{2,1,0:T(8,128)(2,1)S(1)}, f32[2560,128]{1,0:T(8,128)S(1)}, bf16[2560,128]{1,0:T(8,128)(2,1)S(1)}) custom-call(bf16[2560,256]{1,0:T(8,128)(2,1)S(1)} %copy-done.3, bf16[216,256]{1,0:T(8,128)(2,1)S(1)} %copy-done.5, bf16[8,216,640]{2,1,0:T(8,128)(2,1)S(1)} %all-to-all-done.weight_ref), custom_call_target="tpu_custom_call" | custom-call | tf_op jit(solution)/shard_map/pallas_call | solution.py:179
  62.4 2.8 %collective-permute-start.3 = (bf16[2560,128]{1,0:T(8,128)(2,1)S(1)}, bf16[2560,128]{1,0:T(8,128)(2,1)S(1)}, u32[]{:S(2)}, u32[]{:S(2)}) collective-permute-start(bf16[2560,128]{1,0:T(8,128)(2,1)S(1)} %get-tuple-element.24), channel_id=1, source_target_pairs={{0,16},{16,0},{1,17},{17,1},{2,18},{18,2},{3,19},{19,3},{4,20},{20... | collective-permute-start | bytes 1966088 | tf_op jit(solution)/shard_map/ppermute | solution.py:19
  65.3 1.6 %collective-permute-done.3.other_ref = bf16[2560,128]{1,0:T(8,128)(2,1)S(1)} collective-permute-done((bf16[2560,128]{1,0:T(8,128)(2,1)S(1)}, bf16[2560,128]{1,0:T(8,128)(2,1)S(1)}, u32[]{:S(2)}, u32[]{:S(2)}) %collective-permute-start.3) | collective-permute-done | bytes 655392 | tf_op jit(solution)/shard_map/ppermute | solution.py:19
  66.9 1.3 shard_map.95
  68.2 10.9 %all-to-all-start.1 = ((bf16[16,176,128]{2,1,0:T(8,128)(2,1)}), bf16[16,176,128]{2,1,0:T(8,128)(2,1)}, u32[]{:S(2)}, u32[]{:S(2)}) async-start(bf16[16,176,128]{2,1,0:T(8,128)(2,1)} %shard_map.95), calls=%async_computation.1 | async-start | bytes 1441792 | tf_op jit(solution)/shard_map/all_to_all | solution.py:203
  79.2 0.9 copy-done.7
  80.1 1.0 shard_map.94
  81.1 2.0 %collective-permute-start.4 = (bf16[2,216,640]{2,1,0:T(8,128)(2,1)S(1)}, bf16[2,216,640]{2,1,0:T(8,128)(2,1)S(1)}, u32[]{:S(2)}, u32[]{:S(2)}) collective-permute-start(bf16[2,216,640]{2,1,0:T(8,128)(2,1)S(1)} %get-tuple-element.26), channel_id=1, source_target_pairs={{0,256},{128,384},{256,0},{384,128},{1,257},{129,385},{257,1},{385... | collective-permute-start | bytes 1658888 | tf_op jit(solution)/shard_map/ppermute | solution.py:27
  83.1 3.3 %collective-permute-start.5 = (bf16[2,216,640]{2,1,0:T(8,128)(2,1)S(1)}, bf16[2,216,640]{2,1,0:T(8,128)(2,1)S(1)}, u32[]{:S(2)}, u32[]{:S(2)}) collective-permute-start(bf16[2,216,640]{2,1,0:T(8,128)(2,1)S(1)} %get-tuple-element.27), channel_id=1, source_target_pairs={{0,128},{128,256},{256,384},{384,0},{1,129},{129,257},{257,385},{3... | collective-permute-start | bytes 1658888 | tf_op jit(solution)/shard_map/ppermute | solution.py:27
  86.4 3.2 %collective-permute-start.6 = (bf16[2,216,640]{2,1,0:T(8,128)(2,1)S(1)}, bf16[2,216,640]{2,1,0:T(8,128)(2,1)}, u32[]{:S(2)}, u32[]{:S(2)}) collective-permute-start(bf16[2,216,640]{2,1,0:T(8,128)(2,1)S(1)} %get-tuple-element.28), channel_id=1, source_target_pairs={{0,384},{128,0},{256,128},{384,256},{1,385},{129,1},{257,129},{385... | collective-permute-start | bytes 1658888 | tf_op jit(solution)/shard_map/ppermute | solution.py:27
  89.6 8.5 %collective-permute-done.4 = bf16[2,216,640]{2,1,0:T(8,128)(2,1)S(1)} collective-permute-done((bf16[2,216,640]{2,1,0:T(8,128)(2,1)S(1)}, bf16[2,216,640]{2,1,0:T(8,128)(2,1)S(1)}, u32[]{:S(2)}, u32[]{:S(2)}) %collective-permute-start.4) | collective-permute-done | bytes 552992 | tf_op jit(solution)/shard_map/ppermute | solution.py:27
  98.1 12.7 %collective-permute-done.5 = bf16[2,216,640]{2,1,0:T(8,128)(2,1)S(1)} collective-permute-done((bf16[2,216,640]{2,1,0:T(8,128)(2,1)S(1)}, bf16[2,216,640]{2,1,0:T(8,128)(2,1)S(1)}, u32[]{:S(2)}, u32[]{:S(2)}) %collective-permute-start.5) | collective-permute-done | bytes 552992 | tf_op jit(solution)/shard_map/ppermute | solution.py:27
  110.8 1.3 add_convert_fusion
  112.2 1.1 copy.21
  113.3 5.7 %all-to-all-start.2 = ((bf16[8,80,432]{2,1,0:T(8,128)(2,1)}), bf16[8,80,432]{2,1,0:T(8,128)(2,1)S(1)}, u32[]{:S(2)}, u32[]{:S(2)}) async-start(bf16[8,80,432]{2,1,0:T(8,128)(2,1)} %bitcast.9), calls=%async_computation.2 | async-start | bytes 1310720 | tf_op jit(solution)/shard_map/all_to_all | solution.py:227
  119.1 1.9 %collective-permute-start.2 = (bf16[216,128]{1,0:T(8,128)(2,1)S(1)}, bf16[216,128]{1,0:T(8,128)(2,1)S(1)}, u32[]{:S(2)}, u32[]{:S(2)}) collective-permute-start(bf16[216,128]{1,0:T(8,128)(2,1)S(1)} %get-tuple-element.42), channel_id=1, source_target_pairs={{0,16},{16,0},{1,17},{17,1},{2,18},{18,2},{3,19},{19,3},{4,20},{20... | collective-permute-start | bytes 165896 | tf_op jit(solution)/shard_map/ppermute | solution.py:19
  121.0 1.2 convert_reduce_fusion
  122.2 0.8 multiply_reduce_fusion
  123.0 7.2 %psum.14 = f32[160]{0:T(256)S(1)} all-reduce(f32[160]{0:T(256)S(1)} %get-tuple-element.33), channel_id=1, replica_groups=mesh['x'=4,'z'=4,'c'=2,'y'=8,'h'=2] {'x'}, use_global_device_ids=true, to_apply=%region_3.4 | all-reduce | flops 160 | bytes 1280 | tf_op jit(solution)/shard_map/psum | solution.py:220
  130.2 10.1 %psum.15 = f32[160]{0:T(256)S(1)} all-reduce(f32[160]{0:T(256)S(1)} %psum.14), channel_id=1, replica_groups=mesh['x'=4,'z'=4,'c'=2,'y'=8,'h'=2] {'z'}, use_global_device_ids=true, to_apply=%region_4.5 | all-reduce | flops 160 | bytes 1280 | tf_op jit(solution)/shard_map/psum | solution.py:220
  140.4 5.8 %collective-permute-start.7 = (f32[160]{0:T(256)S(1)}, f32[160]{0:T(256)S(1)}, u32[]{:S(2)}, u32[]{:S(2)}) collective-permute-start(f32[160]{0:T(256)S(1)} %psum.15), channel_id=1, source_target_pairs={{0,16},{16,0},{1,17},{17,1},{2,18},{18,2},{3,19},{19,3},{4,20},{20... | collective-permute-start | bytes 1928 | tf_op jit(solution)/shard_map/ppermute | solution.py:19
  146.2 0.7 fusion
  146.9 0.1 collective-permute-done.7
  147.0 0.6 add.38
  147.6 0.1 convert_reduce_fusion.1
  147.7 0.1 slice_bitcast_fusion.1
  147.8 0.9 pad_maximum_fusion.1
  (29 shorter events, 0.3 us)
Async XLA Ops:
  22.0 8.5 %copy-start.10 = (bf16[128,2560]{1,0:T(8,128)(2,1)S(1)}, bf16[128,2560]{1,0:T(8,128)(2,1)}, u32[]{:S(2)}) copy-start(bf16[128,2560]{1,0:T(8,128)(2,1)} %param.5) | copy-start | bytes 1966084
  22.0 36.1 %all-to-all-start = ((bf16[8,216,640]{2,1,0:T(8,128)(2,1)}), bf16[8,216,640]{2,1,0:T(8,128)(2,1)S(1)}, u32[]{:S(2)}, u32[]{:S(2)}) async-start(bf16[8,216,640]{2,1,0:T(8,128)(2,1)} %bitcast.30), calls=%async_computation | async-start | bytes 4423680 | tf_op jit(solution)/shard_map/all_to_all | solution.py:167
  30.8 6.8 %collective-permute-start = (bf16[128,2560]{0,1:T(8,128)(2,1)S(1)}, bf16[128,2560]{0,1:T(8,128)(2,1)S(1)}, u32[]{:S(2)}, u32[]{:S(2)}) collective-permute-start(bf16[128,2560]{0,1:T(8,128)(2,1)S(1)} %copy.19), channel_id=1, source_target_pairs={{0,16},{16,0},{1,17},{17,1},{2,18},{18,2},{3,19},{19,3},{4,20},{20... | collective-permute-start | bytes 1966088 | tf_op jit(solution)/shard_map/ppermute | solution.py:19
  33.8 3.2 %collective-permute-start.1 = (bf16[216,128]{1,0:T(8,128)(2,1)S(1)}, bf16[216,128]{1,0:T(8,128)(2,1)S(1)}, u32[]{:S(2)}, u32[]{:S(2)}) collective-permute-start(bf16[216,128]{1,0:T(8,128)(2,1)S(1)} %get-tuple-element.44), channel_id=1, source_target_pairs={{0,16},{16,0},{1,17},{17,1},{2,18},{18,2},{3,19},{19,3},{4,20},{20... | collective-permute-start | bytes 165896 | tf_op jit(solution)/shard_map/ppermute | solution.py:19
  37.6 0.7 copy-start.11
  38.3 1.1 copy-start
  39.9 1.1 copy-start.2
  58.1 1.3 copy-start.3
  59.4 0.9 copy-start.5
  60.3 4.9 %copy-start.1 = (bf16[2560,256]{1,0:T(8,128)(2,1)S(1)}, bf16[2560,256]{1,0:T(8,128)(2,1)}, u32[]{:S(2)}) copy-start(bf16[2560,256]{1,0:T(8,128)(2,1)} %copy-done) | copy-start | bytes 3932164
  62.4 4.5 %copy-start.6 = (bf16[2,216,256]{2,1,0:T(8,128)(2,1)}, bf16[2,216,256]{2,1,0:T(8,128)(2,1)S(1)}, u32[]{:S(2)}) copy-start(bf16[2,216,256]{2,1,0:T(8,128)(2,1)S(1)} %get-tuple-element.21.back_ref) | copy-start | bytes 663556
  62.4 4.5 %copy-start.8 = (bf16[216,256]{1,0:T(8,128)(2,1)}, bf16[216,256]{1,0:T(8,128)(2,1)S(1)}, u32[]{:S(2)}) copy-start(bf16[216,256]{1,0:T(8,128)(2,1)S(1)} %get-tuple-element.20) | copy-start | bytes 331780
  62.4 4.5 %collective-permute-start.3 = (bf16[2560,128]{1,0:T(8,128)(2,1)S(1)}, bf16[2560,128]{1,0:T(8,128)(2,1)S(1)}, u32[]{:S(2)}, u32[]{:S(2)}) collective-permute-start(bf16[2560,128]{1,0:T(8,128)(2,1)S(1)} %get-tuple-element.24), channel_id=1, source_target_pairs={{0,16},{16,0},{1,17},{17,1},{2,18},{18,2},{3,19},{19,3},{4,20},{20... | collective-permute-start | bytes 1966088 | tf_op jit(solution)/shard_map/ppermute | solution.py:19
  68.2 11.0 %copy-start.4 = (bf16[2560,256]{1,0:T(8,128)(2,1)S(1)}, bf16[2560,256]{1,0:T(8,128)(2,1)}, u32[]{:S(2)}) copy-start(bf16[2560,256]{1,0:T(8,128)(2,1)} %copy-done.2) | copy-start | bytes 3932164
  68.2 42.6 %all-to-all-start.1 = ((bf16[16,176,128]{2,1,0:T(8,128)(2,1)}), bf16[16,176,128]{2,1,0:T(8,128)(2,1)}, u32[]{:S(2)}, u32[]{:S(2)}) async-start(bf16[16,176,128]{2,1,0:T(8,128)(2,1)} %shard_map.95), calls=%async_computation.1 | async-start | bytes 1441792 | tf_op jit(solution)/shard_map/all_to_all | solution.py:203
  79.1 0.9 copy-start.7
  81.1 17.0 %collective-permute-start.4 = (bf16[2,216,640]{2,1,0:T(8,128)(2,1)S(1)}, bf16[2,216,640]{2,1,0:T(8,128)(2,1)S(1)}, u32[]{:S(2)}, u32[]{:S(2)}) collective-permute-start(bf16[2,216,640]{2,1,0:T(8,128)(2,1)S(1)} %get-tuple-element.26), channel_id=1, source_target_pairs={{0,256},{128,384},{256,0},{384,128},{1,257},{129,385},{257,1},{385... | collective-permute-start | bytes 1658888 | tf_op jit(solution)/shard_map/ppermute | solution.py:27
  83.1 27.7 %collective-permute-start.5 = (bf16[2,216,640]{2,1,0:T(8,128)(2,1)S(1)}, bf16[2,216,640]{2,1,0:T(8,128)(2,1)S(1)}, u32[]{:S(2)}, u32[]{:S(2)}) collective-permute-start(bf16[2,216,640]{2,1,0:T(8,128)(2,1)S(1)} %get-tuple-element.27), channel_id=1, source_target_pairs={{0,128},{128,256},{256,384},{384,0},{1,129},{129,257},{257,385},{3... | collective-permute-start | bytes 1658888 | tf_op jit(solution)/shard_map/ppermute | solution.py:27
  86.4 24.4 %collective-permute-start.6 = (bf16[2,216,640]{2,1,0:T(8,128)(2,1)S(1)}, bf16[2,216,640]{2,1,0:T(8,128)(2,1)}, u32[]{:S(2)}, u32[]{:S(2)}) collective-permute-start(bf16[2,216,640]{2,1,0:T(8,128)(2,1)S(1)} %get-tuple-element.28), channel_id=1, source_target_pairs={{0,384},{128,0},{256,128},{384,256},{1,385},{129,1},{257,129},{385... | collective-permute-start | bytes 1658888 | tf_op jit(solution)/shard_map/ppermute | solution.py:27
  112.2 6.9 %copy-start.9 = (bf16[216,256]{1,0:T(8,128)(2,1)S(1)}, bf16[216,256]{1,0:T(8,128)(2,1)}, u32[]{:S(2)}) copy-start(bf16[216,256]{1,0:T(8,128)(2,1)} %copy-done.8) | copy-start | bytes 331780
  113.3 34.3 %all-to-all-start.2 = ((bf16[8,80,432]{2,1,0:T(8,128)(2,1)}), bf16[8,80,432]{2,1,0:T(8,128)(2,1)S(1)}, u32[]{:S(2)}, u32[]{:S(2)}) async-start(bf16[8,80,432]{2,1,0:T(8,128)(2,1)} %bitcast.9), calls=%async_computation.2 | async-start | bytes 1310720 | tf_op jit(solution)/shard_map/all_to_all | solution.py:227
  119.1 27.1 %collective-permute-start.2 = (bf16[216,128]{1,0:T(8,128)(2,1)S(1)}, bf16[216,128]{1,0:T(8,128)(2,1)S(1)}, u32[]{:S(2)}, u32[]{:S(2)}) collective-permute-start(bf16[216,128]{1,0:T(8,128)(2,1)S(1)} %get-tuple-element.42), channel_id=1, source_target_pairs={{0,16},{16,0},{1,17},{17,1},{2,18},{18,2},{3,19},{19,3},{4,20},{20... | collective-permute-start | bytes 165896 | tf_op jit(solution)/shard_map/ppermute | solution.py:19
  140.4 6.6 %collective-permute-start.7 = (f32[160]{0:T(256)S(1)}, f32[160]{0:T(256)S(1)}, u32[]{:S(2)}, u32[]{:S(2)}) collective-permute-start(f32[160]{0:T(256)S(1)} %psum.15), channel_id=1, source_target_pairs={{0,16},{16,0},{1,17},{17,1},{2,18},{18,2},{3,19},{19,3},{4,20},{20... | collective-permute-start | bytes 1928 | tf_op jit(solution)/shard_map/ppermute | solution.py:19

commit v6 on v5

--- a/solution.py
+++ b/solution.py
@@ -192,16 +192,19 @@
         tuple(shape((2, half, column_rows), F32 if index == 0 else BF) for index in range(NX)),
         [SMEM] + [VMEM] * 2,
     )(spot, normed, back)
+    part_other, terms = lax.optimization_barrier((part_other, terms))
     travelling = [shift_x(terms[steps], steps) for steps in (2, 1, 3)]
     hidden_other = swap_core(hidden_pair[:, tokens:])
-    hidden = ordered(hidden_pair[:, :tokens], hidden_other, 0).T
 
     spare = 16
     sending = call(blocks_kernel, shape((n_dp, features + spare, tokens), BF), [VMEM] * 5)(
         part_own, part_other, inputs_t[:, :tokens], root_mean[:, :tokens], gain_wide
     )
     got = lax.all_to_all(sending, ("y", "h"), 0, 0, tiled=True)
-    got, travelling = lax.optimization_barrier((got, travelling))
+    got, travelling[0], hidden_other = lax.optimization_barrier(
+        (got, travelling[0], hidden_other)
+    )
+    hidden = ordered(hidden_pair[:, :tokens], hidden_other, 0).T
     totals = jnp.sum(got.astype(F32), axis=0)
     own_sums = totals[:features]
     token_totals = totals[features] + totals[features + 1] + totals[features + 2]
@@ -217,7 +220,9 @@
         .T
     )
     gain_part = jnp.sum(own_sums * unit_slice, axis=1)
-    grad_gain = lax.psum(lax.psum(gain_part, "x"), "z")
+    gain_part = lax.psum(gain_part, "x")
+    gain_part, travelling = lax.optimization_barrier((gain_part, travelling))
+    grad_gain = lax.psum(gain_part, "z")
     grad_gain = grad_gain + swap_core(grad_gain)
 
     column_sum = terms[0]

time: 150 us -> 158 us (1.053)
  waiting for transfers between devices: 40.9 us -> 33.8 us
  local copies, waits for them, and re-layouts: 9.52 us -> 16.5 us
  blocking collectives: 35.5 us -> 41.1 us
  Pallas kernels: 4.89 us -> 6.89 us
    ppermute x3, waiting for transfers between devices: 21.2 us -> 6.49 us  [shift_x(): return lax.ppermute(value, 'x', [(x, (x + steps) % NX) for x in range(NX)])]
    all_to_all x1, waiting for transfers between devices: 0.01 us -> 9.21 us  [per_device(): got = lax.all_to_all(sending, ('y', 'h'), 0, 0, tiled=True)]
    unnamed x25 -> x41, local copies, waits for them, and re-layouts: 5.8 us -> 11.6 us
    psum x2, blocking collectives: 17.4 us -> 23 us  [the longest x1 16.2 us: per_device(): grad_gain = lax.psum(gain_part, 'z')]
    all_to_all x1, starting transfers between devices: 5.68 us -> 8.04 us  [per_device(): lax.all_to_all(column_sum.reshape(NC * NZ, rows, columns), ('c', 'z'), 0,...]
    ppermute x5, waiting for transfers between devices: 2.61 us -> 0.99 us  [swap(): return lax.ppermute(value, axis, [(0, 1), (1, 0)])]
  transfers between devices with their start and end apart: 11 -> 11, of which waited for: 6 -> 5; matrix products, arithmetic and copies ran while one was open for 4% -> 4% of each run, Pallas kernels for 1% -> 1%
where the time goes in v6:
time: 158 us; the launch traced here: 157 us
  starting transfers between devices  49.4 us (31%)
  blocking collectives  41.1 us (26%)
  waiting for transfers between devices  33.8 us (21%)
  local copies, waits for them, and re-layouts  16.5 us (10%)
  other arithmetic  8.69 us (6%)
  Pallas kernels  6.89 us (4%)
    all_gather x1, blocking collectives, per_device(): lax.all_gather(jnp.concatenate([w_gate, w_up], 1), 'z', axis=0, tiled=True)  18.1 us
    all_to_all x1, waiting for transfers between devices, per_device(): weight = lax.all_to_all(copies, ('x', 'c'), 0, 0, tiled=True)  17.1 us
    psum x1, blocking collectives, per_device(): grad_gain = lax.psum(gain_part, 'z')  16.2 us
    ppermute x5, starting transfers between devices, swap(): return lax.ppermute(value, axis, [(0, 1), (1, 0)])  13.4 us
    unnamed x41, local copies, waits for them, and re-layouts  11.6 us
    all_to_all x1, starting transfers between devices, per_device(): got = lax.all_to_all(sending, ('y', 'h'), 0, 0, tiled=True)  10.9 us
    all_to_all x1, waiting for transfers between devices, per_device(): got = lax.all_to_all(sending, ('y', 'h'), 0, 0, tiled=True)  9.21 us
    all_to_all x1, starting transfers between devices, per_device(): weight = lax.all_to_all(copies, ('x', 'c'), 0, 0, tiled=True)  8.54 us
  transfers between devices with their start and end apart: 11, of which 5 were waited for; matrix products, arithmetic and copies ran while one was open for 4% of the time, Pallas kernels for 1%

profile of v6, /device:TPU:1, one launch (start us, length us, event | category | flops | bytes accessed | tf_op | source)
XLA Modules:
  0.0 157.4 jit_solution(4086292190965411521)
XLA Ops:
  0.6 1.0 pad_maximum_fusion.3
  1.7 18.1 %all_gather.3 = bf16[320,864]{1,0:T(8,128)(2,1)S(1)} all-gather(bf16[80,864]{1,0:T(8,128)(2,1)S(1)} %pad_maximum_fusion.3), channel_id=1, replica_groups=mesh['x'=4,'z'=4,'c'=2,'y'=8,'h'=2] {'z'}, dimensions={0}, use_global_device_ids=true | all-gather | bytes 691200 | tf_op jit(solution)/shard_map/all_gather | solution.py:162
  20.4 1.5 broadcast_in_dim.5
  22.0 8.5 %all-to-all-start = ((bf16[8,216,640]{2,1,0:T(8,128)(2,1)}), bf16[8,216,640]{2,1,0:T(8,128)(2,1)S(1)}, u32[]{:S(2)}, u32[]{:S(2)}) async-start(bf16[8,216,640]{2,1,0:T(8,128)(2,1)} %bitcast.30), calls=%async_computation | async-start | bytes 4423680 | tf_op jit(solution)/shard_map/all_to_all | solution.py:167
  30.8 2.0 %collective-permute-start = (bf16[128,2560]{0,1:T(8,128)(2,1)S(1)}, bf16[128,2560]{0,1:T(8,128)(2,1)S(1)}, u32[]{:S(2)}, u32[]{:S(2)}) collective-permute-start(bf16[128,2560]{0,1:T(8,128)(2,1)S(1)} %copy.19), channel_id=1, source_target_pairs={{0,16},{16,0},{1,17},{17,1},{2,18},{18,2},{3,19},{19,3},{4,20},{20... | collective-permute-start | bytes 1966088 | tf_op jit(solution)/shard_map/ppermute | solution.py:19
  32.9 0.9 broadcast_select_fusion.1
  33.8 2.3 %collective-permute-start.1 = (bf16[216,128]{1,0:T(8,128)(2,1)S(1)}, bf16[216,128]{1,0:T(8,128)(2,1)S(1)}, u32[]{:S(2)}, u32[]{:S(2)}) collective-permute-start(bf16[216,128]{1,0:T(8,128)(2,1)S(1)} %get-tuple-element.60), channel_id=1, source_target_pairs={{0,16},{16,0},{1,17},{17,1},{2,18},{18,2},{3,19},{19,3},{4,20},{20... | collective-permute-start | bytes 165896 | tf_op jit(solution)/shard_map/ppermute | solution.py:19
  36.1 0.9 collective-permute-done.1
  36.9 0.7 pad_maximum_fusion.4.upstream_ref
  37.7 0.6 copy-done.19
  38.3 0.4 broadcast_in_dim.4.gain_ref
  38.7 0.7 copy-done
  39.4 0.5 shard_map.92
  39.9 1.0 copy-done.1
  41.0 17.1 %all-to-all-done.weight_ref = bf16[8,216,640]{2,1,0:T(8,128)(2,1)S(1)} async-done(((bf16[8,216,640]{2,1,0:T(8,128)(2,1)}), bf16[8,216,640]{2,1,0:T(8,128)(2,1)S(1)}, u32[]{:S(2)}, u32[]{:S(2)}) %all-to-all-start) | async-done | bytes 2211872 | tf_op jit(solution)/shard_map/all_to_all | solution.py:167
  58.1 1.3 copy-done.2
  59.4 0.9 copy-done.8
  60.3 2.9 %shard_map.93 = (bf16[216,256]{1,0:T(8,128)(2,1)S(1)}, bf16[2,216,256]{2,1,0:T(8,128)(2,1)S(1)}, f32[2560,128]{1,0:T(8,128)S(1)}, bf16[2560,128]{1,0:T(8,128)(2,1)}) custom-call(bf16[2560,256]{1,0:T(8,128)(2,1)S(1)} %copy-done.2, bf16[216,256]{1,0:T(8,128)(2,1)S(1)} %copy-done.8, bf16[8,216,640]{2,1,0:T(8,128)(2,1)S(1)} %all-to-all-done.weight_ref), custom_call_target="tpu_custom_call" | custom-call | tf_op jit(solution)/shard_map/pallas_call | solution.py:179
  63.2 1.1 copy-done.4
  64.3 0.7 copy-done.9
  65.0 0.6 copy-done.11
  65.6 2.9 %collective-permute-start.2 = (bf16[2560,128]{1,0:T(8,128)(2,1)}, bf16[2560,128]{1,0:T(8,128)(2,1)}, u32[]{:S(2)}, u32[]{:S(2)}) collective-permute-start(bf16[2560,128]{1,0:T(8,128)(2,1)} %get-tuple-element.30), channel_id=1, source_target_pairs={{0,16},{16,0},{1,17},{17,1},{2,18},{18,2},{3,19},{19,3},{4,20},{20... | collective-permute-start | bytes 1966088 | tf_op jit(solution)/shard_map/ppermute | solution.py:19
  68.6 1.2 slice.60.x_ref
  69.8 0.9 copy-done.10
  70.8 1.0 shard_map.94
  71.8 1.0 copy-done.6
  72.8 0.8 copy-done.13
  73.6 0.8 copy-done.15
  74.4 0.8 copy-done.17
  75.2 2.4 %shard_map.95 = bf16[16,176,128]{2,1,0:T(8,128)(2,1)} custom-call(f32[2560,128]{1,0:T(8,128)S(1)} %copy-done.5, bf16[2560,128]{1,0:T(8,128)(2,1)} %collective-permute-done.2.other_ref, bf16[2560,128]{1,0:T(8,128)(2,1)S(1)} %slice.60.x_ref, f32[1,128]{1,0:T(1,128)S(1)} %get-tuple-element.62.root_ref, f32[2560,128]{1,0:T(8,128)S(1)} %broadcast_in_dim.4.gain_ref), custom_call_target="tpu_custom_call" | custom-call | tf_op jit(solution)/shard_map/pallas_call | solution.py:200
  77.7 10.9 %all-to-all-start.1 = ((bf16[16,176,128]{2,1,0:T(8,128)(2,1)}), bf16[16,176,128]{2,1,0:T(8,128)(2,1)}, u32[]{:S(2)}, u32[]{:S(2)}) async-start(bf16[16,176,128]{2,1,0:T(8,128)(2,1)} %shard_map.95), calls=%async_computation.1 | async-start | bytes 1441792 | tf_op jit(solution)/shard_map/all_to_all | solution.py:203
  88.6 2.0 %collective-permute-start.3 = (bf16[2,216,640]{2,1,0:T(8,128)(2,1)}, bf16[2,216,640]{2,1,0:T(8,128)(2,1)}, u32[]{:S(2)}, u32[]{:S(2)}) collective-permute-start(bf16[2,216,640]{2,1,0:T(8,128)(2,1)} %copy-done.17), channel_id=1, source_target_pairs={{0,256},{128,384},{256,0},{384,128},{1,257},{129,385},{257,1},{385... | collective-permute-start | bytes 1658888 | tf_op jit(solution)/shard_map/ppermute | solution.py:27
  90.6 2.5 %collective-permute-start.4 = (bf16[216,128]{1,0:T(8,128)(2,1)S(1)}, bf16[216,128]{1,0:T(8,128)(2,1)S(1)}, u32[]{:S(2)}, u32[]{:S(2)}) collective-permute-start(bf16[216,128]{1,0:T(8,128)(2,1)S(1)} %get-tuple-element.58), channel_id=1, source_target_pairs={{0,16},{16,0},{1,17},{17,1},{2,18},{18,2},{3,19},{19,3},{4,20},{20... | collective-permute-start | bytes 165896 | tf_op jit(solution)/shard_map/ppermute | solution.py:19
  93.2 3.3 %collective-permute-start.5 = (bf16[2,216,640]{2,1,0:T(8,128)(2,1)S(1)}, bf16[2,216,640]{2,1,0:T(8,128)(2,1)}, u32[]{:S(2)}, u32[]{:S(2)}) collective-permute-start(bf16[2,216,640]{2,1,0:T(8,128)(2,1)S(1)} %copy-done.16), channel_id=1, source_target_pairs={{0,128},{128,256},{256,384},{384,0},{1,129},{129,257},{257,385},{3... | collective-permute-start | bytes 1658888 | tf_op jit(solution)/shard_map/ppermute | solution.py:27
  96.5 3.2 %collective-permute-start.6 = (bf16[2,216,640]{2,1,0:T(8,128)(2,1)S(1)}, bf16[2,216,640]{2,1,0:T(8,128)(2,1)}, u32[]{:S(2)}, u32[]{:S(2)}) collective-permute-start(bf16[2,216,640]{2,1,0:T(8,128)(2,1)S(1)} %copy-done.14), channel_id=1, source_target_pairs={{0,384},{128,0},{256,128},{384,256},{1,385},{129,1},{257,129},{385... | collective-permute-start | bytes 1658888 | tf_op jit(solution)/shard_map/ppermute | solution.py:27
  99.7 6.5 %collective-permute-done.3 = bf16[2,216,640]{2,1,0:T(8,128)(2,1)} collective-permute-done((bf16[2,216,640]{2,1,0:T(8,128)(2,1)}, bf16[2,216,640]{2,1,0:T(8,128)(2,1)}, u32[]{:S(2)}, u32[]{:S(2)}) %collective-permute-start.3) | collective-permute-done | bytes 552992 | tf_op jit(solution)/shard_map/ppermute | solution.py:27
  106.2 9.2 %all-to-all-done.1 = bf16[16,176,128]{2,1,0:T(8,128)(2,1)} async-done(((bf16[16,176,128]{2,1,0:T(8,128)(2,1)}), bf16[16,176,128]{2,1,0:T(8,128)(2,1)}, u32[]{:S(2)}, u32[]{:S(2)}) %all-to-all-start.1) | async-done | bytes 720928 | tf_op jit(solution)/shard_map/all_to_all | solution.py:203
  115.4 1.2 convert_reduce_fusion
  116.7 0.8 fusion.1
  117.4 6.8 %psum.14 = f32[160]{0:T(256)S(1)} all-reduce(f32[160]{0:T(256)S(1)} %get-tuple-element.50), channel_id=1, replica_groups=mesh['x'=4,'z'=4,'c'=2,'y'=8,'h'=2] {'x'}, use_global_device_ids=true, to_apply=%region_2.3 | all-reduce | flops 160 | bytes 1280 | tf_op jit(solution)/shard_map/psum | solution.py:223
  124.3 1.6 %add_convert_fusion = bf16[2,216,640]{2,1,0:T(8,128)(2,1)S(1)} fusion(bf16[2,216,640]{2,1,0:T(8,128)(2,1)} %collective-permute-done.6, bf16[2,216,640]{2,1,0:T(8,128)(2,1)} %collective-permute-done.5, f32[2,216,640]{2,1,0:T(8,128)S(1)} %copy-done.7, bf16[2,216,640]{2,1,0:T(8,128)(2,1)} %collective-permute-done.3), kind=kLoop, calls=%fused_computation.3 | loop fusion | flops 1935360 | bytes 3317760 | tf_op jit(solution)/shard_map/convert_element_type | solution.py:231
  125.9 1.1 copy.21
  127.0 8.0 %all-to-all-start.2 = ((bf16[8,80,432]{2,1,0:T(8,128)(2,1)}), bf16[8,80,432]{2,1,0:T(8,128)(2,1)S(1)}, u32[]{:S(2)}, u32[]{:S(2)}) async-start(bf16[8,80,432]{2,1,0:T(8,128)(2,1)} %bitcast.10), calls=%async_computation.2 | async-start | bytes 1310720 | tf_op jit(solution)/shard_map/all_to_all | solution.py:232
  135.0 16.2 %psum.15 = f32[160]{0:T(256)S(1)} all-reduce(f32[160]{0:T(256)S(1)} %psum.14), channel_id=1, replica_groups=mesh['x'=4,'z'=4,'c'=2,'y'=8,'h'=2] {'z'}, use_global_device_ids=true, to_apply=%region_4.5 | all-reduce | flops 160 | bytes 1280 | tf_op jit(solution)/shard_map/psum | solution.py:225
  151.2 3.7 %collective-permute-start.7 = (f32[160]{0:T(256)S(1)}, f32[160]{0:T(256)S(1)}, u32[]{:S(2)}, u32[]{:S(2)}) collective-permute-start(f32[160]{0:T(256)S(1)} %psum.15), channel_id=1, source_target_pairs={{0,16},{16,0},{1,17},{17,1},{2,18},{18,2},{3,19},{19,3},{4,20},{20... | collective-permute-start | bytes 1928 | tf_op jit(solution)/shard_map/ppermute | solution.py:19
  154.9 0.7 fusion
  155.7 0.6 add.38
  156.5 0.9 pad_maximum_fusion.1
  (45 shorter events, 1.5 us)
Async XLA Ops:
  22.0 8.5 %copy-start.18 = (bf16[128,2560]{1,0:T(8,128)(2,1)S(1)}, bf16[128,2560]{1,0:T(8,128)(2,1)}, u32[]{:S(2)}) copy-start(bf16[128,2560]{1,0:T(8,128)(2,1)} %param.5) | copy-start | bytes 1966084
  22.0 36.1 %all-to-all-start = ((bf16[8,216,640]{2,1,0:T(8,128)(2,1)}), bf16[8,216,640]{2,1,0:T(8,128)(2,1)S(1)}, u32[]{:S(2)}, u32[]{:S(2)}) async-start(bf16[8,216,640]{2,1,0:T(8,128)(2,1)} %bitcast.30), calls=%async_computation | async-start | bytes 4423680 | tf_op jit(solution)/shard_map/all_to_all | solution.py:167
  30.8 6.8 %collective-permute-start = (bf16[128,2560]{0,1:T(8,128)(2,1)S(1)}, bf16[128,2560]{0,1:T(8,128)(2,1)S(1)}, u32[]{:S(2)}, u32[]{:S(2)}) collective-permute-start(bf16[128,2560]{0,1:T(8,128)(2,1)S(1)} %copy.19), channel_id=1, source_target_pairs={{0,16},{16,0},{1,17},{17,1},{2,18},{18,2},{3,19},{19,3},{4,20},{20... | collective-permute-start | bytes 1966088 | tf_op jit(solution)/shard_map/ppermute | solution.py:19
  33.8 3.2 %collective-permute-start.1 = (bf16[216,128]{1,0:T(8,128)(2,1)S(1)}, bf16[216,128]{1,0:T(8,128)(2,1)S(1)}, u32[]{:S(2)}, u32[]{:S(2)}) collective-permute-start(bf16[216,128]{1,0:T(8,128)(2,1)S(1)} %get-tuple-element.60), channel_id=1, source_target_pairs={{0,16},{16,0},{1,17},{17,1},{2,18},{18,2},{3,19},{19,3},{4,20},{20... | collective-permute-start | bytes 165896 | tf_op jit(solution)/shard_map/ppermute | solution.py:19
  37.6 0.7 copy-start.19
  38.3 1.1 copy-start
  39.9 1.1 copy-start.1
  58.1 1.3 copy-start.2
  59.4 0.9 copy-start.8
  63.2 1.1 copy-start.4
  64.3 0.7 copy-start.9
  65.0 0.6 copy-start.11
  65.6 4.2 %copy-start.3 = (bf16[2560,256]{1,0:T(8,128)(2,1)S(1)}, bf16[2560,256]{1,0:T(8,128)(2,1)}, u32[]{:S(2)}) copy-start(bf16[2560,256]{1,0:T(8,128)(2,1)} %copy-done.1) | copy-start | bytes 3932164
  65.6 8.8 %collective-permute-start.2 = (bf16[2560,128]{1,0:T(8,128)(2,1)}, bf16[2560,128]{1,0:T(8,128)(2,1)}, u32[]{:S(2)}, u32[]{:S(2)}) collective-permute-start(bf16[2560,128]{1,0:T(8,128)(2,1)} %get-tuple-element.30), channel_id=1, source_target_pairs={{0,16},{16,0},{1,17},{17,1},{2,18},{18,2},{3,19},{19,3},{4,20},{20... | collective-permute-start | bytes 1966088 | tf_op jit(solution)/shard_map/ppermute | solution.py:19
  68.6 6.7 %copy-start.5 = (f32[2560,128]{1,0:T(8,128)S(1)}, f32[2560,128]{1,0:T(8,128)}, u32[]{:S(2)}) copy-start(f32[2560,128]{1,0:T(8,128)} %copy-done.4) | copy-start | bytes 3932164
  69.8 0.9 copy-start.10
  71.8 1.0 copy-start.6
  72.8 0.8 copy-start.13
  73.6 0.8 copy-start.15
  74.4 0.8 copy-start.17
  75.2 18.0 %copy-start.16 = (bf16[2,216,640]{2,1,0:T(8,128)(2,1)S(1)}, bf16[2,216,640]{2,1,0:T(8,128)(2,1)}, u32[]{:S(2)}) copy-start(bf16[2,216,640]{2,1,0:T(8,128)(2,1)} %copy-done.15) | copy-start | bytes 1658884
  75.2 21.3 %copy-start.14 = (bf16[2,216,640]{2,1,0:T(8,128)(2,1)S(1)}, bf16[2,216,640]{2,1,0:T(8,128)(2,1)}, u32[]{:S(2)}) copy-start(bf16[2,216,640]{2,1,0:T(8,128)(2,1)} %copy-done.13) | copy-start | bytes 1658884
  77.7 13.0 %copy-start.12 = (bf16[216,256]{1,0:T(8,128)(2,1)S(1)}, bf16[216,256]{1,0:T(8,128)(2,1)}, u32[]{:S(2)}) copy-start(bf16[216,256]{1,0:T(8,128)(2,1)} %copy-done.11) | copy-start | bytes 331780
  77.7 46.6 %copy-start.7 = (f32[2,216,640]{2,1,0:T(8,128)S(1)}, f32[2,216,640]{2,1,0:T(8,128)}, u32[]{:S(2)}) copy-start(f32[2,216,640]{2,1,0:T(8,128)} %copy-done.6) | copy-start | bytes 3317764
  77.7 37.8 %all-to-all-start.1 = ((bf16[16,176,128]{2,1,0:T(8,128)(2,1)}), bf16[16,176,128]{2,1,0:T(8,128)(2,1)}, u32[]{:S(2)}, u32[]{:S(2)}) async-start(bf16[16,176,128]{2,1,0:T(8,128)(2,1)} %shard_map.95), calls=%async_computation.1 | async-start | bytes 1441792 | tf_op jit(solution)/shard_map/all_to_all | solution.py:203
  88.6 17.6 %collective-permute-start.3 = (bf16[2,216,640]{2,1,0:T(8,128)(2,1)}, bf16[2,216,640]{2,1,0:T(8,128)(2,1)}, u32[]{:S(2)}, u32[]{:S(2)}) collective-permute-start(bf16[2,216,640]{2,1,0:T(8,128)(2,1)} %copy-done.17), channel_id=1, source_target_pairs={{0,256},{128,384},{256,0},{384,128},{1,257},{129,385},{257,1},{385... | collective-permute-start | bytes 1658888 | tf_op jit(solution)/shard_map/ppermute | solution.py:27
  90.6 9.1 %collective-permute-start.4 = (bf16[216,128]{1,0:T(8,128)(2,1)S(1)}, bf16[216,128]{1,0:T(8,128)(2,1)S(1)}, u32[]{:S(2)}, u32[]{:S(2)}) collective-permute-start(bf16[216,128]{1,0:T(8,128)(2,1)S(1)} %get-tuple-element.58), channel_id=1, source_target_pairs={{0,16},{16,0},{1,17},{17,1},{2,18},{18,2},{3,19},{19,3},{4,20},{20... | collective-permute-start | bytes 165896 | tf_op jit(solution)/shard_map/ppermute | solution.py:19
  93.2 31.1 %collective-permute-start.5 = (bf16[2,216,640]{2,1,0:T(8,128)(2,1)S(1)}, bf16[2,216,640]{2,1,0:T(8,128)(2,1)}, u32[]{:S(2)}, u32[]{:S(2)}) collective-permute-start(bf16[2,216,640]{2,1,0:T(8,128)(2,1)S(1)} %copy-done.16), channel_id=1, source_target_pairs={{0,128},{128,256},{256,384},{384,0},{1,129},{129,257},{257,385},{3... | collective-permute-start | bytes 1658888 | tf_op jit(solution)/shard_map/ppermute | solution.py:27
  96.5 27.8 %collective-permute-start.6 = (bf16[2,216,640]{2,1,0:T(8,128)(2,1)S(1)}, bf16[2,216,640]{2,1,0:T(8,128)(2,1)}, u32[]{:S(2)}, u32[]{:S(2)}) collective-permute-start(bf16[2,216,640]{2,1,0:T(8,128)(2,1)S(1)} %copy-done.14), channel_id=1, source_target_pairs={{0,384},{128,0},{256,128},{384,256},{1,385},{129,1},{257,129},{385... | collective-permute-start | bytes 1658888 | tf_op jit(solution)/shard_map/ppermute | solution.py:27
  127.0 29.3 %all-to-all-start.2 = ((bf16[8,80,432]{2,1,0:T(8,128)(2,1)}), bf16[8,80,432]{2,1,0:T(8,128)(2,1)S(1)}, u32[]{:S(2)}, u32[]{:S(2)}) async-start(bf16[8,80,432]{2,1,0:T(8,128)(2,1)} %bitcast.10), calls=%async_computation.2 | async-start | bytes 1310720 | tf_op jit(solution)/shard_map/all_to_all | solution.py:232
  151.2 4.5 %collective-permute-start.7 = (f32[160]{0:T(256)S(1)}, f32[160]{0:T(256)S(1)}, u32[]{:S(2)}, u32[]{:S(2)}) collective-permute-start(f32[160]{0:T(256)S(1)} %psum.15), channel_id=1, source_target_pairs={{0,16},{16,0},{1,17},{17,1},{2,18},{18,2},{3,19},{19,3},{4,20},{20... | collective-permute-start | bytes 1928 | tf_op jit(solution)/shard_map/ppermute | solution.py:19

commit v7 on v5

--- a/solution.py
+++ b/solution.py
@@ -8,8 +8,8 @@
 BF = jnp.bfloat16
 F32 = jnp.float32
 NX, NZ, NC, NH = 4, 4, 2, 2
+ANY = pl.BlockSpec(memory_space=pl.ANY)
 VMEM = pl.BlockSpec(memory_space=pltpu.VMEM)
-SMEM = pl.BlockSpec(memory_space=pltpu.SMEM)
 PARAMS = pltpu.CompilerParams(vmem_limit_bytes=48 * 1024 * 1024)
 NT = (((1,), (1,)), ((), ()))
 TN = (((0,), (0,)), ((), ()))
@@ -21,10 +21,6 @@
 
 def swap_core(value):
     return swap(value, "c")
-
-
-def shift_x(value, steps):
-    return lax.ppermute(value, "x", [(x, (x + steps) % NX) for x in range(NX)])
 
 
 def moved(block, core):
@@ -76,7 +72,14 @@
     up_pre = product(1)
     sigmoid = 1.0 / (1.0 + jnp.exp(-gate_pre))
     activated = gate_pre * sigmoid
-    hidden_ref[...] = (activated * up_pre).astype(BF)
+    hidden = activated * up_pre
+    hidden_ref[...] = hidden[:, :tokens].astype(BF)
+    width = own_ref.shape[0]
+    extra = other_ref.shape[0] - width
+    riding = jnp.concatenate(
+        [hidden[:, tokens:], jnp.zeros((extra - hidden.shape[0], tokens), F32)], axis=0
+    )
+    other_ref[width : width + extra, :] = riding.astype(BF)
     upstream = upstream_ref[...].astype(F32)
     back_up = (upstream * activated).astype(BF)
     back_gate = (upstream * up_pre * sigmoid * (1.0 + gate_pre * (1.0 - sigmoid))).astype(BF)
@@ -90,17 +93,16 @@
         other_ref[rows, :] = part[:, tokens:].astype(BF)
 
 
-def gradient_kernel(spot_ref, normed_ref, back_ref, *outs):
-    size = outs[0].shape[2]
+def gradient_kernel(normed_ref, back_ref, out_ref):
+    size = out_ref.shape[3]
     for index in range(NX):
-        block = (spot_ref[0] + index) % NX
-        rows = normed_ref[pl.ds(pl.multiple_of(block * size, size), size), :]
+        rows = normed_ref[pl.ds(index * size, size), :]
         for which in range(2):
             term = lax.dot_general(back_ref[which], rows, NT, preferred_element_type=F32)
-            outs[index][which] = term.astype(outs[index].dtype)
-
-
-def blocks_kernel(own_ref, other_ref, x_ref, root_ref, gain_ref, out_ref):
+            out_ref[index, which] = term.astype(BF)
+
+
+def blocks_kernel(_, own_ref, other_ref, x_ref, root_ref, gain_ref, out_ref):
     width, tokens = own_ref.shape
     size = width // (NX * NZ)
     root = root_ref[...]
@@ -141,7 +143,6 @@
 
 
 def per_device(inputs, gain, w_gate, w_up, upstream):
-    spot = lax.axis_index("x").astype(jnp.int32).reshape(1)
     first = lax.axis_index("c") == 0
     tokens, width = inputs.shape
     rows, columns = w_gate.shape
@@ -176,32 +177,26 @@
         [VMEM] * 2,
     )(inputs_t, gain_wide)
 
-    hidden_pair, back, part_own, part_other = call(
+    riding = -(-half // 16) * 16
+    hidden_own, back, part_own, part_other = call(
         forward_kernel,
         (
-            shape((half, 2 * tokens), BF),
+            shape((half, tokens), BF),
             shape((2, half, 2 * tokens), BF),
             shape((width, tokens), F32),
-            shape((width, tokens), BF),
+            shape((width + riding, tokens), BF),
         ),
         [VMEM] * 3,
     )(normed, upstream_pair, weight)
     part_other = swap_core(part_other)
-    terms = call(
-        gradient_kernel,
-        tuple(shape((2, half, column_rows), F32 if index == 0 else BF) for index in range(NX)),
-        [SMEM] + [VMEM] * 2,
-    )(spot, normed, back)
-    travelling = [shift_x(terms[steps], steps) for steps in (2, 1, 3)]
-    hidden_other = swap_core(hidden_pair[:, tokens:])
-    hidden = ordered(hidden_pair[:, :tokens], hidden_other, 0).T
+    hidden = ordered(hidden_own, part_other[width : width + half], 0).T
+    terms = call(gradient_kernel, shape((NX, 2, half, column_rows), BF), [VMEM] * 2)(normed, back)
 
     spare = 16
-    sending = call(blocks_kernel, shape((n_dp, features + spare, tokens), BF), [VMEM] * 5)(
-        part_own, part_other, inputs_t[:, :tokens], root_mean[:, :tokens], gain_wide
+    sending = call(blocks_kernel, shape((n_dp, features + spare, tokens), BF), [ANY] + [VMEM] * 5)(
+        terms, part_own, part_other, inputs_t[:, :tokens], root_mean[:, :tokens], gain_wide
     )
     got = lax.all_to_all(sending, ("y", "h"), 0, 0, tiled=True)
-    got, travelling = lax.optimization_barrier((got, travelling))
     totals = jnp.sum(got.astype(F32), axis=0)
     own_sums = totals[:features]
     token_totals = totals[features] + totals[features + 1] + totals[features + 2]
@@ -220,9 +215,8 @@
     grad_gain = lax.psum(lax.psum(gain_part, "x"), "z")
     grad_gain = grad_gain + swap_core(grad_gain)
 
-    column_sum = terms[0]
-    for value in travelling:
-        column_sum = column_sum + value.astype(F32)
+    arrived = lax.all_to_all(terms, "x", 0, 0, tiled=True)
+    column_sum = jnp.sum(arrived.astype(F32), axis=0)
     column_sum = column_sum.reshape(columns, column_rows).T.astype(BF)
     blocks = lax.all_to_all(
         column_sum.reshape(NC * NZ, rows, columns), ("c", "z"), 0, 0, tiled=True

time: 150 us -> 169 us (1.13)
  waiting for transfers between devices: 40.9 us -> 62.1 us
  starting transfers between devices: 48.5 us -> 43.6 us
  Pallas kernels: 4.89 us -> 7.02 us
    all_to_all x1, waiting for transfers between devices: 0.01 us -> 22.4 us  [per_device(): got = lax.all_to_all(sending, ('y', 'h'), 0, 0, tiled=True)]
    ppermute x3 -> x0, waiting for transfers between devices: 21.2 us -> none  [shift_x(): return lax.ppermute(value, 'x', [(x, (x + steps) % NX) for x in range(NX)])]
    all_to_all x0 -> x1, waiting for transfers between devices: none -> 19.8 us  [per_device(): arrived = lax.all_to_all(terms, 'x', 0, 0, tiled=True)]
    ppermute x3 -> x0, starting transfers between devices: 8.5 us -> none  [shift_x(): return lax.ppermute(value, 'x', [(x, (x + steps) % NX) for x in range(NX)])]
    all_to_all x0 -> x1, starting transfers between devices: none -> 4.61 us  [per_device(): arrived = lax.all_to_all(terms, 'x', 0, 0, tiled=True)]
    reduce_sum x0 -> x1, other arithmetic: none -> 2.15 us  [per_device(): column_sum = jnp.sum(arrived.astype(F32), axis=0)]
    pallas_call x3, Pallas kernels: 4.35 us -> 6.48 us  [the longest x1 2.89 us: per_device(): call(forward_kernel, (shape((half, tokens), BF), shape((2, half, 2 * toke...]
    ppermute x5 -> x4, starting transfers between devices: 14.8 us -> 13.2 us  [swap(): return lax.ppermute(value, axis, [(0, 1), (1, 0)])]
  transfers between devices with their start and end apart: 11 -> 8, of which waited for: 6 -> 6; matrix products, arithmetic and copies ran while one was open for 4% -> 5% of each run, Pallas kernels for 1% -> 1%
where the time goes in v7:
time: 169 us; the launch traced here: 168 us
  waiting for transfers between devices  62.1 us (37%)
  starting transfers between devices  43.6 us (26%)
  blocking collectives  35.2 us (21%)
  local copies, waits for them, and re-layouts  11.2 us (7%)
  other arithmetic  8.09 us (5%)
  Pallas kernels  7.02 us (4%)
    all_to_all x1, waiting for transfers between devices, per_device(): got = lax.all_to_all(sending, ('y', 'h'), 0, 0, tiled=True)  22.4 us
    all_to_all x1, waiting for transfers between devices, per_device(): arrived = lax.all_to_all(terms, 'x', 0, 0, tiled=True)  19.8 us
    all_gather x1, blocking collectives, per_device(): lax.all_gather(jnp.concatenate([w_gate, w_up], 1), 'z', axis=0, tiled=True)  18.1 us
    all_to_all x1, waiting for transfers between devices, per_device(): weight = lax.all_to_all(copies, ('x', 'c'), 0, 0, tiled=True)  17.1 us
    psum x2, blocking collectives, per_device(): grad_gain = lax.psum(lax.psum(gain_part, 'x'), 'z')  17 us
    ppermute x4, starting transfers between devices, swap(): return lax.ppermute(value, axis, [(0, 1), (1, 0)])  13.2 us
    all_to_all x1, starting transfers between devices, per_device(): got = lax.all_to_all(sending, ('y', 'h'), 0, 0, tiled=True)  10.8 us
    all_to_all x1, starting transfers between devices, per_device(): weight = lax.all_to_all(copies, ('x', 'c'), 0, 0, tiled=True)  8.54 us
  transfers between devices with their start and end apart: 8, of which 6 were waited for; matrix products, arithmetic and copies ran while one was open for 5% of the time, Pallas kernels for 1%

profile of v7, /device:TPU:1, one launch (start us, length us, event | category | flops | bytes accessed | tf_op | source)
XLA Modules:
  0.0 168.0 jit_solution(970376161549985061)
XLA Ops:
  0.6 1.0 pad_maximum_fusion.3
  1.7 18.1 %all_gather.3 = bf16[320,864]{1,0:T(8,128)(2,1)S(1)} all-gather(bf16[80,864]{1,0:T(8,128)(2,1)S(1)} %pad_maximum_fusion.3), channel_id=1, replica_groups=mesh['x'=4,'z'=4,'c'=2,'y'=8,'h'=2] {'z'}, dimensions={0}, use_global_device_ids=true | all-gather | bytes 691200 | tf_op jit(solution)/shard_map/all_gather | solution.py:163
  19.8 0.4 copy.24
  20.2 0.2 pad_maximum_fusion
  20.4 1.5 broadcast_in_dim.5
  22.0 8.5 %all-to-all-start = ((bf16[8,216,640]{2,1,0:T(8,128)(2,1)}), bf16[8,216,640]{2,1,0:T(8,128)(2,1)S(1)}, u32[]{:S(2)}, u32[]{:S(2)}) async-start(bf16[8,216,640]{2,1,0:T(8,128)(2,1)} %bitcast.29), calls=%async_computation | async-start | bytes 4423680 | tf_op jit(solution)/shard_map/all_to_all | solution.py:168
  30.5 0.3 copy.23
  30.8 2.0 %collective-permute-start = (bf16[128,2560]{0,1:T(8,128)(2,1)S(1)}, bf16[128,2560]{0,1:T(8,128)(2,1)S(1)}, u32[]{:S(2)}, u32[]{:S(2)}) collective-permute-start(bf16[128,2560]{0,1:T(8,128)(2,1)S(1)} %copy.23), channel_id=1, source_target_pairs={{0,16},{16,0},{1,17},{17,1},{2,18},{18,2},{3,19},{19,3},{4,20},{20... | collective-permute-start | bytes 1966088 | tf_op jit(solution)/shard_map/ppermute | solution.py:19
  32.9 0.9 broadcast_select_fusion.1
  33.7 2.3 %collective-permute-start.1 = (bf16[216,128]{1,0:T(8,128)(2,1)S(1)}, bf16[216,128]{1,0:T(8,128)(2,1)S(1)}, u32[]{:S(2)}, u32[]{:S(2)}) collective-permute-start(bf16[216,128]{1,0:T(8,128)(2,1)S(1)} %get-tuple-element.26), channel_id=1, source_target_pairs={{0,16},{16,0},{1,17},{17,1},{2,18},{18,2},{3,19},{19,3},{4,20},{20... | collective-permute-start | bytes 165896 | tf_op jit(solution)/shard_map/ppermute | solution.py:19
  36.0 0.9 collective-permute-done.1
  36.9 0.7 pad_maximum_fusion.4.upstream_ref
  37.6 0.1 maximum_bitcast_fusion.x_ref
  37.7 0.6 copy-done.11
  38.3 0.4 broadcast_in_dim.4.gain_ref
  38.7 0.7 copy-done
  39.4 0.5 shard_map.92
  40.0 1.1 copy-done.2
  41.0 17.1 %all-to-all-done.weight_ref = bf16[8,216,640]{2,1,0:T(8,128)(2,1)S(1)} async-done(((bf16[8,216,640]{2,1,0:T(8,128)(2,1)}), bf16[8,216,640]{2,1,0:T(8,128)(2,1)S(1)}, u32[]{:S(2)}, u32[]{:S(2)}) %all-to-all-start) | async-done | bytes 2211872 | tf_op jit(solution)/shard_map/all_to_all | solution.py:168
  58.1 1.3 copy-done.3
  59.4 0.9 copy-done.7
  60.3 2.9 %shard_map.93 = (bf16[216,128]{1,0:T(8,128)(2,1)S(1)}, bf16[2,216,256]{2,1,0:T(8,128)(2,1)S(1)}, f32[2560,128]{1,0:T(8,128)S(1)}, bf16[2784,128]{1,0:T(8,128)(2,1)}) custom-call(bf16[2560,256]{1,0:T(8,128)(2,1)S(1)} %copy-done.3, bf16[216,256]{1,0:T(8,128)(2,1)S(1)} %copy-done.7, bf16[8,216,640]{2,1,0:T(8,128)(2,1)S(1)} %all-to-all-done.weight_ref), custom_call_target="tpu_custom_call" | custom-call | tf_op jit(solution)/shard_map/pallas_call | solution.py:181
  63.2 1.1 copy-done.4
  64.3 0.6 copy-done.8
  64.9 2.3 %shard_map.94._ = bf16[4,2,216,640]{3,2,1,0:T(8,128)(2,1)} custom-call(bf16[2560,256]{1,0:T(8,128)(2,1)S(1)} %copy-done.3, bf16[2,216,256]{2,1,0:T(8,128)(2,1)S(1)} %get-tuple-element.14.back_ref), custom_call_target="tpu_custom_call" | custom-call | tf_op jit(solution)/shard_map/pallas_call | solution.py:193
  67.3 4.6 %all-to-all-start.1 = ((bf16[4,2,216,640]{3,2,1,0:T(8,128)(2,1)}), bf16[4,2,216,640]{3,2,1,0:T(8,128)(2,1)}, u32[]{:S(2)}, u32[]{:S(2)}) async-start(bf16[4,2,216,640]{3,2,1,0:T(8,128)(2,1)} %shard_map.94._), calls=%async_computation.1 | async-start | bytes 4423680 | tf_op jit(solution)/shard_map/all_to_all | solution.py:218
  71.9 2.9 %collective-permute-start.2 = (bf16[2784,128]{1,0:T(8,128)(2,1)}, bf16[2784,128]{1,0:T(8,128)(2,1)S(1)}, u32[]{:S(2)}, u32[]{:S(2)}) collective-permute-start(bf16[2784,128]{1,0:T(8,128)(2,1)} %get-tuple-element.13), channel_id=1, source_target_pairs={{0,16},{16,0},{1,17},{17,1},{2,18},{18,2},{3,19},{19,3},{4,20},{20... | collective-permute-start | bytes 2138120 | tf_op jit(solution)/shard_map/ppermute | solution.py:19
  74.9 1.9 %collective-permute-done.2.other_ref = bf16[2784,128]{1,0:T(8,128)(2,1)S(1)} collective-permute-done((bf16[2784,128]{1,0:T(8,128)(2,1)}, bf16[2784,128]{1,0:T(8,128)(2,1)S(1)}, u32[]{:S(2)}, u32[]{:S(2)}) %collective-permute-start.2) | collective-permute-done | bytes 712736 | tf_op jit(solution)/shard_map/ppermute | solution.py:19
  76.8 0.9 copy-done.6
  77.7 1.2 shard_map.95
  78.9 19.8 %all-to-all-done.1 = bf16[4,2,216,640]{3,2,1,0:T(8,128)(2,1)} async-done(((bf16[4,2,216,640]{3,2,1,0:T(8,128)(2,1)}), bf16[4,2,216,640]{3,2,1,0:T(8,128)(2,1)}, u32[]{:S(2)}, u32[]{:S(2)}) %all-to-all-start.1) | async-done | bytes 2211872 | tf_op jit(solution)/shard_map/all_to_all | solution.py:218
  98.7 10.8 %all-to-all-start.3 = ((bf16[16,176,128]{2,1,0:T(8,128)(2,1)}), bf16[16,176,128]{2,1,0:T(8,128)(2,1)S(1)}, u32[]{:S(2)}, u32[]{:S(2)}) async-start(bf16[16,176,128]{2,1,0:T(8,128)(2,1)} %shard_map.95), calls=%async_computation.3 | async-start | bytes 1441792 | tf_op jit(solution)/shard_map/all_to_all | solution.py:199
  109.5 2.1 %reduce_sum.39 = bf16[2,216,640]{2,1,0:T(8,128)(2,1)S(1)} reduce(bf16[4,2,216,640]{3,2,1,0:T(8,128)(2,1)} %all-to-all-done.1, bf16[]{:T(256)} %constant.20.clone.1), dimensions={0}, to_apply=%region_0.1 | reduce | flops 829440 | bytes 2764802 | tf_op jit(solution)/shard_map/reduce_sum | solution.py:219
  111.6 1.1 copy.25
  112.7 22.4 %all-to-all-done.3 = bf16[16,176,128]{2,1,0:T(8,128)(2,1)S(1)} async-done(((bf16[16,176,128]{2,1,0:T(8,128)(2,1)}), bf16[16,176,128]{2,1,0:T(8,128)(2,1)S(1)}, u32[]{:S(2)}, u32[]{:S(2)}) %all-to-all-start.3) | async-done | bytes 720928 | tf_op jit(solution)/shard_map/all_to_all | solution.py:199
  135.2 6.5 %all-to-all-start.2 = ((bf16[8,80,432]{2,1,0:T(8,128)(2,1)}), bf16[8,80,432]{2,1,0:T(8,128)(2,1)S(1)}, u32[]{:S(2)}, u32[]{:S(2)}) async-start(bf16[8,80,432]{2,1,0:T(8,128)(2,1)} %bitcast.8), calls=%async_computation.2 | async-start | bytes 1310720 | tf_op jit(solution)/shard_map/all_to_all | solution.py:221
  141.7 0.1 dynamic_slice.6
  141.7 0.1 convert_reduce_fusion
  141.8 0.8 multiply_reduce_fusion
  142.6 7.0 %psum.14 = f32[160]{0:T(256)S(1)} all-reduce(f32[160]{0:T(256)S(1)} %get-tuple-element.17), channel_id=1, replica_groups=mesh['x'=4,'z'=4,'c'=2,'y'=8,'h'=2] {'x'}, use_global_device_ids=true, to_apply=%region_4.5 | all-reduce | flops 160 | bytes 1280 | tf_op jit(solution)/shard_map/psum | solution.py:215
  149.6 10.0 %psum.15 = f32[160]{0:T(256)S(1)} all-reduce(f32[160]{0:T(256)S(1)} %psum.14), channel_id=1, replica_groups=mesh['x'=4,'z'=4,'c'=2,'y'=8,'h'=2] {'z'}, use_global_device_ids=true, to_apply=%region_5.6 | all-reduce | flops 160 | bytes 1280 | tf_op jit(solution)/shard_map/psum | solution.py:215
  159.6 5.9 %collective-permute-start.3 = (f32[160]{0:T(256)S(1)}, f32[160]{0:T(256)S(1)}, u32[]{:S(2)}, u32[]{:S(2)}) collective-permute-start(f32[160]{0:T(256)S(1)} %psum.15), channel_id=1, source_target_pairs={{0,16},{16,0},{1,17},{17,1},{2,18},{18,2},{3,19},{19,3},{4,20},{20... | collective-permute-start | bytes 1928 | tf_op jit(solution)/shard_map/ppermute | solution.py:19
  165.6 0.7 fusion
  166.3 0.1 collective-permute-done.3
  166.4 0.6 add.26
  166.9 0.1 convert_reduce_fusion.1
  167.0 0.1 slice_bitcast_fusion.1
  167.1 0.9 pad_maximum_fusion.1
  (24 shorter events, 0.2 us)
Async XLA Ops:
  22.0 8.5 %copy-start.10 = (bf16[128,2560]{1,0:T(8,128)(2,1)S(1)}, bf16[128,2560]{1,0:T(8,128)(2,1)}, u32[]{:S(2)}) copy-start(bf16[128,2560]{1,0:T(8,128)(2,1)} %param.5) | copy-start | bytes 1966084
  22.0 36.1 %all-to-all-start = ((bf16[8,216,640]{2,1,0:T(8,128)(2,1)}), bf16[8,216,640]{2,1,0:T(8,128)(2,1)S(1)}, u32[]{:S(2)}, u32[]{:S(2)}) async-start(bf16[8,216,640]{2,1,0:T(8,128)(2,1)} %bitcast.29), calls=%async_computation | async-start | bytes 4423680 | tf_op jit(solution)/shard_map/all_to_all | solution.py:168
  30.8 6.8 %collective-permute-start = (bf16[128,2560]{0,1:T(8,128)(2,1)S(1)}, bf16[128,2560]{0,1:T(8,128)(2,1)S(1)}, u32[]{:S(2)}, u32[]{:S(2)}) collective-permute-start(bf16[128,2560]{0,1:T(8,128)(2,1)S(1)} %copy.23), channel_id=1, source_target_pairs={{0,16},{16,0},{1,17},{17,1},{2,18},{18,2},{3,19},{19,3},{4,20},{20... | collective-permute-start | bytes 1966088 | tf_op jit(solution)/shard_map/ppermute | solution.py:19
  33.7 3.2 %collective-permute-start.1 = (bf16[216,128]{1,0:T(8,128)(2,1)S(1)}, bf16[216,128]{1,0:T(8,128)(2,1)S(1)}, u32[]{:S(2)}, u32[]{:S(2)}) collective-permute-start(bf16[216,128]{1,0:T(8,128)(2,1)S(1)} %get-tuple-element.26), channel_id=1, source_target_pairs={{0,16},{16,0},{1,17},{17,1},{2,18},{18,2},{3,19},{19,3},{4,20},{20... | collective-permute-start | bytes 165896 | tf_op jit(solution)/shard_map/ppermute | solution.py:19
  37.6 0.7 copy-start.11
  38.3 1.1 copy-start
  39.9 1.1 copy-start.2
  58.1 1.3 copy-start.3
  59.4 0.9 copy-start.7
  63.2 1.1 copy-start.4
  64.3 0.6 copy-start.8
  67.3 7.5 %copy-start.1 = (bf16[2560,256]{1,0:T(8,128)(2,1)S(1)}, bf16[2560,256]{1,0:T(8,128)(2,1)}, u32[]{:S(2)}) copy-start(bf16[2560,256]{1,0:T(8,128)(2,1)} %copy-done) | copy-start | bytes 3932164
  67.3 31.4 %all-to-all-start.1 = ((bf16[4,2,216,640]{3,2,1,0:T(8,128)(2,1)}), bf16[4,2,216,640]{3,2,1,0:T(8,128)(2,1)}, u32[]{:S(2)}, u32[]{:S(2)}) async-start(bf16[4,2,216,640]{3,2,1,0:T(8,128)(2,1)} %shard_map.94._), calls=%async_computation.1 | async-start | bytes 4423680 | tf_op jit(solution)/shard_map/all_to_all | solution.py:218
  71.9 5.8 %copy-start.5 = (f32[2560,128]{1,0:T(8,128)S(1)}, f32[2560,128]{1,0:T(8,128)}, u32[]{:S(2)}) copy-start(f32[2560,128]{1,0:T(8,128)} %copy-done.4) | copy-start | bytes 3932164
  71.9 4.9 %collective-permute-start.2 = (bf16[2784,128]{1,0:T(8,128)(2,1)}, bf16[2784,128]{1,0:T(8,128)(2,1)S(1)}, u32[]{:S(2)}, u32[]{:S(2)}) collective-permute-start(bf16[2784,128]{1,0:T(8,128)(2,1)} %get-tuple-element.13), channel_id=1, source_target_pairs={{0,16},{16,0},{1,17},{17,1},{2,18},{18,2},{3,19},{19,3},{4,20},{20... | collective-permute-start | bytes 2138120 | tf_op jit(solution)/shard_map/ppermute | solution.py:19
  76.8 0.9 copy-start.6
  98.7 36.5 %all-to-all-start.3 = ((bf16[16,176,128]{2,1,0:T(8,128)(2,1)}), bf16[16,176,128]{2,1,0:T(8,128)(2,1)S(1)}, u32[]{:S(2)}, u32[]{:S(2)}) async-start(bf16[16,176,128]{2,1,0:T(8,128)(2,1)} %shard_map.95), calls=%async_computation.3 | async-start | bytes 1441792 | tf_op jit(solution)/shard_map/all_to_all | solution.py:199
  112.7 52.8 %slice-start = ((bf16[2784,128]{1,0:T(8,128)(2,1)}), bf16[216,128]{1,0:T(8,128)(2,1)S(1)}, s32[]{:S(2)}) async-start(bf16[2784,128]{1,0:T(8,128)(2,1)} %copy-done.6), calls=%async_computation.4 | async-start | bytes 110592 | tf_op jit(solution)/shard_map/slice | solution.py:192
  112.7 52.8 %copy-start.9 = (bf16[216,128]{1,0:T(8,128)(2,1)S(1)}, bf16[216,128]{1,0:T(8,128)(2,1)}, u32[]{:S(2)}) copy-start(bf16[216,128]{1,0:T(8,128)(2,1)} %copy-done.8) | copy-start | bytes 165892
  135.2 31.8 %all-to-all-start.2 = ((bf16[8,80,432]{2,1,0:T(8,128)(2,1)}), bf16[8,80,432]{2,1,0:T(8,128)(2,1)S(1)}, u32[]{:S(2)}, u32[]{:S(2)}) async-start(bf16[8,80,432]{2,1,0:T(8,128)(2,1)} %bitcast.8), calls=%async_computation.2 | async-start | bytes 1310720 | tf_op jit(solution)/shard_map/all_to_all | solution.py:221
  159.6 6.7 %collective-permute-start.3 = (f32[160]{0:T(256)S(1)}, f32[160]{0:T(256)S(1)}, u32[]{:S(2)}, u32[]{:S(2)}) collective-permute-start(f32[160]{0:T(256)S(1)} %psum.15), channel_id=1, source_target_pairs={{0,16},{16,0},{1,17},{17,1},{2,18},{18,2},{3,19},{19,3},{4,20},{20... | collective-permute-start | bytes 1928 | tf_op jit(solution)/shard_map/ppermute | solution.py:19

commit v8 on v5

--- a/solution.py
+++ b/solution.py
@@ -8,6 +8,7 @@
 BF = jnp.bfloat16
 F32 = jnp.float32
 NX, NZ, NC, NH = 4, 4, 2, 2
+ANY = pl.BlockSpec(memory_space=pl.ANY)
 VMEM = pl.BlockSpec(memory_space=pltpu.VMEM)
 SMEM = pl.BlockSpec(memory_space=pltpu.SMEM)
 PARAMS = pltpu.CompilerParams(vmem_limit_bytes=48 * 1024 * 1024)
@@ -53,30 +54,36 @@
 
 
 def forward_kernel(
-    normed_ref, upstream_ref, weight_ref, hidden_ref, back_ref, own_ref, other_ref
+    normed_ref, upstream_ref, weight_ref, hidden_ref, back_ref, own_ref, other_ref, held, sems
 ):
     size = weight_ref.shape[2] // 2
     tokens = own_ref.shape[1]
+    width = own_ref.shape[0]
+    copies = [
+        pltpu.make_async_copy(weight_ref.at[index], held.at[index], sems.at[index])
+        for index in range(NX * NC)
+    ]
+    for copy in copies:
+        copy.start()
 
     def piece(index, which):
-        return weight_ref[index, :, which * size : (which + 1) * size]
-
-    def product(which):
-        total = None
-        for index in range(NX * NC):
-            term = jnp.dot(
-                piece(index, which),
-                normed_ref[pl.ds(index * size, size), :],
-                preferred_element_type=F32,
-            )
-            total = term if total is None else total + term
-        return total
-
-    gate_pre = product(0)
-    up_pre = product(1)
+        return held[index, :, which * size : (which + 1) * size]
+
+    gate_pre, up_pre = 0.0, 0.0
+    for index in range(NX * NC):
+        copies[index].wait()
+        rows = normed_ref[pl.ds(index * size, size), :]
+        gate_pre += jnp.dot(piece(index, 0), rows, preferred_element_type=F32)
+        up_pre += jnp.dot(piece(index, 1), rows, preferred_element_type=F32)
     sigmoid = 1.0 / (1.0 + jnp.exp(-gate_pre))
     activated = gate_pre * sigmoid
-    hidden_ref[...] = (activated * up_pre).astype(BF)
+    hidden = activated * up_pre
+    hidden_ref[...] = hidden[:, :tokens].astype(BF)
+    extra = other_ref.shape[0] - width
+    riding = jnp.concatenate(
+        [hidden[:, tokens:], jnp.zeros((extra - hidden.shape[0], tokens), F32)], axis=0
+    )
+    other_ref[width : width + extra, :] = riding.astype(BF)
     upstream = upstream_ref[...].astype(F32)
     back_up = (upstream * activated).astype(BF)
     back_gate = (upstream * up_pre * sigmoid * (1.0 + gate_pre * (1.0 - sigmoid))).astype(BF)
@@ -126,11 +133,20 @@
         out_ref[index, size : size + spare, :] = rows.astype(BF)
 
 
-def call(kernel, outs, specs):
+def column_kernel(own_ref, first_ref, second_ref, third_ref, out_ref):
+    half = own_ref.shape[1]
+    for which in range(2):
+        total = own_ref[which] + first_ref[which].astype(F32)
+        total += second_ref[which].astype(F32) + third_ref[which].astype(F32)
+        out_ref[:, which * half : (which + 1) * half] = total.T.astype(BF)
+
+
+def call(kernel, outs, specs, scratch=()):
     return pl.pallas_call(
         kernel,
         out_shape=outs,
         in_specs=specs,
+        scratch_shapes=scratch,
         out_specs=jax.tree.map(lambda _: VMEM, outs),
         compiler_params=PARAMS,
     )
@@ -176,32 +192,32 @@
         [VMEM] * 2,
     )(inputs_t, gain_wide)
 
-    hidden_pair, back, part_own, part_other = call(
+    riding = -(-half // 16) * 16
+    hidden_own, back, part_own, part_other = call(
         forward_kernel,
         (
-            shape((half, 2 * tokens), BF),
+            shape((half, tokens), BF),
             shape((2, half, 2 * tokens), BF),
             shape((width, tokens), F32),
-            shape((width, tokens), BF),
+            shape((width + riding, tokens), BF),
         ),
-        [VMEM] * 3,
+        [VMEM, VMEM, ANY],
+        [pltpu.VMEM(weight.shape, BF), pltpu.SemaphoreType.DMA((NX * NC,))],
     )(normed, upstream_pair, weight)
     part_other = swap_core(part_other)
+    hidden = ordered(hidden_own, part_other[width : width + half], 0).T
     terms = call(
         gradient_kernel,
         tuple(shape((2, half, column_rows), F32 if index == 0 else BF) for index in range(NX)),
         [SMEM] + [VMEM] * 2,
     )(spot, normed, back)
     travelling = [shift_x(terms[steps], steps) for steps in (2, 1, 3)]
-    hidden_other = swap_core(hidden_pair[:, tokens:])
-    hidden = ordered(hidden_pair[:, :tokens], hidden_other, 0).T
 
     spare = 16
     sending = call(blocks_kernel, shape((n_dp, features + spare, tokens), BF), [VMEM] * 5)(
         part_own, part_other, inputs_t[:, :tokens], root_mean[:, :tokens], gain_wide
     )
     got = lax.all_to_all(sending, ("y", "h"), 0, 0, tiled=True)
-    got, travelling = lax.optimization_barrier((got, travelling))
     totals = jnp.sum(got.astype(F32), axis=0)
     own_sums = totals[:features]
     token_totals = totals[features] + totals[features + 1] + totals[features + 2]
@@ -217,13 +233,12 @@
         .T
     )
     gain_part = jnp.sum(own_sums * unit_slice, axis=1)
-    grad_gain = lax.psum(lax.psum(gain_part, "x"), "z")
-    grad_gain = grad_gain + swap_core(grad_gain)
-
-    column_sum = terms[0]
-    for value in travelling:
-        column_sum = column_sum + value.astype(F32)
-    column_sum = column_sum.reshape(columns, column_rows).T.astype(BF)
+    gain_part, travelling = lax.optimization_barrier((gain_part, travelling))
+    grad_gain = lax.psum(lax.psum(gain_part, "x"), ("z", "c"))
+
+    column_sum = call(column_kernel, shape((column_rows, columns), BF), [VMEM] * 4)(
+        terms[0], *travelling
+    )
     blocks = lax.all_to_all(
         column_sum.reshape(NC * NZ, rows, columns), ("c", "z"), 0, 0, tiled=True
     )

time: 150 us -> 148 us (0.987)
  starting transfers between devices: 48.5 us -> 40.9 us
  blocking collectives: 35.5 us -> 41.1 us
  Pallas kernels: 4.89 us -> 9.32 us
  other arithmetic: 8.41 us -> 6.5 us
  waiting for transfers between devices: 40.9 us -> 39.1 us
    ppermute x3, waiting for transfers between devices: 21.2 us -> 4.03 us  [shift_x(): return lax.ppermute(value, 'x', [(x, (x + steps) % NX) for x in range(NX)])]
    all_to_all x1, waiting for transfers between devices: 0.01 us -> 15.4 us  [per_device(): got = lax.all_to_all(sending, ('y', 'h'), 0, 0, tiled=True)]
    ppermute x5 -> x3, starting transfers between devices: 14.8 us -> 7.11 us  [swap(): return lax.ppermute(value, axis, [(0, 1), (1, 0)])]
    psum x2, blocking collectives: 17.4 us -> 23 us  [per_device(): grad_gain = lax.psum(lax.psum(gain_part, 'x'), ('z', 'c'))]
    pallas_call x1 -> x2, Pallas kernels: 2.07 us -> 5.7 us  [the longest x1 3.29 us: per_device(): call(forward_kernel, (shape((half, tokens), BF), shape((2, half, 2 * toke...]
    unnamed x25 -> x27, local copies, waits for them, and re-layouts: 5.8 us -> 6.67 us
  transfers between devices with their start and end apart: 11 -> 9, of which waited for: 6 -> 5; matrix products, arithmetic and copies ran while one was open for 4% -> 4% of each run, Pallas kernels for 1% -> 2%
where the time goes in v8:
time: 148 us; the launch traced here: 147 us
  blocking collectives  41.1 us (28%)
  starting transfers between devices  40.9 us (28%)
  waiting for transfers between devices  39.1 us (26%)
  Pallas kernels  9.32 us (6%)
  local copies, waits for them, and re-layouts  9.26 us (6%)
  other arithmetic  6.5 us (4%)
    psum x2, blocking collectives, per_device(): grad_gain = lax.psum(lax.psum(gain_part, 'x'), ('z', 'c'))  23 us
    all_gather x1, blocking collectives, per_device(): lax.all_gather(jnp.concatenate([w_gate, w_up], 1), 'z', axis=0, tiled=True)  18.1 us
    all_to_all x1, waiting for transfers between devices, per_device(): weight = lax.all_to_all(copies, ('x', 'c'), 0, 0, tiled=True)  17.1 us
    all_to_all x1, waiting for transfers between devices, per_device(): got = lax.all_to_all(sending, ('y', 'h'), 0, 0, tiled=True)  15.4 us
    all_to_all x1, starting transfers between devices, per_device(): got = lax.all_to_all(sending, ('y', 'h'), 0, 0, tiled=True)  10.9 us
    all_to_all x1, starting transfers between devices, per_device(): weight = lax.all_to_all(copies, ('x', 'c'), 0, 0, tiled=True)  8.54 us
    ppermute x3, starting transfers between devices, shift_x(): return lax.ppermute(value, 'x', [(x, (x + steps) % NX) for x in range(NX)])  8.48 us
    ppermute x3, starting transfers between devices, swap(): return lax.ppermute(value, axis, [(0, 1), (1, 0)])  7.11 us
  transfers between devices with their start and end apart: 9, of which 5 were waited for; matrix products, arithmetic and copies ran while one was open for 4% of the time, Pallas kernels for 2%

profile of v8, /device:TPU:1, one launch (start us, length us, event | category | flops | bytes accessed | tf_op | source)
XLA Modules:
  0.0 147.0 jit_solution(16927977668400736000)
XLA Ops:
  0.6 1.0 pad_maximum_fusion.3
  1.7 18.1 %all_gather.3 = bf16[320,864]{1,0:T(8,128)(2,1)S(1)} all-gather(bf16[80,864]{1,0:T(8,128)(2,1)S(1)} %pad_maximum_fusion.3), channel_id=1, replica_groups=mesh['x'=4,'z'=4,'c'=2,'y'=8,'h'=2] {'z'}, dimensions={0}, use_global_device_ids=true | all-gather | bytes 691200 | tf_op jit(solution)/shard_map/all_gather | solution.py:178
  19.8 0.4 copy.19
  20.2 0.1 fusion.4
  20.2 0.2 pad_maximum_fusion
  20.4 1.6 %broadcast_in_dim.5 = bf16[4,2,216,640]{3,2,1,0:T(8,128)(2,1)} broadcast(bf16[2,216,640]{2,1,0:T(8,128)(2,1)S(1)} %bitcast.29), dimensions={1,2,3} | broadcast | bytes 2764800 | tf_op jit(solution)/shard_map/broadcast_in_dim | solution.py:180
  22.0 8.5 %all-to-all-start = ((bf16[8,216,640]{2,1,0:T(8,128)(2,1)}), bf16[8,216,640]{2,1,0:T(8,128)(2,1)S(1)}, u32[]{:S(2)}, u32[]{:S(2)}) async-start(bf16[8,216,640]{2,1,0:T(8,128)(2,1)} %bitcast.27), calls=%async_computation | async-start | bytes 4423680 | tf_op jit(solution)/shard_map/all_to_all | solution.py:183
  30.5 0.3 copy.18
  30.8 2.0 %collective-permute-start = (bf16[128,2560]{0,1:T(8,128)(2,1)S(1)}, bf16[128,2560]{0,1:T(8,128)(2,1)S(1)}, u32[]{:S(2)}, u32[]{:S(2)}) collective-permute-start(bf16[128,2560]{0,1:T(8,128)(2,1)S(1)} %copy.18), channel_id=1, source_target_pairs={{0,16},{16,0},{1,17},{17,1},{2,18},{18,2},{3,19},{19,3},{4,20},{20... | collective-permute-start | bytes 1966088 | tf_op jit(solution)/shard_map/ppermute | solution.py:20
  32.9 0.9 broadcast_select_fusion.1
  33.8 2.3 %collective-permute-start.1 = (bf16[216,128]{1,0:T(8,128)(2,1)S(1)}, bf16[216,128]{1,0:T(8,128)(2,1)S(1)}, u32[]{:S(2)}, u32[]{:S(2)}) collective-permute-start(bf16[216,128]{1,0:T(8,128)(2,1)S(1)} %get-tuple-element.42), channel_id=1, source_target_pairs={{0,16},{16,0},{1,17},{17,1},{2,18},{18,2},{3,19},{19,3},{4,20},{20... | collective-permute-start | bytes 165896 | tf_op jit(solution)/shard_map/ppermute | solution.py:20
  36.1 0.9 collective-permute-done.1
  36.9 0.7 pad_maximum_fusion.4.upstream_ref
  37.6 0.0 collective-permute-done
  37.6 0.1 maximum_bitcast_fusion.x_ref
  37.7 0.6 copy-done.12
  38.3 0.4 broadcast_in_dim.4.gain_ref
  38.7 0.7 copy-done
  39.4 0.5 shard_map.92
  39.9 1.1 copy-done.2
  41.0 17.1 %all-to-all-done.weight_ref = bf16[8,216,640]{2,1,0:T(8,128)(2,1)S(1)} async-done(((bf16[8,216,640]{2,1,0:T(8,128)(2,1)}), bf16[8,216,640]{2,1,0:T(8,128)(2,1)S(1)}, u32[]{:S(2)}, u32[]{:S(2)}) %all-to-all-start) | async-done | bytes 2211872 | tf_op jit(solution)/shard_map/all_to_all | solution.py:183
  58.1 1.3 copy-done.3
  59.4 0.9 copy-done.6
  60.3 3.3 %shard_map.93 = (bf16[216,128]{1,0:T(8,128)(2,1)S(1)}, bf16[2,216,256]{2,1,0:T(8,128)(2,1)S(1)}, f32[2560,128]{1,0:T(8,128)S(1)}, bf16[2784,128]{1,0:T(8,128)(2,1)S(1)}) custom-call(bf16[2560,256]{1,0:T(8,128)(2,1)S(1)} %copy-done.3, bf16[216,256]{1,0:T(8,128)(2,1)S(1)} %copy-done.6, bf16[8,216,640]{2,1,0:T(8,128)(2,1)S(1)} %all-to-all-done.weight_ref), custom_call_target="tpu_custom_call" | custom-call | tf_op jit(solution)/shard_map/pallas_call | solution.py:196
  63.6 0.0 copy-start.9
  63.6 2.8 %collective-permute-start.2 = (bf16[2784,128]{1,0:T(8,128)(2,1)S(1)}, bf16[2784,128]{1,0:T(8,128)(2,1)S(1)}, u32[]{:S(2)}, u32[]{:S(2)}) collective-permute-start(bf16[2784,128]{1,0:T(8,128)(2,1)S(1)} %get-tuple-element.21), channel_id=1, source_target_pairs={{0,16},{16,0},{1,17},{17,1},{2,18},{18,2},{3,19},{19,3},{4,20},{20... | collective-permute-start | bytes 2138120 | tf_op jit(solution)/shard_map/ppermute | solution.py:20
  66.5 1.7 %collective-permute-done.2.other_ref = bf16[2784,128]{1,0:T(8,128)(2,1)S(1)} collective-permute-done((bf16[2784,128]{1,0:T(8,128)(2,1)S(1)}, bf16[2784,128]{1,0:T(8,128)(2,1)S(1)}, u32[]{:S(2)}, u32[]{:S(2)}) %collective-permute-start.2) | collective-permute-done | bytes 712736 | tf_op jit(solution)/shard_map/ppermute | solution.py:20
  68.2 1.3 shard_map.95
  69.5 0.9 copy-done.5
  70.3 10.9 %all-to-all-start.1 = ((bf16[16,176,128]{2,1,0:T(8,128)(2,1)}), bf16[16,176,128]{2,1,0:T(8,128)(2,1)}, u32[]{:S(2)}, u32[]{:S(2)}) async-start(bf16[16,176,128]{2,1,0:T(8,128)(2,1)} %shard_map.95), calls=%async_computation.1 | async-start | bytes 1441792 | tf_op jit(solution)/shard_map/all_to_all | solution.py:220
  81.3 0.1 dynamic_slice.7
  81.4 0.9 copy-done.8
  82.3 1.8 %shard_map.94 = (f32[2,216,640]{2,1,0:T(8,128)S(1)}, bf16[2,216,640]{2,1,0:T(8,128)(2,1)}, bf16[2,216,640]{2,1,0:T(8,128)(2,1)}, bf16[2,216,640]{2,1,0:T(8,128)(2,1)}) custom-call(s32[1]{0:T(128)} %bitcast.6.spot_ref, bf16[2560,256]{1,0:T(8,128)(2,1)S(1)} %copy-done.4, bf16[2,216,256]{2,1,0:T(8,128)(2,1)S(1)} %copy-done.8), custom_call_target="tpu_custom_call" | custom-call | tf_op jit(solution)/shard_map/pallas_call | solution.py:209
  84.1 2.0 %collective-permute-start.3 = (bf16[2,216,640]{2,1,0:T(8,128)(2,1)}, bf16[2,216,640]{2,1,0:T(8,128)(2,1)S(1)}, u32[]{:S(2)}, u32[]{:S(2)}) collective-permute-start(bf16[2,216,640]{2,1,0:T(8,128)(2,1)} %get-tuple-element.26), channel_id=1, source_target_pairs={{0,256},{128,384},{256,0},{384,128},{1,257},{129,385},{257,1},{385... | collective-permute-start | bytes 1658888 | tf_op jit(solution)/shard_map/ppermute | solution.py:28
  86.1 3.3 %collective-permute-start.4 = (bf16[2,216,640]{2,1,0:T(8,128)(2,1)}, bf16[2,216,640]{2,1,0:T(8,128)(2,1)S(1)}, u32[]{:S(2)}, u32[]{:S(2)}) collective-permute-start(bf16[2,216,640]{2,1,0:T(8,128)(2,1)} %get-tuple-element.27), channel_id=1, source_target_pairs={{0,128},{128,256},{256,384},{384,0},{1,129},{129,257},{257,385},{3... | collective-permute-start | bytes 1658888 | tf_op jit(solution)/shard_map/ppermute | solution.py:28
  89.4 3.2 %collective-permute-start.5 = (bf16[2,216,640]{2,1,0:T(8,128)(2,1)}, bf16[2,216,640]{2,1,0:T(8,128)(2,1)}, u32[]{:S(2)}, u32[]{:S(2)}) collective-permute-start(bf16[2,216,640]{2,1,0:T(8,128)(2,1)} %get-tuple-element.28), channel_id=1, source_target_pairs={{0,384},{128,0},{256,128},{384,256},{1,385},{129,1},{257,129},{385... | collective-permute-start | bytes 1658888 | tf_op jit(solution)/shard_map/ppermute | solution.py:28
  92.6 15.4 %all-to-all-done.1 = bf16[16,176,128]{2,1,0:T(8,128)(2,1)} async-done(((bf16[16,176,128]{2,1,0:T(8,128)(2,1)}), bf16[16,176,128]{2,1,0:T(8,128)(2,1)}, u32[]{:S(2)}, u32[]{:S(2)}) %all-to-all-start.1) | async-done | bytes 720928 | tf_op jit(solution)/shard_map/all_to_all | solution.py:220
  108.0 1.2 convert_reduce_fusion
  109.2 0.8 fusion.1
  110.0 4.0 %collective-permute-done.4.second_ref = bf16[2,216,640]{2,1,0:T(8,128)(2,1)S(1)} collective-permute-done((bf16[2,216,640]{2,1,0:T(8,128)(2,1)}, bf16[2,216,640]{2,1,0:T(8,128)(2,1)S(1)}, u32[]{:S(2)}, u32[]{:S(2)}) %collective-permute-start.4) | collective-permute-done | bytes 552992 | tf_op jit(solution)/shard_map/ppermute | solution.py:28
  114.0 2.4 %shard_map.96 = bf16[640,432]{1,0:T(8,128)(2,1)} custom-call(f32[2,216,640]{2,1,0:T(8,128)S(1)} %get-tuple-element.23.own_ref, bf16[2,216,640]{2,1,0:T(8,128)(2,1)S(1)} %collective-permute-done.3.first_ref, bf16[2,216,640]{2,1,0:T(8,128)(2,1)S(1)} %collective-permute-done.4.second_ref, bf16[2,216,640]{2,1,0:T(8,128)(2,1)} %collective-permute-done.5.third_ref), custom_call_target="tpu_custom_call" | custom-call | tf_op jit(solution)/shard_map/pallas_call | solution.py:239
  116.4 5.8 %all-to-all-start.2 = ((bf16[8,80,432]{2,1,0:T(8,128)(2,1)}), bf16[8,80,432]{2,1,0:T(8,128)(2,1)S(1)}, u32[]{:S(2)}, u32[]{:S(2)}) async-start(bf16[8,80,432]{2,1,0:T(8,128)(2,1)} %bitcast.8), calls=%async_computation.2 | async-start | bytes 1310720 | tf_op jit(solution)/shard_map/all_to_all | solution.py:242
  122.3 0.7 fusion
  123.0 6.9 %psum.14 = f32[160]{0:T(256)S(1)} all-reduce(f32[160]{0:T(256)S(1)} %get-tuple-element.32), channel_id=1, replica_groups=mesh['x'=4,'z'=4,'c'=2,'y'=8,'h'=2] {'x'}, use_global_device_ids=true, to_apply=%region_3.4 | all-reduce | flops 160 | bytes 1280 | tf_op jit(solution)/shard_map/psum | solution.py:237
  129.9 16.0 %psum.15 = f32[160]{0:T(256)} all-reduce(f32[160]{0:T(256)S(1)} %psum.14), channel_id=1, replica_groups=mesh['x'=4,'z'=4,'c'=2,'y'=8,'h'=2] {'z','c'}, use_global_device_ids=true, to_apply=%region_4.5 | all-reduce | flops 160 | bytes 1280 | tf_op jit(solution)/shard_map/psum | solution.py:237
  146.0 0.1 convert_reduce_fusion.1
  146.0 0.1 slice_bitcast_fusion.1
  146.2 0.9 pad_maximum_fusion.1
  (26 shorter events, 0.1 us)
Async XLA Ops:
  22.0 8.5 %copy-start.11 = (bf16[128,2560]{1,0:T(8,128)(2,1)S(1)}, bf16[128,2560]{1,0:T(8,128)(2,1)}, u32[]{:S(2)}) copy-start(bf16[128,2560]{1,0:T(8,128)(2,1)} %param.5) | copy-start | bytes 1966084
  22.0 36.1 %all-to-all-start = ((bf16[8,216,640]{2,1,0:T(8,128)(2,1)}), bf16[8,216,640]{2,1,0:T(8,128)(2,1)S(1)}, u32[]{:S(2)}, u32[]{:S(2)}) async-start(bf16[8,216,640]{2,1,0:T(8,128)(2,1)} %bitcast.27), calls=%async_computation | async-start | bytes 4423680 | tf_op jit(solution)/shard_map/all_to_all | solution.py:183
  30.8 6.8 %collective-permute-start = (bf16[128,2560]{0,1:T(8,128)(2,1)S(1)}, bf16[128,2560]{0,1:T(8,128)(2,1)S(1)}, u32[]{:S(2)}, u32[]{:S(2)}) collective-permute-start(bf16[128,2560]{0,1:T(8,128)(2,1)S(1)} %copy.18), channel_id=1, source_target_pairs={{0,16},{16,0},{1,17},{17,1},{2,18},{18,2},{3,19},{19,3},{4,20},{20... | collective-permute-start | bytes 1966088 | tf_op jit(solution)/shard_map/ppermute | solution.py:20
  33.8 3.2 %collective-permute-start.1 = (bf16[216,128]{1,0:T(8,128)(2,1)S(1)}, bf16[216,128]{1,0:T(8,128)(2,1)S(1)}, u32[]{:S(2)}, u32[]{:S(2)}) collective-permute-start(bf16[216,128]{1,0:T(8,128)(2,1)S(1)} %get-tuple-element.42), channel_id=1, source_target_pairs={{0,16},{16,0},{1,17},{17,1},{2,18},{18,2},{3,19},{19,3},{4,20},{20... | collective-permute-start | bytes 165896 | tf_op jit(solution)/shard_map/ppermute | solution.py:20
  37.6 0.7 copy-start.12
  38.3 1.1 copy-start
  39.9 1.1 copy-start.2
  58.1 1.3 copy-start.3
  59.4 0.9 copy-start.6
  60.3 6.1 %copy-start.1 = (bf16[2560,256]{1,0:T(8,128)(2,1)S(1)}, bf16[2560,256]{1,0:T(8,128)(2,1)}, u32[]{:S(2)}) copy-start(bf16[2560,256]{1,0:T(8,128)(2,1)} %copy-done) | copy-start | bytes 3932164
  63.6 4.6 %copy-start.7 = (bf16[2,216,256]{2,1,0:T(8,128)(2,1)}, bf16[2,216,256]{2,1,0:T(8,128)(2,1)S(1)}, u32[]{:S(2)}) copy-start(bf16[2,216,256]{2,1,0:T(8,128)(2,1)S(1)} %get-tuple-element.22.back_ref) | copy-start | bytes 663556
  63.6 4.6 %copy-start.9 = (bf16[216,128]{1,0:T(8,128)(2,1)}, bf16[216,128]{1,0:T(8,128)(2,1)S(1)}, u32[]{:S(2)}) copy-start(bf16[216,128]{1,0:T(8,128)(2,1)S(1)} %get-tuple-element.20) | copy-start | bytes 165892
  63.6 4.6 %collective-permute-start.2 = (bf16[2784,128]{1,0:T(8,128)(2,1)S(1)}, bf16[2784,128]{1,0:T(8,128)(2,1)S(1)}, u32[]{:S(2)}, u32[]{:S(2)}) collective-permute-start(bf16[2784,128]{1,0:T(8,128)(2,1)S(1)} %get-tuple-element.21), channel_id=1, source_target_pairs={{0,16},{16,0},{1,17},{17,1},{2,18},{18,2},{3,19},{19,3},{4,20},{20... | collective-permute-start | bytes 2138120 | tf_op jit(solution)/shard_map/ppermute | solution.py:20
  69.5 0.9 copy-start.5
  70.3 11.0 %copy-start.4 = (bf16[2560,256]{1,0:T(8,128)(2,1)S(1)}, bf16[2560,256]{1,0:T(8,128)(2,1)}, u32[]{:S(2)}) copy-start(bf16[2560,256]{1,0:T(8,128)(2,1)} %copy-done.2) | copy-start | bytes 3932164
  70.3 37.7 %all-to-all-start.1 = ((bf16[16,176,128]{2,1,0:T(8,128)(2,1)}), bf16[16,176,128]{2,1,0:T(8,128)(2,1)}, u32[]{:S(2)}, u32[]{:S(2)}) async-start(bf16[16,176,128]{2,1,0:T(8,128)(2,1)} %shard_map.95), calls=%async_computation.1 | async-start | bytes 1441792 | tf_op jit(solution)/shard_map/all_to_all | solution.py:220
  81.4 0.9 copy-start.8
  84.1 25.9 %collective-permute-start.3 = (bf16[2,216,640]{2,1,0:T(8,128)(2,1)}, bf16[2,216,640]{2,1,0:T(8,128)(2,1)S(1)}, u32[]{:S(2)}, u32[]{:S(2)}) collective-permute-start(bf16[2,216,640]{2,1,0:T(8,128)(2,1)} %get-tuple-element.26), channel_id=1, source_target_pairs={{0,256},{128,384},{256,0},{384,128},{1,257},{129,385},{257,1},{385... | collective-permute-start | bytes 1658888 | tf_op jit(solution)/shard_map/ppermute | solution.py:28
  86.1 27.9 %collective-permute-start.4 = (bf16[2,216,640]{2,1,0:T(8,128)(2,1)}, bf16[2,216,640]{2,1,0:T(8,128)(2,1)S(1)}, u32[]{:S(2)}, u32[]{:S(2)}) collective-permute-start(bf16[2,216,640]{2,1,0:T(8,128)(2,1)} %get-tuple-element.27), channel_id=1, source_target_pairs={{0,128},{128,256},{256,384},{384,0},{1,129},{129,257},{257,385},{3... | collective-permute-start | bytes 1658888 | tf_op jit(solution)/shard_map/ppermute | solution.py:28
  89.4 24.6 %collective-permute-start.5 = (bf16[2,216,640]{2,1,0:T(8,128)(2,1)}, bf16[2,216,640]{2,1,0:T(8,128)(2,1)}, u32[]{:S(2)}, u32[]{:S(2)}) collective-permute-start(bf16[2,216,640]{2,1,0:T(8,128)(2,1)} %get-tuple-element.28), channel_id=1, source_target_pairs={{0,384},{128,0},{256,128},{384,256},{1,385},{129,1},{257,129},{385... | collective-permute-start | bytes 1658888 | tf_op jit(solution)/shard_map/ppermute | solution.py:28
  116.4 5.8 %slice-start = ((bf16[2784,128]{1,0:T(8,128)(2,1)}), bf16[216,128]{1,0:T(8,128)(2,1)S(1)}, s32[]{:S(2)}) async-start(bf16[2784,128]{1,0:T(8,128)(2,1)} %copy-done.5), calls=%async_computation.3 | async-start | bytes 110592 | tf_op jit(solution)/shard_map/slice | solution.py:208
  116.4 5.8 %copy-start.10 = (bf16[216,128]{1,0:T(8,128)(2,1)S(1)}, bf16[216,128]{1,0:T(8,128)(2,1)}, u32[]{:S(2)}) copy-start(bf16[216,128]{1,0:T(8,128)(2,1)} %copy-done.9) | copy-start | bytes 165892
  116.4 29.5 %all-to-all-start.2 = ((bf16[8,80,432]{2,1,0:T(8,128)(2,1)}), bf16[8,80,432]{2,1,0:T(8,128)(2,1)S(1)}, u32[]{:S(2)}, u32[]{:S(2)}) async-start(bf16[8,80,432]{2,1,0:T(8,128)(2,1)} %bitcast.8), calls=%async_computation.2 | async-start | bytes 1310720 | tf_op jit(solution)/shard_map/all_to_all | solution.py:242

commit v9 on v8

--- a/solution.py
+++ b/solution.py
@@ -8,10 +8,9 @@
 BF = jnp.bfloat16
 F32 = jnp.float32
 NX, NZ, NC, NH = 4, 4, 2, 2
-ANY = pl.BlockSpec(memory_space=pl.ANY)
 VMEM = pl.BlockSpec(memory_space=pltpu.VMEM)
 SMEM = pl.BlockSpec(memory_space=pltpu.SMEM)
-PARAMS = pltpu.CompilerParams(vmem_limit_bytes=48 * 1024 * 1024)
+PARAMS = pltpu.CompilerParams(vmem_limit_bytes=14 * 1024 * 1024)
 NT = (((1,), (1,)), ((), ()))
 TN = (((0,), (0,)), ((), ()))
 
@@ -54,24 +53,17 @@
 
 
 def forward_kernel(
-    normed_ref, upstream_ref, weight_ref, hidden_ref, back_ref, own_ref, other_ref, held, sems
+    normed_ref, upstream_ref, weight_ref, hidden_ref, back_ref, own_ref, other_ref
 ):
     size = weight_ref.shape[2] // 2
     tokens = own_ref.shape[1]
     width = own_ref.shape[0]
-    copies = [
-        pltpu.make_async_copy(weight_ref.at[index], held.at[index], sems.at[index])
-        for index in range(NX * NC)
-    ]
-    for copy in copies:
-        copy.start()
 
     def piece(index, which):
-        return held[index, :, which * size : (which + 1) * size]
+        return weight_ref[index, :, which * size : (which + 1) * size]
 
     gate_pre, up_pre = 0.0, 0.0
     for index in range(NX * NC):
-        copies[index].wait()
         rows = normed_ref[pl.ds(index * size, size), :]
         gate_pre += jnp.dot(piece(index, 0), rows, preferred_element_type=F32)
         up_pre += jnp.dot(piece(index, 1), rows, preferred_element_type=F32)
@@ -141,12 +133,11 @@
         out_ref[:, which * half : (which + 1) * half] = total.T.astype(BF)
 
 
-def call(kernel, outs, specs, scratch=()):
+def call(kernel, outs, specs):
     return pl.pallas_call(
         kernel,
         out_shape=outs,
         in_specs=specs,
-        scratch_shapes=scratch,
         out_specs=jax.tree.map(lambda _: VMEM, outs),
         compiler_params=PARAMS,
     )
@@ -201,8 +192,7 @@
             shape((width, tokens), F32),
             shape((width + riding, tokens), BF),
         ),
-        [VMEM, VMEM, ANY],
-        [pltpu.VMEM(weight.shape, BF), pltpu.SemaphoreType.DMA((NX * NC,))],
+        [VMEM] * 3,
     )(normed, upstream_pair, weight)
     part_other = swap_core(part_other)
     hidden = ordered(hidden_own, part_other[width : width + half], 0).T
@@ -233,8 +223,10 @@
         .T
     )
     gain_part = jnp.sum(own_sums * unit_slice, axis=1)
+    gain_part = lax.psum(gain_part, "x")
     gain_part, travelling = lax.optimization_barrier((gain_part, travelling))
-    grad_gain = lax.psum(lax.psum(gain_part, "x"), ("z", "c"))
+    grad_gain = lax.psum(gain_part, "z")
+    grad_gain = grad_gain + swap_core(grad_gain)
 
     column_sum = call(column_kernel, shape((column_rows, columns), BF), [VMEM] * 4)(
         terms[0], *travelling

time: 148 us -> 149 us (level)
  starting transfers between devices: 40.9 us -> 46.7 us
  waiting for transfers between devices: 39.1 us -> 35.1 us
    ppermute x3, waiting for transfers between devices: 4.03 us -> 0.01 us  [shift_x(): return lax.ppermute(value, 'x', [(x, (x + steps) % NX) for x in range(NX)])]
    ppermute x3 -> x4, starting transfers between devices: 7.11 us -> 10.8 us  [swap(): return lax.ppermute(value, axis, [(0, 1), (1, 0)])]
    all_to_all x1, starting transfers between devices: 5.82 us -> 7.95 us  [per_device(): lax.all_to_all(column_sum.reshape(NC * NZ, rows, columns), ('c', 'z'), 0,...]
  transfers between devices with their start and end apart: 9 -> 10, of which waited for: 5 -> 5; matrix products, arithmetic and copies ran while one was open for 4% -> 4% of each run, Pallas kernels for 2% -> 2%
where the time goes in v9:
time: 149 us; the launch traced here: 148 us
  starting transfers between devices  46.7 us (31%)
  blocking collectives  41.2 us (28%)
  waiting for transfers between devices  35.1 us (24%)
  local copies, waits for them, and re-layouts  9.26 us (6%)
  Pallas kernels  8.07 us (5%)
  other arithmetic  7.06 us (5%)
    all_gather x1, blocking collectives, per_device(): lax.all_gather(jnp.concatenate([w_gate, w_up], 1), 'z', axis=0, tiled=True)  18.1 us
    all_to_all x1, waiting for transfers between devices, per_device(): weight = lax.all_to_all(copies, ('x', 'c'), 0, 0, tiled=True)  17.1 us
    psum x1, blocking collectives, per_device(): grad_gain = lax.psum(gain_part, 'z')  16.2 us
    all_to_all x1, waiting for transfers between devices, per_device(): got = lax.all_to_all(sending, ('y', 'h'), 0, 0, tiled=True)  15.4 us
    all_to_all x1, starting transfers between devices, per_device(): got = lax.all_to_all(sending, ('y', 'h'), 0, 0, tiled=True)  10.9 us
    ppermute x4, starting transfers between devices, swap(): return lax.ppermute(value, axis, [(0, 1), (1, 0)])  10.8 us
    all_to_all x1, starting transfers between devices, per_device(): weight = lax.all_to_all(copies, ('x', 'c'), 0, 0, tiled=True)  8.54 us
    ppermute x3, starting transfers between devices, shift_x(): return lax.ppermute(value, 'x', [(x, (x + steps) % NX) for x in range(NX)])  8.48 us
  transfers between devices with their start and end apart: 10, of which 5 were waited for; matrix products, arithmetic and copies ran while one was open for 4% of the time, Pallas kernels for 2%

profile of v9, /device:TPU:1, one launch (start us, length us, event | category | flops | bytes accessed | tf_op | source)
XLA Modules:
  0.0 148.3 jit_solution(516965643916541634)
XLA Ops:
  0.6 1.0 pad_maximum_fusion.3
  1.7 18.1 %all_gather.3 = bf16[320,864]{1,0:T(8,128)(2,1)S(1)} all-gather(bf16[80,864]{1,0:T(8,128)(2,1)S(1)} %pad_maximum_fusion.3), channel_id=1, replica_groups=mesh['x'=4,'z'=4,'c'=2,'y'=8,'h'=2] {'z'}, dimensions={0}, use_global_device_ids=true | all-gather | bytes 691200 | tf_op jit(solution)/shard_map/all_gather | solution.py:169
  19.8 0.4 copy.19
  20.2 0.1 fusion.4
  20.2 0.2 pad_maximum_fusion
  20.4 1.5 %broadcast_in_dim.5 = bf16[4,2,216,640]{3,2,1,0:T(8,128)(2,1)} broadcast(bf16[2,216,640]{2,1,0:T(8,128)(2,1)S(1)} %bitcast.29), dimensions={1,2,3} | broadcast | bytes 2764800 | tf_op jit(solution)/shard_map/broadcast_in_dim | solution.py:171
  22.0 8.5 %all-to-all-start = ((bf16[8,216,640]{2,1,0:T(8,128)(2,1)}), bf16[8,216,640]{2,1,0:T(8,128)(2,1)S(1)}, u32[]{:S(2)}, u32[]{:S(2)}) async-start(bf16[8,216,640]{2,1,0:T(8,128)(2,1)} %bitcast.27), calls=%async_computation | async-start | bytes 4423680 | tf_op jit(solution)/shard_map/all_to_all | solution.py:174
  30.5 0.3 copy.18
  30.8 2.0 %collective-permute-start = (bf16[128,2560]{0,1:T(8,128)(2,1)S(1)}, bf16[128,2560]{0,1:T(8,128)(2,1)S(1)}, u32[]{:S(2)}, u32[]{:S(2)}) collective-permute-start(bf16[128,2560]{0,1:T(8,128)(2,1)S(1)} %copy.18), channel_id=1, source_target_pairs={{0,16},{16,0},{1,17},{17,1},{2,18},{18,2},{3,19},{19,3},{4,20},{20... | collective-permute-start | bytes 1966088 | tf_op jit(solution)/shard_map/ppermute | solution.py:19
  32.9 0.9 broadcast_select_fusion.1
  33.7 2.3 %collective-permute-start.1 = (bf16[216,128]{1,0:T(8,128)(2,1)S(1)}, bf16[216,128]{1,0:T(8,128)(2,1)S(1)}, u32[]{:S(2)}, u32[]{:S(2)}) collective-permute-start(bf16[216,128]{1,0:T(8,128)(2,1)S(1)} %get-tuple-element.42), channel_id=1, source_target_pairs={{0,16},{16,0},{1,17},{17,1},{2,18},{18,2},{3,19},{19,3},{4,20},{20... | collective-permute-start | bytes 165896 | tf_op jit(solution)/shard_map/ppermute | solution.py:19
  36.1 0.9 collective-permute-done.1
  36.9 0.7 pad_maximum_fusion.4.upstream_ref
  37.6 0.1 maximum_bitcast_fusion.x_ref
  37.7 0.6 copy-done.12
  38.3 0.4 broadcast_in_dim.4.gain_ref
  38.7 0.7 copy-done
  39.4 0.6 shard_map.92
  39.9 1.1 copy-done.2
  41.0 17.1 %all-to-all-done.weight_ref = bf16[8,216,640]{2,1,0:T(8,128)(2,1)S(1)} async-done(((bf16[8,216,640]{2,1,0:T(8,128)(2,1)}), bf16[8,216,640]{2,1,0:T(8,128)(2,1)S(1)}, u32[]{:S(2)}, u32[]{:S(2)}) %all-to-all-start) | async-done | bytes 2211872 | tf_op jit(solution)/shard_map/all_to_all | solution.py:174
  58.1 1.3 copy-done.3
  59.4 0.9 copy-done.6
  60.3 2.0 %shard_map.93 = (bf16[216,128]{1,0:T(8,128)(2,1)S(1)}, bf16[2,216,256]{2,1,0:T(8,128)(2,1)S(1)}, f32[2560,128]{1,0:T(8,128)S(1)}, bf16[2784,128]{1,0:T(8,128)(2,1)S(1)}) custom-call(bf16[2560,256]{1,0:T(8,128)(2,1)S(1)} %copy-done.3, bf16[216,256]{1,0:T(8,128)(2,1)S(1)} %copy-done.6, bf16[8,216,640]{2,1,0:T(8,128)(2,1)S(1)} %all-to-all-done.weight_ref), custom_call_target="tpu_custom_call" | custom-call | tf_op jit(solution)/shard_map/pallas_call | solution.py:187
  62.4 2.8 %collective-permute-start.2 = (bf16[2784,128]{1,0:T(8,128)(2,1)S(1)}, bf16[2784,128]{1,0:T(8,128)(2,1)S(1)}, u32[]{:S(2)}, u32[]{:S(2)}) collective-permute-start(bf16[2784,128]{1,0:T(8,128)(2,1)S(1)} %get-tuple-element.21), channel_id=1, source_target_pairs={{0,16},{16,0},{1,17},{17,1},{2,18},{18,2},{3,19},{19,3},{4,20},{20... | collective-permute-start | bytes 2138120 | tf_op jit(solution)/shard_map/ppermute | solution.py:19
  65.2 1.7 %collective-permute-done.2.other_ref = bf16[2784,128]{1,0:T(8,128)(2,1)S(1)} collective-permute-done((bf16[2784,128]{1,0:T(8,128)(2,1)S(1)}, bf16[2784,128]{1,0:T(8,128)(2,1)S(1)}, u32[]{:S(2)}, u32[]{:S(2)}) %collective-permute-start.2) | collective-permute-done | bytes 712736 | tf_op jit(solution)/shard_map/ppermute | solution.py:19
  66.9 1.3 shard_map.95
  68.2 0.8 copy-done.5
  69.1 10.9 %all-to-all-start.1 = ((bf16[16,176,128]{2,1,0:T(8,128)(2,1)}), bf16[16,176,128]{2,1,0:T(8,128)(2,1)}, u32[]{:S(2)}, u32[]{:S(2)}) async-start(bf16[16,176,128]{2,1,0:T(8,128)(2,1)} %shard_map.95), calls=%async_computation.1 | async-start | bytes 1441792 | tf_op jit(solution)/shard_map/all_to_all | solution.py:210
  80.0 0.1 dynamic_slice.7
  80.1 0.9 copy-done.8
  81.0 1.8 %shard_map.94 = (f32[2,216,640]{2,1,0:T(8,128)S(1)}, bf16[2,216,640]{2,1,0:T(8,128)(2,1)}, bf16[2,216,640]{2,1,0:T(8,128)(2,1)}, bf16[2,216,640]{2,1,0:T(8,128)(2,1)}) custom-call(s32[1]{0:T(128)} %bitcast.6.spot_ref, bf16[2560,256]{1,0:T(8,128)(2,1)S(1)} %copy-done.4, bf16[2,216,256]{2,1,0:T(8,128)(2,1)S(1)} %copy-done.8), custom_call_target="tpu_custom_call" | custom-call | tf_op jit(solution)/shard_map/pallas_call | solution.py:199
  82.8 2.0 %collective-permute-start.3 = (bf16[2,216,640]{2,1,0:T(8,128)(2,1)}, bf16[2,216,640]{2,1,0:T(8,128)(2,1)S(1)}, u32[]{:S(2)}, u32[]{:S(2)}) collective-permute-start(bf16[2,216,640]{2,1,0:T(8,128)(2,1)} %get-tuple-element.26), channel_id=1, source_target_pairs={{0,256},{128,384},{256,0},{384,128},{1,257},{129,385},{257,1},{385... | collective-permute-start | bytes 1658888 | tf_op jit(solution)/shard_map/ppermute | solution.py:27
  84.8 3.3 %collective-permute-start.4 = (bf16[2,216,640]{2,1,0:T(8,128)(2,1)}, bf16[2,216,640]{2,1,0:T(8,128)(2,1)S(1)}, u32[]{:S(2)}, u32[]{:S(2)}) collective-permute-start(bf16[2,216,640]{2,1,0:T(8,128)(2,1)} %get-tuple-element.27), channel_id=1, source_target_pairs={{0,128},{128,256},{256,384},{384,0},{1,129},{129,257},{257,385},{3... | collective-permute-start | bytes 1658888 | tf_op jit(solution)/shard_map/ppermute | solution.py:27
  88.1 3.2 %collective-permute-start.5 = (bf16[2,216,640]{2,1,0:T(8,128)(2,1)}, bf16[2,216,640]{2,1,0:T(8,128)(2,1)}, u32[]{:S(2)}, u32[]{:S(2)}) collective-permute-start(bf16[2,216,640]{2,1,0:T(8,128)(2,1)} %get-tuple-element.28), channel_id=1, source_target_pairs={{0,384},{128,0},{256,128},{384,256},{1,385},{129,1},{257,129},{385... | collective-permute-start | bytes 1658888 | tf_op jit(solution)/shard_map/ppermute | solution.py:27
  91.4 15.4 %all-to-all-done.1 = bf16[16,176,128]{2,1,0:T(8,128)(2,1)} async-done(((bf16[16,176,128]{2,1,0:T(8,128)(2,1)}), bf16[16,176,128]{2,1,0:T(8,128)(2,1)}, u32[]{:S(2)}, u32[]{:S(2)}) %all-to-all-start.1) | async-done | bytes 720928 | tf_op jit(solution)/shard_map/all_to_all | solution.py:210
  106.7 1.2 convert_reduce_fusion
  107.9 0.8 fusion.1
  108.7 6.8 %psum.14 = f32[160]{0:T(256)S(1)} all-reduce(f32[160]{0:T(256)S(1)} %get-tuple-element.34), channel_id=1, replica_groups=mesh['x'=4,'z'=4,'c'=2,'y'=8,'h'=2] {'x'}, use_global_device_ids=true, to_apply=%region_2.3 | all-reduce | flops 160 | bytes 1280 | tf_op jit(solution)/shard_map/psum | solution.py:226
  115.6 2.4 %shard_map.96 = bf16[640,432]{1,0:T(8,128)(2,1)} custom-call(f32[2,216,640]{2,1,0:T(8,128)S(1)} %get-tuple-element.23.own_ref, bf16[2,216,640]{2,1,0:T(8,128)(2,1)S(1)} %collective-permute-done.3.first_ref, bf16[2,216,640]{2,1,0:T(8,128)(2,1)S(1)} %collective-permute-done.4.second_ref, bf16[2,216,640]{2,1,0:T(8,128)(2,1)} %collective-permute-done.5.third_ref), custom_call_target="tpu_custom_call" | custom-call | tf_op jit(solution)/shard_map/pallas_call | solution.py:231
  118.0 7.9 %all-to-all-start.2 = ((bf16[8,80,432]{2,1,0:T(8,128)(2,1)}), bf16[8,80,432]{2,1,0:T(8,128)(2,1)S(1)}, u32[]{:S(2)}, u32[]{:S(2)}) async-start(bf16[8,80,432]{2,1,0:T(8,128)(2,1)} %bitcast.8), calls=%async_computation.2 | async-start | bytes 1310720 | tf_op jit(solution)/shard_map/all_to_all | solution.py:234
  126.0 16.2 %psum.15 = f32[160]{0:T(256)S(1)} all-reduce(f32[160]{0:T(256)S(1)} %psum.14), channel_id=1, replica_groups=mesh['x'=4,'z'=4,'c'=2,'y'=8,'h'=2] {'z'}, use_global_device_ids=true, to_apply=%region_4.5 | all-reduce | flops 160 | bytes 1280 | tf_op jit(solution)/shard_map/psum | solution.py:228
  142.1 3.7 %collective-permute-start.6 = (f32[160]{0:T(256)S(1)}, f32[160]{0:T(256)S(1)}, u32[]{:S(2)}, u32[]{:S(2)}) collective-permute-start(f32[160]{0:T(256)S(1)} %psum.15), channel_id=1, source_target_pairs={{0,16},{16,0},{1,17},{17,1},{2,18},{18,2},{3,19},{19,3},{4,20},{20... | collective-permute-start | bytes 1928 | tf_op jit(solution)/shard_map/ppermute | solution.py:19
  145.9 0.7 fusion
  146.6 0.1 collective-permute-done.6
  146.7 0.6 add.26
  147.2 0.1 convert_reduce_fusion.1
  147.3 0.1 slice_bitcast_fusion.1
  147.4 0.9 pad_maximum_fusion.1
  (29 shorter events, 0.1 us)
Async XLA Ops:
  22.0 8.5 %copy-start.11 = (bf16[128,2560]{1,0:T(8,128)(2,1)S(1)}, bf16[128,2560]{1,0:T(8,128)(2,1)}, u32[]{:S(2)}) copy-start(bf16[128,2560]{1,0:T(8,128)(2,1)} %param.5) | copy-start | bytes 1966084
  22.0 36.1 %all-to-all-start = ((bf16[8,216,640]{2,1,0:T(8,128)(2,1)}), bf16[8,216,640]{2,1,0:T(8,128)(2,1)S(1)}, u32[]{:S(2)}, u32[]{:S(2)}) async-start(bf16[8,216,640]{2,1,0:T(8,128)(2,1)} %bitcast.27), calls=%async_computation | async-start | bytes 4423680 | tf_op jit(solution)/shard_map/all_to_all | solution.py:174
  30.8 6.8 %collective-permute-start = (bf16[128,2560]{0,1:T(8,128)(2,1)S(1)}, bf16[128,2560]{0,1:T(8,128)(2,1)S(1)}, u32[]{:S(2)}, u32[]{:S(2)}) collective-permute-start(bf16[128,2560]{0,1:T(8,128)(2,1)S(1)} %copy.18), channel_id=1, source_target_pairs={{0,16},{16,0},{1,17},{17,1},{2,18},{18,2},{3,19},{19,3},{4,20},{20... | collective-permute-start | bytes 1966088 | tf_op jit(solution)/shard_map/ppermute | solution.py:19
  33.7 3.2 %collective-permute-start.1 = (bf16[216,128]{1,0:T(8,128)(2,1)S(1)}, bf16[216,128]{1,0:T(8,128)(2,1)S(1)}, u32[]{:S(2)}, u32[]{:S(2)}) collective-permute-start(bf16[216,128]{1,0:T(8,128)(2,1)S(1)} %get-tuple-element.42), channel_id=1, source_target_pairs={{0,16},{16,0},{1,17},{17,1},{2,18},{18,2},{3,19},{19,3},{4,20},{20... | collective-permute-start | bytes 165896 | tf_op jit(solution)/shard_map/ppermute | solution.py:19
  37.6 0.7 copy-start.12
  38.3 1.1 copy-start
  39.9 1.1 copy-start.2
  58.1 1.3 copy-start.3
  59.4 0.9 copy-start.6
  60.3 4.8 %copy-start.1 = (bf16[2560,256]{1,0:T(8,128)(2,1)S(1)}, bf16[2560,256]{1,0:T(8,128)(2,1)}, u32[]{:S(2)}) copy-start(bf16[2560,256]{1,0:T(8,128)(2,1)} %copy-done) | copy-start | bytes 3932164
  62.3 4.6 %copy-start.7 = (bf16[2,216,256]{2,1,0:T(8,128)(2,1)}, bf16[2,216,256]{2,1,0:T(8,128)(2,1)S(1)}, u32[]{:S(2)}) copy-start(bf16[2,216,256]{2,1,0:T(8,128)(2,1)S(1)} %get-tuple-element.22.back_ref) | copy-start | bytes 663556
  62.4 4.6 %copy-start.9 = (bf16[216,128]{1,0:T(8,128)(2,1)}, bf16[216,128]{1,0:T(8,128)(2,1)S(1)}, u32[]{:S(2)}) copy-start(bf16[216,128]{1,0:T(8,128)(2,1)S(1)} %get-tuple-element.20) | copy-start | bytes 165892
  62.4 4.6 %collective-permute-start.2 = (bf16[2784,128]{1,0:T(8,128)(2,1)S(1)}, bf16[2784,128]{1,0:T(8,128)(2,1)S(1)}, u32[]{:S(2)}, u32[]{:S(2)}) collective-permute-start(bf16[2784,128]{1,0:T(8,128)(2,1)S(1)} %get-tuple-element.21), channel_id=1, source_target_pairs={{0,16},{16,0},{1,17},{17,1},{2,18},{18,2},{3,19},{19,3},{4,20},{20... | collective-permute-start | bytes 2138120 | tf_op jit(solution)/shard_map/ppermute | solution.py:19
  68.2 0.9 copy-start.5
  69.1 11.0 %copy-start.4 = (bf16[2560,256]{1,0:T(8,128)(2,1)S(1)}, bf16[2560,256]{1,0:T(8,128)(2,1)}, u32[]{:S(2)}) copy-start(bf16[2560,256]{1,0:T(8,128)(2,1)} %copy-done.2) | copy-start | bytes 3932164
  69.1 37.7 %all-to-all-start.1 = ((bf16[16,176,128]{2,1,0:T(8,128)(2,1)}), bf16[16,176,128]{2,1,0:T(8,128)(2,1)}, u32[]{:S(2)}, u32[]{:S(2)}) async-start(bf16[16,176,128]{2,1,0:T(8,128)(2,1)} %shard_map.95), calls=%async_computation.1 | async-start | bytes 1441792 | tf_op jit(solution)/shard_map/all_to_all | solution.py:210
  80.1 0.9 copy-start.8
  82.8 32.7 %collective-permute-start.3 = (bf16[2,216,640]{2,1,0:T(8,128)(2,1)}, bf16[2,216,640]{2,1,0:T(8,128)(2,1)S(1)}, u32[]{:S(2)}, u32[]{:S(2)}) collective-permute-start(bf16[2,216,640]{2,1,0:T(8,128)(2,1)} %get-tuple-element.26), channel_id=1, source_target_pairs={{0,256},{128,384},{256,0},{384,128},{1,257},{129,385},{257,1},{385... | collective-permute-start | bytes 1658888 | tf_op jit(solution)/shard_map/ppermute | solution.py:27
  84.8 30.7 %collective-permute-start.4 = (bf16[2,216,640]{2,1,0:T(8,128)(2,1)}, bf16[2,216,640]{2,1,0:T(8,128)(2,1)S(1)}, u32[]{:S(2)}, u32[]{:S(2)}) collective-permute-start(bf16[2,216,640]{2,1,0:T(8,128)(2,1)} %get-tuple-element.27), channel_id=1, source_target_pairs={{0,128},{128,256},{256,384},{384,0},{1,129},{129,257},{257,385},{3... | collective-permute-start | bytes 1658888 | tf_op jit(solution)/shard_map/ppermute | solution.py:27
  88.1 27.5 %collective-permute-start.5 = (bf16[2,216,640]{2,1,0:T(8,128)(2,1)}, bf16[2,216,640]{2,1,0:T(8,128)(2,1)}, u32[]{:S(2)}, u32[]{:S(2)}) collective-permute-start(bf16[2,216,640]{2,1,0:T(8,128)(2,1)} %get-tuple-element.28), channel_id=1, source_target_pairs={{0,384},{128,0},{256,128},{384,256},{1,385},{129,1},{257,129},{385... | collective-permute-start | bytes 1658888 | tf_op jit(solution)/shard_map/ppermute | solution.py:27
  118.0 27.9 %slice-start = ((bf16[2784,128]{1,0:T(8,128)(2,1)}), bf16[216,128]{1,0:T(8,128)(2,1)S(1)}, s32[]{:S(2)}) async-start(bf16[2784,128]{1,0:T(8,128)(2,1)} %copy-done.5), calls=%async_computation.3 | async-start | bytes 110592 | tf_op jit(solution)/shard_map/slice | solution.py:198
  118.0 27.9 %copy-start.10 = (bf16[216,128]{1,0:T(8,128)(2,1)S(1)}, bf16[216,128]{1,0:T(8,128)(2,1)}, u32[]{:S(2)}) copy-start(bf16[216,128]{1,0:T(8,128)(2,1)} %copy-done.9) | copy-start | bytes 165892
  118.0 29.2 %all-to-all-start.2 = ((bf16[8,80,432]{2,1,0:T(8,128)(2,1)}), bf16[8,80,432]{2,1,0:T(8,128)(2,1)S(1)}, u32[]{:S(2)}, u32[]{:S(2)}) async-start(bf16[8,80,432]{2,1,0:T(8,128)(2,1)} %bitcast.8), calls=%async_computation.2 | async-start | bytes 1310720 | tf_op jit(solution)/shard_map/all_to_all | solution.py:234
  142.1 4.5 %collective-permute-start.6 = (f32[160]{0:T(256)S(1)}, f32[160]{0:T(256)S(1)}, u32[]{:S(2)}, u32[]{:S(2)}) collective-permute-start(f32[160]{0:T(256)S(1)} %psum.15), channel_id=1, source_target_pairs={{0,16},{16,0},{1,17},{17,1},{2,18},{18,2},{3,19},{19,3},{4,20},{20... | collective-permute-start | bytes 1928 | tf_op jit(solution)/shard_map/ppermute | solution.py:19

commit v10 on v9

--- a/solution.py
+++ b/solution.py
@@ -8,6 +8,7 @@
 BF = jnp.bfloat16
 F32 = jnp.float32
 NX, NZ, NC, NH = 4, 4, 2, 2
+ANY = pl.BlockSpec(memory_space=pl.ANY)
 VMEM = pl.BlockSpec(memory_space=pltpu.VMEM)
 SMEM = pl.BlockSpec(memory_space=pltpu.SMEM)
 PARAMS = pltpu.CompilerParams(vmem_limit_bytes=14 * 1024 * 1024)
@@ -53,17 +54,40 @@
 
 
 def forward_kernel(
-    normed_ref, upstream_ref, weight_ref, hidden_ref, back_ref, own_ref, other_ref
+    normed_from,
+    upstream_from,
+    weight_ref,
+    hidden_ref,
+    back_ref,
+    own_ref,
+    other_ref,
+    normed_ref,
+    upstream_ref,
+    sems,
 ):
     size = weight_ref.shape[2] // 2
     tokens = own_ref.shape[1]
     width = own_ref.shape[0]
+    strip = width // NX
+    fetches = [
+        pltpu.make_async_copy(
+            normed_from.at[pl.ds(index * strip, strip)],
+            normed_ref.at[pl.ds(index * strip, strip)],
+            sems.at[index],
+        )
+        for index in range(NX)
+    ]
+    fetches.append(pltpu.make_async_copy(upstream_from, upstream_ref, sems.at[NX]))
+    for fetch in fetches:
+        fetch.start()
 
     def piece(index, which):
         return weight_ref[index, :, which * size : (which + 1) * size]
 
     gate_pre, up_pre = 0.0, 0.0
     for index in range(NX * NC):
+        if index % NC == 0:
+            fetches[index // NC].wait()
         rows = normed_ref[pl.ds(index * size, size), :]
         gate_pre += jnp.dot(piece(index, 0), rows, preferred_element_type=F32)
         up_pre += jnp.dot(piece(index, 1), rows, preferred_element_type=F32)
@@ -76,6 +100,7 @@
         [hidden[:, tokens:], jnp.zeros((extra - hidden.shape[0], tokens), F32)], axis=0
     )
     other_ref[width : width + extra, :] = riding.astype(BF)
+    fetches[NX].wait()
     upstream = upstream_ref[...].astype(F32)
     back_up = (upstream * activated).astype(BF)
     back_gate = (upstream * up_pre * sigmoid * (1.0 + gate_pre * (1.0 - sigmoid))).astype(BF)
@@ -99,8 +124,17 @@
             outs[index][which] = term.astype(outs[index].dtype)
 
 
-def blocks_kernel(own_ref, other_ref, x_ref, root_ref, gain_ref, out_ref):
+def blocks_kernel(
+    core_ref, own_ref, other_ref, x_ref, root_ref, gain_ref, mine_ref, out_ref, hidden_ref
+):
     width, tokens = own_ref.shape
+    half = mine_ref.shape[0]
+    mine = mine_ref[...].astype(F32)
+    theirs = other_ref[width:, :].astype(F32)[:half]
+    first = core_ref[0] == 0
+    hidden_ref[...] = jnp.concatenate(
+        [jnp.where(first, mine, theirs), jnp.where(first, theirs, mine)], axis=0
+    ).astype(BF)
     size = width // (NX * NZ)
     root = root_ref[...]
     total = jnp.zeros((size, tokens), F32)
@@ -133,11 +167,12 @@
         out_ref[:, which * half : (which + 1) * half] = total.T.astype(BF)
 
 
-def call(kernel, outs, specs):
+def call(kernel, outs, specs, scratch=()):
     return pl.pallas_call(
         kernel,
         out_shape=outs,
         in_specs=specs,
+        scratch_shapes=scratch,
         out_specs=jax.tree.map(lambda _: VMEM, outs),
         compiler_params=PARAMS,
     )
@@ -157,11 +192,6 @@
     features = width // n_dp
     column_rows = rows * NZ * NC
 
-    def ordered(own, other, axis):
-        return jnp.where(
-            first, jnp.concatenate([own, other], axis), jnp.concatenate([other, own], axis)
-        )
-
     def halves(value, axis):
         low, high = jnp.split(value, 2, axis)
         return jnp.where(first, low, high), jnp.where(first, high, low)
@@ -192,10 +222,14 @@
             shape((width, tokens), F32),
             shape((width + riding, tokens), BF),
         ),
-        [VMEM] * 3,
+        [ANY, ANY, VMEM],
+        [
+            pltpu.VMEM((width, 2 * tokens), BF),
+            pltpu.VMEM((half, 2 * tokens), BF),
+            pltpu.SemaphoreType.DMA((NX + 1,)),
+        ],
     )(normed, upstream_pair, weight)
     part_other = swap_core(part_other)
-    hidden = ordered(hidden_own, part_other[width : width + half], 0).T
     terms = call(
         gradient_kernel,
         tuple(shape((2, half, column_rows), F32 if index == 0 else BF) for index in range(NX)),
@@ -204,9 +238,20 @@
     travelling = [shift_x(terms[steps], steps) for steps in (2, 1, 3)]
 
     spare = 16
-    sending = call(blocks_kernel, shape((n_dp, features + spare, tokens), BF), [VMEM] * 5)(
-        part_own, part_other, inputs_t[:, :tokens], root_mean[:, :tokens], gain_wide
-    )
+    sending, hidden = call(
+        blocks_kernel,
+        (shape((n_dp, features + spare, tokens), BF), shape((columns, tokens), BF)),
+        [SMEM] + [VMEM] * 6,
+    )(
+        lax.axis_index("c").astype(jnp.int32).reshape(1),
+        part_own,
+        part_other,
+        inputs_t[:, :tokens],
+        root_mean[:, :tokens],
+        gain_wide,
+        hidden_own,
+    )
+    hidden = hidden.T
     got = lax.all_to_all(sending, ("y", "h"), 0, 0, tiled=True)
     totals = jnp.sum(got.astype(F32), axis=0)
     own_sums = totals[:features]
@@ -223,9 +268,9 @@
         .T
     )
     gain_part = jnp.sum(own_sums * unit_slice, axis=1)
-    gain_part = lax.psum(gain_part, "x")
+    gain_part = lax.psum(gain_part, "z")
     gain_part, travelling = lax.optimization_barrier((gain_part, travelling))
-    grad_gain = lax.psum(gain_part, "z")
+    grad_gain = lax.psum(gain_part, "x")
     grad_gain = grad_gain + swap_core(grad_gain)
 
     column_sum = call(column_kernel, shape((column_rows, columns), BF), [VMEM] * 4)(

time: 149 us -> 148 us (level)
  blocking collectives: 41.2 us -> 34.1 us
  waiting for transfers between devices: 35.1 us -> 41 us
  Pallas kernels: 8.07 us -> 9.57 us
    psum x2, blocking collectives: 23 us -> 15.9 us  [the longest x1 9.09 us: per_device(): gain_part = lax.psum(gain_part, 'z')]
    all_to_all x1, waiting for transfers between devices: 0.01 us -> 5.19 us  [per_device(): lax.all_to_all(column_sum.reshape(NC * NZ, rows, columns), ('c', 'z'), 0,...]
    unnamed x27 -> x21, local copies, waits for them, and re-layouts: 6.67 us -> 5.79 us
  transfers between devices with their start and end apart: 10 -> 10, of which waited for: 5 -> 6; matrix products, arithmetic and copies ran while one was open for 4% -> 3% of each run, Pallas kernels for 2% -> 2%
where the time goes in v10:
time: 148 us; the launch traced here: 147 us
  starting transfers between devices  46.4 us (31%)
  waiting for transfers between devices  41 us (28%)
  blocking collectives  34.1 us (23%)
  Pallas kernels  9.57 us (6%)
  local copies, waits for them, and re-layouts  8.37 us (6%)
  other arithmetic  6.39 us (4%)
    all_gather x1, blocking collectives, per_device(): lax.all_gather(jnp.concatenate([w_gate, w_up], 1), 'z', axis=0, tiled=True)  18.1 us
    all_to_all x1, waiting for transfers between devices, per_device(): weight = lax.all_to_all(copies, ('x', 'c'), 0, 0, tiled=True)  17.1 us
    all_to_all x1, waiting for transfers between devices, per_device(): got = lax.all_to_all(sending, ('y', 'h'), 0, 0, tiled=True)  15.4 us
    ppermute x4, starting transfers between devices, swap(): return lax.ppermute(value, axis, [(0, 1), (1, 0)])  11.2 us
    all_to_all x1, starting transfers between devices, per_device(): got = lax.all_to_all(sending, ('y', 'h'), 0, 0, tiled=True)  10.9 us
    psum x1, blocking collectives, per_device(): gain_part = lax.psum(gain_part, 'z')  9.09 us
    all_to_all x1, starting transfers between devices, per_device(): weight = lax.all_to_all(copies, ('x', 'c'), 0, 0, tiled=True)  8.54 us
    ppermute x3, starting transfers between devices, shift_x(): return lax.ppermute(value, 'x', [(x, (x + steps) % NX) for x in range(NX)])  8.48 us
  transfers between devices with their start and end apart: 10, of which 6 were waited for; matrix products, arithmetic and copies ran while one was open for 3% of the time, Pallas kernels for 2%

profile of v10, /device:TPU:1, one launch (start us, length us, event | category | flops | bytes accessed | tf_op | source)
XLA Modules:
  0.0 146.6 jit_solution(4897996973911403276)
XLA Ops:
  0.6 1.0 pad_maximum_fusion.3
  1.7 18.1 %all_gather.3 = bf16[320,864]{1,0:T(8,128)(2,1)S(1)} all-gather(bf16[80,864]{1,0:T(8,128)(2,1)S(1)} %pad_maximum_fusion.3), channel_id=1, replica_groups=mesh['x'=4,'z'=4,'c'=2,'y'=8,'h'=2] {'z'}, dimensions={0}, use_global_device_ids=true | all-gather | bytes 691200 | tf_op jit(solution)/shard_map/all_gather | solution.py:199
  19.8 0.4 copy.19
  20.2 0.1 fusion.3
  20.2 0.2 pad_maximum_fusion
  20.4 1.5 %broadcast_in_dim.5 = bf16[4,2,216,640]{3,2,1,0:T(8,128)(2,1)} broadcast(bf16[2,216,640]{2,1,0:T(8,128)(2,1)S(1)} %bitcast.29), dimensions={1,2,3} | broadcast | bytes 2764800 | tf_op jit(solution)/shard_map/broadcast_in_dim | solution.py:201
  22.0 8.5 %all-to-all-start = ((bf16[8,216,640]{2,1,0:T(8,128)(2,1)}), bf16[8,216,640]{2,1,0:T(8,128)(2,1)S(1)}, u32[]{:S(2)}, u32[]{:S(2)}) async-start(bf16[8,216,640]{2,1,0:T(8,128)(2,1)} %bitcast.27), calls=%async_computation | async-start | bytes 4423680 | tf_op jit(solution)/shard_map/all_to_all | solution.py:204
  30.5 0.3 copy.18
  30.8 2.0 %collective-permute-start = (bf16[128,2560]{0,1:T(8,128)(2,1)S(1)}, bf16[128,2560]{0,1:T(8,128)(2,1)S(1)}, u32[]{:S(2)}, u32[]{:S(2)}) collective-permute-start(bf16[128,2560]{0,1:T(8,128)(2,1)S(1)} %copy.18), channel_id=1, source_target_pairs={{0,16},{16,0},{1,17},{17,1},{2,18},{18,2},{3,19},{19,3},{4,20},{20... | collective-permute-start | bytes 1966088 | tf_op jit(solution)/shard_map/ppermute | solution.py:20
  32.9 0.9 broadcast_select_fusion.1
  33.7 2.3 %collective-permute-start.1 = (bf16[216,128]{1,0:T(8,128)(2,1)S(1)}, bf16[216,128]{1,0:T(8,128)(2,1)S(1)}, u32[]{:S(2)}, u32[]{:S(2)}) collective-permute-start(bf16[216,128]{1,0:T(8,128)(2,1)S(1)} %get-tuple-element.46), channel_id=1, source_target_pairs={{0,16},{16,0},{1,17},{17,1},{2,18},{18,2},{3,19},{19,3},{4,20},{20... | collective-permute-start | bytes 165896 | tf_op jit(solution)/shard_map/ppermute | solution.py:20
  36.1 0.9 collective-permute-done.1
  36.9 0.7 pad_maximum_fusion.4.upstream_from
  37.6 0.0 collective-permute-done
  37.6 0.1 maximum_bitcast_fusion.x_ref
  37.7 0.6 copy-done.9
  38.3 0.4 broadcast_in_dim.4.gain_ref
  38.7 0.7 copy-done
  39.4 0.6 shard_map.92
  39.9 1.1 copy-done.2
  41.0 17.1 %all-to-all-done.weight_ref = bf16[8,216,640]{2,1,0:T(8,128)(2,1)S(1)} async-done(((bf16[8,216,640]{2,1,0:T(8,128)(2,1)}), bf16[8,216,640]{2,1,0:T(8,128)(2,1)S(1)}, u32[]{:S(2)}, u32[]{:S(2)}) %all-to-all-start) | async-done | bytes 2211872 | tf_op jit(solution)/shard_map/all_to_all | solution.py:204
  58.1 1.3 copy-done.3
  59.4 0.9 copy-done.5
  60.3 3.5 %shard_map.93 = (bf16[216,128]{1,0:T(8,128)(2,1)S(1)}, bf16[2,216,256]{2,1,0:T(8,128)(2,1)S(1)}, f32[2560,128]{1,0:T(8,128)S(1)}, bf16[2784,128]{1,0:T(8,128)(2,1)S(1)}) custom-call(bf16[2560,256]{1,0:T(8,128)(2,1)S(1)} %copy-done.3, bf16[216,256]{1,0:T(8,128)(2,1)S(1)} %copy-done.5, bf16[8,216,640]{2,1,0:T(8,128)(2,1)S(1)} %all-to-all-done.weight_ref), custom_call_target="tpu_custom_call" | custom-call | tf_op jit(solution)/shard_map/pallas_call | solution.py:217
  63.8 2.8 %collective-permute-start.2 = (bf16[2784,128]{1,0:T(8,128)(2,1)S(1)}, bf16[2784,128]{1,0:T(8,128)(2,1)S(1)}, u32[]{:S(2)}, u32[]{:S(2)}) collective-permute-start(bf16[2784,128]{1,0:T(8,128)(2,1)S(1)} %get-tuple-element.23), channel_id=1, source_target_pairs={{0,16},{16,0},{1,17},{17,1},{2,18},{18,2},{3,19},{19,3},{4,20},{20... | collective-permute-start | bytes 2138120 | tf_op jit(solution)/shard_map/ppermute | solution.py:20
  66.7 1.7 %collective-permute-done.2.other_ref = bf16[2784,128]{1,0:T(8,128)(2,1)S(1)} collective-permute-done((bf16[2784,128]{1,0:T(8,128)(2,1)S(1)}, bf16[2784,128]{1,0:T(8,128)(2,1)S(1)}, u32[]{:S(2)}, u32[]{:S(2)}) %collective-permute-start.2) | collective-permute-done | bytes 712736 | tf_op jit(solution)/shard_map/ppermute | solution.py:20
  68.4 1.3 shard_map.94
  69.7 10.9 %all-to-all-start.1 = ((bf16[16,176,128]{2,1,0:T(8,128)(2,1)}), bf16[16,176,128]{2,1,0:T(8,128)(2,1)}, u32[]{:S(2)}, u32[]{:S(2)}) async-start(bf16[16,176,128]{2,1,0:T(8,128)(2,1)} %get-tuple-element.29), calls=%async_computation.1 | async-start | bytes 1441792 | tf_op jit(solution)/shard_map/all_to_all | solution.py:255
  80.7 0.1 dynamic_slice.7
  80.8 0.9 copy-done.7
  81.7 1.8 %shard_map.95 = (f32[2,216,640]{2,1,0:T(8,128)S(1)}, bf16[2,216,640]{2,1,0:T(8,128)(2,1)}, bf16[2,216,640]{2,1,0:T(8,128)(2,1)}, bf16[2,216,640]{2,1,0:T(8,128)(2,1)}) custom-call(s32[1]{0:T(128)} %bitcast.7.spot_ref, bf16[2560,256]{1,0:T(8,128)(2,1)S(1)} %copy-done.4, bf16[2,216,256]{2,1,0:T(8,128)(2,1)S(1)} %copy-done.7), custom_call_target="tpu_custom_call" | custom-call | tf_op jit(solution)/shard_map/pallas_call | solution.py:233
  83.5 2.0 %collective-permute-start.3 = (bf16[2,216,640]{2,1,0:T(8,128)(2,1)}, bf16[2,216,640]{2,1,0:T(8,128)(2,1)S(1)}, u32[]{:S(2)}, u32[]{:S(2)}) collective-permute-start(bf16[2,216,640]{2,1,0:T(8,128)(2,1)} %get-tuple-element.30), channel_id=1, source_target_pairs={{0,256},{128,384},{256,0},{384,128},{1,257},{129,385},{257,1},{385... | collective-permute-start | bytes 1658888 | tf_op jit(solution)/shard_map/ppermute | solution.py:28
  85.5 3.3 %collective-permute-start.4 = (bf16[2,216,640]{2,1,0:T(8,128)(2,1)}, bf16[2,216,640]{2,1,0:T(8,128)(2,1)S(1)}, u32[]{:S(2)}, u32[]{:S(2)}) collective-permute-start(bf16[2,216,640]{2,1,0:T(8,128)(2,1)} %get-tuple-element.31), channel_id=1, source_target_pairs={{0,128},{128,256},{256,384},{384,0},{1,129},{129,257},{257,385},{3... | collective-permute-start | bytes 1658888 | tf_op jit(solution)/shard_map/ppermute | solution.py:28
  88.8 3.2 %collective-permute-start.5 = (bf16[2,216,640]{2,1,0:T(8,128)(2,1)}, bf16[2,216,640]{2,1,0:T(8,128)(2,1)}, u32[]{:S(2)}, u32[]{:S(2)}) collective-permute-start(bf16[2,216,640]{2,1,0:T(8,128)(2,1)} %get-tuple-element.32), channel_id=1, source_target_pairs={{0,384},{128,0},{256,128},{384,256},{1,385},{129,1},{257,129},{385... | collective-permute-start | bytes 1658888 | tf_op jit(solution)/shard_map/ppermute | solution.py:28
  92.0 15.4 %all-to-all-done.1 = bf16[16,176,128]{2,1,0:T(8,128)(2,1)} async-done(((bf16[16,176,128]{2,1,0:T(8,128)(2,1)}), bf16[16,176,128]{2,1,0:T(8,128)(2,1)}, u32[]{:S(2)}, u32[]{:S(2)}) %all-to-all-start.1) | async-done | bytes 720928 | tf_op jit(solution)/shard_map/all_to_all | solution.py:255
  107.4 1.2 convert_reduce_fusion
  108.6 0.8 fusion
  109.4 9.1 %psum.14 = f32[160]{0:T(256)S(1)} all-reduce(f32[160]{0:T(256)S(1)} %get-tuple-element.38), channel_id=1, replica_groups=mesh['x'=4,'z'=4,'c'=2,'y'=8,'h'=2] {'z'}, use_global_device_ids=true, to_apply=%region_2.3 | all-reduce | flops 160 | bytes 1280 | tf_op jit(solution)/shard_map/psum | solution.py:271
  118.5 2.4 %shard_map.96 = bf16[640,432]{1,0:T(8,128)(2,1)} custom-call(f32[2,216,640]{2,1,0:T(8,128)S(1)} %get-tuple-element.28.own_ref, bf16[2,216,640]{2,1,0:T(8,128)(2,1)S(1)} %collective-permute-done.3.first_ref, bf16[2,216,640]{2,1,0:T(8,128)(2,1)S(1)} %collective-permute-done.4.second_ref, bf16[2,216,640]{2,1,0:T(8,128)(2,1)} %collective-permute-done.5.third_ref), custom_call_target="tpu_custom_call" | custom-call | tf_op jit(solution)/shard_map/pallas_call | solution.py:276
  120.9 7.2 %all-to-all-start.2 = ((bf16[8,80,432]{2,1,0:T(8,128)(2,1)}), bf16[8,80,432]{2,1,0:T(8,128)(2,1)S(1)}, u32[]{:S(2)}, u32[]{:S(2)}) async-start(bf16[8,80,432]{2,1,0:T(8,128)(2,1)} %bitcast.9), calls=%async_computation.2 | async-start | bytes 1310720 | tf_op jit(solution)/shard_map/all_to_all | solution.py:279
  128.1 6.9 %psum.15 = f32[160]{0:T(256)S(1)} all-reduce(f32[160]{0:T(256)S(1)} %psum.14), channel_id=1, replica_groups=mesh['x'=4,'z'=4,'c'=2,'y'=8,'h'=2] {'x'}, use_global_device_ids=true, to_apply=%region_4.5 | all-reduce | flops 160 | bytes 1280 | tf_op jit(solution)/shard_map/psum | solution.py:273
  135.0 4.1 %collective-permute-start.6 = (f32[160]{0:T(256)S(1)}, f32[160]{0:T(256)S(1)}, u32[]{:S(2)}, u32[]{:S(2)}) collective-permute-start(f32[160]{0:T(256)S(1)} %psum.15), channel_id=1, source_target_pairs={{0,16},{16,0},{1,17},{17,1},{2,18},{18,2},{3,19},{19,3},{4,20},{20... | collective-permute-start | bytes 1928 | tf_op jit(solution)/shard_map/ppermute | solution.py:20
  139.0 0.8 collective-permute-done.6
  139.8 0.6 add.26
  140.4 5.2 %all-to-all-done.2 = bf16[8,80,432]{2,1,0:T(8,128)(2,1)S(1)} async-done(((bf16[8,80,432]{2,1,0:T(8,128)(2,1)}), bf16[8,80,432]{2,1,0:T(8,128)(2,1)S(1)}, u32[]{:S(2)}, u32[]{:S(2)}) %all-to-all-start.2) | async-done | bytes 552992 | tf_op jit(solution)/shard_map/all_to_all | solution.py:279
  145.6 0.1 convert_reduce_fusion.1
  145.7 0.1 slice_bitcast_fusion.1
  145.8 0.9 pad_maximum_fusion.1
  (20 shorter events, 0.1 us)
Async XLA Ops:
  22.0 8.5 %copy-start.8 = (bf16[128,2560]{1,0:T(8,128)(2,1)S(1)}, bf16[128,2560]{1,0:T(8,128)(2,1)}, u32[]{:S(2)}) copy-start(bf16[128,2560]{1,0:T(8,128)(2,1)} %param.5) | copy-start | bytes 1966084
  22.0 36.1 %all-to-all-start = ((bf16[8,216,640]{2,1,0:T(8,128)(2,1)}), bf16[8,216,640]{2,1,0:T(8,128)(2,1)S(1)}, u32[]{:S(2)}, u32[]{:S(2)}) async-start(bf16[8,216,640]{2,1,0:T(8,128)(2,1)} %bitcast.27), calls=%async_computation | async-start | bytes 4423680 | tf_op jit(solution)/shard_map/all_to_all | solution.py:204
  30.8 6.8 %collective-permute-start = (bf16[128,2560]{0,1:T(8,128)(2,1)S(1)}, bf16[128,2560]{0,1:T(8,128)(2,1)S(1)}, u32[]{:S(2)}, u32[]{:S(2)}) collective-permute-start(bf16[128,2560]{0,1:T(8,128)(2,1)S(1)} %copy.18), channel_id=1, source_target_pairs={{0,16},{16,0},{1,17},{17,1},{2,18},{18,2},{3,19},{19,3},{4,20},{20... | collective-permute-start | bytes 1966088 | tf_op jit(solution)/shard_map/ppermute | solution.py:20
  33.7 3.2 %collective-permute-start.1 = (bf16[216,128]{1,0:T(8,128)(2,1)S(1)}, bf16[216,128]{1,0:T(8,128)(2,1)S(1)}, u32[]{:S(2)}, u32[]{:S(2)}) collective-permute-start(bf16[216,128]{1,0:T(8,128)(2,1)S(1)} %get-tuple-element.46), channel_id=1, source_target_pairs={{0,16},{16,0},{1,17},{17,1},{2,18},{18,2},{3,19},{19,3},{4,20},{20... | collective-permute-start | bytes 165896 | tf_op jit(solution)/shard_map/ppermute | solution.py:20
  37.6 0.7 copy-start.9
  38.3 1.1 copy-start
  39.9 1.1 copy-start.2
  58.1 1.3 copy-start.3
  59.4 0.9 copy-start.5
  60.3 6.3 %copy-start.1 = (bf16[2560,256]{1,0:T(8,128)(2,1)S(1)}, bf16[2560,256]{1,0:T(8,128)(2,1)}, u32[]{:S(2)}) copy-start(bf16[2560,256]{1,0:T(8,128)(2,1)} %copy-done) | copy-start | bytes 3932164
  63.8 5.9 %copy-start.6 = (bf16[2,216,256]{2,1,0:T(8,128)(2,1)}, bf16[2,216,256]{2,1,0:T(8,128)(2,1)S(1)}, u32[]{:S(2)}) copy-start(bf16[2,216,256]{2,1,0:T(8,128)(2,1)S(1)} %get-tuple-element.27.back_ref) | copy-start | bytes 663556
  63.8 4.6 %collective-permute-start.2 = (bf16[2784,128]{1,0:T(8,128)(2,1)S(1)}, bf16[2784,128]{1,0:T(8,128)(2,1)S(1)}, u32[]{:S(2)}, u32[]{:S(2)}) collective-permute-start(bf16[2784,128]{1,0:T(8,128)(2,1)S(1)} %get-tuple-element.23), channel_id=1, source_target_pairs={{0,16},{16,0},{1,17},{17,1},{2,18},{18,2},{3,19},{19,3},{4,20},{20... | collective-permute-start | bytes 2138120 | tf_op jit(solution)/shard_map/ppermute | solution.py:20
  69.7 11.0 %copy-start.4 = (bf16[2560,256]{1,0:T(8,128)(2,1)S(1)}, bf16[2560,256]{1,0:T(8,128)(2,1)}, u32[]{:S(2)}) copy-start(bf16[2560,256]{1,0:T(8,128)(2,1)} %copy-done.2) | copy-start | bytes 3932164
  69.7 37.7 %all-to-all-start.1 = ((bf16[16,176,128]{2,1,0:T(8,128)(2,1)}), bf16[16,176,128]{2,1,0:T(8,128)(2,1)}, u32[]{:S(2)}, u32[]{:S(2)}) async-start(bf16[16,176,128]{2,1,0:T(8,128)(2,1)} %get-tuple-element.29), calls=%async_computation.1 | async-start | bytes 1441792 | tf_op jit(solution)/shard_map/all_to_all | solution.py:255
  80.8 0.9 copy-start.7
  83.5 35.0 %collective-permute-start.3 = (bf16[2,216,640]{2,1,0:T(8,128)(2,1)}, bf16[2,216,640]{2,1,0:T(8,128)(2,1)S(1)}, u32[]{:S(2)}, u32[]{:S(2)}) collective-permute-start(bf16[2,216,640]{2,1,0:T(8,128)(2,1)} %get-tuple-element.30), channel_id=1, source_target_pairs={{0,256},{128,384},{256,0},{384,128},{1,257},{129,385},{257,1},{385... | collective-permute-start | bytes 1658888 | tf_op jit(solution)/shard_map/ppermute | solution.py:28
  85.5 33.0 %collective-permute-start.4 = (bf16[2,216,640]{2,1,0:T(8,128)(2,1)}, bf16[2,216,640]{2,1,0:T(8,128)(2,1)S(1)}, u32[]{:S(2)}, u32[]{:S(2)}) collective-permute-start(bf16[2,216,640]{2,1,0:T(8,128)(2,1)} %get-tuple-element.31), channel_id=1, source_target_pairs={{0,128},{128,256},{256,384},{384,0},{1,129},{129,257},{257,385},{3... | collective-permute-start | bytes 1658888 | tf_op jit(solution)/shard_map/ppermute | solution.py:28
  88.8 29.7 %collective-permute-start.5 = (bf16[2,216,640]{2,1,0:T(8,128)(2,1)}, bf16[2,216,640]{2,1,0:T(8,128)(2,1)}, u32[]{:S(2)}, u32[]{:S(2)}) collective-permute-start(bf16[2,216,640]{2,1,0:T(8,128)(2,1)} %get-tuple-element.32), channel_id=1, source_target_pairs={{0,384},{128,0},{256,128},{384,256},{1,385},{129,1},{257,129},{385... | collective-permute-start | bytes 1658888 | tf_op jit(solution)/shard_map/ppermute | solution.py:28
  120.9 24.7 %all-to-all-start.2 = ((bf16[8,80,432]{2,1,0:T(8,128)(2,1)}), bf16[8,80,432]{2,1,0:T(8,128)(2,1)S(1)}, u32[]{:S(2)}, u32[]{:S(2)}) async-start(bf16[8,80,432]{2,1,0:T(8,128)(2,1)} %bitcast.9), calls=%async_computation.2 | async-start | bytes 1310720 | tf_op jit(solution)/shard_map/all_to_all | solution.py:279
  135.0 4.9 %collective-permute-start.6 = (f32[160]{0:T(256)S(1)}, f32[160]{0:T(256)S(1)}, u32[]{:S(2)}, u32[]{:S(2)}) collective-permute-start(f32[160]{0:T(256)S(1)} %psum.15), channel_id=1, source_target_pairs={{0,16},{16,0},{1,17},{17,1},{2,18},{18,2},{3,19},{19,3},{4,20},{20... | collective-permute-start | bytes 1928 | tf_op jit(solution)/shard_map/ppermute | solution.py:20

commit v11 on v9

--- a/solution.py
+++ b/solution.py
@@ -99,8 +99,17 @@
             outs[index][which] = term.astype(outs[index].dtype)
 
 
-def blocks_kernel(own_ref, other_ref, x_ref, root_ref, gain_ref, out_ref):
+def blocks_kernel(
+    core_ref, own_ref, other_ref, x_ref, root_ref, gain_ref, mine_ref, out_ref, hidden_ref
+):
     width, tokens = own_ref.shape
+    half = mine_ref.shape[0]
+    mine = mine_ref[...].astype(F32)
+    theirs = other_ref[width:, :].astype(F32)[:half]
+    first = core_ref[0] == 0
+    hidden_ref[...] = jnp.concatenate(
+        [jnp.where(first, mine, theirs), jnp.where(first, theirs, mine)], axis=0
+    ).astype(BF)
     size = width // (NX * NZ)
     root = root_ref[...]
     total = jnp.zeros((size, tokens), F32)
@@ -157,11 +166,6 @@
     features = width // n_dp
     column_rows = rows * NZ * NC
 
-    def ordered(own, other, axis):
-        return jnp.where(
-            first, jnp.concatenate([own, other], axis), jnp.concatenate([other, own], axis)
-        )
-
     def halves(value, axis):
         low, high = jnp.split(value, 2, axis)
         return jnp.where(first, low, high), jnp.where(first, high, low)
@@ -195,7 +199,6 @@
         [VMEM] * 3,
     )(normed, upstream_pair, weight)
     part_other = swap_core(part_other)
-    hidden = ordered(hidden_own, part_other[width : width + half], 0).T
     terms = call(
         gradient_kernel,
         tuple(shape((2, half, column_rows), F32 if index == 0 else BF) for index in range(NX)),
@@ -204,29 +207,51 @@
     travelling = [shift_x(terms[steps], steps) for steps in (2, 1, 3)]
 
     spare = 16
-    sending = call(blocks_kernel, shape((n_dp, features + spare, tokens), BF), [VMEM] * 5)(
-        part_own, part_other, inputs_t[:, :tokens], root_mean[:, :tokens], gain_wide
-    )
-    got = lax.all_to_all(sending, ("y", "h"), 0, 0, tiled=True)
-    totals = jnp.sum(got.astype(F32), axis=0)
+    sending, hidden = call(
+        blocks_kernel,
+        (shape((n_dp, features + spare, tokens), BF), shape((columns, tokens), BF)),
+        [SMEM] + [VMEM] * 6,
+    )(
+        lax.axis_index("c").astype(jnp.int32).reshape(1),
+        part_own,
+        part_other,
+        inputs_t[:, :tokens],
+        root_mean[:, :tokens],
+        gain_wide,
+        hidden_own,
+    )
+    hidden = hidden.T
+    got = lax.all_to_all(
+        sending.reshape(n_dp // NH, NH * (features + spare), tokens), "y", 0, 0, tiled=True
+    )
+    y_sums = jnp.sum(got.astype(F32), axis=0).reshape(NH, features + spare, tokens)
+    root_own = root_mean[:, :tokens]
+    tokens_own = inputs_t[:, :tokens]
+    span = NH * features
+    unit_span = (
+        lax.dynamic_slice_in_dim(tokens_own, lax.axis_index("y") * span, span, 0).astype(F32)
+        / root_own
+    ).reshape(NH, features, tokens)
+    gain_part = jnp.sum(y_sums[:, :features] * unit_span, axis=2)
+    gain_part = lax.psum(gain_part, ("z", "h"))
+    gain_part, travelling = lax.optimization_barrier((gain_part, travelling))
+    low_half = lax.axis_index("h") == 0
+    gain_part = lax.psum(jnp.where(low_half, gain_part[0], gain_part[1]), "x")
+    grad_gain = gain_part + swap_core(gain_part)
+
+    totals = jnp.where(low_half, y_sums[0], y_sums[1]) + swap(
+        jnp.where(low_half, y_sums[1], y_sums[0]), "h"
+    )
     own_sums = totals[:features]
     token_totals = totals[features] + totals[features + 1] + totals[features + 2]
     start = lax.axis_index(("y", "h")) * features
     gain_slice = lax.dynamic_slice_in_dim(gain, start, features, 0)[:, None]
-    root_own = root_mean[:, :tokens]
-    unit_slice = (
-        lax.dynamic_slice_in_dim(inputs_t[:, :tokens], start, features, 0).astype(F32) / root_own
-    )
+    unit_slice = jnp.where(low_half, unit_span[0], unit_span[1])
     grad_input = (
         ((own_sums * gain_slice - unit_slice * (token_totals / width)[None, :]) / root_own)
         .astype(BF)
         .T
     )
-    gain_part = jnp.sum(own_sums * unit_slice, axis=1)
-    gain_part = lax.psum(gain_part, "x")
-    gain_part, travelling = lax.optimization_barrier((gain_part, travelling))
-    grad_gain = lax.psum(gain_part, "z")
-    grad_gain = grad_gain + swap_core(grad_gain)
 
     column_sum = call(column_kernel, shape((column_rows, columns), BF), [VMEM] * 4)(
         terms[0], *travelling

time: 149 us -> 153 us (1.027)
  blocking collectives: 41.2 us -> 47.8 us
  starting transfers between devices: 46.7 us -> 43.8 us
  waiting for transfers between devices: 35.1 us -> 37 us
    psum x2, blocking collectives: 23 us -> 29.7 us  [the longest x1 22.6 us: per_device(): gain_part = lax.psum(gain_part, ('z', 'h'))]
    all_to_all x1, starting transfers between devices: 10.9 us -> 5.16 us  [per_device(): lax.all_to_all(sending.reshape(n_dp // NH, NH * (features + spare), token...]
    all_to_all x1, waiting for transfers between devices: 0.01 us -> 5.65 us  [per_device(): lax.all_to_all(column_sum.reshape(NC * NZ, rows, columns), ('c', 'z'), 0,...]
    all_to_all x1, waiting for transfers between devices: 15.4 us -> 11 us  [per_device(): lax.all_to_all(sending.reshape(n_dp // NH, NH * (features + spare), token...]
    ppermute x4 -> x5, starting transfers between devices: 10.8 us -> 13.6 us  [swap(): return lax.ppermute(value, axis, [(0, 1), (1, 0)])]
    unnamed x27 -> x21, local copies, waits for them, and re-layouts: 6.67 us -> 5.78 us
    ppermute x4 -> x5, waiting for transfers between devices: 2.68 us -> 3.29 us  [swap(): return lax.ppermute(value, axis, [(0, 1), (1, 0)])]
  transfers between devices with their start and end apart: 10 -> 11, of which waited for: 5 -> 6; matrix products, arithmetic and copies ran while one was open for 4% -> 3% of each run, Pallas kernels for 2% -> 2%
where the time goes in v11:
time: 153 us
  blocking collectives  47.8 us (31%)
  starting transfers between devices  43.8 us (29%)
  waiting for transfers between devices  37 us (24%)
  local copies, waits for them, and re-layouts  8.37 us (5%)
  Pallas kernels  8.16 us (5%)
  other arithmetic  6.53 us (4%)
    psum x1, blocking collectives, per_device(): gain_part = lax.psum(gain_part, ('z', 'h'))  22.6 us
    all_gather x1, blocking collectives, per_device(): lax.all_gather(jnp.concatenate([w_gate, w_up], 1), 'z', axis=0, tiled=True)  18.1 us
    all_to_all x1, waiting for transfers between devices, per_device(): weight = lax.all_to_all(copies, ('x', 'c'), 0, 0, tiled=True)  17.1 us
    ppermute x5, starting transfers between devices, swap(): return lax.ppermute(value, axis, [(0, 1), (1, 0)])  13.6 us
    all_to_all x1, waiting for transfers between devices, per_device(): lax.all_to_all(sending.reshape(n_dp // NH, NH * (features + spare), token...  11 us
    all_to_all x1, starting transfers between devices, per_device(): weight = lax.all_to_all(copies, ('x', 'c'), 0, 0, tiled=True)  8.54 us
    ppermute x3, starting transfers between devices, shift_x(): return lax.ppermute(value, 'x', [(x, (x + steps) % NX) for x in range(NX)])  8.49 us
    all_to_all x1, starting transfers between devices, per_device(): lax.all_to_all(column_sum.reshape(NC * NZ, rows, columns), ('c', 'z'), 0,...  7.97 us
  transfers between devices with their start and end apart: 11, of which 6 were waited for; matrix products, arithmetic and copies ran while one was open for 3% of the time, Pallas kernels for 2%

profile of v11, /device:TPU:1, one launch (start us, length us, event | category | flops | bytes accessed | tf_op | source)
XLA Modules:
  0.0 152.5 jit_solution(5298524495929175241)
XLA Ops:
  0.6 1.0 pad_maximum_fusion.3
  1.7 18.1 %all_gather.3 = bf16[320,864]{1,0:T(8,128)(2,1)S(1)} all-gather(bf16[80,864]{1,0:T(8,128)(2,1)S(1)} %pad_maximum_fusion.3), channel_id=1, replica_groups=mesh['x'=4,'z'=4,'c'=2,'y'=8,'h'=2] {'z'}, dimensions={0}, use_global_device_ids=true | all-gather | bytes 691200 | tf_op jit(solution)/shard_map/all_gather | solution.py:173
  19.8 0.4 copy.19
  20.2 0.2 pad_maximum_fusion
  20.4 1.5 %broadcast_in_dim.5 = bf16[4,2,216,640]{3,2,1,0:T(8,128)(2,1)} broadcast(bf16[2,216,640]{2,1,0:T(8,128)(2,1)S(1)} %bitcast.34), dimensions={1,2,3} | broadcast | bytes 2764800 | tf_op jit(solution)/shard_map/broadcast_in_dim | solution.py:175
  22.0 8.5 %all-to-all-start = ((bf16[8,216,640]{2,1,0:T(8,128)(2,1)}), bf16[8,216,640]{2,1,0:T(8,128)(2,1)S(1)}, u32[]{:S(2)}, u32[]{:S(2)}) async-start(bf16[8,216,640]{2,1,0:T(8,128)(2,1)} %bitcast.31), calls=%async_computation | async-start | bytes 4423680 | tf_op jit(solution)/shard_map/all_to_all | solution.py:178
  30.5 0.3 copy.18
  30.8 2.0 %collective-permute-start = (bf16[128,2560]{0,1:T(8,128)(2,1)S(1)}, bf16[128,2560]{0,1:T(8,128)(2,1)S(1)}, u32[]{:S(2)}, u32[]{:S(2)}) collective-permute-start(bf16[128,2560]{0,1:T(8,128)(2,1)S(1)} %copy.18), channel_id=1, source_target_pairs={{0,16},{16,0},{1,17},{17,1},{2,18},{18,2},{3,19},{19,3},{4,20},{20... | collective-permute-start | bytes 1966088 | tf_op jit(solution)/shard_map/ppermute | solution.py:19
  32.9 0.9 broadcast_select_fusion.1
  33.7 2.3 %collective-permute-start.1 = (bf16[216,128]{1,0:T(8,128)(2,1)S(1)}, bf16[216,128]{1,0:T(8,128)(2,1)S(1)}, u32[]{:S(2)}, u32[]{:S(2)}) collective-permute-start(bf16[216,128]{1,0:T(8,128)(2,1)S(1)} %get-tuple-element.44), channel_id=1, source_target_pairs={{0,16},{16,0},{1,17},{17,1},{2,18},{18,2},{3,19},{19,3},{4,20},{20... | collective-permute-start | bytes 165896 | tf_op jit(solution)/shard_map/ppermute | solution.py:19
  36.1 0.9 collective-permute-done.1
  36.9 0.7 pad_maximum_fusion.4.upstream_ref
  37.6 0.1 maximum_bitcast_fusion.x_ref
  37.7 0.6 copy-done.9
  38.3 0.4 broadcast_in_dim.4.gain_ref
  38.7 0.7 copy-done
  39.4 0.6 shard_map.92
  39.9 1.1 copy-done.2
  41.0 17.1 %all-to-all-done.weight_ref = bf16[8,216,640]{2,1,0:T(8,128)(2,1)S(1)} async-done(((bf16[8,216,640]{2,1,0:T(8,128)(2,1)}), bf16[8,216,640]{2,1,0:T(8,128)(2,1)S(1)}, u32[]{:S(2)}, u32[]{:S(2)}) %all-to-all-start) | async-done | bytes 2211872 | tf_op jit(solution)/shard_map/all_to_all | solution.py:178
  58.1 1.3 copy-done.3
  59.4 0.9 copy-done.5
  60.3 2.1 %shard_map.93 = (bf16[216,128]{1,0:T(8,128)(2,1)S(1)}, bf16[2,216,256]{2,1,0:T(8,128)(2,1)S(1)}, f32[2560,128]{1,0:T(8,128)S(1)}, bf16[2784,128]{1,0:T(8,128)(2,1)S(1)}) custom-call(bf16[2560,256]{1,0:T(8,128)(2,1)S(1)} %copy-done.3, bf16[216,256]{1,0:T(8,128)(2,1)S(1)} %copy-done.5, bf16[8,216,640]{2,1,0:T(8,128)(2,1)S(1)} %all-to-all-done.weight_ref), custom_call_target="tpu_custom_call" | custom-call | tf_op jit(solution)/shard_map/pallas_call | solution.py:191
  62.4 2.8 %collective-permute-start.2 = (bf16[2784,128]{1,0:T(8,128)(2,1)S(1)}, bf16[2784,128]{1,0:T(8,128)(2,1)S(1)}, u32[]{:S(2)}, u32[]{:S(2)}) collective-permute-start(bf16[2784,128]{1,0:T(8,128)(2,1)S(1)} %get-tuple-element.23), channel_id=1, source_target_pairs={{0,16},{16,0},{1,17},{17,1},{2,18},{18,2},{3,19},{19,3},{4,20},{20... | collective-permute-start | bytes 2138120 | tf_op jit(solution)/shard_map/ppermute | solution.py:19
  65.3 1.7 %collective-permute-done.2.other_ref = bf16[2784,128]{1,0:T(8,128)(2,1)S(1)} collective-permute-done((bf16[2784,128]{1,0:T(8,128)(2,1)S(1)}, bf16[2784,128]{1,0:T(8,128)(2,1)S(1)}, u32[]{:S(2)}, u32[]{:S(2)}) %collective-permute-start.2) | collective-permute-done | bytes 712736 | tf_op jit(solution)/shard_map/ppermute | solution.py:19
  67.0 1.3 shard_map.94
  68.3 5.2 %all-to-all-start.1 = ((bf16[8,352,128]{2,1,0:T(8,128)(2,1)}), bf16[8,352,128]{2,1,0:T(8,128)(2,1)}, u32[]{:S(2)}, u32[]{:S(2)}) async-start(bf16[8,352,128]{2,1,0:T(8,128)(2,1)} %bitcast.8), calls=%async_computation.1 | async-start | bytes 1441792 | tf_op jit(solution)/shard_map/all_to_all | solution.py:224
  73.5 0.9 copy-done.7
  74.4 1.8 %shard_map.95 = (f32[2,216,640]{2,1,0:T(8,128)S(1)}, bf16[2,216,640]{2,1,0:T(8,128)(2,1)}, bf16[2,216,640]{2,1,0:T(8,128)(2,1)}, bf16[2,216,640]{2,1,0:T(8,128)(2,1)}) custom-call(s32[1]{0:T(128)} %bitcast.7.spot_ref, bf16[2560,256]{1,0:T(8,128)(2,1)S(1)} %copy-done.4, bf16[2,216,256]{2,1,0:T(8,128)(2,1)S(1)} %copy-done.7), custom_call_target="tpu_custom_call" | custom-call | tf_op jit(solution)/shard_map/pallas_call | solution.py:202
  76.2 2.0 %collective-permute-start.3 = (bf16[2,216,640]{2,1,0:T(8,128)(2,1)}, bf16[2,216,640]{2,1,0:T(8,128)(2,1)S(1)}, u32[]{:S(2)}, u32[]{:S(2)}) collective-permute-start(bf16[2,216,640]{2,1,0:T(8,128)(2,1)} %get-tuple-element.30), channel_id=1, source_target_pairs={{0,256},{128,384},{256,0},{384,128},{1,257},{129,385},{257,1},{385... | collective-permute-start | bytes 1658888 | tf_op jit(solution)/shard_map/ppermute | solution.py:27
  78.2 3.3 %collective-permute-start.4 = (bf16[2,216,640]{2,1,0:T(8,128)(2,1)}, bf16[2,216,640]{2,1,0:T(8,128)(2,1)S(1)}, u32[]{:S(2)}, u32[]{:S(2)}) collective-permute-start(bf16[2,216,640]{2,1,0:T(8,128)(2,1)} %get-tuple-element.31), channel_id=1, source_target_pairs={{0,128},{128,256},{256,384},{384,0},{1,129},{129,257},{257,385},{3... | collective-permute-start | bytes 1658888 | tf_op jit(solution)/shard_map/ppermute | solution.py:27
  81.5 3.2 %collective-permute-start.5 = (bf16[2,216,640]{2,1,0:T(8,128)(2,1)}, bf16[2,216,640]{2,1,0:T(8,128)(2,1)}, u32[]{:S(2)}, u32[]{:S(2)}) collective-permute-start(bf16[2,216,640]{2,1,0:T(8,128)(2,1)} %get-tuple-element.32), channel_id=1, source_target_pairs={{0,384},{128,0},{256,128},{384,256},{1,385},{129,1},{257,129},{385... | collective-permute-start | bytes 1658888 | tf_op jit(solution)/shard_map/ppermute | solution.py:27
  84.8 11.0 %all-to-all-done.1 = bf16[8,352,128]{2,1,0:T(8,128)(2,1)} async-done(((bf16[8,352,128]{2,1,0:T(8,128)(2,1)}), bf16[8,352,128]{2,1,0:T(8,128)(2,1)}, u32[]{:S(2)}, u32[]{:S(2)}) %all-to-all-start.1) | async-done | bytes 720928 | tf_op jit(solution)/shard_map/all_to_all | solution.py:224
  95.7 1.2 convert_reduce_fusion
  97.0 0.1 fusion
  97.1 22.6 %psum.14 = f32[2,160]{1,0:T(2,128)S(1)} all-reduce(f32[2,160]{1,0:T(2,128)S(1)} %fusion), channel_id=1, replica_groups=mesh['x'=4,'z'=4,'c'=2,'y'=8,'h'=2] {'z','h'}, use_global_device_ids=true, to_apply=%region_2.3 | all-reduce | flops 320 | bytes 2560 | tf_op jit(solution)/shard_map/psum | solution.py:236
  119.8 2.4 %shard_map.96 = bf16[640,432]{1,0:T(8,128)(2,1)} custom-call(f32[2,216,640]{2,1,0:T(8,128)S(1)} %get-tuple-element.28.own_ref, bf16[2,216,640]{2,1,0:T(8,128)(2,1)S(1)} %collective-permute-done.3.first_ref, bf16[2,216,640]{2,1,0:T(8,128)(2,1)S(1)} %collective-permute-done.4.second_ref, bf16[2,216,640]{2,1,0:T(8,128)(2,1)} %collective-permute-done.5.third_ref), custom_call_target="tpu_custom_call" | custom-call | tf_op jit(solution)/shard_map/pallas_call | solution.py:256
  122.2 8.0 %all-to-all-start.2 = ((bf16[8,80,432]{2,1,0:T(8,128)(2,1)}), bf16[8,80,432]{2,1,0:T(8,128)(2,1)S(1)}, u32[]{:S(2)}, u32[]{:S(2)}) async-start(bf16[8,80,432]{2,1,0:T(8,128)(2,1)} %bitcast.12), calls=%async_computation.2 | async-start | bytes 1310720 | tf_op jit(solution)/shard_map/all_to_all | solution.py:259
  130.2 2.5 %collective-permute-start.6 = (f32[176,128]{1,0:T(8,128)S(1)}, f32[176,128]{1,0:T(8,128)S(1)}, u32[]{:S(2)}, u32[]{:S(2)}) collective-permute-start(f32[176,128]{1,0:T(8,128)S(1)} %slice_select_fusion), channel_id=1, source_target_pairs={{0,1},{1,0},{2,3},{3,2},{4,5},{5,4},{6,7},{7,6},{8,9},{9,8},{10,11... | collective-permute-start | bytes 270344 | tf_op jit(solution)/shard_map/ppermute | solution.py:19
  132.6 7.0 %psum.15 = f32[160]{0:T(256)S(1)} all-reduce(f32[160]{0:T(256)S(1)} %bitcast.37), channel_id=1, replica_groups=mesh['x'=4,'z'=4,'c'=2,'y'=8,'h'=2] {'x'}, use_global_device_ids=true, to_apply=%region_4.5 | all-reduce | flops 160 | bytes 1280 | tf_op jit(solution)/shard_map/psum | solution.py:239
  139.7 4.1 %collective-permute-start.7 = (f32[160]{0:T(256)S(1)}, f32[160]{0:T(256)S(1)}, u32[]{:S(2)}, u32[]{:S(2)}) collective-permute-start(f32[160]{0:T(256)S(1)} %psum.15), channel_id=1, source_target_pairs={{0,16},{16,0},{1,17},{17,1},{2,18},{18,2},{3,19},{19,3},{4,20},{20... | collective-permute-start | bytes 1928 | tf_op jit(solution)/shard_map/ppermute | solution.py:19
  143.7 0.1 dynamic_slice.7
  143.8 0.7 collective-permute-done.7
  144.5 0.6 add.33
  145.1 0.7 fusion.5
  145.8 5.6 %all-to-all-done.2 = bf16[8,80,432]{2,1,0:T(8,128)(2,1)S(1)} async-done(((bf16[8,80,432]{2,1,0:T(8,128)(2,1)}), bf16[8,80,432]{2,1,0:T(8,128)(2,1)S(1)}, u32[]{:S(2)}, u32[]{:S(2)}) %all-to-all-start.2) | async-done | bytes 552992 | tf_op jit(solution)/shard_map/all_to_all | solution.py:259
  151.5 0.1 convert_reduce_fusion.1
  151.6 0.1 slice_bitcast_fusion.1
  151.7 0.9 pad_maximum_fusion.1
  (27 shorter events, 0.2 us)
Async XLA Ops:
  22.0 8.5 %copy-start.8 = (bf16[128,2560]{1,0:T(8,128)(2,1)S(1)}, bf16[128,2560]{1,0:T(8,128)(2,1)}, u32[]{:S(2)}) copy-start(bf16[128,2560]{1,0:T(8,128)(2,1)} %param.5) | copy-start | bytes 1966084
  22.0 36.1 %all-to-all-start = ((bf16[8,216,640]{2,1,0:T(8,128)(2,1)}), bf16[8,216,640]{2,1,0:T(8,128)(2,1)S(1)}, u32[]{:S(2)}, u32[]{:S(2)}) async-start(bf16[8,216,640]{2,1,0:T(8,128)(2,1)} %bitcast.31), calls=%async_computation | async-start | bytes 4423680 | tf_op jit(solution)/shard_map/all_to_all | solution.py:178
  30.8 6.8 %collective-permute-start = (bf16[128,2560]{0,1:T(8,128)(2,1)S(1)}, bf16[128,2560]{0,1:T(8,128)(2,1)S(1)}, u32[]{:S(2)}, u32[]{:S(2)}) collective-permute-start(bf16[128,2560]{0,1:T(8,128)(2,1)S(1)} %copy.18), channel_id=1, source_target_pairs={{0,16},{16,0},{1,17},{17,1},{2,18},{18,2},{3,19},{19,3},{4,20},{20... | collective-permute-start | bytes 1966088 | tf_op jit(solution)/shard_map/ppermute | solution.py:19
  33.7 3.2 %collective-permute-start.1 = (bf16[216,128]{1,0:T(8,128)(2,1)S(1)}, bf16[216,128]{1,0:T(8,128)(2,1)S(1)}, u32[]{:S(2)}, u32[]{:S(2)}) collective-permute-start(bf16[216,128]{1,0:T(8,128)(2,1)S(1)} %get-tuple-element.44), channel_id=1, source_target_pairs={{0,16},{16,0},{1,17},{17,1},{2,18},{18,2},{3,19},{19,3},{4,20},{20... | collective-permute-start | bytes 165896 | tf_op jit(solution)/shard_map/ppermute | solution.py:19
  37.6 0.7 copy-start.9
  38.3 1.1 copy-start
  39.9 1.1 copy-start.2
  58.1 1.3 copy-start.3
  59.4 0.9 copy-start.5
  60.3 4.9 %copy-start.1 = (bf16[2560,256]{1,0:T(8,128)(2,1)S(1)}, bf16[2560,256]{1,0:T(8,128)(2,1)}, u32[]{:S(2)}) copy-start(bf16[2560,256]{1,0:T(8,128)(2,1)} %copy-done) | copy-start | bytes 3932164
  62.4 5.9 %copy-start.6 = (bf16[2,216,256]{2,1,0:T(8,128)(2,1)}, bf16[2,216,256]{2,1,0:T(8,128)(2,1)S(1)}, u32[]{:S(2)}) copy-start(bf16[2,216,256]{2,1,0:T(8,128)(2,1)S(1)} %get-tuple-element.27.back_ref) | copy-start | bytes 663556
  62.4 4.6 %collective-permute-start.2 = (bf16[2784,128]{1,0:T(8,128)(2,1)S(1)}, bf16[2784,128]{1,0:T(8,128)(2,1)S(1)}, u32[]{:S(2)}, u32[]{:S(2)}) collective-permute-start(bf16[2784,128]{1,0:T(8,128)(2,1)S(1)} %get-tuple-element.23), channel_id=1, source_target_pairs={{0,16},{16,0},{1,17},{17,1},{2,18},{18,2},{3,19},{19,3},{4,20},{20... | collective-permute-start | bytes 2138120 | tf_op jit(solution)/shard_map/ppermute | solution.py:19
  68.3 5.2 %copy-start.4 = (bf16[2560,256]{1,0:T(8,128)(2,1)S(1)}, bf16[2560,256]{1,0:T(8,128)(2,1)}, u32[]{:S(2)}) copy-start(bf16[2560,256]{1,0:T(8,128)(2,1)} %copy-done.2) | copy-start | bytes 3932164
  68.3 27.4 %all-to-all-start.1 = ((bf16[8,352,128]{2,1,0:T(8,128)(2,1)}), bf16[8,352,128]{2,1,0:T(8,128)(2,1)}, u32[]{:S(2)}, u32[]{:S(2)}) async-start(bf16[8,352,128]{2,1,0:T(8,128)(2,1)} %bitcast.8), calls=%async_computation.1 | async-start | bytes 1441792 | tf_op jit(solution)/shard_map/all_to_all | solution.py:224
  73.5 0.9 copy-start.7
  76.2 43.6 %collective-permute-start.3 = (bf16[2,216,640]{2,1,0:T(8,128)(2,1)}, bf16[2,216,640]{2,1,0:T(8,128)(2,1)S(1)}, u32[]{:S(2)}, u32[]{:S(2)}) collective-permute-start(bf16[2,216,640]{2,1,0:T(8,128)(2,1)} %get-tuple-element.30), channel_id=1, source_target_pairs={{0,256},{128,384},{256,0},{384,128},{1,257},{129,385},{257,1},{385... | collective-permute-start | bytes 1658888 | tf_op jit(solution)/shard_map/ppermute | solution.py:27
  78.2 41.6 %collective-permute-start.4 = (bf16[2,216,640]{2,1,0:T(8,128)(2,1)}, bf16[2,216,640]{2,1,0:T(8,128)(2,1)S(1)}, u32[]{:S(2)}, u32[]{:S(2)}) collective-permute-start(bf16[2,216,640]{2,1,0:T(8,128)(2,1)} %get-tuple-element.31), channel_id=1, source_target_pairs={{0,128},{128,256},{256,384},{384,0},{1,129},{129,257},{257,385},{3... | collective-permute-start | bytes 1658888 | tf_op jit(solution)/shard_map/ppermute | solution.py:27
  81.5 38.3 %collective-permute-start.5 = (bf16[2,216,640]{2,1,0:T(8,128)(2,1)}, bf16[2,216,640]{2,1,0:T(8,128)(2,1)}, u32[]{:S(2)}, u32[]{:S(2)}) collective-permute-start(bf16[2,216,640]{2,1,0:T(8,128)(2,1)} %get-tuple-element.32), channel_id=1, source_target_pairs={{0,384},{128,0},{256,128},{384,256},{1,385},{129,1},{257,129},{385... | collective-permute-start | bytes 1658888 | tf_op jit(solution)/shard_map/ppermute | solution.py:27
  122.2 29.3 %all-to-all-start.2 = ((bf16[8,80,432]{2,1,0:T(8,128)(2,1)}), bf16[8,80,432]{2,1,0:T(8,128)(2,1)S(1)}, u32[]{:S(2)}, u32[]{:S(2)}) async-start(bf16[8,80,432]{2,1,0:T(8,128)(2,1)} %bitcast.12), calls=%async_computation.2 | async-start | bytes 1310720 | tf_op jit(solution)/shard_map/all_to_all | solution.py:259
  130.2 14.9 %collective-permute-start.6 = (f32[176,128]{1,0:T(8,128)S(1)}, f32[176,128]{1,0:T(8,128)S(1)}, u32[]{:S(2)}, u32[]{:S(2)}) collective-permute-start(f32[176,128]{1,0:T(8,128)S(1)} %slice_select_fusion), channel_id=1, source_target_pairs={{0,1},{1,0},{2,3},{3,2},{4,5},{5,4},{6,7},{7,6},{8,9},{9,8},{10,11... | collective-permute-start | bytes 270344 | tf_op jit(solution)/shard_map/ppermute | solution.py:19
  139.7 4.9 %collective-permute-start.7 = (f32[160]{0:T(256)S(1)}, f32[160]{0:T(256)S(1)}, u32[]{:S(2)}, u32[]{:S(2)}) collective-permute-start(f32[160]{0:T(256)S(1)} %psum.15), channel_id=1, source_target_pairs={{0,16},{16,0},{1,17},{17,1},{2,18},{18,2},{3,19},{19,3},{4,20},{20... | collective-permute-start | bytes 1928 | tf_op jit(solution)/shard_map/ppermute | solution.py:19

commit v12 on v11

--- a/solution.py
+++ b/solution.py
@@ -233,15 +233,20 @@
         / root_own
     ).reshape(NH, features, tokens)
     gain_part = jnp.sum(y_sums[:, :features] * unit_span, axis=2)
-    gain_part = lax.psum(gain_part, ("z", "h"))
+    gain_part = lax.psum(gain_part, "z")
     gain_part, travelling = lax.optimization_barrier((gain_part, travelling))
+
     low_half = lax.axis_index("h") == 0
-    gain_part = lax.psum(jnp.where(low_half, gain_part[0], gain_part[1]), "x")
-    grad_gain = gain_part + swap_core(gain_part)
-
+    lines = -(-features // tokens)
+    gain_lines = jnp.pad(gain_part, ((0, 0), (0, lines * tokens - features)))
+    y_sums = jnp.concatenate(
+        [y_sums[:, : features + 3], gain_lines.reshape(NH, lines, tokens)], 1
+    )
     totals = jnp.where(low_half, y_sums[0], y_sums[1]) + swap(
         jnp.where(low_half, y_sums[1], y_sums[0]), "h"
     )
+    gain_part = lax.psum(totals[features + 3 :].reshape(lines * tokens)[:features], "x")
+    grad_gain = gain_part + swap_core(gain_part)
     own_sums = totals[:features]
     token_totals = totals[features] + totals[features + 1] + totals[features + 2]
     start = lax.axis_index(("y", "h")) * features

time: 153 us -> 143 us (0.935)
  blocking collectives: 47.8 us -> 35.2 us
  starting transfers between devices: 43.8 us -> 47.5 us
    psum x2, blocking collectives: 29.7 us -> 17 us  [the longest x1 10.2 us: per_device(): gain_part = lax.psum(gain_part, 'z')]
    ppermute x5, starting transfers between devices: 13.6 us -> 19 us  [swap(): return lax.ppermute(value, axis, [(0, 1), (1, 0)])]
    all_to_all x1, starting transfers between devices: 7.97 us -> 6.29 us  [per_device(): lax.all_to_all(column_sum.reshape(NC * NZ, rows, columns), ('c', 'z'), 0,...]
  transfers between devices with their start and end apart: 11 -> 11, of which waited for: 6 -> 6; matrix products, arithmetic and copies ran while one was open for 3% -> 4% of each run, Pallas kernels for 2% -> 3%
where the time goes in v12:
time: 143 us
  starting transfers between devices  47.5 us (33%)
  waiting for transfers between devices  35.9 us (25%)
  blocking collectives  35.2 us (25%)
  local copies, waits for them, and re-layouts  8.4 us (6%)
  Pallas kernels  8.16 us (6%)
  other arithmetic  6.53 us (5%)
    ppermute x5, starting transfers between devices, swap(): return lax.ppermute(value, axis, [(0, 1), (1, 0)])  19 us
    all_gather x1, blocking collectives, per_device(): lax.all_gather(jnp.concatenate([w_gate, w_up], 1), 'z', axis=0, tiled=True)  18.1 us
    all_to_all x1, waiting for transfers between devices, per_device(): weight = lax.all_to_all(copies, ('x', 'c'), 0, 0, tiled=True)  17.1 us
    all_to_all x1, waiting for transfers between devices, per_device(): lax.all_to_all(sending.reshape(n_dp // NH, NH * (features + spare), token...  11 us
    psum x1, blocking collectives, per_device(): gain_part = lax.psum(gain_part, 'z')  10.2 us
    all_to_all x1, starting transfers between devices, per_device(): weight = lax.all_to_all(copies, ('x', 'c'), 0, 0, tiled=True)  8.54 us
    ppermute x3, starting transfers between devices, shift_x(): return lax.ppermute(value, 'x', [(x, (x + steps) % NX) for x in range(NX)])  8.49 us
    psum x1, blocking collectives, per_device(): lax.psum(totals[features + 3:].reshape(lines * tokens)[:features], 'x')  6.87 us
  transfers between devices with their start and end apart: 11, of which 6 were waited for; matrix products, arithmetic and copies ran while one was open for 4% of the time, Pallas kernels for 3%

profile of v12, /device:TPU:1, one launch (start us, length us, event | category | flops | bytes accessed | tf_op | source)
XLA Modules:
  0.0 142.5 jit_solution(5720432092803305173)
XLA Ops:
  0.6 1.0 pad_maximum_fusion.3
  1.7 18.1 %all_gather.3 = bf16[320,864]{1,0:T(8,128)(2,1)S(1)} all-gather(bf16[80,864]{1,0:T(8,128)(2,1)S(1)} %pad_maximum_fusion.3), channel_id=1, replica_groups=mesh['x'=4,'z'=4,'c'=2,'y'=8,'h'=2] {'z'}, dimensions={0}, use_global_device_ids=true | all-gather | bytes 691200 | tf_op jit(solution)/shard_map/all_gather | solution.py:173
  19.8 0.4 copy.19
  20.2 0.2 pad_maximum_fusion
  20.4 1.5 %broadcast_in_dim.5 = bf16[4,2,216,640]{3,2,1,0:T(8,128)(2,1)} broadcast(bf16[2,216,640]{2,1,0:T(8,128)(2,1)S(1)} %bitcast.39), dimensions={1,2,3} | broadcast | bytes 2764800 | tf_op jit(solution)/shard_map/broadcast_in_dim | solution.py:175
  22.0 8.5 %all-to-all-start = ((bf16[8,216,640]{2,1,0:T(8,128)(2,1)}), bf16[8,216,640]{2,1,0:T(8,128)(2,1)S(1)}, u32[]{:S(2)}, u32[]{:S(2)}) async-start(bf16[8,216,640]{2,1,0:T(8,128)(2,1)} %bitcast.37), calls=%async_computation | async-start | bytes 4423680 | tf_op jit(solution)/shard_map/all_to_all | solution.py:178
  30.5 0.3 copy.18
  30.8 2.0 %collective-permute-start = (bf16[128,2560]{0,1:T(8,128)(2,1)S(1)}, bf16[128,2560]{0,1:T(8,128)(2,1)S(1)}, u32[]{:S(2)}, u32[]{:S(2)}) collective-permute-start(bf16[128,2560]{0,1:T(8,128)(2,1)S(1)} %copy.18), channel_id=1, source_target_pairs={{0,16},{16,0},{1,17},{17,1},{2,18},{18,2},{3,19},{19,3},{4,20},{20... | collective-permute-start | bytes 1966088 | tf_op jit(solution)/shard_map/ppermute | solution.py:19
  32.9 0.9 broadcast_select_fusion.1
  33.7 2.3 %collective-permute-start.1 = (bf16[216,128]{1,0:T(8,128)(2,1)S(1)}, bf16[216,128]{1,0:T(8,128)(2,1)S(1)}, u32[]{:S(2)}, u32[]{:S(2)}) collective-permute-start(bf16[216,128]{1,0:T(8,128)(2,1)S(1)} %get-tuple-element.44), channel_id=1, source_target_pairs={{0,16},{16,0},{1,17},{17,1},{2,18},{18,2},{3,19},{19,3},{4,20},{20... | collective-permute-start | bytes 165896 | tf_op jit(solution)/shard_map/ppermute | solution.py:19
  36.1 0.9 collective-permute-done.1
  36.9 0.7 pad_maximum_fusion.4.upstream_ref
  37.6 0.1 maximum_bitcast_fusion.x_ref
  37.7 0.6 copy-done.9
  38.3 0.4 broadcast_in_dim.4.gain_ref
  38.7 0.7 copy-done
  39.4 0.6 shard_map.92
  39.9 1.1 copy-done.2
  41.0 17.1 %all-to-all-done.weight_ref = bf16[8,216,640]{2,1,0:T(8,128)(2,1)S(1)} async-done(((bf16[8,216,640]{2,1,0:T(8,128)(2,1)}), bf16[8,216,640]{2,1,0:T(8,128)(2,1)S(1)}, u32[]{:S(2)}, u32[]{:S(2)}) %all-to-all-start) | async-done | bytes 2211872 | tf_op jit(solution)/shard_map/all_to_all | solution.py:178
  58.1 1.3 copy-done.3
  59.4 0.9 copy-done.5
  60.3 2.1 %shard_map.93 = (bf16[216,128]{1,0:T(8,128)(2,1)S(1)}, bf16[2,216,256]{2,1,0:T(8,128)(2,1)S(1)}, f32[2560,128]{1,0:T(8,128)S(1)}, bf16[2784,128]{1,0:T(8,128)(2,1)S(1)}) custom-call(bf16[2560,256]{1,0:T(8,128)(2,1)S(1)} %copy-done.3, bf16[216,256]{1,0:T(8,128)(2,1)S(1)} %copy-done.5, bf16[8,216,640]{2,1,0:T(8,128)(2,1)S(1)} %all-to-all-done.weight_ref), custom_call_target="tpu_custom_call" | custom-call | tf_op jit(solution)/shard_map/pallas_call | solution.py:191
  62.4 2.8 %collective-permute-start.2 = (bf16[2784,128]{1,0:T(8,128)(2,1)S(1)}, bf16[2784,128]{1,0:T(8,128)(2,1)S(1)}, u32[]{:S(2)}, u32[]{:S(2)}) collective-permute-start(bf16[2784,128]{1,0:T(8,128)(2,1)S(1)} %get-tuple-element.23), channel_id=1, source_target_pairs={{0,16},{16,0},{1,17},{17,1},{2,18},{18,2},{3,19},{19,3},{4,20},{20... | collective-permute-start | bytes 2138120 | tf_op jit(solution)/shard_map/ppermute | solution.py:19
  65.3 1.7 %collective-permute-done.2.other_ref = bf16[2784,128]{1,0:T(8,128)(2,1)S(1)} collective-permute-done((bf16[2784,128]{1,0:T(8,128)(2,1)S(1)}, bf16[2784,128]{1,0:T(8,128)(2,1)S(1)}, u32[]{:S(2)}, u32[]{:S(2)}) %collective-permute-start.2) | collective-permute-done | bytes 712736 | tf_op jit(solution)/shard_map/ppermute | solution.py:19
  67.0 1.3 shard_map.94
  68.3 5.2 %all-to-all-start.1 = ((bf16[8,352,128]{2,1,0:T(8,128)(2,1)}), bf16[8,352,128]{2,1,0:T(8,128)(2,1)}, u32[]{:S(2)}, u32[]{:S(2)}) async-start(bf16[8,352,128]{2,1,0:T(8,128)(2,1)} %bitcast.8), calls=%async_computation.1 | async-start | bytes 1441792 | tf_op jit(solution)/shard_map/all_to_all | solution.py:224
  73.5 0.9 copy-done.7
  74.4 1.8 %shard_map.95 = (f32[2,216,640]{2,1,0:T(8,128)S(1)}, bf16[2,216,640]{2,1,0:T(8,128)(2,1)}, bf16[2,216,640]{2,1,0:T(8,128)(2,1)}, bf16[2,216,640]{2,1,0:T(8,128)(2,1)}) custom-call(s32[1]{0:T(128)} %bitcast.7.spot_ref, bf16[2560,256]{1,0:T(8,128)(2,1)S(1)} %copy-done.4, bf16[2,216,256]{2,1,0:T(8,128)(2,1)S(1)} %copy-done.7), custom_call_target="tpu_custom_call" | custom-call | tf_op jit(solution)/shard_map/pallas_call | solution.py:202
  76.2 2.0 %collective-permute-start.3 = (bf16[2,216,640]{2,1,0:T(8,128)(2,1)}, bf16[2,216,640]{2,1,0:T(8,128)(2,1)S(1)}, u32[]{:S(2)}, u32[]{:S(2)}) collective-permute-start(bf16[2,216,640]{2,1,0:T(8,128)(2,1)} %get-tuple-element.30), channel_id=1, source_target_pairs={{0,256},{128,384},{256,0},{384,128},{1,257},{129,385},{257,1},{385... | collective-permute-start | bytes 1658888 | tf_op jit(solution)/shard_map/ppermute | solution.py:27
  78.2 3.3 %collective-permute-start.4 = (bf16[2,216,640]{2,1,0:T(8,128)(2,1)}, bf16[2,216,640]{2,1,0:T(8,128)(2,1)S(1)}, u32[]{:S(2)}, u32[]{:S(2)}) collective-permute-start(bf16[2,216,640]{2,1,0:T(8,128)(2,1)} %get-tuple-element.31), channel_id=1, source_target_pairs={{0,128},{128,256},{256,384},{384,0},{1,129},{129,257},{257,385},{3... | collective-permute-start | bytes 1658888 | tf_op jit(solution)/shard_map/ppermute | solution.py:27
  81.5 3.2 %collective-permute-start.5 = (bf16[2,216,640]{2,1,0:T(8,128)(2,1)}, bf16[2,216,640]{2,1,0:T(8,128)(2,1)}, u32[]{:S(2)}, u32[]{:S(2)}) collective-permute-start(bf16[2,216,640]{2,1,0:T(8,128)(2,1)} %get-tuple-element.32), channel_id=1, source_target_pairs={{0,384},{128,0},{256,128},{384,256},{1,385},{129,1},{257,129},{385... | collective-permute-start | bytes 1658888 | tf_op jit(solution)/shard_map/ppermute | solution.py:27
  84.8 11.0 %all-to-all-done.1 = bf16[8,352,128]{2,1,0:T(8,128)(2,1)} async-done(((bf16[8,352,128]{2,1,0:T(8,128)(2,1)}), bf16[8,352,128]{2,1,0:T(8,128)(2,1)}, u32[]{:S(2)}, u32[]{:S(2)}) %all-to-all-start.1) | async-done | bytes 720928 | tf_op jit(solution)/shard_map/all_to_all | solution.py:224
  95.7 1.2 convert_reduce_fusion
  97.0 0.2 fusion
  97.1 10.2 %psum.14 = f32[2,160]{1,0:T(2,128)S(1)} all-reduce(f32[2,160]{1,0:T(2,128)S(1)} %fusion), channel_id=1, replica_groups=mesh['x'=4,'z'=4,'c'=2,'y'=8,'h'=2] {'z'}, use_global_device_ids=true, to_apply=%region_2.3 | all-reduce | flops 320 | bytes 2560 | tf_op jit(solution)/shard_map/psum | solution.py:236
  107.4 7.9 %collective-permute-start.6 = (f32[165,128]{1,0:T(8,128)S(1)}, f32[165,128]{1,0:T(8,128)S(1)}, u32[]{:S(2)}, u32[]{:S(2)}) collective-permute-start(f32[165,128]{1,0:T(8,128)S(1)} %select_bitcast_fusion), channel_id=1, source_target_pairs={{0,1},{1,0},{2,3},{3,2},{4,5},{5,4},{6,7},{7,6},{8,9},{9,8},{10,11... | collective-permute-start | bytes 253448 | tf_op jit(solution)/shard_map/ppermute | solution.py:19
  115.3 2.4 %shard_map.96 = bf16[640,432]{1,0:T(8,128)(2,1)} custom-call(f32[2,216,640]{2,1,0:T(8,128)S(1)} %get-tuple-element.28.own_ref, bf16[2,216,640]{2,1,0:T(8,128)(2,1)S(1)} %collective-permute-done.3.first_ref, bf16[2,216,640]{2,1,0:T(8,128)(2,1)S(1)} %collective-permute-done.4.second_ref, bf16[2,216,640]{2,1,0:T(8,128)(2,1)} %collective-permute-done.5.third_ref), custom_call_target="tpu_custom_call" | custom-call | tf_op jit(solution)/shard_map/pallas_call | solution.py:261
  117.7 6.3 %all-to-all-start.2 = ((bf16[8,80,432]{2,1,0:T(8,128)(2,1)}), bf16[8,80,432]{2,1,0:T(8,128)(2,1)S(1)}, u32[]{:S(2)}, u32[]{:S(2)}) async-start(bf16[8,80,432]{2,1,0:T(8,128)(2,1)} %bitcast.12), calls=%async_computation.2 | async-start | bytes 1310720 | tf_op jit(solution)/shard_map/all_to_all | solution.py:264
  124.0 0.1 dynamic_slice.7
  124.1 6.9 %psum.15 = f32[160]{0:T(256)S(1)} all-reduce(f32[160]{0:T(256)S(1)} %bitcast.44), channel_id=1, replica_groups=mesh['x'=4,'z'=4,'c'=2,'y'=8,'h'=2] {'x'}, use_global_device_ids=true, to_apply=%region_4.5 | all-reduce | flops 160 | bytes 1280 | tf_op jit(solution)/shard_map/psum | solution.py:248
  131.0 4.0 %collective-permute-start.7 = (f32[160]{0:T(256)S(1)}, f32[160]{0:T(256)S(1)}, u32[]{:S(2)}, u32[]{:S(2)}) collective-permute-start(f32[160]{0:T(256)S(1)} %psum.15), channel_id=1, source_target_pairs={{0,16},{16,0},{1,17},{17,1},{2,18},{18,2},{3,19},{19,3},{4,20},{20... | collective-permute-start | bytes 1928 | tf_op jit(solution)/shard_map/ppermute | solution.py:19
  135.0 0.7 fusion.6
  135.7 0.1 collective-permute-done.7
  135.8 0.6 add.35
  136.3 5.1 %all-to-all-done.2 = bf16[8,80,432]{2,1,0:T(8,128)(2,1)S(1)} async-done(((bf16[8,80,432]{2,1,0:T(8,128)(2,1)}), bf16[8,80,432]{2,1,0:T(8,128)(2,1)S(1)}, u32[]{:S(2)}, u32[]{:S(2)}) %all-to-all-start.2) | async-done | bytes 552992 | tf_op jit(solution)/shard_map/all_to_all | solution.py:264
  141.5 0.1 convert_reduce_fusion.1
  141.6 0.1 slice_bitcast_fusion.1
  141.7 0.9 pad_maximum_fusion.1
  (30 shorter events, 0.3 us)
Async XLA Ops:
  22.0 8.5 %copy-start.8 = (bf16[128,2560]{1,0:T(8,128)(2,1)S(1)}, bf16[128,2560]{1,0:T(8,128)(2,1)}, u32[]{:S(2)}) copy-start(bf16[128,2560]{1,0:T(8,128)(2,1)} %param.5) | copy-start | bytes 1966084
  22.0 36.1 %all-to-all-start = ((bf16[8,216,640]{2,1,0:T(8,128)(2,1)}), bf16[8,216,640]{2,1,0:T(8,128)(2,1)S(1)}, u32[]{:S(2)}, u32[]{:S(2)}) async-start(bf16[8,216,640]{2,1,0:T(8,128)(2,1)} %bitcast.37), calls=%async_computation | async-start | bytes 4423680 | tf_op jit(solution)/shard_map/all_to_all | solution.py:178
  30.8 6.8 %collective-permute-start = (bf16[128,2560]{0,1:T(8,128)(2,1)S(1)}, bf16[128,2560]{0,1:T(8,128)(2,1)S(1)}, u32[]{:S(2)}, u32[]{:S(2)}) collective-permute-start(bf16[128,2560]{0,1:T(8,128)(2,1)S(1)} %copy.18), channel_id=1, source_target_pairs={{0,16},{16,0},{1,17},{17,1},{2,18},{18,2},{3,19},{19,3},{4,20},{20... | collective-permute-start | bytes 1966088 | tf_op jit(solution)/shard_map/ppermute | solution.py:19
  33.7 3.2 %collective-permute-start.1 = (bf16[216,128]{1,0:T(8,128)(2,1)S(1)}, bf16[216,128]{1,0:T(8,128)(2,1)S(1)}, u32[]{:S(2)}, u32[]{:S(2)}) collective-permute-start(bf16[216,128]{1,0:T(8,128)(2,1)S(1)} %get-tuple-element.44), channel_id=1, source_target_pairs={{0,16},{16,0},{1,17},{17,1},{2,18},{18,2},{3,19},{19,3},{4,20},{20... | collective-permute-start | bytes 165896 | tf_op jit(solution)/shard_map/ppermute | solution.py:19
  37.6 0.7 copy-start.9
  38.3 1.1 copy-start
  39.9 1.1 copy-start.2
  58.1 1.3 copy-start.3
  59.4 0.9 copy-start.5
  60.3 4.9 %copy-start.1 = (bf16[2560,256]{1,0:T(8,128)(2,1)S(1)}, bf16[2560,256]{1,0:T(8,128)(2,1)}, u32[]{:S(2)}) copy-start(bf16[2560,256]{1,0:T(8,128)(2,1)} %copy-done) | copy-start | bytes 3932164
  62.4 5.9 %copy-start.6 = (bf16[2,216,256]{2,1,0:T(8,128)(2,1)}, bf16[2,216,256]{2,1,0:T(8,128)(2,1)S(1)}, u32[]{:S(2)}) copy-start(bf16[2,216,256]{2,1,0:T(8,128)(2,1)S(1)} %get-tuple-element.27.back_ref) | copy-start | bytes 663556
  62.4 4.6 %collective-permute-start.2 = (bf16[2784,128]{1,0:T(8,128)(2,1)S(1)}, bf16[2784,128]{1,0:T(8,128)(2,1)S(1)}, u32[]{:S(2)}, u32[]{:S(2)}) collective-permute-start(bf16[2784,128]{1,0:T(8,128)(2,1)S(1)} %get-tuple-element.23), channel_id=1, source_target_pairs={{0,16},{16,0},{1,17},{17,1},{2,18},{18,2},{3,19},{19,3},{4,20},{20... | collective-permute-start | bytes 2138120 | tf_op jit(solution)/shard_map/ppermute | solution.py:19
  68.3 5.2 %copy-start.4 = (bf16[2560,256]{1,0:T(8,128)(2,1)S(1)}, bf16[2560,256]{1,0:T(8,128)(2,1)}, u32[]{:S(2)}) copy-start(bf16[2560,256]{1,0:T(8,128)(2,1)} %copy-done.2) | copy-start | bytes 3932164
  68.3 27.4 %all-to-all-start.1 = ((bf16[8,352,128]{2,1,0:T(8,128)(2,1)}), bf16[8,352,128]{2,1,0:T(8,128)(2,1)}, u32[]{:S(2)}, u32[]{:S(2)}) async-start(bf16[8,352,128]{2,1,0:T(8,128)(2,1)} %bitcast.8), calls=%async_computation.1 | async-start | bytes 1441792 | tf_op jit(solution)/shard_map/all_to_all | solution.py:224
  73.5 0.9 copy-start.7
  76.2 31.1 %collective-permute-start.3 = (bf16[2,216,640]{2,1,0:T(8,128)(2,1)}, bf16[2,216,640]{2,1,0:T(8,128)(2,1)S(1)}, u32[]{:S(2)}, u32[]{:S(2)}) collective-permute-start(bf16[2,216,640]{2,1,0:T(8,128)(2,1)} %get-tuple-element.30), channel_id=1, source_target_pairs={{0,256},{128,384},{256,0},{384,128},{1,257},{129,385},{257,1},{385... | collective-permute-start | bytes 1658888 | tf_op jit(solution)/shard_map/ppermute | solution.py:27
  78.2 29.1 %collective-permute-start.4 = (bf16[2,216,640]{2,1,0:T(8,128)(2,1)}, bf16[2,216,640]{2,1,0:T(8,128)(2,1)S(1)}, u32[]{:S(2)}, u32[]{:S(2)}) collective-permute-start(bf16[2,216,640]{2,1,0:T(8,128)(2,1)} %get-tuple-element.31), channel_id=1, source_target_pairs={{0,128},{128,256},{256,384},{384,0},{1,129},{129,257},{257,385},{3... | collective-permute-start | bytes 1658888 | tf_op jit(solution)/shard_map/ppermute | solution.py:27
  81.5 25.8 %collective-permute-start.5 = (bf16[2,216,640]{2,1,0:T(8,128)(2,1)}, bf16[2,216,640]{2,1,0:T(8,128)(2,1)}, u32[]{:S(2)}, u32[]{:S(2)}) collective-permute-start(bf16[2,216,640]{2,1,0:T(8,128)(2,1)} %get-tuple-element.32), channel_id=1, source_target_pairs={{0,384},{128,0},{256,128},{384,256},{1,385},{129,1},{257,129},{385... | collective-permute-start | bytes 1658888 | tf_op jit(solution)/shard_map/ppermute | solution.py:27
  107.4 16.7 %collective-permute-start.6 = (f32[165,128]{1,0:T(8,128)S(1)}, f32[165,128]{1,0:T(8,128)S(1)}, u32[]{:S(2)}, u32[]{:S(2)}) collective-permute-start(f32[165,128]{1,0:T(8,128)S(1)} %select_bitcast_fusion), channel_id=1, source_target_pairs={{0,1},{1,0},{2,3},{3,2},{4,5},{5,4},{6,7},{7,6},{8,9},{9,8},{10,11... | collective-permute-start | bytes 253448 | tf_op jit(solution)/shard_map/ppermute | solution.py:19
  117.7 23.8 %all-to-all-start.2 = ((bf16[8,80,432]{2,1,0:T(8,128)(2,1)}), bf16[8,80,432]{2,1,0:T(8,128)(2,1)S(1)}, u32[]{:S(2)}, u32[]{:S(2)}) async-start(bf16[8,80,432]{2,1,0:T(8,128)(2,1)} %bitcast.12), calls=%async_computation.2 | async-start | bytes 1310720 | tf_op jit(solution)/shard_map/all_to_all | solution.py:264
  131.0 4.8 %collective-permute-start.7 = (f32[160]{0:T(256)S(1)}, f32[160]{0:T(256)S(1)}, u32[]{:S(2)}, u32[]{:S(2)}) collective-permute-start(f32[160]{0:T(256)S(1)} %psum.15), channel_id=1, source_target_pairs={{0,16},{16,0},{1,17},{17,1},{2,18},{18,2},{3,19},{19,3},{4,20},{20... | collective-permute-start | bytes 1928 | tf_op jit(solution)/shard_map/ppermute | solution.py:19

commit v13 on v12

--- a/solution.py
+++ b/solution.py
@@ -31,9 +31,14 @@
     return (block // NZ * NC + core) * NZ + block % NZ
 
 
-def norm_kernel(x_ref, gain_ref, normed_ref, root_ref):
+def norm_kernel(x_ref, gain_ref, upstream_ref, normed_ref, root_ref):
     width, tokens = x_ref.shape
     size = width // (NX * NZ)
+    half = upstream_ref.shape[0]
+    extra = normed_ref.shape[0] - width
+    normed_ref[width:, :] = jnp.concatenate(
+        [upstream_ref[...].astype(F32), jnp.zeros((extra - half, tokens), F32)], axis=0
+    ).astype(BF)
     total = jnp.zeros((size, tokens), F32)
     for index in range(NX * NZ):
         value = x_ref[pl.ds(index * size, size), :].astype(F32)
@@ -53,7 +58,7 @@
 
 
 def forward_kernel(
-    normed_ref, upstream_ref, weight_ref, hidden_ref, back_ref, own_ref, other_ref
+    normed_ref, weight_ref, hidden_ref, back_ref, own_ref, other_ref
 ):
     size = weight_ref.shape[2] // 2
     tokens = own_ref.shape[1]
@@ -76,7 +81,7 @@
         [hidden[:, tokens:], jnp.zeros((extra - hidden.shape[0], tokens), F32)], axis=0
     )
     other_ref[width : width + extra, :] = riding.astype(BF)
-    upstream = upstream_ref[...].astype(F32)
+    upstream = normed_ref[width:, :].astype(F32)[: weight_ref.shape[1]]
     back_up = (upstream * activated).astype(BF)
     back_gate = (upstream * up_pre * sigmoid * (1.0 + gate_pre * (1.0 - sigmoid))).astype(BF)
     back_ref[0] = back_gate
@@ -181,13 +186,13 @@
     upstream_mine, upstream_other = halves(upstream.T, 0)
     upstream_pair = jnp.concatenate([upstream_mine, swap_core(upstream_other)], 1)
     gain_wide = jnp.broadcast_to(gain[:, None], (width, tokens))
+    riding = -(-half // 16) * 16
     normed, root_mean = call(
         norm_kernel,
-        (shape((width, 2 * tokens), BF), shape((1, 2 * tokens), F32)),
-        [VMEM] * 2,
-    )(inputs_t, gain_wide)
-
-    riding = -(-half // 16) * 16
+        (shape((width + riding, 2 * tokens), BF), shape((1, 2 * tokens), F32)),
+        [VMEM] * 3,
+    )(inputs_t, gain_wide, upstream_pair)
+
     hidden_own, back, part_own, part_other = call(
         forward_kernel,
         (
@@ -196,8 +201,8 @@
             shape((width, tokens), F32),
             shape((width + riding, tokens), BF),
         ),
-        [VMEM] * 3,
-    )(normed, upstream_pair, weight)
+        [VMEM] * 2,
+    )(normed, weight)
     part_other = swap_core(part_other)
     terms = call(
         gradient_kernel,
@@ -235,6 +240,9 @@
     gain_part = jnp.sum(y_sums[:, :features] * unit_span, axis=2)
     gain_part = lax.psum(gain_part, "z")
     gain_part, travelling = lax.optimization_barrier((gain_part, travelling))
+    column_sum = call(column_kernel, shape((column_rows, columns), BF), [VMEM] * 4)(
+        terms[0], *travelling
+    )
 
     low_half = lax.axis_index("h") == 0
     lines = -(-features // tokens)
@@ -242,6 +250,7 @@
     y_sums = jnp.concatenate(
         [y_sums[:, : features + 3], gain_lines.reshape(NH, lines, tokens)], 1
     )
+    y_sums, column_sum = lax.optimization_barrier((y_sums, column_sum))
     totals = jnp.where(low_half, y_sums[0], y_sums[1]) + swap(
         jnp.where(low_half, y_sums[1], y_sums[0]), "h"
     )
@@ -258,9 +267,6 @@
         .T
     )
 
-    column_sum = call(column_kernel, shape((column_rows, columns), BF), [VMEM] * 4)(
-        terms[0], *travelling
-    )
     blocks = lax.all_to_all(
         column_sum.reshape(NC * NZ, rows, columns), ("c", "z"), 0, 0, tiled=True
     )

time: 143 us -> 143 us (level)
    unnamed x21 -> x19, local copies, waits for them, and re-layouts: 5.78 us -> 4.96 us
  transfers between devices with their start and end apart: 11 -> 11, of which waited for: 6 -> 6; matrix products, arithmetic and copies ran while one was open for 4% -> 3% of each run, Pallas kernels for 3% -> 2%
where the time goes in v13:
time: 143 us; the launch traced here: 142 us
  starting transfers between devices  47.5 us (33%)
  waiting for transfers between devices  36.4 us (25%)
  blocking collectives  35.2 us (25%)
  Pallas kernels  8.18 us (6%)
  local copies, waits for them, and re-layouts  7.58 us (5%)
  other arithmetic  5.9 us (4%)
    ppermute x5, starting transfers between devices, swap(): return lax.ppermute(value, axis, [(0, 1), (1, 0)])  19 us
    all_gather x1, blocking collectives, per_device(): lax.all_gather(jnp.concatenate([w_gate, w_up], 1), 'z', axis=0, tiled=True)  18.1 us
    all_to_all x1, waiting for transfers between devices, per_device(): weight = lax.all_to_all(copies, ('x', 'c'), 0, 0, tiled=True)  17.7 us
    all_to_all x1, waiting for transfers between devices, per_device(): lax.all_to_all(sending.reshape(n_dp // NH, NH * (features + spare), token...  11 us
    psum x1, blocking collectives, per_device(): gain_part = lax.psum(gain_part, 'z')  10.2 us
    all_to_all x1, starting transfers between devices, per_device(): weight = lax.all_to_all(copies, ('x', 'c'), 0, 0, tiled=True)  8.54 us
    ppermute x3, starting transfers between devices, shift_x(): return lax.ppermute(value, 'x', [(x, (x + steps) % NX) for x in range(NX)])  8.48 us
    psum x1, blocking collectives, per_device(): lax.psum(totals[features + 3:].reshape(lines * tokens)[:features], 'x')  6.87 us
  transfers between devices with their start and end apart: 11, of which 6 were waited for; matrix products, arithmetic and copies ran while one was open for 3% of the time, Pallas kernels for 2%

profile of v13, /device:TPU:1, one launch (start us, length us, event | category | flops | bytes accessed | tf_op | source)
XLA Modules:
  0.0 141.7 jit_solution(13238598403750720545)
XLA Ops:
  0.6 1.0 pad_maximum_fusion.4
  1.7 18.1 %all_gather.3 = bf16[320,864]{1,0:T(8,128)(2,1)S(1)} all-gather(bf16[80,864]{1,0:T(8,128)(2,1)S(1)} %pad_maximum_fusion.4), channel_id=1, replica_groups=mesh['x'=4,'z'=4,'c'=2,'y'=8,'h'=2] {'z'}, dimensions={0}, use_global_device_ids=true | all-gather | bytes 691200 | tf_op jit(solution)/shard_map/all_gather | solution.py:178
  19.8 0.4 copy.19
  20.2 0.1 fusion.8
  20.2 0.2 pad_maximum_fusion
  20.4 1.5 %broadcast_in_dim.5 = bf16[4,2,216,640]{3,2,1,0:T(8,128)(2,1)} broadcast(bf16[2,216,640]{2,1,0:T(8,128)(2,1)S(1)} %bitcast.39), dimensions={1,2,3} | broadcast | bytes 2764800 | tf_op jit(solution)/shard_map/broadcast_in_dim | solution.py:180
  22.0 8.5 %all-to-all-start = ((bf16[8,216,640]{2,1,0:T(8,128)(2,1)}), bf16[8,216,640]{2,1,0:T(8,128)(2,1)S(1)}, u32[]{:S(2)}, u32[]{:S(2)}) async-start(bf16[8,216,640]{2,1,0:T(8,128)(2,1)} %bitcast.37), calls=%async_computation | async-start | bytes 4423680 | tf_op jit(solution)/shard_map/all_to_all | solution.py:183
  30.5 0.3 copy.18
  30.8 2.0 %collective-permute-start = (bf16[128,2560]{0,1:T(8,128)(2,1)S(1)}, bf16[128,2560]{0,1:T(8,128)(2,1)S(1)}, u32[]{:S(2)}, u32[]{:S(2)}) collective-permute-start(bf16[128,2560]{0,1:T(8,128)(2,1)S(1)} %copy.18), channel_id=1, source_target_pairs={{0,16},{16,0},{1,17},{17,1},{2,18},{18,2},{3,19},{19,3},{4,20},{20... | collective-permute-start | bytes 1966088 | tf_op jit(solution)/shard_map/ppermute | solution.py:19
  32.9 0.9 broadcast_select_fusion.1
  33.7 2.3 %collective-permute-start.1 = (bf16[216,128]{1,0:T(8,128)(2,1)S(1)}, bf16[216,128]{1,0:T(8,128)(2,1)S(1)}, u32[]{:S(2)}, u32[]{:S(2)}) collective-permute-start(bf16[216,128]{1,0:T(8,128)(2,1)S(1)} %get-tuple-element.48), channel_id=1, source_target_pairs={{0,16},{16,0},{1,17},{17,1},{2,18},{18,2},{3,19},{19,3},{4,20},{20... | collective-permute-start | bytes 165896 | tf_op jit(solution)/shard_map/ppermute | solution.py:19
  36.1 0.9 collective-permute-done.1
  36.9 0.0 copy-start.8
  37.0 0.1 maximum_bitcast_fusion.x_ref
  37.1 0.5 copy-done.8
  37.7 0.4 broadcast_in_dim.4.gain_ref
  38.1 0.7 copy-done
  38.7 0.6 shard_map.92
  39.3 1.1 copy-done.2
  40.4 17.7 %all-to-all-done.weight_ref = bf16[8,216,640]{2,1,0:T(8,128)(2,1)S(1)} async-done(((bf16[8,216,640]{2,1,0:T(8,128)(2,1)}), bf16[8,216,640]{2,1,0:T(8,128)(2,1)S(1)}, u32[]{:S(2)}, u32[]{:S(2)}) %all-to-all-start) | async-done | bytes 2211872 | tf_op jit(solution)/shard_map/all_to_all | solution.py:183
  58.1 1.4 copy-done.3
  59.5 2.1 %shard_map.93 = (bf16[216,128]{1,0:T(8,128)(2,1)S(1)}, bf16[2,216,256]{2,1,0:T(8,128)(2,1)S(1)}, f32[2560,128]{1,0:T(8,128)S(1)}, bf16[2784,128]{1,0:T(8,128)(2,1)S(1)}) custom-call(bf16[2784,256]{1,0:T(8,128)(2,1)S(1)} %copy-done.3, bf16[8,216,640]{2,1,0:T(8,128)(2,1)S(1)} %all-to-all-done.weight_ref), custom_call_target="tpu_custom_call" | custom-call | tf_op jit(solution)/shard_map/pallas_call | solution.py:196
  61.5 2.8 %collective-permute-start.2 = (bf16[2784,128]{1,0:T(8,128)(2,1)S(1)}, bf16[2784,128]{1,0:T(8,128)(2,1)S(1)}, u32[]{:S(2)}, u32[]{:S(2)}) collective-permute-start(bf16[2784,128]{1,0:T(8,128)(2,1)S(1)} %get-tuple-element.25), channel_id=1, source_target_pairs={{0,16},{16,0},{1,17},{17,1},{2,18},{18,2},{3,19},{19,3},{4,20},{20... | collective-permute-start | bytes 2138120 | tf_op jit(solution)/shard_map/ppermute | solution.py:19
  64.4 1.7 %collective-permute-done.2.other_ref = bf16[2784,128]{1,0:T(8,128)(2,1)S(1)} collective-permute-done((bf16[2784,128]{1,0:T(8,128)(2,1)S(1)}, bf16[2784,128]{1,0:T(8,128)(2,1)S(1)}, u32[]{:S(2)}, u32[]{:S(2)}) %collective-permute-start.2) | collective-permute-done | bytes 712736 | tf_op jit(solution)/shard_map/ppermute | solution.py:19
  66.1 1.3 shard_map.94
  67.4 5.2 %all-to-all-start.1 = ((bf16[8,352,128]{2,1,0:T(8,128)(2,1)}), bf16[8,352,128]{2,1,0:T(8,128)(2,1)}, u32[]{:S(2)}, u32[]{:S(2)}) async-start(bf16[8,352,128]{2,1,0:T(8,128)(2,1)} %bitcast.7), calls=%async_computation.1 | async-start | bytes 1441792 | tf_op jit(solution)/shard_map/all_to_all | solution.py:229
  72.6 0.9 copy-done.6
  73.5 1.8 %shard_map.95 = (f32[2,216,640]{2,1,0:T(8,128)S(1)}, bf16[2,216,640]{2,1,0:T(8,128)(2,1)}, bf16[2,216,640]{2,1,0:T(8,128)(2,1)}, bf16[2,216,640]{2,1,0:T(8,128)(2,1)}) custom-call(s32[1]{0:T(128)} %bitcast.11.spot_ref, bf16[2784,256]{1,0:T(8,128)(2,1)S(1)} %copy-done.4, bf16[2,216,256]{2,1,0:T(8,128)(2,1)S(1)} %copy-done.6), custom_call_target="tpu_custom_call" | custom-call | tf_op jit(solution)/shard_map/pallas_call | solution.py:207
  75.4 2.0 %collective-permute-start.3 = (bf16[2,216,640]{2,1,0:T(8,128)(2,1)}, bf16[2,216,640]{2,1,0:T(8,128)(2,1)S(1)}, u32[]{:S(2)}, u32[]{:S(2)}) collective-permute-start(bf16[2,216,640]{2,1,0:T(8,128)(2,1)} %get-tuple-element.31), channel_id=1, source_target_pairs={{0,256},{128,384},{256,0},{384,128},{1,257},{129,385},{257,1},{385... | collective-permute-start | bytes 1658888 | tf_op jit(solution)/shard_map/ppermute | solution.py:27
  77.4 3.3 %collective-permute-start.4 = (bf16[2,216,640]{2,1,0:T(8,128)(2,1)}, bf16[2,216,640]{2,1,0:T(8,128)(2,1)S(1)}, u32[]{:S(2)}, u32[]{:S(2)}) collective-permute-start(bf16[2,216,640]{2,1,0:T(8,128)(2,1)} %get-tuple-element.32), channel_id=1, source_target_pairs={{0,128},{128,256},{256,384},{384,0},{1,129},{129,257},{257,385},{3... | collective-permute-start | bytes 1658888 | tf_op jit(solution)/shard_map/ppermute | solution.py:27
  80.6 3.2 %collective-permute-start.5 = (bf16[2,216,640]{2,1,0:T(8,128)(2,1)}, bf16[2,216,640]{2,1,0:T(8,128)(2,1)}, u32[]{:S(2)}, u32[]{:S(2)}) collective-permute-start(bf16[2,216,640]{2,1,0:T(8,128)(2,1)} %get-tuple-element.33), channel_id=1, source_target_pairs={{0,384},{128,0},{256,128},{384,256},{1,385},{129,1},{257,129},{385... | collective-permute-start | bytes 1658888 | tf_op jit(solution)/shard_map/ppermute | solution.py:27
  83.9 11.0 %all-to-all-done.1 = bf16[8,352,128]{2,1,0:T(8,128)(2,1)} async-done(((bf16[8,352,128]{2,1,0:T(8,128)(2,1)}), bf16[8,352,128]{2,1,0:T(8,128)(2,1)}, u32[]{:S(2)}, u32[]{:S(2)}) %all-to-all-start.1) | async-done | bytes 720928 | tf_op jit(solution)/shard_map/all_to_all | solution.py:229
  94.9 1.2 convert_reduce_fusion
  96.1 0.2 fusion
  96.3 10.2 %psum.14 = f32[2,160]{1,0:T(2,128)S(1)} all-reduce(f32[2,160]{1,0:T(2,128)S(1)} %fusion), channel_id=1, replica_groups=mesh['x'=4,'z'=4,'c'=2,'y'=8,'h'=2] {'z'}, use_global_device_ids=true, to_apply=%region_2.3 | all-reduce | flops 320 | bytes 2560 | tf_op jit(solution)/shard_map/psum | solution.py:241
  106.5 2.4 %shard_map.96 = bf16[640,432]{1,0:T(8,128)(2,1)} custom-call(f32[2,216,640]{2,1,0:T(8,128)S(1)} %get-tuple-element.35.own_ref, bf16[2,216,640]{2,1,0:T(8,128)(2,1)S(1)} %collective-permute-done.3.first_ref, bf16[2,216,640]{2,1,0:T(8,128)(2,1)S(1)} %collective-permute-done.4.second_ref, bf16[2,216,640]{2,1,0:T(8,128)(2,1)} %collective-permute-done.5.third_ref), custom_call_target="tpu_custom_call" | custom-call | tf_op jit(solution)/shard_map/pallas_call | solution.py:243
  108.9 7.9 %collective-permute-start.6 = (f32[165,128]{1,0:T(8,128)S(1)}, f32[165,128]{1,0:T(8,128)S(1)}, u32[]{:S(2)}, u32[]{:S(2)}) collective-permute-start(f32[165,128]{1,0:T(8,128)S(1)} %select_bitcast_fusion), channel_id=1, source_target_pairs={{0,1},{1,0},{2,3},{3,2},{4,5},{5,4},{6,7},{7,6},{8,9},{9,8},{10,11... | collective-permute-start | bytes 253448 | tf_op jit(solution)/shard_map/ppermute | solution.py:19
  116.9 6.3 %all-to-all-start.2 = ((bf16[8,80,432]{2,1,0:T(8,128)(2,1)}), bf16[8,80,432]{2,1,0:T(8,128)(2,1)S(1)}, u32[]{:S(2)}, u32[]{:S(2)}) async-start(bf16[8,80,432]{2,1,0:T(8,128)(2,1)} %bitcast.12), calls=%async_computation.2 | async-start | bytes 1310720 | tf_op jit(solution)/shard_map/all_to_all | solution.py:270
  123.2 0.1 dynamic_slice.7
  123.3 6.9 %psum.15 = f32[160]{0:T(256)S(1)} all-reduce(f32[160]{0:T(256)S(1)} %bitcast.44), channel_id=1, replica_groups=mesh['x'=4,'z'=4,'c'=2,'y'=8,'h'=2] {'x'}, use_global_device_ids=true, to_apply=%region_4.5 | all-reduce | flops 160 | bytes 1280 | tf_op jit(solution)/shard_map/psum | solution.py:257
  130.1 4.0 %collective-permute-start.7 = (f32[160]{0:T(256)S(1)}, f32[160]{0:T(256)S(1)}, u32[]{:S(2)}, u32[]{:S(2)}) collective-permute-start(f32[160]{0:T(256)S(1)} %psum.15), channel_id=1, source_target_pairs={{0,16},{16,0},{1,17},{17,1},{2,18},{18,2},{3,19},{19,3},{4,20},{20... | collective-permute-start | bytes 1928 | tf_op jit(solution)/shard_map/ppermute | solution.py:19
  134.2 0.7 fusion.5
  134.9 0.1 collective-permute-done.7
  134.9 0.6 add.35
  135.5 5.1 %all-to-all-done.2 = bf16[8,80,432]{2,1,0:T(8,128)(2,1)S(1)} async-done(((bf16[8,80,432]{2,1,0:T(8,128)(2,1)}), bf16[8,80,432]{2,1,0:T(8,128)(2,1)S(1)}, u32[]{:S(2)}, u32[]{:S(2)}) %all-to-all-start.2) | async-done | bytes 552992 | tf_op jit(solution)/shard_map/all_to_all | solution.py:270
  140.6 0.1 convert_reduce_fusion.1
  140.7 0.1 slice_bitcast_fusion.1
  140.8 0.9 pad_maximum_fusion.2
  (29 shorter events, 0.2 us)
Async XLA Ops:
  22.0 8.5 %copy-start.7 = (bf16[128,2560]{1,0:T(8,128)(2,1)S(1)}, bf16[128,2560]{1,0:T(8,128)(2,1)}, u32[]{:S(2)}) copy-start(bf16[128,2560]{1,0:T(8,128)(2,1)} %param.5) | copy-start | bytes 1966084
  22.0 36.1 %all-to-all-start = ((bf16[8,216,640]{2,1,0:T(8,128)(2,1)}), bf16[8,216,640]{2,1,0:T(8,128)(2,1)S(1)}, u32[]{:S(2)}, u32[]{:S(2)}) async-start(bf16[8,216,640]{2,1,0:T(8,128)(2,1)} %bitcast.37), calls=%async_computation | async-start | bytes 4423680 | tf_op jit(solution)/shard_map/all_to_all | solution.py:183
  30.8 6.1 %collective-permute-start = (bf16[128,2560]{0,1:T(8,128)(2,1)S(1)}, bf16[128,2560]{0,1:T(8,128)(2,1)S(1)}, u32[]{:S(2)}, u32[]{:S(2)}) collective-permute-start(bf16[128,2560]{0,1:T(8,128)(2,1)S(1)} %copy.18), channel_id=1, source_target_pairs={{0,16},{16,0},{1,17},{17,1},{2,18},{18,2},{3,19},{19,3},{4,20},{20... | collective-permute-start | bytes 1966088 | tf_op jit(solution)/shard_map/ppermute | solution.py:19
  33.7 3.2 %collective-permute-start.1 = (bf16[216,128]{1,0:T(8,128)(2,1)S(1)}, bf16[216,128]{1,0:T(8,128)(2,1)S(1)}, u32[]{:S(2)}, u32[]{:S(2)}) collective-permute-start(bf16[216,128]{1,0:T(8,128)(2,1)S(1)} %get-tuple-element.48), channel_id=1, source_target_pairs={{0,16},{16,0},{1,17},{17,1},{2,18},{18,2},{3,19},{19,3},{4,20},{20... | collective-permute-start | bytes 165896 | tf_op jit(solution)/shard_map/ppermute | solution.py:19
  36.9 0.7 copy-start.8
  37.7 1.1 copy-start
  39.3 1.1 copy-start.2
  58.1 1.4 copy-start.3
  59.5 4.9 %copy-start.1 = (bf16[2560,256]{1,0:T(8,128)(2,1)S(1)}, bf16[2560,256]{1,0:T(8,128)(2,1)}, u32[]{:S(2)}) copy-start(bf16[2560,256]{1,0:T(8,128)(2,1)} %copy-done) | copy-start | bytes 3932164
  61.5 5.9 %copy-start.5 = (bf16[2,216,256]{2,1,0:T(8,128)(2,1)}, bf16[2,216,256]{2,1,0:T(8,128)(2,1)S(1)}, u32[]{:S(2)}) copy-start(bf16[2,216,256]{2,1,0:T(8,128)(2,1)S(1)} %get-tuple-element.30.back_ref) | copy-start | bytes 663556
  61.5 4.6 %collective-permute-start.2 = (bf16[2784,128]{1,0:T(8,128)(2,1)S(1)}, bf16[2784,128]{1,0:T(8,128)(2,1)S(1)}, u32[]{:S(2)}, u32[]{:S(2)}) collective-permute-start(bf16[2784,128]{1,0:T(8,128)(2,1)S(1)} %get-tuple-element.25), channel_id=1, source_target_pairs={{0,16},{16,0},{1,17},{17,1},{2,18},{18,2},{3,19},{19,3},{4,20},{20... | collective-permute-start | bytes 2138120 | tf_op jit(solution)/shard_map/ppermute | solution.py:19
  67.4 5.2 %copy-start.4 = (bf16[2784,256]{1,0:T(8,128)(2,1)S(1)}, bf16[2784,256]{1,0:T(8,128)(2,1)}, u32[]{:S(2)}) copy-start(bf16[2784,256]{1,0:T(8,128)(2,1)} %copy-done.2) | copy-start | bytes 4276228
  67.4 27.4 %all-to-all-start.1 = ((bf16[8,352,128]{2,1,0:T(8,128)(2,1)}), bf16[8,352,128]{2,1,0:T(8,128)(2,1)}, u32[]{:S(2)}, u32[]{:S(2)}) async-start(bf16[8,352,128]{2,1,0:T(8,128)(2,1)} %bitcast.7), calls=%async_computation.1 | async-start | bytes 1441792 | tf_op jit(solution)/shard_map/all_to_all | solution.py:229
  72.6 0.9 copy-start.6
  75.4 31.1 %collective-permute-start.3 = (bf16[2,216,640]{2,1,0:T(8,128)(2,1)}, bf16[2,216,640]{2,1,0:T(8,128)(2,1)S(1)}, u32[]{:S(2)}, u32[]{:S(2)}) collective-permute-start(bf16[2,216,640]{2,1,0:T(8,128)(2,1)} %get-tuple-element.31), channel_id=1, source_target_pairs={{0,256},{128,384},{256,0},{384,128},{1,257},{129,385},{257,1},{385... | collective-permute-start | bytes 1658888 | tf_op jit(solution)/shard_map/ppermute | solution.py:27
  77.4 29.1 %collective-permute-start.4 = (bf16[2,216,640]{2,1,0:T(8,128)(2,1)}, bf16[2,216,640]{2,1,0:T(8,128)(2,1)S(1)}, u32[]{:S(2)}, u32[]{:S(2)}) collective-permute-start(bf16[2,216,640]{2,1,0:T(8,128)(2,1)} %get-tuple-element.32), channel_id=1, source_target_pairs={{0,128},{128,256},{256,384},{384,0},{1,129},{129,257},{257,385},{3... | collective-permute-start | bytes 1658888 | tf_op jit(solution)/shard_map/ppermute | solution.py:27
  80.6 25.8 %collective-permute-start.5 = (bf16[2,216,640]{2,1,0:T(8,128)(2,1)}, bf16[2,216,640]{2,1,0:T(8,128)(2,1)}, u32[]{:S(2)}, u32[]{:S(2)}) collective-permute-start(bf16[2,216,640]{2,1,0:T(8,128)(2,1)} %get-tuple-element.33), channel_id=1, source_target_pairs={{0,384},{128,0},{256,128},{384,256},{1,385},{129,1},{257,129},{385... | collective-permute-start | bytes 1658888 | tf_op jit(solution)/shard_map/ppermute | solution.py:27
  108.9 14.3 %collective-permute-start.6 = (f32[165,128]{1,0:T(8,128)S(1)}, f32[165,128]{1,0:T(8,128)S(1)}, u32[]{:S(2)}, u32[]{:S(2)}) collective-permute-start(f32[165,128]{1,0:T(8,128)S(1)} %select_bitcast_fusion), channel_id=1, source_target_pairs={{0,1},{1,0},{2,3},{3,2},{4,5},{5,4},{6,7},{7,6},{8,9},{9,8},{10,11... | collective-permute-start | bytes 253448 | tf_op jit(solution)/shard_map/ppermute | solution.py:19
  116.9 23.8 %all-to-all-start.2 = ((bf16[8,80,432]{2,1,0:T(8,128)(2,1)}), bf16[8,80,432]{2,1,0:T(8,128)(2,1)S(1)}, u32[]{:S(2)}, u32[]{:S(2)}) async-start(bf16[8,80,432]{2,1,0:T(8,128)(2,1)} %bitcast.12), calls=%async_computation.2 | async-start | bytes 1310720 | tf_op jit(solution)/shard_map/all_to_all | solution.py:270
  130.1 4.8 %collective-permute-start.7 = (f32[160]{0:T(256)S(1)}, f32[160]{0:T(256)S(1)}, u32[]{:S(2)}, u32[]{:S(2)}) collective-permute-start(f32[160]{0:T(256)S(1)} %psum.15), channel_id=1, source_target_pairs={{0,16},{16,0},{1,17},{17,1},{2,18},{18,2},{3,19},{19,3},{4,20},{20... | collective-permute-start | bytes 1928 | tf_op jit(solution)/shard_map/ppermute | solution.py:19

commit v14 on v13

--- a/solution.py
+++ b/solution.py
@@ -94,7 +94,8 @@
         other_ref[rows, :] = part[:, tokens:].astype(BF)
 
 
-def gradient_kernel(spot_ref, normed_ref, back_ref, *outs):
+def gradient_kernel(spot_ref, normed_ref, back_ref, ready_ref, *outs):
+    ready_ref[...] = jnp.zeros_like(ready_ref)
     size = outs[0].shape[2]
     for index in range(NX):
         block = (spot_ref[0] + index) % NX
@@ -105,7 +106,7 @@
 
 
 def blocks_kernel(
-    core_ref, own_ref, other_ref, x_ref, root_ref, gain_ref, mine_ref, out_ref, hidden_ref
+    core_ref, _, own_ref, other_ref, x_ref, root_ref, gain_ref, mine_ref, out_ref, hidden_ref
 ):
     width, tokens = own_ref.shape
     half = mine_ref.shape[0]
@@ -204,9 +205,10 @@
         [VMEM] * 2,
     )(normed, weight)
     part_other = swap_core(part_other)
-    terms = call(
+    ready, *terms = call(
         gradient_kernel,
-        tuple(shape((2, half, column_rows), F32 if index == 0 else BF) for index in range(NX)),
+        (shape((8, 128), F32),)
+        + tuple(shape((2, half, column_rows), F32 if index == 0 else BF) for index in range(NX)),
         [SMEM] + [VMEM] * 2,
     )(spot, normed, back)
     travelling = [shift_x(terms[steps], steps) for steps in (2, 1, 3)]
@@ -215,9 +217,10 @@
     sending, hidden = call(
         blocks_kernel,
         (shape((n_dp, features + spare, tokens), BF), shape((columns, tokens), BF)),
-        [SMEM] + [VMEM] * 6,
+        [SMEM] + [VMEM] * 7,
     )(
         lax.axis_index("c").astype(jnp.int32).reshape(1),
+        ready,
         part_own,
         part_other,
         inputs_t[:, :tokens],

time: 143 us -> 151 us (1.056)
  local copies, waits for them, and re-layouts: 7.58 us -> 14.3 us
    unnamed x19 -> x31, local copies, waits for them, and re-layouts: 4.96 us -> 10.5 us
    all_to_all x1, waiting for transfers between devices: 11 us -> 13.8 us  [per_device(): lax.all_to_all(sending.reshape(n_dp // NH, NH * (features + spare), token...]
    ppermute x5, waiting for transfers between devices: 2.65 us -> 0.94 us  [swap(): return lax.ppermute(value, axis, [(0, 1), (1, 0)])]
  transfers between devices with their start and end apart: 11 -> 11, of which waited for: 6 -> 5; matrix products, arithmetic and copies ran while one was open for 3% -> 4% of each run, Pallas kernels for 2% -> 1%
where the time goes in v14:
time: 151 us; the launch traced here: 150 us
  starting transfers between devices  47.3 us (31%)
  waiting for transfers between devices  37.5 us (25%)
  blocking collectives  35.2 us (23%)
  local copies, waits for them, and re-layouts  14.3 us (9%)
  Pallas kernels  9.26 us (6%)
  other arithmetic  5.89 us (4%)
    ppermute x5, starting transfers between devices, swap(): return lax.ppermute(value, axis, [(0, 1), (1, 0)])  19 us
    all_gather x1, blocking collectives, per_device(): lax.all_gather(jnp.concatenate([w_gate, w_up], 1), 'z', axis=0, tiled=True)  18.1 us
    all_to_all x1, waiting for transfers between devices, per_device(): weight = lax.all_to_all(copies, ('x', 'c'), 0, 0, tiled=True)  17.7 us
    all_to_all x1, waiting for transfers between devices, per_device(): lax.all_to_all(sending.reshape(n_dp // NH, NH * (features + spare), token...  13.8 us
    unnamed x31, local copies, waits for them, and re-layouts  10.5 us
    psum x1, blocking collectives, per_device(): gain_part = lax.psum(gain_part, 'z')  10.2 us
    all_to_all x1, starting transfers between devices, per_device(): weight = lax.all_to_all(copies, ('x', 'c'), 0, 0, tiled=True)  8.54 us
    ppermute x3, starting transfers between devices, shift_x(): return lax.ppermute(value, 'x', [(x, (x + steps) % NX) for x in range(NX)])  8.48 us
  transfers between devices with their start and end apart: 11, of which 5 were waited for; matrix products, arithmetic and copies ran while one was open for 4% of the time, Pallas kernels for 1%

profile of v14, /device:TPU:1, one launch (start us, length us, event | category | flops | bytes accessed | tf_op | source)
XLA Modules:
  0.0 150.5 jit_solution(15360296640993146628)
XLA Ops:
  0.6 1.0 pad_maximum_fusion.4
  1.7 18.1 %all_gather.3 = bf16[320,864]{1,0:T(8,128)(2,1)S(1)} all-gather(bf16[80,864]{1,0:T(8,128)(2,1)S(1)} %pad_maximum_fusion.4), channel_id=1, replica_groups=mesh['x'=4,'z'=4,'c'=2,'y'=8,'h'=2] {'z'}, dimensions={0}, use_global_device_ids=true | all-gather | bytes 691200 | tf_op jit(solution)/shard_map/all_gather | solution.py:179
  19.8 0.4 copy.19
  20.2 0.2 pad_maximum_fusion
  20.4 1.6 %broadcast_in_dim.5 = bf16[4,2,216,640]{3,2,1,0:T(8,128)(2,1)} broadcast(bf16[2,216,640]{2,1,0:T(8,128)(2,1)S(1)} %bitcast.40), dimensions={1,2,3} | broadcast | bytes 2764800 | tf_op jit(solution)/shard_map/broadcast_in_dim | solution.py:181
  22.0 8.5 %all-to-all-start = ((bf16[8,216,640]{2,1,0:T(8,128)(2,1)}), bf16[8,216,640]{2,1,0:T(8,128)(2,1)S(1)}, u32[]{:S(2)}, u32[]{:S(2)}) async-start(bf16[8,216,640]{2,1,0:T(8,128)(2,1)} %bitcast.38), calls=%async_computation | async-start | bytes 4423680 | tf_op jit(solution)/shard_map/all_to_all | solution.py:184
  30.5 0.3 copy.18
  30.9 2.0 %collective-permute-start = (bf16[128,2560]{0,1:T(8,128)(2,1)S(1)}, bf16[128,2560]{0,1:T(8,128)(2,1)S(1)}, u32[]{:S(2)}, u32[]{:S(2)}) collective-permute-start(bf16[128,2560]{0,1:T(8,128)(2,1)S(1)} %copy.18), channel_id=1, source_target_pairs={{0,16},{16,0},{1,17},{17,1},{2,18},{18,2},{3,19},{19,3},{4,20},{20... | collective-permute-start | bytes 1966088 | tf_op jit(solution)/shard_map/ppermute | solution.py:19
  32.9 0.9 broadcast_select_fusion.1
  33.8 2.3 %collective-permute-start.1 = (bf16[216,128]{1,0:T(8,128)(2,1)S(1)}, bf16[216,128]{1,0:T(8,128)(2,1)S(1)}, u32[]{:S(2)}, u32[]{:S(2)}) collective-permute-start(bf16[216,128]{1,0:T(8,128)(2,1)S(1)} %get-tuple-element.50), channel_id=1, source_target_pairs={{0,16},{16,0},{1,17},{17,1},{2,18},{18,2},{3,19},{19,3},{4,20},{20... | collective-permute-start | bytes 165896 | tf_op jit(solution)/shard_map/ppermute | solution.py:19
  36.1 0.9 collective-permute-done.1
  37.1 0.5 copy-done.14
  37.7 0.4 broadcast_in_dim.4.gain_ref
  38.1 0.7 copy-done
  38.7 0.6 shard_map.92
  39.3 1.1 copy-done.1
  40.4 17.7 %all-to-all-done.weight_ref = bf16[8,216,640]{2,1,0:T(8,128)(2,1)S(1)} async-done(((bf16[8,216,640]{2,1,0:T(8,128)(2,1)}), bf16[8,216,640]{2,1,0:T(8,128)(2,1)S(1)}, u32[]{:S(2)}, u32[]{:S(2)}) %all-to-all-start) | async-done | bytes 2211872 | tf_op jit(solution)/shard_map/all_to_all | solution.py:184
  58.1 1.4 copy-done.2
  59.5 2.9 %shard_map.93 = (bf16[216,128]{1,0:T(8,128)(2,1)S(1)}, bf16[2,216,256]{2,1,0:T(8,128)(2,1)S(1)}, f32[2560,128]{1,0:T(8,128)S(1)}, bf16[2784,128]{1,0:T(8,128)(2,1)}) custom-call(bf16[2784,256]{1,0:T(8,128)(2,1)S(1)} %copy-done.2, bf16[8,216,640]{2,1,0:T(8,128)(2,1)S(1)} %all-to-all-done.weight_ref), custom_call_target="tpu_custom_call" | custom-call | tf_op jit(solution)/shard_map/pallas_call | solution.py:197
  62.4 1.1 copy-done.4
  63.4 0.7 copy-done.7
  64.1 0.6 copy-done.9
  64.8 2.8 %collective-permute-start.2 = (bf16[2784,128]{1,0:T(8,128)(2,1)}, bf16[2784,128]{1,0:T(8,128)(2,1)}, u32[]{:S(2)}, u32[]{:S(2)}) collective-permute-start(bf16[2784,128]{1,0:T(8,128)(2,1)} %get-tuple-element.28), channel_id=1, source_target_pairs={{0,16},{16,0},{1,17},{17,1},{2,18},{18,2},{3,19},{19,3},{4,20},{20... | collective-permute-start | bytes 2138120 | tf_op jit(solution)/shard_map/ppermute | solution.py:19
  67.5 1.2 slice.88.x_ref
  68.8 1.3 copy-done.3
  70.2 0.9 copy-done.8
  71.1 1.6 %shard_map.94 = (f32[8,128]{1,0:T(8,128)S(1)}, f32[2,216,640]{2,1,0:T(8,128)S(1)}, bf16[2,216,640]{2,1,0:T(8,128)(2,1)S(1)}, bf16[2,216,640]{2,1,0:T(8,128)(2,1)}, bf16[2,216,640]{2,1,0:T(8,128)(2,1)S(1)}) custom-call(s32[1]{0:T(128)} %bitcast.1.spot_ref, bf16[2784,256]{1,0:T(8,128)(2,1)S(1)} %copy-done.3, bf16[2,216,256]{2,1,0:T(8,128)(2,1)S(1)} %copy-done.8), custom_call_target="tpu_custom_call" | custom-call | tf_op jit(solution)/shard_map/pallas_call | solution.py:208
  72.7 0.8 copy-done.11
  73.5 0.2 copy-done.12
  73.7 1.8 %shard_map.95 = (bf16[16,176,128]{2,1,0:T(8,128)(2,1)S(1)}, bf16[432,128]{1,0:T(8,128)(2,1)}) custom-call(s32[1]{0:T(128)} %bitcast.core_ref, f32[8,128]{1,0:T(8,128)S(1)} %get-tuple-element.26._, f32[2560,128]{1,0:T(8,128)S(1)} %copy-done.5, bf16[2784,128]{1,0:T(8,128)(2,1)} %collective-permute-done.2.other_ref, bf16[2560,128]{1,0:T(8,128)(2,1)S(1)} %slice.88.x_ref, ...), custom_call_target="tpu_custom_call" | custom-call | tf_op jit(solution)/shard_map/pallas_call | solution.py:217
  75.5 0.9 copy-done.6
  76.4 5.0 %all-to-all-start.1 = ((bf16[8,352,128]{2,1,0:T(8,128)(2,1)}), bf16[8,352,128]{2,1,0:T(8,128)(2,1)}, u32[]{:S(2)}, u32[]{:S(2)}) async-start(bf16[8,352,128]{2,1,0:T(8,128)(2,1)} %bitcast.37), calls=%async_computation.1 | async-start | bytes 1441792 | tf_op jit(solution)/shard_map/all_to_all | solution.py:232
  81.4 2.0 %collective-permute-start.3 = (bf16[2,216,640]{2,1,0:T(8,128)(2,1)}, bf16[2,216,640]{2,1,0:T(8,128)(2,1)S(1)}, u32[]{:S(2)}, u32[]{:S(2)}) collective-permute-start(bf16[2,216,640]{2,1,0:T(8,128)(2,1)} %get-tuple-element.33), channel_id=1, source_target_pairs={{0,256},{128,384},{256,0},{384,128},{1,257},{129,385},{257,1},{385... | collective-permute-start | bytes 1658888 | tf_op jit(solution)/shard_map/ppermute | solution.py:27
  83.4 3.3 %collective-permute-start.4 = (bf16[2,216,640]{2,1,0:T(8,128)(2,1)}, bf16[2,216,640]{2,1,0:T(8,128)(2,1)S(1)}, u32[]{:S(2)}, u32[]{:S(2)}) collective-permute-start(bf16[2,216,640]{2,1,0:T(8,128)(2,1)} %copy-done.12), channel_id=1, source_target_pairs={{0,128},{128,256},{256,384},{384,0},{1,129},{129,257},{257,385},{3... | collective-permute-start | bytes 1658888 | tf_op jit(solution)/shard_map/ppermute | solution.py:27
  86.7 3.2 %collective-permute-start.5 = (bf16[2,216,640]{2,1,0:T(8,128)(2,1)}, bf16[2,216,640]{2,1,0:T(8,128)(2,1)}, u32[]{:S(2)}, u32[]{:S(2)}) collective-permute-start(bf16[2,216,640]{2,1,0:T(8,128)(2,1)} %copy-done.11), channel_id=1, source_target_pairs={{0,384},{128,0},{256,128},{384,256},{1,385},{129,1},{257,129},{385... | collective-permute-start | bytes 1658888 | tf_op jit(solution)/shard_map/ppermute | solution.py:27
  89.9 13.8 %all-to-all-done.1 = bf16[8,352,128]{2,1,0:T(8,128)(2,1)} async-done(((bf16[8,352,128]{2,1,0:T(8,128)(2,1)}), bf16[8,352,128]{2,1,0:T(8,128)(2,1)}, u32[]{:S(2)}, u32[]{:S(2)}) %all-to-all-start.1) | async-done | bytes 720928 | tf_op jit(solution)/shard_map/all_to_all | solution.py:232
  103.7 1.2 convert_reduce_fusion
  105.0 0.1 fusion
  105.1 10.2 %psum.14 = f32[2,160]{1,0:T(2,128)S(1)} all-reduce(f32[2,160]{1,0:T(2,128)S(1)} %fusion), channel_id=1, replica_groups=mesh['x'=4,'z'=4,'c'=2,'y'=8,'h'=2] {'z'}, use_global_device_ids=true, to_apply=%region_2.3 | all-reduce | flops 320 | bytes 2560 | tf_op jit(solution)/shard_map/psum | solution.py:244
  115.3 2.4 %shard_map.96 = bf16[640,432]{1,0:T(8,128)(2,1)} custom-call(f32[2,216,640]{2,1,0:T(8,128)S(1)} %get-tuple-element.37.own_ref, bf16[2,216,640]{2,1,0:T(8,128)(2,1)S(1)} %collective-permute-done.3.first_ref, bf16[2,216,640]{2,1,0:T(8,128)(2,1)S(1)} %collective-permute-done.4.second_ref, bf16[2,216,640]{2,1,0:T(8,128)(2,1)} %collective-permute-done.5.third_ref), custom_call_target="tpu_custom_call" | custom-call | tf_op jit(solution)/shard_map/pallas_call | solution.py:246
  117.8 7.9 %collective-permute-start.6 = (f32[165,128]{1,0:T(8,128)S(1)}, f32[165,128]{1,0:T(8,128)S(1)}, u32[]{:S(2)}, u32[]{:S(2)}) collective-permute-start(f32[165,128]{1,0:T(8,128)S(1)} %select_bitcast_fusion), channel_id=1, source_target_pairs={{0,1},{1,0},{2,3},{3,2},{4,5},{5,4},{6,7},{7,6},{8,9},{9,8},{10,11... | collective-permute-start | bytes 253448 | tf_op jit(solution)/shard_map/ppermute | solution.py:19
  125.7 6.2 %all-to-all-start.2 = ((bf16[8,80,432]{2,1,0:T(8,128)(2,1)}), bf16[8,80,432]{2,1,0:T(8,128)(2,1)S(1)}, u32[]{:S(2)}, u32[]{:S(2)}) async-start(bf16[8,80,432]{2,1,0:T(8,128)(2,1)} %bitcast.12), calls=%async_computation.2 | async-start | bytes 1310720 | tf_op jit(solution)/shard_map/all_to_all | solution.py:273
  132.0 6.9 %psum.15 = f32[160]{0:T(256)S(1)} all-reduce(f32[160]{0:T(256)S(1)} %bitcast.45), channel_id=1, replica_groups=mesh['x'=4,'z'=4,'c'=2,'y'=8,'h'=2] {'x'}, use_global_device_ids=true, to_apply=%region_4.5 | all-reduce | flops 160 | bytes 1280 | tf_op jit(solution)/shard_map/psum | solution.py:260
  139.0 4.0 %collective-permute-start.7 = (f32[160]{0:T(256)S(1)}, f32[160]{0:T(256)S(1)}, u32[]{:S(2)}, u32[]{:S(2)}) collective-permute-start(f32[160]{0:T(256)S(1)} %psum.15), channel_id=1, source_target_pairs={{0,16},{16,0},{1,17},{17,1},{2,18},{18,2},{3,19},{19,3},{4,20},{20... | collective-permute-start | bytes 1928 | tf_op jit(solution)/shard_map/ppermute | solution.py:19
  143.0 0.7 fusion.5
  143.8 0.6 add.35
  144.3 5.1 %all-to-all-done.2 = bf16[8,80,432]{2,1,0:T(8,128)(2,1)S(1)} async-done(((bf16[8,80,432]{2,1,0:T(8,128)(2,1)}), bf16[8,80,432]{2,1,0:T(8,128)(2,1)S(1)}, u32[]{:S(2)}, u32[]{:S(2)}) %all-to-all-start.2) | async-done | bytes 552992 | tf_op jit(solution)/shard_map/all_to_all | solution.py:273
  149.6 0.9 pad_maximum_fusion.2
  (41 shorter events, 0.7 us)
Async XLA Ops:
  22.0 8.5 %copy-start.13 = (bf16[128,2560]{1,0:T(8,128)(2,1)S(1)}, bf16[128,2560]{1,0:T(8,128)(2,1)}, u32[]{:S(2)}) copy-start(bf16[128,2560]{1,0:T(8,128)(2,1)} %param.5) | copy-start | bytes 1966084
  22.0 36.1 %all-to-all-start = ((bf16[8,216,640]{2,1,0:T(8,128)(2,1)}), bf16[8,216,640]{2,1,0:T(8,128)(2,1)S(1)}, u32[]{:S(2)}, u32[]{:S(2)}) async-start(bf16[8,216,640]{2,1,0:T(8,128)(2,1)} %bitcast.38), calls=%async_computation | async-start | bytes 4423680 | tf_op jit(solution)/shard_map/all_to_all | solution.py:184
  30.9 6.1 %collective-permute-start = (bf16[128,2560]{0,1:T(8,128)(2,1)S(1)}, bf16[128,2560]{0,1:T(8,128)(2,1)S(1)}, u32[]{:S(2)}, u32[]{:S(2)}) collective-permute-start(bf16[128,2560]{0,1:T(8,128)(2,1)S(1)} %copy.18), channel_id=1, source_target_pairs={{0,16},{16,0},{1,17},{17,1},{2,18},{18,2},{3,19},{19,3},{4,20},{20... | collective-permute-start | bytes 1966088 | tf_op jit(solution)/shard_map/ppermute | solution.py:19
  33.8 3.2 %collective-permute-start.1 = (bf16[216,128]{1,0:T(8,128)(2,1)S(1)}, bf16[216,128]{1,0:T(8,128)(2,1)S(1)}, u32[]{:S(2)}, u32[]{:S(2)}) collective-permute-start(bf16[216,128]{1,0:T(8,128)(2,1)S(1)} %get-tuple-element.50), channel_id=1, source_target_pairs={{0,16},{16,0},{1,17},{17,1},{2,18},{18,2},{3,19},{19,3},{4,20},{20... | collective-permute-start | bytes 165896 | tf_op jit(solution)/shard_map/ppermute | solution.py:19
  37.0 0.7 copy-start.14
  37.7 1.1 copy-start
  39.3 1.1 copy-start.1
  58.1 1.4 copy-start.2
  62.4 1.1 copy-start.4
  63.4 0.7 copy-start.7
  64.1 0.6 copy-start.9
  64.8 8.0 %collective-permute-start.2 = (bf16[2784,128]{1,0:T(8,128)(2,1)}, bf16[2784,128]{1,0:T(8,128)(2,1)}, u32[]{:S(2)}, u32[]{:S(2)}) collective-permute-start(bf16[2784,128]{1,0:T(8,128)(2,1)} %get-tuple-element.28), channel_id=1, source_target_pairs={{0,16},{16,0},{1,17},{17,1},{2,18},{18,2},{3,19},{19,3},{4,20},{20... | collective-permute-start | bytes 2138120 | tf_op jit(solution)/shard_map/ppermute | solution.py:19
  67.5 6.1 %copy-start.5 = (f32[2560,128]{1,0:T(8,128)S(1)}, f32[2560,128]{1,0:T(8,128)}, u32[]{:S(2)}) copy-start(f32[2560,128]{1,0:T(8,128)} %copy-done.4) | copy-start | bytes 3932164
  68.8 1.4 copy-start.3
  70.2 0.9 copy-start.8
  71.1 2.6 %copy-start.10 = (bf16[216,128]{1,0:T(8,128)(2,1)S(1)}, bf16[216,128]{1,0:T(8,128)(2,1)}, u32[]{:S(2)}) copy-start(bf16[216,128]{1,0:T(8,128)(2,1)} %copy-done.9) | copy-start | bytes 165892
  72.7 0.8 copy-start.11
  72.7 1.0 copy-start.12
  75.5 0.9 copy-start.6
  76.4 27.3 %all-to-all-start.1 = ((bf16[8,352,128]{2,1,0:T(8,128)(2,1)}), bf16[8,352,128]{2,1,0:T(8,128)(2,1)}, u32[]{:S(2)}, u32[]{:S(2)}) async-start(bf16[8,352,128]{2,1,0:T(8,128)(2,1)} %bitcast.37), calls=%async_computation.1 | async-start | bytes 1441792 | tf_op jit(solution)/shard_map/all_to_all | solution.py:232
  81.4 33.9 %collective-permute-start.3 = (bf16[2,216,640]{2,1,0:T(8,128)(2,1)}, bf16[2,216,640]{2,1,0:T(8,128)(2,1)S(1)}, u32[]{:S(2)}, u32[]{:S(2)}) collective-permute-start(bf16[2,216,640]{2,1,0:T(8,128)(2,1)} %get-tuple-element.33), channel_id=1, source_target_pairs={{0,256},{128,384},{256,0},{384,128},{1,257},{129,385},{257,1},{385... | collective-permute-start | bytes 1658888 | tf_op jit(solution)/shard_map/ppermute | solution.py:27
  83.4 31.9 %collective-permute-start.4 = (bf16[2,216,640]{2,1,0:T(8,128)(2,1)}, bf16[2,216,640]{2,1,0:T(8,128)(2,1)S(1)}, u32[]{:S(2)}, u32[]{:S(2)}) collective-permute-start(bf16[2,216,640]{2,1,0:T(8,128)(2,1)} %copy-done.12), channel_id=1, source_target_pairs={{0,128},{128,256},{256,384},{384,0},{1,129},{129,257},{257,385},{3... | collective-permute-start | bytes 1658888 | tf_op jit(solution)/shard_map/ppermute | solution.py:27
  86.7 28.6 %collective-permute-start.5 = (bf16[2,216,640]{2,1,0:T(8,128)(2,1)}, bf16[2,216,640]{2,1,0:T(8,128)(2,1)}, u32[]{:S(2)}, u32[]{:S(2)}) collective-permute-start(bf16[2,216,640]{2,1,0:T(8,128)(2,1)} %copy-done.11), channel_id=1, source_target_pairs={{0,384},{128,0},{256,128},{384,256},{1,385},{129,1},{257,129},{385... | collective-permute-start | bytes 1658888 | tf_op jit(solution)/shard_map/ppermute | solution.py:27
  117.8 14.3 %collective-permute-start.6 = (f32[165,128]{1,0:T(8,128)S(1)}, f32[165,128]{1,0:T(8,128)S(1)}, u32[]{:S(2)}, u32[]{:S(2)}) collective-permute-start(f32[165,128]{1,0:T(8,128)S(1)} %select_bitcast_fusion), channel_id=1, source_target_pairs={{0,1},{1,0},{2,3},{3,2},{4,5},{5,4},{6,7},{7,6},{8,9},{9,8},{10,11... | collective-permute-start | bytes 253448 | tf_op jit(solution)/shard_map/ppermute | solution.py:19
  125.7 23.7 %all-to-all-start.2 = ((bf16[8,80,432]{2,1,0:T(8,128)(2,1)}), bf16[8,80,432]{2,1,0:T(8,128)(2,1)S(1)}, u32[]{:S(2)}, u32[]{:S(2)}) async-start(bf16[8,80,432]{2,1,0:T(8,128)(2,1)} %bitcast.12), calls=%async_computation.2 | async-start | bytes 1310720 | tf_op jit(solution)/shard_map/all_to_all | solution.py:273
  139.0 4.8 %collective-permute-start.7 = (f32[160]{0:T(256)S(1)}, f32[160]{0:T(256)S(1)}, u32[]{:S(2)}, u32[]{:S(2)}) collective-permute-start(f32[160]{0:T(256)S(1)} %psum.15), channel_id=1, source_target_pairs={{0,16},{16,0},{1,17},{17,1},{2,18},{18,2},{3,19},{19,3},{4,20},{20... | collective-permute-start | bytes 1928 | tf_op jit(solution)/shard_map/ppermute | solution.py:19

commit v15 on v13

--- a/solution.py
+++ b/solution.py
@@ -1,3 +1,5 @@
+import functools
+
 import jax
 import jax.numpy as jnp
 from jax import lax
@@ -94,10 +96,10 @@
         other_ref[rows, :] = part[:, tokens:].astype(BF)
 
 
-def gradient_kernel(spot_ref, normed_ref, back_ref, *outs):
+def gradient_kernel(steps, spot_ref, normed_ref, back_ref, *outs):
     size = outs[0].shape[2]
-    for index in range(NX):
-        block = (spot_ref[0] + index) % NX
+    for index, step in enumerate(steps):
+        block = (spot_ref[0] + step) % NX
         rows = normed_ref[pl.ds(pl.multiple_of(block * size, size), size), :]
         for which in range(2):
             term = lax.dot_general(back_ref[which], rows, NT, preferred_element_type=F32)
@@ -204,12 +206,17 @@
         [VMEM] * 2,
     )(normed, weight)
     part_other = swap_core(part_other)
-    terms = call(
-        gradient_kernel,
-        tuple(shape((2, half, column_rows), F32 if index == 0 else BF) for index in range(NX)),
-        [SMEM] + [VMEM] * 2,
-    )(spot, normed, back)
-    travelling = [shift_x(terms[steps], steps) for steps in (2, 1, 3)]
+    def gradient(steps, dtype):
+        return call(
+            functools.partial(gradient_kernel, steps),
+            tuple(shape((2, half, column_rows), dtype) for _ in steps),
+            [SMEM] + [VMEM] * 2,
+        )(spot, normed, back)
+
+    (far,) = gradient((2,), BF)
+    after, before = gradient((1, 3), BF)
+    (own_term,) = gradient((0,), F32)
+    travelling = [shift_x(far, 2), shift_x(after, 1), shift_x(before, 3)]
 
     spare = 16
     sending, hidden = call(
@@ -241,7 +248,7 @@
     gain_part = lax.psum(gain_part, "z")
     gain_part, travelling = lax.optimization_barrier((gain_part, travelling))
     column_sum = call(column_kernel, shape((column_rows, columns), BF), [VMEM] * 4)(
-        terms[0], *travelling
+        own_term, *travelling
     )
 
     low_half = lax.axis_index("h") == 0

time: 143 us -> 143 us (level)
  Pallas kernels: 8.18 us -> 10.7 us
  local copies, waits for them, and re-layouts: 7.58 us -> 6 us
    all_to_all x1, waiting for transfers between devices: 17.7 us -> 19.7 us  [per_device(): weight = lax.all_to_all(copies, ('x', 'c'), 0, 0, tiled=True)]
    pallas_call x1, Pallas kernels: 2.07 us -> 3.76 us  [per_device(): call(forward_kernel, (shape((half, tokens), BF), shape((2, half, 2 * toke...]
    unnamed x19, local copies, waits for them, and re-layouts: 4.96 us -> 3.4 us
    pallas_call x1 -> x3, Pallas kernels: 1.81 us -> 3.02 us  [gradient(): call(functools.partial(gradient_kernel, steps), tuple((shape((2, half, co...]
  transfers between devices with their start and end apart: 11 -> 11, of which waited for: 6 -> 6; matrix products, arithmetic and copies ran while one was open for 3% -> 3% of each run, Pallas kernels for 2% -> 3%
where the time goes in v15:
time: 143 us
  starting transfers between devices  47.4 us (33%)
  waiting for transfers between devices  37.2 us (26%)
  blocking collectives  35.3 us (25%)
  Pallas kernels  10.7 us (7%)
  local copies, waits for them, and re-layouts  6 us (4%)
  other arithmetic  5.05 us (4%)
    all_to_all x1, waiting for transfers between devices, per_device(): weight = lax.all_to_all(copies, ('x', 'c'), 0, 0, tiled=True)  19.7 us
    ppermute x5, starting transfers between devices, swap(): return lax.ppermute(value, axis, [(0, 1), (1, 0)])  19 us
    all_gather x1, blocking collectives, per_device(): lax.all_gather(jnp.concatenate([w_gate, w_up], 1), 'z', axis=0, tiled=True)  18.1 us
    psum x1, blocking collectives, per_device(): gain_part = lax.psum(gain_part, 'z')  10.3 us
    all_to_all x1, waiting for transfers between devices, per_device(): lax.all_to_all(sending.reshape(n_dp // NH, NH * (features + spare), token...  9.77 us
    all_to_all x1, starting transfers between devices, per_device(): weight = lax.all_to_all(copies, ('x', 'c'), 0, 0, tiled=True)  9.27 us
    ppermute x3, starting transfers between devices, shift_x(): return lax.ppermute(value, 'x', [(x, (x + steps) % NX) for x in range(NX)])  8.48 us
    psum x1, blocking collectives, per_device(): lax.psum(totals[features + 3:].reshape(lines * tokens)[:features], 'x')  6.9 us
  transfers between devices with their start and end apart: 11, of which 6 were waited for; matrix products, arithmetic and copies ran while one was open for 3% of the time, Pallas kernels for 3%

profile of v15, /device:TPU:1, one launch (start us, length us, event | category | flops | bytes accessed | tf_op | source)
XLA Modules:
  0.0 142.6 jit_solution(12248928577631947194)
XLA Ops:
  0.6 1.0 pad_maximum_fusion.4
  1.7 18.1 %all_gather.3 = bf16[320,864]{1,0:T(8,128)(2,1)S(1)} all-gather(bf16[80,864]{1,0:T(8,128)(2,1)S(1)} %pad_maximum_fusion.4), channel_id=1, replica_groups=mesh['x'=4,'z'=4,'c'=2,'y'=8,'h'=2] {'z'}, dimensions={0}, use_global_device_ids=true | all-gather | bytes 691200 | tf_op jit(solution)/shard_map/all_gather | solution.py:180
  19.8 0.4 copy.19
  20.2 0.1 fusion.8
  20.2 0.2 pad_maximum_fusion
  20.4 1.5 %broadcast_in_dim.5 = bf16[4,2,216,640]{3,2,1,0:T(8,128)(2,1)} broadcast(bf16[2,216,640]{2,1,0:T(8,128)(2,1)S(1)} %bitcast.39), dimensions={1,2,3} | broadcast | bytes 2764800 | tf_op jit(solution)/shard_map/broadcast_in_dim | solution.py:182
  21.9 9.3 %all-to-all-start = ((bf16[8,216,640]{2,1,0:T(8,128)(2,1)}), bf16[8,216,640]{2,1,0:T(8,128)(2,1)}, u32[]{:S(2)}, u32[]{:S(2)}) async-start(bf16[8,216,640]{2,1,0:T(8,128)(2,1)} %bitcast.5), calls=%async_computation | async-start | bytes 4423680 | tf_op jit(solution)/shard_map/all_to_all | solution.py:185
  31.2 0.3 copy.18
  31.5 2.1 %collective-permute-start = (bf16[128,2560]{0,1:T(8,128)(2,1)S(1)}, bf16[128,2560]{0,1:T(8,128)(2,1)S(1)}, u32[]{:S(2)}, u32[]{:S(2)}) collective-permute-start(bf16[128,2560]{0,1:T(8,128)(2,1)S(1)} %copy.18), channel_id=1, source_target_pairs={{0,16},{16,0},{1,17},{17,1},{2,18},{18,2},{3,19},{19,3},{4,20},{20... | collective-permute-start | bytes 1966088 | tf_op jit(solution)/shard_map/ppermute | solution.py:21
  33.7 2.3 %collective-permute-start.1 = (bf16[216,128]{1,0:T(8,128)(2,1)S(1)}, bf16[216,128]{1,0:T(8,128)(2,1)S(1)}, u32[]{:S(2)}, u32[]{:S(2)}) collective-permute-start(bf16[216,128]{1,0:T(8,128)(2,1)S(1)} %get-tuple-element.44), channel_id=1, source_target_pairs={{0,16},{16,0},{1,17},{17,1},{2,18},{18,2},{3,19},{19,3},{4,20},{20... | collective-permute-start | bytes 165896 | tf_op jit(solution)/shard_map/ppermute | solution.py:21
  35.9 0.9 collective-permute-done.1
  36.8 0.0 copy-start.8
  36.8 0.1 maximum_bitcast_fusion.x_ref
  37.0 0.5 copy-done.8
  37.5 0.4 broadcast_in_dim.4.gain_ref
  37.9 0.7 copy-done
  38.6 0.6 shard_map.92
  39.2 19.7 %all-to-all-done.weight_ref = bf16[8,216,640]{2,1,0:T(8,128)(2,1)} async-done(((bf16[8,216,640]{2,1,0:T(8,128)(2,1)}), bf16[8,216,640]{2,1,0:T(8,128)(2,1)}, u32[]{:S(2)}, u32[]{:S(2)}) %all-to-all-start) | async-done | bytes 2211872 | tf_op jit(solution)/shard_map/all_to_all | solution.py:185
  58.9 3.8 %shard_map.93 = (bf16[216,128]{1,0:T(8,128)(2,1)S(1)}, bf16[2,216,256]{2,1,0:T(8,128)(2,1)S(1)}, f32[2560,128]{1,0:T(8,128)S(1)}, bf16[2784,128]{1,0:T(8,128)(2,1)S(1)}) custom-call(bf16[2784,256]{1,0:T(8,128)(2,1)S(1)} %get-tuple-element.21.normed_ref, bf16[8,216,640]{2,1,0:T(8,128)(2,1)} %all-to-all-done.weight_ref), custom_call_target="tpu_custom_call" | custom-call | tf_op jit(solution)/shard_map/pallas_call | solution.py:198
  62.7 2.8 %collective-permute-start.2 = (bf16[2784,128]{1,0:T(8,128)(2,1)S(1)}, bf16[2784,128]{1,0:T(8,128)(2,1)S(1)}, u32[]{:S(2)}, u32[]{:S(2)}) collective-permute-start(bf16[2784,128]{1,0:T(8,128)(2,1)S(1)} %get-tuple-element.23), channel_id=1, source_target_pairs={{0,16},{16,0},{1,17},{17,1},{2,18},{18,2},{3,19},{19,3},{4,20},{20... | collective-permute-start | bytes 2138120 | tf_op jit(solution)/shard_map/ppermute | solution.py:21
  65.5 1.7 %collective-permute-done.2.other_ref = bf16[2784,128]{1,0:T(8,128)(2,1)S(1)} collective-permute-done((bf16[2784,128]{1,0:T(8,128)(2,1)S(1)}, bf16[2784,128]{1,0:T(8,128)(2,1)S(1)}, u32[]{:S(2)}, u32[]{:S(2)}) %collective-permute-start.2) | collective-permute-done | bytes 712736 | tf_op jit(solution)/shard_map/ppermute | solution.py:21
  67.2 0.8 shard_map.94
  68.1 0.9 copy-done.5
  69.0 4.4 %all-to-all-start.1 = ((bf16[8,352,128]{2,1,0:T(8,128)(2,1)}), bf16[8,352,128]{2,1,0:T(8,128)(2,1)}, u32[]{:S(2)}, u32[]{:S(2)}) async-start(bf16[8,352,128]{2,1,0:T(8,128)(2,1)} %bitcast.37), calls=%async_computation.1 | async-start | bytes 1441792 | tf_op jit(solution)/shard_map/all_to_all | solution.py:236
  73.4 1.2 shard_map.95
  74.6 1.4 %shard_map.96 = (bf16[2,216,640]{2,1,0:T(8,128)(2,1)}, bf16[2,216,640]{2,1,0:T(8,128)(2,1)}) custom-call(s32[1]{0:T(128)} %bitcast.11.spot_ref, bf16[2784,256]{1,0:T(8,128)(2,1)S(1)} %get-tuple-element.21.normed_ref, bf16[2,216,256]{2,1,0:T(8,128)(2,1)S(1)} %copy-done.3), custom_call_target="tpu_custom_call" | custom-call | tf_op jit(solution)/shard_map/pallas_call | solution.py:210
  76.1 2.0 %collective-permute-start.3 = (bf16[2,216,640]{2,1,0:T(8,128)(2,1)}, bf16[2,216,640]{2,1,0:T(8,128)(2,1)S(1)}, u32[]{:S(2)}, u32[]{:S(2)}) collective-permute-start(bf16[2,216,640]{2,1,0:T(8,128)(2,1)} %shard_map.95), channel_id=1, source_target_pairs={{0,256},{128,384},{256,0},{384,128},{1,257},{129,385},{257,1},{385... | collective-permute-start | bytes 1658888 | tf_op jit(solution)/shard_map/ppermute | solution.py:29
  78.1 3.3 %collective-permute-start.4 = (bf16[2,216,640]{2,1,0:T(8,128)(2,1)}, bf16[2,216,640]{2,1,0:T(8,128)(2,1)}, u32[]{:S(2)}, u32[]{:S(2)}) collective-permute-start(bf16[2,216,640]{2,1,0:T(8,128)(2,1)} %get-tuple-element.29), channel_id=1, source_target_pairs={{0,128},{128,256},{256,384},{384,0},{1,129},{129,257},{257,385},{3... | collective-permute-start | bytes 1658888 | tf_op jit(solution)/shard_map/ppermute | solution.py:29
  81.4 3.2 %collective-permute-start.5 = (bf16[2,216,640]{2,1,0:T(8,128)(2,1)}, bf16[2,216,640]{2,1,0:T(8,128)(2,1)}, u32[]{:S(2)}, u32[]{:S(2)}) collective-permute-start(bf16[2,216,640]{2,1,0:T(8,128)(2,1)} %get-tuple-element.30), channel_id=1, source_target_pairs={{0,384},{128,0},{256,128},{384,256},{1,385},{129,1},{257,129},{385... | collective-permute-start | bytes 1658888 | tf_op jit(solution)/shard_map/ppermute | solution.py:29
  84.6 0.9 copy-done.4
  85.5 0.4 shard_map.97.own_ref
  85.9 9.8 %all-to-all-done.1 = bf16[8,352,128]{2,1,0:T(8,128)(2,1)} async-done(((bf16[8,352,128]{2,1,0:T(8,128)(2,1)}), bf16[8,352,128]{2,1,0:T(8,128)(2,1)}, u32[]{:S(2)}, u32[]{:S(2)}) %all-to-all-start.1) | async-done | bytes 720928 | tf_op jit(solution)/shard_map/all_to_all | solution.py:236
  95.7 1.2 convert_reduce_fusion
  96.9 0.1 fusion
  97.1 10.3 %psum.14 = f32[2,160]{1,0:T(2,128)S(1)} all-reduce(f32[2,160]{1,0:T(2,128)S(1)} %fusion), channel_id=1, replica_groups=mesh['x'=4,'z'=4,'c'=2,'y'=8,'h'=2] {'z'}, use_global_device_ids=true, to_apply=%region_2.3 | all-reduce | flops 320 | bytes 2560 | tf_op jit(solution)/shard_map/psum | solution.py:248
  107.4 2.5 %shard_map.98 = bf16[640,432]{1,0:T(8,128)(2,1)} custom-call(f32[2,216,640]{2,1,0:T(8,128)S(1)} %shard_map.97.own_ref, bf16[2,216,640]{2,1,0:T(8,128)(2,1)S(1)} %collective-permute-done.3.first_ref, bf16[2,216,640]{2,1,0:T(8,128)(2,1)} %collective-permute-done.4.second_ref, bf16[2,216,640]{2,1,0:T(8,128)(2,1)} %collective-permute-done.5.third_ref), custom_call_target="tpu_custom_call" | custom-call | tf_op jit(solution)/shard_map/pallas_call | solution.py:250
  110.0 7.9 %collective-permute-start.6 = (f32[165,128]{1,0:T(8,128)S(1)}, f32[165,128]{1,0:T(8,128)S(1)}, u32[]{:S(2)}, u32[]{:S(2)}) collective-permute-start(f32[165,128]{1,0:T(8,128)S(1)} %select_bitcast_fusion), channel_id=1, source_target_pairs={{0,1},{1,0},{2,3},{3,2},{4,5},{5,4},{6,7},{7,6},{8,9},{9,8},{10,11... | collective-permute-start | bytes 253448 | tf_op jit(solution)/shard_map/ppermute | solution.py:21
  117.9 6.2 %all-to-all-start.2 = ((bf16[8,80,432]{2,1,0:T(8,128)(2,1)}), bf16[8,80,432]{2,1,0:T(8,128)(2,1)S(1)}, u32[]{:S(2)}, u32[]{:S(2)}) async-start(bf16[8,80,432]{2,1,0:T(8,128)(2,1)} %bitcast.12), calls=%async_computation.2 | async-start | bytes 1310720 | tf_op jit(solution)/shard_map/all_to_all | solution.py:277
  124.1 0.1 dynamic_slice.7
  124.2 6.9 %psum.15 = f32[160]{0:T(256)S(1)} all-reduce(f32[160]{0:T(256)S(1)} %bitcast.44), channel_id=1, replica_groups=mesh['x'=4,'z'=4,'c'=2,'y'=8,'h'=2] {'x'}, use_global_device_ids=true, to_apply=%region_4.5 | all-reduce | flops 160 | bytes 1280 | tf_op jit(solution)/shard_map/psum | solution.py:264
  131.1 4.0 %collective-permute-start.7 = (f32[160]{0:T(256)S(1)}, f32[160]{0:T(256)S(1)}, u32[]{:S(2)}, u32[]{:S(2)}) collective-permute-start(f32[160]{0:T(256)S(1)} %psum.15), channel_id=1, source_target_pairs={{0,16},{16,0},{1,17},{17,1},{2,18},{18,2},{3,19},{19,3},{4,20},{20... | collective-permute-start | bytes 1928 | tf_op jit(solution)/shard_map/ppermute | solution.py:21
  135.1 0.7 fusion.5
  135.8 0.1 collective-permute-done.7
  135.9 0.6 add.35
  136.5 5.1 %all-to-all-done.2 = bf16[8,80,432]{2,1,0:T(8,128)(2,1)S(1)} async-done(((bf16[8,80,432]{2,1,0:T(8,128)(2,1)}), bf16[8,80,432]{2,1,0:T(8,128)(2,1)S(1)}, u32[]{:S(2)}, u32[]{:S(2)}) %all-to-all-start.2) | async-done | bytes 552992 | tf_op jit(solution)/shard_map/all_to_all | solution.py:277
  141.6 0.1 convert_reduce_fusion.1
  141.7 0.1 slice_bitcast_fusion.1
  141.8 0.9 pad_maximum_fusion.2
  (31 shorter events, 0.2 us)
Async XLA Ops:
  21.9 9.3 %copy-start.6 = (bf16[128,2560]{1,0:T(8,128)(2,1)S(1)}, bf16[128,2560]{1,0:T(8,128)(2,1)}, u32[]{:S(2)}) copy-start(bf16[128,2560]{1,0:T(8,128)(2,1)} %param.5) | copy-start | bytes 1966084
  21.9 37.0 %all-to-all-start = ((bf16[8,216,640]{2,1,0:T(8,128)(2,1)}), bf16[8,216,640]{2,1,0:T(8,128)(2,1)}, u32[]{:S(2)}, u32[]{:S(2)}) async-start(bf16[8,216,640]{2,1,0:T(8,128)(2,1)} %bitcast.5), calls=%async_computation | async-start | bytes 4423680 | tf_op jit(solution)/shard_map/all_to_all | solution.py:185
  31.2 2.4 %copy-start.7 = (bf16[128,432]{0,1:T(8,128)(2,1)S(1)}, bf16[128,432]{0,1:T(8,128)(2,1)}, u32[]{:S(2)}) copy-start(bf16[128,432]{0,1:T(8,128)(2,1)} %param.9) | copy-start | bytes 331780
  31.5 5.3 %collective-permute-start = (bf16[128,2560]{0,1:T(8,128)(2,1)S(1)}, bf16[128,2560]{0,1:T(8,128)(2,1)S(1)}, u32[]{:S(2)}, u32[]{:S(2)}) collective-permute-start(bf16[128,2560]{0,1:T(8,128)(2,1)S(1)} %copy.18), channel_id=1, source_target_pairs={{0,16},{16,0},{1,17},{17,1},{2,18},{18,2},{3,19},{19,3},{4,20},{20... | collective-permute-start | bytes 1966088 | tf_op jit(solution)/shard_map/ppermute | solution.py:21
  33.7 3.1 %collective-permute-start.1 = (bf16[216,128]{1,0:T(8,128)(2,1)S(1)}, bf16[216,128]{1,0:T(8,128)(2,1)S(1)}, u32[]{:S(2)}, u32[]{:S(2)}) collective-permute-start(bf16[216,128]{1,0:T(8,128)(2,1)S(1)} %get-tuple-element.44), channel_id=1, source_target_pairs={{0,16},{16,0},{1,17},{17,1},{2,18},{18,2},{3,19},{19,3},{4,20},{20... | collective-permute-start | bytes 165896 | tf_op jit(solution)/shard_map/ppermute | solution.py:21
  36.8 0.7 copy-start.8
  37.5 1.1 copy-start
  58.9 6.6 %copy-start.1 = (bf16[2560,256]{1,0:T(8,128)(2,1)S(1)}, bf16[2560,256]{1,0:T(8,128)(2,1)}, u32[]{:S(2)}) copy-start(bf16[2560,256]{1,0:T(8,128)(2,1)} %copy-done) | copy-start | bytes 3932164
  62.7 5.4 %copy-start.2 = (bf16[2,216,256]{2,1,0:T(8,128)(2,1)}, bf16[2,216,256]{2,1,0:T(8,128)(2,1)S(1)}, u32[]{:S(2)}) copy-start(bf16[2,216,256]{2,1,0:T(8,128)(2,1)S(1)} %get-tuple-element.28.back_ref) | copy-start | bytes 663556
  62.7 4.6 %collective-permute-start.2 = (bf16[2784,128]{1,0:T(8,128)(2,1)S(1)}, bf16[2784,128]{1,0:T(8,128)(2,1)S(1)}, u32[]{:S(2)}, u32[]{:S(2)}) collective-permute-start(bf16[2784,128]{1,0:T(8,128)(2,1)S(1)} %get-tuple-element.23), channel_id=1, source_target_pairs={{0,16},{16,0},{1,17},{17,1},{2,18},{18,2},{3,19},{19,3},{4,20},{20... | collective-permute-start | bytes 2138120 | tf_op jit(solution)/shard_map/ppermute | solution.py:21
  68.1 0.9 copy-start.5
  69.0 4.4 %copy-start.3 = (bf16[2,216,256]{2,1,0:T(8,128)(2,1)S(1)}, bf16[2,216,256]{2,1,0:T(8,128)(2,1)}, u32[]{:S(2)}) copy-start(bf16[2,216,256]{2,1,0:T(8,128)(2,1)} %copy-done.2) | copy-start | bytes 663556
  69.0 26.7 %all-to-all-start.1 = ((bf16[8,352,128]{2,1,0:T(8,128)(2,1)}), bf16[8,352,128]{2,1,0:T(8,128)(2,1)}, u32[]{:S(2)}, u32[]{:S(2)}) async-start(bf16[8,352,128]{2,1,0:T(8,128)(2,1)} %bitcast.37), calls=%async_computation.1 | async-start | bytes 1441792 | tf_op jit(solution)/shard_map/all_to_all | solution.py:236
  76.1 31.3 %collective-permute-start.3 = (bf16[2,216,640]{2,1,0:T(8,128)(2,1)}, bf16[2,216,640]{2,1,0:T(8,128)(2,1)S(1)}, u32[]{:S(2)}, u32[]{:S(2)}) collective-permute-start(bf16[2,216,640]{2,1,0:T(8,128)(2,1)} %shard_map.95), channel_id=1, source_target_pairs={{0,256},{128,384},{256,0},{384,128},{1,257},{129,385},{257,1},{385... | collective-permute-start | bytes 1658888 | tf_op jit(solution)/shard_map/ppermute | solution.py:29
  78.1 29.3 %collective-permute-start.4 = (bf16[2,216,640]{2,1,0:T(8,128)(2,1)}, bf16[2,216,640]{2,1,0:T(8,128)(2,1)}, u32[]{:S(2)}, u32[]{:S(2)}) collective-permute-start(bf16[2,216,640]{2,1,0:T(8,128)(2,1)} %get-tuple-element.29), channel_id=1, source_target_pairs={{0,128},{128,256},{256,384},{384,0},{1,129},{129,257},{257,385},{3... | collective-permute-start | bytes 1658888 | tf_op jit(solution)/shard_map/ppermute | solution.py:29
  81.4 26.0 %collective-permute-start.5 = (bf16[2,216,640]{2,1,0:T(8,128)(2,1)}, bf16[2,216,640]{2,1,0:T(8,128)(2,1)}, u32[]{:S(2)}, u32[]{:S(2)}) collective-permute-start(bf16[2,216,640]{2,1,0:T(8,128)(2,1)} %get-tuple-element.30), channel_id=1, source_target_pairs={{0,384},{128,0},{256,128},{384,256},{1,385},{129,1},{257,129},{385... | collective-permute-start | bytes 1658888 | tf_op jit(solution)/shard_map/ppermute | solution.py:29
  84.6 0.9 copy-start.4
  110.0 14.2 %collective-permute-start.6 = (f32[165,128]{1,0:T(8,128)S(1)}, f32[165,128]{1,0:T(8,128)S(1)}, u32[]{:S(2)}, u32[]{:S(2)}) collective-permute-start(f32[165,128]{1,0:T(8,128)S(1)} %select_bitcast_fusion), channel_id=1, source_target_pairs={{0,1},{1,0},{2,3},{3,2},{4,5},{5,4},{6,7},{7,6},{8,9},{9,8},{10,11... | collective-permute-start | bytes 253448 | tf_op jit(solution)/shard_map/ppermute | solution.py:21
  117.9 23.6 %all-to-all-start.2 = ((bf16[8,80,432]{2,1,0:T(8,128)(2,1)}), bf16[8,80,432]{2,1,0:T(8,128)(2,1)S(1)}, u32[]{:S(2)}, u32[]{:S(2)}) async-start(bf16[8,80,432]{2,1,0:T(8,128)(2,1)} %bitcast.12), calls=%async_computation.2 | async-start | bytes 1310720 | tf_op jit(solution)/shard_map/all_to_all | solution.py:277
  131.1 4.8 %collective-permute-start.7 = (f32[160]{0:T(256)S(1)}, f32[160]{0:T(256)S(1)}, u32[]{:S(2)}, u32[]{:S(2)}) collective-permute-start(f32[160]{0:T(256)S(1)} %psum.15), channel_id=1, source_target_pairs={{0,16},{16,0},{1,17},{17,1},{2,18},{18,2},{3,19},{19,3},{4,20},{20... | collective-permute-start | bytes 1928 | tf_op jit(solution)/shard_map/ppermute | solution.py:21
